TPU v7x, 512 devices: a whole 4x8x8 slice. The times are simulated.
512 devices in a mesh: dp: 64 (over y, z_hi, core), mp: 8 (over z_lo, x).
Axes of the slice: x: 4, y: 8, z: 8 (z_hi: 4, z_lo: 2; z = z_hi * 2 + z_lo), core: 2. Of those that a mesh axis runs over, the one named last changes fastest.
Arguments:
- tokens: bfloat16 [24576, 3072], P('dp', 'mp'), may hold values from -6 to 6
- gain: bfloat16 [3072], P('mp'), may hold values from 0.099609375 to 1.8984375
- pre_act: bfloat16 [24576, 12288], P('dp', 'mp'), may hold values from -6 to 6
- w_in: bfloat16 [3072, 12288], P('dp', 'mp'), may hold values from -0.109375 to 0.109375
- act_cotangent: bfloat16 [24576, 12288], P('dp', 'mp'), may hold values from -6 to 6
Outputs:
- token_gradient: bfloat16 [24576, 3072], P('dp', 'mp')
- gain_gradient: float32 [3072], P('mp')
All inputs are finite; a program needn't handle non-finite values.
Results may differ from a plain program's by a relative error of at most 0.019.
Values may be sent and summed in bfloat16 or wider, within the bound.
No kernel may reach another device: no remote copies, remote signals or barrier semaphores. Data moves between devices by JAX's collectives and lax.ppermute only.
A program may use at most 64 MiB of HBM per device.

v0:
```python
import jax
import jax.numpy as jnp
from jax import lax
from jax.sharding import PartitionSpec as P


def gelu_exact(value):
    return jax.nn.gelu(value, approximate=False)


def on_device(tokens, gain, pre_act, w_in, act_cotangent):
    rows_bf, gain_row = (
        lax.all_gather(tokens, "mp", axis=1, tiled=True),
        lax.all_gather(gain.reshape(1, -1), "mp", axis=1, tiled=True),
    )
    local_share = tokens.shape[1]
    offset_value = lax.axis_index("mp") * local_share
    rows = rows_bf.astype(jnp.float32)
    mean_row = jnp.mean(rows, axis=1, keepdims=True)
    centered_input = rows - mean_row
    inverse_deviation = 1.0 / jnp.sqrt(
        jnp.mean(centered_input * centered_input, axis=1, keepdims=True) + 1e-06
    )
    standardized = centered_input * inverse_deviation
    gain_complete = gain_row[0].astype(jnp.float32)
    act_f, gelu_back = jax.vjp(gelu_exact, pre_act.astype(jnp.float32))
    d_pre = gelu_back(act_cotangent.astype(jnp.float32))[0].astype(jnp.bfloat16)
    partial_rows = lax.dot_general(
        d_pre,
        lax.all_gather(w_in, "dp", axis=0, tiled=True),
        (((1,), (1,)), ((), ())),
        preferred_element_type=jnp.float32,
    )
    partial_rows = partial_rows.astype(jnp.bfloat16).astype(jnp.float32)
    standardized_share = lax.dynamic_slice_in_dim(standardized, offset_value, local_share, 1)
    normed_gradient = lax.psum(partial_rows.astype(jnp.bfloat16), "mp").astype(jnp.float32)
    scaled_rows = normed_gradient * gain_complete
    first_moment = jnp.mean(scaled_rows, axis=1, keepdims=True)
    second_moment = jnp.mean(scaled_rows * standardized, axis=1, keepdims=True)
    complete_gradient = inverse_deviation * (
        scaled_rows - first_moment - standardized * second_moment
    )
    token_gradient = lax.dynamic_slice_in_dim(
        complete_gradient, offset_value, local_share, 1
    ).astype(jnp.bfloat16)
    share_gradient = lax.dynamic_slice_in_dim(normed_gradient, offset_value, local_share, 1)
    gain_gradient = lax.psum(jnp.sum(share_gradient * standardized_share, axis=0), "dp")
    return (token_gradient, gain_gradient)


def solution(mesh):
    placed = (P("dp", "mp"), P("mp"), P("dp", "mp"), P("dp", "mp"), P("dp", "mp"))
    return jax.shard_map(
        on_device, mesh=mesh, in_specs=placed, out_specs=(P("dp", "mp"), P("mp")), check_vma=False
    )
```

profile of v0, /device:TPU:1, one launch (start us, length us, event | category | flops | bytes accessed | tf_op | source)
XLA Modules:
  0.0 418.6 jit_solution(6743782993166762084)
XLA Ops:
  7.2 0.0 all-gather.7.cloned.1.call-start
  7.2 0.7 all-gather.7.cloned.1.call-update
  7.9 0.0 all-gather.5.cloned.1.call-start
  7.9 0.7 all-gather.5.cloned.1.call-update
  8.6 0.0 all-reduce.2.cloned.1.call-start
  8.7 117.1 %all-gather.7.cloned.1.call-done = bf16[3072,1536]{1,0:T(8,128)(2,1)} async-done(((bf16[48,1536]{1,0:T(8,128)(2,1)}), bf16[3072,1536]{1,0:T(8,128)(2,1)}) %all-gather.7.cloned.1.call-update) | async-done | bytes 9437200 | tf_op jit(solution)/shard_map/all_gather | solution.py:30
  125.8 16.1 %convolution_convert_fusion = bf16[384,3072]{1,0:T(8,128)(2,1)} fusion(bf16[3072,1536]{1,0:T(8,128)(2,1)} %all-gather.7.cloned.1.call-done, bf16[384,1536]{1,0:T(8,128)(2,1)} %param.9, bf16[384,1536]{1,0:T(8,128)(2,1)} %param.7), kind=kOutput, calls=%fused_computation.6 | convolution fusion | flops 3668705280 | bytes 14155776 | tf_op jit(solution)/shard_map/dot_general | solution.py:28
  141.9 0.0 copy-start.2
  141.9 0.0 all-reduce.2.cloned.1.call-update
  142.0 0.6 copy-done.2
  142.6 21.1 %all-gather.1 = bf16[8,1,384]{2,1,0:T(2,128)(2,1)S(1)} all-gather(bf16[1,1,384]{2,1,0:T(2,128)(2,1)S(1)} %reshape.33), channel_id=2, replica_groups=mesh['dp'=64,'mp'=8] {'mp'}, dimensions={0}, use_global_device_ids=true | all-gather | bytes 6912 | tf_op jit(solution)/shard_map/all_gather | solution.py:14
  163.7 3.0 all-gather.5.cloned.1.call-done
  166.7 0.0 copy-start
  166.7 2.2 convert_reduce_fusion
  169.0 0.2 copy-done
  169.1 0.8 fusion.2
  169.9 95.2 %all-reduce.2.cloned.1.call-done = bf16[384,3072]{1,0:T(8,128)(2,1)} async-done(((bf16[384,3072]{1,0:T(8,128)(2,1)}), bf16[384,3072]{1,0:T(8,128)(2,1)}) %all-reduce.2.cloned.1.call-update) | async-done | bytes 2359312 | tf_op jit(solution)/shard_map/psum | solution.py:36
  265.1 0.0 copy-start.1
  265.1 3.1 fusion.40
  268.2 0.0 copy-done.1
  268.2 0.6 convert_element_type.30
  268.8 1.0 multiply_reduce_fusion.1
  269.7 142.4 %psum.15 = f32[384]{0:T(512)} all-reduce(f32[384]{0:T(512)S(1)} %get-tuple-element.4), channel_id=1, replica_groups=mesh['dp'=64,'mp'=8] {'dp'}, use_global_device_ids=true, to_apply=%region_6.0 | all-reduce | flops 384 | bytes 3072 | tf_op jit(solution)/shard_map/psum | solution.py:47
  (5 shorter events, 0.0 us)
Async XLA Ops:
  7.2 118.6 %all-gather.7.cloned.1.call-start = ((), (), s32[]{:S(2)}) async-start(), calls=%async_computation.1 | async-start | bytes 9584640 | tf_op jit(solution)/shard_map/all_gather | solution.py:30
  7.9 158.8 %all-gather.5.cloned.1.call-start = ((), (), s32[]{:S(2)}) async-start(), calls=%async_computation | async-start | bytes 2654208 | tf_op jit(solution)/shard_map/all_gather | solution.py:13
  8.6 256.4 %all-reduce.2.cloned.1.call-start = ((), (), s32[]{:S(2)}) async-start(), calls=%async_computation.2 | async-start | bytes 4718592 | tf_op jit(solution)/shard_map/psum | solution.py:36
  141.9 0.7 copy-start.2
  166.7 2.4 copy-start
  265.1 3.2 copy-start.1
Sparse Core Ops, SparseCore 0:
  11.3 114.4 all-gather.6
  127.9 38.8 all-gather.4
  169.7 95.2 all-reduce.1
where the time goes:
time: 420 us; the launch traced here: 419 us
  waiting for transfers between devices  217 us (52%)
  blocking collectives  163 us (39%)
  matrix products  16.1 us (4%)
  between operations  13.8 us (3%)
  other arithmetic  7.65 us (2%)
    psum x1, blocking collectives, on_device(): lax.psum(jnp.sum(share_gradient * standardized_share, axis=0), 'dp')  142 us
    all_gather x1, waiting for transfers between devices, on_device(): lax.all_gather(w_in, 'dp', axis=0, tiled=True)  117 us
    psum x1, waiting for transfers between devices, on_device(): lax.psum(partial_rows.astype(jnp.bfloat16), 'mp').astype(jnp.float32)  95.2 us
    all_gather x1, blocking collectives, on_device(): lax.all_gather(gain.reshape(1, -1), 'mp', axis=1, tiled=True)  21.1 us
    dot_general x1, matrix products, on_device(): lax.dot_general(d_pre, lax.all_gather(w_in, 'dp', axis=0, tiled=True), ((...  16.1 us
  transfers between devices with their start and end apart: 3, of which 3 were waited for; matrix products, arithmetic and copies ran while one was open for 5% of the time, Pallas kernels for 0%

commit v1 on v0

v1 whole, which is shorter than its diff:
```python
import jax
import jax.numpy as jnp
from jax import lax
from jax.experimental import pallas as pl
from jax.experimental.pallas import tpu as pltpu
from jax.sharding import Mesh, PartitionSpec as P

NAMES = ("y", "zh", "c", "zl", "x")
SIZES = (8, 4, 2, 2, 4)
DP, MP = ("y", "zh", "c"), ("zl", "x")
F32, BF16 = jnp.float32, jnp.bfloat16


def gelu_exact(value):
    return jax.nn.gelu(value, approximate=False)


def spread(row, axes, n):
    return lax.all_to_all(jnp.broadcast_to(row, (n,) + row.shape), axes, 0, 0)


def matmul_kernel(w_ref, d_ref, out_ref):
    out_ref[...] = lax.dot_general(
        w_ref[...], d_ref[0], (((1,), (1,)), ((), ())), preferred_element_type=F32
    ).astype(BF16)[None, None]


def partial_products(w_half, d_pair):
    rows, hidden = w_half.shape
    block, tokens = rows // 8, d_pair.shape[1]
    return pl.pallas_call(
        matmul_kernel,
        grid=(2, 8),
        in_specs=[
            pl.BlockSpec((block, hidden), lambda t, m: (m, 0)),
            pl.BlockSpec((1, tokens, hidden), lambda t, m: (t, 0, 0)),
        ],
        out_specs=pl.BlockSpec((1, 1, block, tokens), lambda t, m: (t, m, 0, 0)),
        out_shape=jax.ShapeDtypeStruct((2, 8, block, tokens), BF16),
        compiler_params=pltpu.CompilerParams(vmem_limit_bytes=32 * 1024 * 1024),
        cost_estimate=pl.CostEstimate(
            flops=4 * rows * hidden * tokens, bytes_accessed=12 << 20, transcendentals=0
        ),
    )(w_half, d_pair)


def sum_kernel(parts_ref, xhat_ref, gain_ref, d_ref, moments_ref, share_ref):
    first, second = 0.0, 0.0
    for z in range(4):
        for c in range(2):
            total = parts_ref[c * 8, pl.ds(z * 48, 48), :].astype(F32)
            for m in range(1, 8):
                total += parts_ref[c * 8 + m, pl.ds(z * 48, 48), :].astype(F32)
            at = pl.ds((z * 2 + c) * 48, 48)
            d_ref[at, :] = total
            xhat = xhat_ref[at, :]
            product = total * xhat
            share_ref[at, :] = jnp.sum(product, axis=1, keepdims=True)
            first += jnp.sum(total * gain_ref[at, :], axis=0, keepdims=True)
            second += jnp.sum(product * gain_ref[at, :], axis=0, keepdims=True)
    moments_ref[...] = jnp.concatenate([first, second, jnp.zeros((6, first.shape[1]), F32)], axis=0)


def final_kernel(d_ref, xhat_ref, gain_ref, moments_ref, rstd_ref, out_ref):
    both = moments_ref[0]
    for m in range(1, 8):
        both += moments_ref[m]
    both = both * (1.0 / 3072)
    g = d_ref[...] * gain_ref[...]
    value = rstd_ref[...] * (g - both[0:1] - xhat_ref[...] * both[1:2])
    out_ref[...] = value.T.astype(BF16)


def on_device(tokens, gain, pre_act, w_in, act_cotangent):
    rows, share = tokens.shape
    core = lax.axis_index("c")

    w_half = lax.all_gather(w_in, "zh", axis=0, tiled=True)
    w_half = lax.all_gather(w_half, "y", axis=0, tiled=True)

    x = tokens.astype(F32).T
    local_mean = jnp.mean(x, axis=0, keepdims=True)
    local_square = jnp.sum((x - local_mean) ** 2, axis=0, keepdims=True)
    stats = spread(jnp.concatenate([local_mean, local_square] * 4, axis=0), MP, 8)
    means, squares = stats[:, 0], stats[:, 1]
    mean = jnp.mean(means, axis=0, keepdims=True)
    variance = (
        jnp.sum(squares, axis=0, keepdims=True)
        + share * jnp.sum((means - mean) ** 2, axis=0, keepdims=True)
    ) / (8 * share)
    rstd = 1.0 / jnp.sqrt(variance + 1e-06)
    xhat = (x - mean) * rstd
    gain_column = gain.astype(F32)[:, None]

    _, gelu_back = jax.vjp(gelu_exact, pre_act.astype(F32))
    d_pre = gelu_back(act_cotangent.astype(F32))[0].astype(BF16)
    other = lax.ppermute(d_pre, "c", [(0, 1), (1, 0)])
    d_pair = jnp.stack([jnp.where(core == 0, d_pre, other), jnp.where(core == 0, other, d_pre)])

    parts = partial_products(w_half, d_pair)
    parts = parts.reshape(16, share // 2, rows)
    parts = lax.all_to_all(parts, ("c", "zl", "x"), 0, 0)

    d_normed, moments, gain_share = pl.pallas_call(
        sum_kernel,
        out_shape=[
            jax.ShapeDtypeStruct((share, rows), F32),
            jax.ShapeDtypeStruct((8, rows), F32),
            jax.ShapeDtypeStruct((share, 1), F32),
        ],
        compiler_params=pltpu.CompilerParams(vmem_limit_bytes=32 * 1024 * 1024),
    )(parts, xhat, gain_column)

    moments = spread(moments, MP, 8)
    token_gradient = pl.pallas_call(
        final_kernel,
        out_shape=jax.ShapeDtypeStruct((rows, share), BF16),
        compiler_params=pltpu.CompilerParams(vmem_limit_bytes=32 * 1024 * 1024),
    )(d_normed, xhat, gain_column, moments, rstd)

    gain_share = jnp.pad(gain_share.reshape(3, 128), ((0, 5), (0, 0)))
    gain_gradient = jnp.sum(spread(gain_share, DP, 64), axis=0)[:3].reshape(share)
    return (token_gradient, gain_gradient)


def solution(mesh):
    fine = Mesh(mesh.devices.reshape(SIZES), NAMES)
    placed = (P(DP, MP), P(MP), P(DP, MP), P(DP, MP), P(DP, MP))
    return jax.shard_map(
        on_device, mesh=fine, in_specs=placed, out_specs=(P(DP, MP), P(MP)), check_vma=False
    )
```

time: 420 us -> 190 us (0.45)
  blocking collectives: 163 us -> 22.2 us
  waiting for transfers between devices: 217 us -> 93.8 us
  starting transfers between devices: 0.11 us -> 32.8 us
  matrix products: 16.1 us -> 0 us
  Pallas kernels: 0 us -> 10.4 us
  local copies, waits for them, and re-layouts: 0.82 us -> 8.57 us
    psum x1 -> x0, blocking collectives: 142 us -> none  [on_device(): lax.psum(jnp.sum(share_gradient * standardized_share, axis=0), 'dp')]
    psum x1 -> x0, waiting for transfers between devices: 95.2 us -> none  [on_device(): lax.psum(partial_rows.astype(jnp.bfloat16), 'mp').astype(jnp.float32)]
    all_gather x2 -> x1, waiting for transfers between devices: 120 us -> 45 us  [on_device(): w_half = lax.all_gather(w_half, 'y', axis=0, tiled=True)]
    all_to_all x0 -> x4, waiting for transfers between devices: none -> 48.7 us  [the longest x1 30.1 us: on_device(): parts = lax.all_to_all(parts, ('c', 'zl', 'x'), 0, 0)]
    all_to_all x0 -> x4, starting transfers between devices: none -> 28 us  [the longest x3 21.9 us: spread(): return lax.all_to_all(jnp.broadcast_to(row, (n,) + row.shape), axes, 0, 0)]
    dot_general x1 -> x0, matrix products: 16.1 us -> none  [on_device(): lax.dot_general(d_pre, lax.all_gather(w_in, 'dp', axis=0, tiled=True), ((...]
    pallas_call x0 -> x3, Pallas kernels: none -> 10.4 us  [the longest x1 8.9 us: partial_products(): pl.pallas_call(matmul_kernel, grid=(2, 8), in_specs=[pl.BlockSpec((block,...]
    reduce_sum x4 -> x5, other arithmetic: 7.06 us -> 0.32 us  [the longest x1 0.11 us: on_device(): local_square = jnp.sum((x - local_mean) ** 2, axis=0, keepdims=True)]
  transfers between devices with their start and end apart: 3 -> 6, of which waited for: 3 -> 4; matrix products, arithmetic and copies ran while one was open for 5% -> 5% of each run, Pallas kernels for 0% -> 5%
where the time goes in v1:
time: 190 us
  waiting for transfers between devices  93.8 us (49%)
  starting transfers between devices  32.8 us (17%)
  blocking collectives  22.2 us (12%)
  between operations  14.2 us (7%)
  Pallas kernels  10.4 us (5%)
  local copies, waits for them, and re-layouts  8.57 us (5%)
  other arithmetic  7.73 us (4%)
    all_gather x1, waiting for transfers between devices, on_device(): w_half = lax.all_gather(w_half, 'y', axis=0, tiled=True)  45 us
    all_to_all x1, waiting for transfers between devices, on_device(): parts = lax.all_to_all(parts, ('c', 'zl', 'x'), 0, 0)  30.1 us
    all_gather x1, blocking collectives, on_device(): w_half = lax.all_gather(w_in, 'zh', axis=0, tiled=True)  22.2 us
    all_to_all x3, starting transfers between devices, spread(): return lax.all_to_all(jnp.broadcast_to(row, (n,) + row.shape), axes, 0, 0)  21.9 us
    all_to_all x3, waiting for transfers between devices, spread(): return lax.all_to_all(jnp.broadcast_to(row, (n,) + row.shape), axes, 0, 0)  18.7 us
    pallas_call x1, Pallas kernels, partial_products(): pl.pallas_call(matmul_kernel, grid=(2, 8), in_specs=[pl.BlockSpec((block,...  8.9 us
    convert_element_type x1, other arithmetic, on_device(): d_pre = gelu_back(act_cotangent.astype(F32))[0].astype(BF16)  6.81 us
    all_to_all x1, starting transfers between devices, on_device(): parts = lax.all_to_all(parts, ('c', 'zl', 'x'), 0, 0)  6.16 us
  transfers between devices with their start and end apart: 6, of which 4 were waited for; matrix products, arithmetic and copies ran while one was open for 5% of the time, Pallas kernels for 5%

profile of v1, /device:TPU:1, one launch (start us, length us, event | category | flops | bytes accessed | tf_op | source)
XLA Modules:
  0.0 189.6 jit_solution(936025876021587597)
XLA Ops:
  7.2 0.0 copy-start.4
  7.2 0.0 all-gather.2.cloned.1.call-start
  7.2 22.2 %all_gather.6 = bf16[192,1536]{1,0:T(8,128)(2,1)} all-gather(bf16[48,1536]{1,0:T(8,128)(2,1)} %param.8), channel_id=1, replica_groups=mesh['y'=8,'zh'=4,'c'=2,'zl'=2,'x'=4] {'zh'}, dimensions={0}, use_global_device_ids=true | all-gather | bytes 737280 | tf_op jit(solution)/shard_map/all_gather | solution.py:78
  29.4 0.0 all-gather.2.cloned.1.call-update
  29.4 6.8 %fusion.34 = bf16[384,1536]{1,0:T(8,128)(2,1)S(1)} fusion(bf16[384,1536]{1,0:T(8,128)(2,1)} %param.9, bf16[384,1536]{1,0:T(8,128)(2,1)} %param.7), kind=kLoop, calls=%fused_computation.39 | loop fusion | flops 43646976 | bytes 3538944 | tf_op jit(solution)/shard_map/convert_element_type | solution.py:96
  36.2 4.8 %collective-permute-start = (bf16[384,1536]{1,0:T(8,128)(2,1)S(1)}, bf16[384,1536]{1,0:T(8,128)(2,1)S(1)}, u32[]{:S(2)}, u32[]{:S(2)}) collective-permute-start(bf16[384,1536]{1,0:T(8,128)(2,1)S(1)} %fusion.34), channel_id=1, source_target_pairs={{0,8},{8,0},{1,9},{9,1},{2,10},{10,2},{3,11},{11,3},{4,12},{12,4},... | collective-permute-start | bytes 3538952 | tf_op jit(solution)/shard_map/ppermute | solution.py:97
  41.0 0.0 copy-done.4
  41.0 0.2 copy.14
  41.2 0.1 convert_reduce_fusion
  41.3 0.1 fusion.37
  41.5 0.7 broadcast_in_dim.22
  42.1 6.0 %all-to-all-start.1 = ((f32[8,8,384]{2,1,0:T(8,128)}), f32[8,8,384]{2,1,0:T(8,128)S(1)}, u32[]{:S(2)}, u32[]{:S(2)}) async-start(f32[8,8,384]{2,1,0:T(8,128)} %broadcast_in_dim.22), calls=%async_computation.1 | async-start | bytes 196608 | tf_op jit(solution)/shard_map/all_to_all | solution.py:19
  48.1 0.0 collective-permute-done
  48.1 0.2 select_bitcast_fusion.1
  48.3 0.2 pad_maximum_fusion.d_ref
  48.5 45.0 %all-gather.2.cloned.1.call-done.w_ref = bf16[1536,1536]{1,0:T(8,128)(2,1)} async-done(((bf16[192,1536]{1,0:T(8,128)(2,1)}), bf16[1536,1536]{1,0:T(8,128)(2,1)}) %all-gather.2.cloned.1.call-update) | async-done | bytes 4718608 | tf_op jit(solution)/shard_map/all_gather | solution.py:79
  93.5 0.0 copy-start.3
  93.5 2.3 %copy-done.3 = bf16[1536,1536]{1,0:T(8,128)(2,1)S(1)} copy-done((bf16[1536,1536]{1,0:T(8,128)(2,1)S(1)}, bf16[1536,1536]{1,0:T(8,128)(2,1)}, u32[]{:S(2)}) %copy-start.3) | copy-done | bytes 4718616
  95.9 8.9 %shard_map.68 = bf16[2,8,192,384]{3,2,1,0:T(8,128)(2,1)S(1)} custom-call(bf16[1536,1536]{1,0:T(8,128)(2,1)S(1)} %copy-done.3, bf16[2,384,1536]{2,1,0:T(8,128)(2,1)S(1)} %pad_maximum_fusion.d_ref), custom_call_target="tpu_custom_call" | custom-call | flops 3623878656 | bytes 12582912 | tf_op jit(solution)/shard_map/pallas_call | solution.py:31
  104.8 0.0 copy-start
  104.8 1.4 copy-done
  106.2 0.0 all-to-all-done.1
  106.2 0.0 copy-start.5
  106.2 6.2 %all-to-all-start = ((bf16[16,192,384]{2,1,0:T(8,128)(2,1)}), bf16[16,192,384]{2,1,0:T(8,128)(2,1)S(1)}, u32[]{:S(2)}, u32[]{:S(2)}) async-start(bf16[16,192,384]{2,1,0:T(8,128)(2,1)} %bitcast.16), calls=%async_computation | async-start | bytes 4718592 | tf_op jit(solution)/shard_map/all_to_all | solution.py:102
  112.3 0.0 copy-done.5
  112.3 0.1 reshape.68.gain_ref
  112.5 0.1 fusion.39.xhat_ref
  112.6 30.1 %all-to-all-done.parts_ref = bf16[16,192,384]{2,1,0:T(8,128)(2,1)S(1)} async-done(((bf16[16,192,384]{2,1,0:T(8,128)(2,1)}), bf16[16,192,384]{2,1,0:T(8,128)(2,1)S(1)}, u32[]{:S(2)}, u32[]{:S(2)}) %all-to-all-start) | async-done | bytes 2359328 | tf_op jit(solution)/shard_map/all_to_all | solution.py:102
  142.7 0.5 shard_map.69
  143.2 0.0 copy-start.1
  143.2 0.8 copy-done.1
  144.0 0.6 broadcast_in_dim.25
  144.7 4.2 %all-to-all-start.2 = ((f32[8,8,384]{2,1,0:T(8,128)}), f32[8,8,384]{2,1,0:T(8,128)S(1)}, u32[]{:S(2)}, u32[]{:S(2)}) async-start(f32[8,8,384]{2,1,0:T(8,128)} %broadcast_in_dim.25), calls=%async_computation.2 | async-start | bytes 196608 | tf_op jit(solution)/shard_map/all_to_all | solution.py:19
  148.8 0.1 reduce.4
  149.0 5.1 %all-to-all-done.2.moments_ref = f32[8,8,384]{2,1,0:T(8,128)S(1)} async-done(((f32[8,8,384]{2,1,0:T(8,128)}), f32[8,8,384]{2,1,0:T(8,128)S(1)}, u32[]{:S(2)}, u32[]{:S(2)}) %all-to-all-start.2) | async-done | bytes 98336 | tf_op jit(solution)/shard_map/all_to_all | solution.py:19
  154.1 0.7 broadcast_in_dim.26
  154.9 11.7 %all-to-all-start.3 = ((f32[64,8,128]{2,1,0:T(8,128)}), f32[64,8,128]{2,1,0:T(8,128)S(1)}, u32[]{:S(2)}, u32[]{:S(2)}) async-start(f32[64,8,128]{2,1,0:T(8,128)} %broadcast_in_dim.26), calls=%async_computation.3 | async-start | bytes 524288 | tf_op jit(solution)/shard_map/all_to_all | solution.py:19
  166.6 0.0 copy-start.2
  166.6 1.1 copy-done.2
  167.6 1.0 shard_map.70
  168.6 13.5 %all-to-all-done.3 = f32[64,8,128]{2,1,0:T(8,128)S(1)} async-done(((f32[64,8,128]{2,1,0:T(8,128)}), f32[64,8,128]{2,1,0:T(8,128)S(1)}, u32[]{:S(2)}, u32[]{:S(2)}) %all-to-all-start.3) | async-done | bytes 262176 | tf_op jit(solution)/shard_map/all_to_all | solution.py:19
  182.1 0.1 reduce_sum.59
  182.2 0.6 slice_bitcast_fusion
  (10 shorter events, 0.1 us)
Async XLA Ops:
  7.2 33.8 %copy-start.4 = (bf16[384,384]{1,0:T(8,128)(2,1)S(1)}, bf16[384,384]{1,0:T(8,128)(2,1)}, u32[]{:S(2)}) copy-start(bf16[384,384]{1,0:T(8,128)(2,1)} %param.5) | copy-start | bytes 884740
  7.2 86.3 %all-gather.2.cloned.1.call-start = ((), (), s32[]{:S(2)}) async-start(), calls=%async_computation.4 | async-start | bytes 5308416 | tf_op jit(solution)/shard_map/all_gather | solution.py:79
  36.2 11.9 %collective-permute-start = (bf16[384,1536]{1,0:T(8,128)(2,1)S(1)}, bf16[384,1536]{1,0:T(8,128)(2,1)S(1)}, u32[]{:S(2)}, u32[]{:S(2)}) collective-permute-start(bf16[384,1536]{1,0:T(8,128)(2,1)S(1)} %fusion.34), channel_id=1, source_target_pairs={{0,8},{8,0},{1,9},{9,1},{2,10},{10,2},{3,11},{11,3},{4,12},{12,4},... | collective-permute-start | bytes 3538952 | tf_op jit(solution)/shard_map/ppermute | solution.py:97
  42.1 64.0 %all-to-all-start.1 = ((f32[8,8,384]{2,1,0:T(8,128)}), f32[8,8,384]{2,1,0:T(8,128)S(1)}, u32[]{:S(2)}, u32[]{:S(2)}) async-start(f32[8,8,384]{2,1,0:T(8,128)} %broadcast_in_dim.22), calls=%async_computation.1 | async-start | bytes 196608 | tf_op jit(solution)/shard_map/all_to_all | solution.py:19
  93.5 2.3 %copy-start.3 = (bf16[1536,1536]{1,0:T(8,128)(2,1)S(1)}, bf16[1536,1536]{1,0:T(8,128)(2,1)}, u32[]{:S(2)}) copy-start(bf16[1536,1536]{1,0:T(8,128)(2,1)} %all-gather.2.cloned.1.call-done.w_ref) | copy-start | bytes 14155780
  104.8 1.4 copy-start
  106.2 6.2 %copy-start.5 = (bf16[384]{0:T(512)(128)(2,1)S(1)}, bf16[384]{0:T(512)(128)(2,1)}, u32[]{:S(2)}) copy-start(bf16[384]{0:T(512)(128)(2,1)} %param.6) | copy-start | bytes 2308
  106.2 36.5 %all-to-all-start = ((bf16[16,192,384]{2,1,0:T(8,128)(2,1)}), bf16[16,192,384]{2,1,0:T(8,128)(2,1)S(1)}, u32[]{:S(2)}, u32[]{:S(2)}) async-start(bf16[16,192,384]{2,1,0:T(8,128)(2,1)} %bitcast.16), calls=%async_computation | async-start | bytes 4718592 | tf_op jit(solution)/shard_map/all_to_all | solution.py:102
  143.2 0.8 copy-start.1
  144.7 9.5 %all-to-all-start.2 = ((f32[8,8,384]{2,1,0:T(8,128)}), f32[8,8,384]{2,1,0:T(8,128)S(1)}, u32[]{:S(2)}, u32[]{:S(2)}) async-start(f32[8,8,384]{2,1,0:T(8,128)} %broadcast_in_dim.25), calls=%async_computation.2 | async-start | bytes 196608 | tf_op jit(solution)/shard_map/all_to_all | solution.py:19
  154.9 27.3 %all-to-all-start.3 = ((f32[64,8,128]{2,1,0:T(8,128)}), f32[64,8,128]{2,1,0:T(8,128)S(1)}, u32[]{:S(2)}, u32[]{:S(2)}) async-start(f32[64,8,128]{2,1,0:T(8,128)} %broadcast_in_dim.26), calls=%async_computation.3 | async-start | bytes 524288 | tf_op jit(solution)/shard_map/all_to_all | solution.py:19
  166.6 1.1 copy-start.2
Sparse Core Ops, SparseCore 0:
  29.5 63.9 all-gather.1

commit v2 on v1

v2 whole, which is shorter than its diff:
```python
import jax
import jax.numpy as jnp
from jax import lax
from jax.experimental import pallas as pl
from jax.experimental.pallas import tpu as pltpu
from jax.sharding import Mesh, PartitionSpec as P

NAMES = ("y", "zh", "c", "zl", "x")
SIZES = (8, 4, 2, 2, 4)
DP, MP = ("y", "zh", "c"), ("zl", "x")
F32, BF16 = jnp.float32, jnp.bfloat16
SHARD = 48
MEMORY = 40 * 1024 * 1024
CHUNKS = ((0,), (1, 3, 2))


def gelu_exact(value):
    return jax.nn.gelu(value, approximate=False)


def spread(row, axes, n):
    return lax.all_to_all(jnp.broadcast_to(row, (n,) + row.shape), axes, 0, 0)


def shift(array, axis, n, by):
    return lax.ppermute(array, axis, [(i, (i - by) % n) for i in range(n)])


def ring(block, beside=None):
    pieces = [(0, 0, block)]
    behind = ahead = block
    for s in range(1, 4):
        if s == 3:
            behind, ahead, beside = lax.optimization_barrier((behind, ahead, beside))
        behind, ahead = shift(behind, "y", 8, -1), shift(ahead, "y", 8, 1)
        pieces += [(-s, 0, behind), (s, 0, ahead)]
    cut = (block.shape[0] // 2 + 15) // 16 * 16
    pieces += [
        (4, 0, shift(behind[:cut], "y", 8, -1)),
        (4, cut, shift(ahead[cut:], "y", 8, 1)),
    ]
    return pieces, beside


def products(pieces, rows, d_pair, here, name):
    tokens, hidden = d_pair.shape[2], d_pair.shape[1]

    def kernel(here_ref, d_ref, *refs):
        w_refs, out_ref = refs[:-1], refs[-1]
        every = jnp.concatenate([w[...] for w in w_refs], axis=0)
        product = jnp.dot(every, d_ref[0], preferred_element_type=F32).astype(BF16)
        at = 0
        for (offset, first, piece), w in zip(pieces, w_refs, strict=True):
            for k in range(max(piece.shape[0] // rows, 1)):
                height = min(piece.shape[0], rows)
                block = lax.rem(here_ref[0] + (offset + k) % 8, 8)
                out_ref[0, block, first : first + height] = product[at : at + height]
                at += height

    blocks = [w for _, _, w in pieces]
    with jax.named_scope(name):
        return pl.pallas_call(
            kernel,
            grid_spec=pltpu.PrefetchScalarGridSpec(
                num_scalar_prefetch=1,
                grid=(2,),
                in_specs=[pl.BlockSpec((1, hidden, tokens), lambda t, _: (t, 0, 0))]
                + [pl.BlockSpec(w.shape, lambda t, _: (0, 0)) for w in blocks],
                out_specs=pl.BlockSpec((1, 8, rows, tokens), lambda t, _: (t, 0, 0, 0)),
            ),
            out_shape=jax.ShapeDtypeStruct((2, 8, rows, tokens), BF16),
            compiler_params=pltpu.CompilerParams(vmem_limit_bytes=MEMORY),
            cost_estimate=pl.CostEstimate(
                flops=32 * rows * hidden * tokens, bytes_accessed=8 << 20, transcendentals=0
            ),
        )(here, d_pair, *blocks)


def sum_kernel(zh_ref, xhat_ref, gain_ref, *refs):
    parts, (d_ref, moments_ref, share_ref) = refs[:-3], refs[-3:]
    first, second = 0.0, 0.0
    for chunk, ref in zip(CHUNKS, parts, strict=True):
        for k, offset in enumerate(chunk):
            zh = lax.rem(zh_ref[0] + offset, 4)
            for c in range(2):
                total = ref[c * 8, pl.ds(k * SHARD, SHARD), :].astype(F32)
                for m in range(1, 8):
                    total += ref[c * 8 + m, pl.ds(k * SHARD, SHARD), :].astype(F32)
                at = pl.ds(pl.multiple_of((zh * 2 + c) * SHARD, SHARD), SHARD)
                d_ref[at, :] = total
                xhat = xhat_ref[at, :]
                product = total * xhat
                share_ref[at, :] = jnp.sum(product, axis=1, keepdims=True)
                first += jnp.sum(total * gain_ref[at, :], axis=0, keepdims=True)
                second += jnp.sum(product * gain_ref[at, :], axis=0, keepdims=True)
    moments_ref[...] = jnp.concatenate([first, second, jnp.zeros((6, first.shape[1]), F32)], axis=0)


def final_kernel(d_ref, xhat_ref, gain_ref, moments_ref, rstd_ref, out_ref):
    both = moments_ref[0]
    for m in range(1, 8):
        both += moments_ref[m]
    both = both * (1.0 / 3072)
    g = d_ref[...] * gain_ref[...]
    value = rstd_ref[...] * (g - both[0:1] - xhat_ref[...] * both[1:2])
    out_ref[...] = value.T.astype(BF16)


def on_device(tokens, gain, pre_act, w_in, act_cotangent):
    rows, share = tokens.shape
    core = lax.axis_index("c")
    here_y = lax.axis_index("y").astype(jnp.int32).reshape(1)
    here_zh = lax.axis_index("zh").astype(jnp.int32).reshape(1)

    own = lax.all_gather(w_in, "y", axis=0, tiled=True)
    rest = jnp.concatenate([shift(w_in, "zh", 4, k) for k in CHUNKS[1]], axis=0)
    rest, pre_act, act_cotangent, tokens = lax.optimization_barrier(
        (rest, pre_act, act_cotangent, tokens)
    )

    x = tokens.astype(F32).T
    local_mean = jnp.mean(x, axis=0, keepdims=True)
    local_square = jnp.sum((x - local_mean) ** 2, axis=0, keepdims=True)
    stats = spread(jnp.concatenate([local_mean, local_square] * 4, axis=0), MP, 8)
    means, squares = stats[:, 0], stats[:, 1]
    mean = jnp.mean(means, axis=0, keepdims=True)
    variance = (
        jnp.sum(squares, axis=0, keepdims=True)
        + share * jnp.sum((means - mean) ** 2, axis=0, keepdims=True)
    ) / (8 * share)
    rstd = 1.0 / jnp.sqrt(variance + 1e-06)
    xhat = (x - mean) * rstd
    gain_column = gain.astype(F32)[:, None]

    _, gelu_back = jax.vjp(gelu_exact, pre_act.astype(F32))
    d_pre = gelu_back(act_cotangent.astype(F32))[0].astype(BF16).T
    other = lax.ppermute(d_pre, "c", [(0, 1), (1, 0)])
    d_pair = jnp.stack([jnp.where(core == 0, d_pre, other), jnp.where(core == 0, other, d_pre)])

    def exchange(part):
        return lax.all_to_all(part.reshape(16, -1, rows), ("c", "zl", "x"), 0, 0)

    own = products([(0, 0, own)], SHARD, d_pair, here_y * 0, "own")
    rest, own = ring(rest, own)
    parts = [exchange(own), exchange(products(rest, 3 * SHARD, d_pair, here_y, "rest"))]

    whole = lambda shape: pl.BlockSpec(shape, lambda i, _: (0,) * len(shape))
    outs = [
        jax.ShapeDtypeStruct((share, rows), F32),
        jax.ShapeDtypeStruct((8, rows), F32),
        jax.ShapeDtypeStruct((share, 1), F32),
    ]
    d_normed, moments, gain_share = pl.pallas_call(
        sum_kernel,
        grid_spec=pltpu.PrefetchScalarGridSpec(
            num_scalar_prefetch=1,
            grid=(1,),
            in_specs=[whole(a.shape) for a in (xhat, gain_column, *parts)],
            out_specs=[whole(o.shape) for o in outs],
        ),
        out_shape=outs,
        compiler_params=pltpu.CompilerParams(vmem_limit_bytes=MEMORY),
    )(here_zh, xhat, gain_column, *parts)

    gain_share = jnp.pad(gain_share.reshape(3, 128), ((0, 5), (0, 0)))
    gain_share += shift(gain_share, "c", 2, 1)
    gain_gradient = jnp.sum(spread(gain_share, ("y", "zh"), 32), axis=0)[:3].reshape(share)

    moments = spread(moments, MP, 8)
    token_gradient = pl.pallas_call(
        final_kernel,
        out_shape=jax.ShapeDtypeStruct((rows, share), BF16),
        compiler_params=pltpu.CompilerParams(vmem_limit_bytes=MEMORY),
    )(d_normed, xhat, gain_column, moments, rstd)
    return (token_gradient, gain_gradient)


def solution(mesh):
    fine = Mesh(mesh.devices.reshape(SIZES), NAMES)
    placed = (P(DP, MP), P(MP), P(DP, MP), P(DP, MP), P(DP, MP))
    return jax.shard_map(
        on_device, mesh=fine, in_specs=placed, out_specs=(P(DP, MP), P(MP)), check_vma=False
    )
```

time: 190 us -> 215 us (1.13)
  starting transfers between devices: 32.8 us -> 84.3 us
  blocking collectives: 22.2 us -> 0 us
  waiting for transfers between devices: 93.8 us -> 78.4 us
  local copies, waits for them, and re-layouts: 8.57 us -> 17.4 us
    ppermute x0 -> x12, starting transfers between devices: none -> 47.2 us  [shift(): return lax.ppermute(array, axis, [(i, (i - by) % n) for i in range(n)])]
    all_gather x1, waiting for transfers between devices: 45 us -> 15 us  [on_device(): own = lax.all_gather(w_in, 'y', axis=0, tiled=True)]
    ppermute x0 -> x12, waiting for transfers between devices: none -> 25.1 us  [shift(): return lax.ppermute(array, axis, [(i, (i - by) % n) for i in range(n)])]
    all_gather x1 -> x0, blocking collectives: 22.2 us -> none  [on_device(): w_half = lax.all_gather(w_in, 'zh', axis=0, tiled=True)]
    all_to_all x1 -> x2, starting transfers between devices: 6.16 us -> 15.3 us  [exchange(): return lax.all_to_all(part.reshape(16, -1, rows), ('c', 'zl', 'x'), 0, 0)]
    convert_element_type x1 -> x0, other arithmetic: 6.81 us -> none  [on_device(): d_pre = gelu_back(act_cotangent.astype(F32))[0].astype(BF16)]
    transpose x0 -> x1, other arithmetic: none -> 6.73 us  [on_device(): d_pre = gelu_back(act_cotangent.astype(F32))[0].astype(BF16).T]
    all_to_all x1 -> x2, waiting for transfers between devices: 30.1 us -> 23.7 us  [exchange(): return lax.all_to_all(part.reshape(16, -1, rows), ('c', 'zl', 'x'), 0, 0)]
  transfers between devices with their start and end apart: 6 -> 19, of which waited for: 4 -> 10; matrix products, arithmetic and copies ran while one was open for 5% -> 3% of each run, Pallas kernels for 5% -> 4%
where the time goes in v2:
time: 215 us; the launch traced here: 213 us
  starting transfers between devices  84.3 us (39%)
  waiting for transfers between devices  78.4 us (36%)
  local copies, waits for them, and re-layouts  17.4 us (8%)
  between operations  14.4 us (7%)
  Pallas kernels  9.24 us (4%)
  other arithmetic  9.05 us (4%)
    ppermute x12, starting transfers between devices, shift(): return lax.ppermute(array, axis, [(i, (i - by) % n) for i in range(n)])  47.2 us
    ppermute x12, waiting for transfers between devices, shift(): return lax.ppermute(array, axis, [(i, (i - by) % n) for i in range(n)])  25.1 us
    all_to_all x2, waiting for transfers between devices, exchange(): return lax.all_to_all(part.reshape(16, -1, rows), ('c', 'zl', 'x'), 0, 0)  23.7 us
    all_to_all x3, starting transfers between devices, spread(): return lax.all_to_all(jnp.broadcast_to(row, (n,) + row.shape), axes, 0, 0)  17.8 us
    all_to_all x2, starting transfers between devices, exchange(): return lax.all_to_all(part.reshape(16, -1, rows), ('c', 'zl', 'x'), 0, 0)  15.3 us
    all_gather x1, waiting for transfers between devices, on_device(): own = lax.all_gather(w_in, 'y', axis=0, tiled=True)  15 us
    all_to_all x3, waiting for transfers between devices, spread(): return lax.all_to_all(jnp.broadcast_to(row, (n,) + row.shape), axes, 0, 0)  14.5 us
    unnamed x28, local copies, waits for them, and re-layouts  8.96 us
  transfers between devices with their start and end apart: 19, of which 10 were waited for; matrix products, arithmetic and copies ran while one was open for 3% of the time, Pallas kernels for 4%

profile of v2, /device:TPU:1, one launch (start us, length us, event | category | flops | bytes accessed | tf_op | source)
XLA Modules:
  0.0 212.7 jit_solution(11317908024853815729)
XLA Ops:
  7.2 11.6 %collective-permute-start = (bf16[48,1536]{1,0:T(8,128)(2,1)}, bf16[48,1536]{1,0:T(8,128)(2,1)S(1)}, u32[]{:S(2)}, u32[]{:S(2)}) collective-permute-start(bf16[48,1536]{1,0:T(8,128)(2,1)} %param.8), channel_id=1, source_target_pairs={{0,48},{16,0},{32,16},{48,32},{1,49},{17,1},{33,17},{49,33},{2,50}... | collective-permute-start | bytes 442376 | tf_op jit(solution)/shard_map/ppermute | solution.py:26
  18.8 1.9 collective-permute-start.1
  20.8 4.2 %collective-permute-start.2 = (bf16[48,1536]{1,0:T(8,128)(2,1)}, bf16[48,1536]{1,0:T(8,128)(2,1)S(1)}, u32[]{:S(2)}, u32[]{:S(2)}) collective-permute-start(bf16[48,1536]{1,0:T(8,128)(2,1)} %param.8), channel_id=1, source_target_pairs={{0,32},{16,48},{32,0},{48,16},{1,33},{17,49},{33,1},{49,17},{2,34}... | collective-permute-start | bytes 442376 | tf_op jit(solution)/shard_map/ppermute | solution.py:26
  25.0 2.4 %collective-permute-done.1 = bf16[48,1536]{1,0:T(8,128)(2,1)S(1)} collective-permute-done((bf16[48,1536]{1,0:T(8,128)(2,1)}, bf16[48,1536]{1,0:T(8,128)(2,1)S(1)}, u32[]{:S(2)}, u32[]{:S(2)}) %collective-permute-start.1) | collective-permute-done | bytes 147488 | tf_op jit(solution)/shard_map/ppermute | solution.py:26
  27.5 7.5 %collective-permute-done.2 = bf16[48,1536]{1,0:T(8,128)(2,1)S(1)} collective-permute-done((bf16[48,1536]{1,0:T(8,128)(2,1)}, bf16[48,1536]{1,0:T(8,128)(2,1)S(1)}, u32[]{:S(2)}, u32[]{:S(2)}) %collective-permute-start.2) | collective-permute-done | bytes 147488 | tf_op jit(solution)/shard_map/ppermute | solution.py:26
  35.0 1.7 copy.23
  36.7 1.4 copy.24
  38.2 6.7 %fusion.36 = bf16[1536,384]{1,0:T(8,128)(2,1)S(1)} fusion(bf16[384,1536]{0,1:T(8,128)(2,1)} %copy.24, bf16[384,1536]{0,1:T(8,128)(2,1)S(1)} %copy.23), kind=kLoop, calls=%fused_computation.44 | loop fusion | flops 43646976 | bytes 3538944 | tf_op jit(solution)/shard_map/transpose | solution.py:136
  44.9 3.9 %collective-permute-start.7 = (bf16[1536,384]{1,0:T(8,128)(2,1)S(1)}, bf16[1536,384]{1,0:T(8,128)(2,1)}, u32[]{:S(2)}, u32[]{:S(2)}) collective-permute-start(bf16[1536,384]{1,0:T(8,128)(2,1)S(1)} %fusion.36), channel_id=1, source_target_pairs={{0,8},{8,0},{1,9},{9,1},{2,10},{10,2},{3,11},{11,3},{4,12},{12,4},... | collective-permute-start | bytes 3538952 | tf_op jit(solution)/shard_map/ppermute | solution.py:137
  48.8 3.2 %collective-permute-start.3 = (bf16[144,1536]{1,0:T(8,128)(2,1)S(1)}, bf16[144,1536]{1,0:T(8,128)(2,1)S(1)}, u32[]{:S(2)}, u32[]{:S(2)}) collective-permute-start(bf16[144,1536]{1,0:T(8,128)(2,1)S(1)} %pad_maximum_fusion.1.refs_0_), channel_id=1, source_target_pairs={{0,64},{64,128},{128,192},{192,256},{256,320},{320,384},{384,448},... | collective-permute-start | bytes 1327112 | tf_op jit(solution)/shard_map/ppermute | solution.py:26
  52.0 3.8 %collective-permute-start.5 = (bf16[144,1536]{1,0:T(8,128)(2,1)S(1)}, bf16[144,1536]{1,0:T(8,128)(2,1)}, u32[]{:S(2)}, u32[]{:S(2)}) collective-permute-start(bf16[144,1536]{1,0:T(8,128)(2,1)S(1)} %pad_maximum_fusion.1.refs_0_), channel_id=1, source_target_pairs={{0,448},{64,0},{128,64},{192,128},{256,192},{320,256},{384,320},{4... | collective-permute-start | bytes 1327112 | tf_op jit(solution)/shard_map/ppermute | solution.py:26
  55.8 1.2 copy.20
  57.9 4.0 %all-to-all-start = ((f32[8,8,384]{2,1,0:T(8,128)}), f32[8,8,384]{2,1,0:T(8,128)S(1)}, u32[]{:S(2)}, u32[]{:S(2)}) async-start(f32[8,8,384]{2,1,0:T(8,128)} %broadcast_in_dim.22), calls=%async_computation | async-start | bytes 196608 | tf_op jit(solution)/shard_map/all_to_all | solution.py:22
  61.9 2.5 %collective-permute-done.3.refs_1_ = bf16[144,1536]{1,0:T(8,128)(2,1)S(1)} collective-permute-done((bf16[144,1536]{1,0:T(8,128)(2,1)S(1)}, bf16[144,1536]{1,0:T(8,128)(2,1)S(1)}, u32[]{:S(2)}, u32[]{:S(2)}) %collective-permute-start.3) | collective-permute-done | bytes 442400 | tf_op jit(solution)/shard_map/ppermute | solution.py:26
  64.4 1.9 collective-permute-start.4
  66.3 0.8 collective-permute-done.5.refs_2_
  67.1 5.4 %collective-permute-start.6 = (bf16[144,1536]{1,0:T(8,128)(2,1)}, bf16[144,1536]{1,0:T(8,128)(2,1)}, u32[]{:S(2)}, u32[]{:S(2)}) collective-permute-start(bf16[144,1536]{1,0:T(8,128)(2,1)} %collective-permute-done.5.refs_2_), channel_id=1, source_target_pairs={{0,448},{64,0},{128,64},{192,128},{256,192},{320,256},{384,320},{4... | collective-permute-start | bytes 1327112 | tf_op jit(solution)/shard_map/ppermute | solution.py:26
  72.6 1.5 select_bitcast_fusion.1
  74.4 15.0 %all-gather.2.cloned.1.call-done.refs_0_ = bf16[384,1536]{1,0:T(8,128)(2,1)} async-done(((bf16[48,1536]{1,0:T(8,128)(2,1)}), bf16[384,1536]{1,0:T(8,128)(2,1)}) %all-gather.2.cloned.1.call-update) | async-done | bytes 1179664 | tf_op jit(solution)/shard_map/all_gather | solution.py:115
  89.4 1.3 copy-done.1
  90.6 2.3 %own.1 = bf16[2,8,48,384]{3,2,1,0:T(8,128)(2,1)} custom-call(s32[1]{0:T(128)} %constant.17.clone.1.here_ref, bf16[2,1536,384]{2,1,0:T(8,128)(2,1)S(1)} %pad_maximum_fusion.d_ref, bf16[384,1536]{1,0:T(8,128)(2,1)S(1)} %copy-done.1), custom_call_target="tpu_custom_call" | custom-call | flops 905969664 | bytes 8388608 | tf_op jit(solution)/shard_map/own/pallas_call | solution.py:62
  92.9 8.1 %all-to-all-start.1 = ((bf16[16,48,384]{2,1,0:T(8,128)(2,1)}), bf16[16,48,384]{2,1,0:T(8,128)(2,1)S(1)}, u32[]{:S(2)}, u32[]{:S(2)}) async-start(bf16[16,48,384]{2,1,0:T(8,128)(2,1)} %bitcast.5), calls=%async_computation.1 | async-start | bytes 1179648 | tf_op jit(solution)/shard_map/all_to_all | solution.py:141
  101.0 3.0 %collective-permute-start.8 = (bf16[144,1536]{1,0:T(8,128)(2,1)}, bf16[144,1536]{1,0:T(8,128)(2,1)S(1)}, u32[]{:S(2)}, u32[]{:S(2)}) collective-permute-start(bf16[144,1536]{1,0:T(8,128)(2,1)} %collective-permute-done.4.refs_3_), channel_id=1, source_target_pairs={{0,64},{64,128},{128,192},{192,256},{256,320},{320,384},{384,448},... | collective-permute-start | bytes 1327112 | tf_op jit(solution)/shard_map/ppermute | solution.py:26
  104.1 3.5 %collective-permute-start.9 = (bf16[144,1536]{1,0:T(8,128)(2,1)}, bf16[144,1536]{1,0:T(8,128)(2,1)S(1)}, u32[]{:S(2)}, u32[]{:S(2)}) collective-permute-start(bf16[144,1536]{1,0:T(8,128)(2,1)} %collective-permute-done.6.refs_4_), channel_id=1, source_target_pairs={{0,448},{64,0},{128,64},{192,128},{256,192},{320,256},{384,320},{4... | collective-permute-start | bytes 1327112 | tf_op jit(solution)/shard_map/ppermute | solution.py:26
  107.5 8.5 %collective-permute-done.8.refs_5_ = bf16[144,1536]{1,0:T(8,128)(2,1)S(1)} collective-permute-done((bf16[144,1536]{1,0:T(8,128)(2,1)}, bf16[144,1536]{1,0:T(8,128)(2,1)S(1)}, u32[]{:S(2)}, u32[]{:S(2)}) %collective-permute-start.8) | collective-permute-done | bytes 442400 | tf_op jit(solution)/shard_map/ppermute | solution.py:26
  116.1 0.7 slice.22
  116.8 0.8 copy-done.4
  117.5 1.9 collective-permute-start.10
  119.5 0.7 slice.23
  120.1 0.8 copy-done.6
  120.9 4.6 %collective-permute-start.11 = (bf16[64,1536]{1,0:T(8,128)(2,1)}, bf16[64,1536]{1,0:T(8,128)(2,1)}, u32[]{:S(2)}, u32[]{:S(2)}) collective-permute-start(bf16[64,1536]{1,0:T(8,128)(2,1)} %slice.23), channel_id=1, source_target_pairs={{0,448},{64,0},{128,64},{192,128},{256,192},{320,256},{384,320},{4... | collective-permute-start | bytes 589832 | tf_op jit(solution)/shard_map/ppermute | solution.py:26
  125.5 3.3 %collective-permute-done.11.refs_8_ = bf16[64,1536]{1,0:T(8,128)(2,1)} collective-permute-done((bf16[64,1536]{1,0:T(8,128)(2,1)}, bf16[64,1536]{1,0:T(8,128)(2,1)}, u32[]{:S(2)}, u32[]{:S(2)}) %collective-permute-start.11) | collective-permute-done | bytes 196640 | tf_op jit(solution)/shard_map/ppermute | solution.py:26
  128.8 1.0 copy-done.5
  129.8 1.0 copy-done.7
  130.8 1.0 copy-done.9
  131.9 5.5 %rest.1 = bf16[2,8,144,384]{3,2,1,0:T(8,128)(2,1)S(1)} custom-call(s32[1]{0:T(128)} %bitcast.6.here_ref, bf16[2,1536,384]{2,1,0:T(8,128)(2,1)S(1)} %pad_maximum_fusion.d_ref, bf16[144,1536]{1,0:T(8,128)(2,1)S(1)} %pad_maximum_fusion.1.refs_0_, bf16[144,1536]{1,0:T(8,128)(2,1)S(1)} %copy-done.9, bf16[144,1536]{1,0:T(8,128)(2,1)} %collective-permute-done.5.refs_2_, ...), custom_call_target="tpu_custom_call" | custom-call | flops 2717908992 | bytes 8388608 | tf_op jit(solution)/shard_map/rest/pallas_call | solution.py:62
  137.3 1.2 copy-done
  138.6 7.2 %all-to-all-start.2 = ((bf16[16,144,384]{2,1,0:T(8,128)(2,1)}), bf16[16,144,384]{2,1,0:T(8,128)(2,1)S(1)}, u32[]{:S(2)}, u32[]{:S(2)}) async-start(bf16[16,144,384]{2,1,0:T(8,128)(2,1)} %bitcast.21), calls=%async_computation.2 | async-start | bytes 3538944 | tf_op jit(solution)/shard_map/all_to_all | solution.py:141
  146.1 23.7 %all-to-all-done.2.refs_1_ = bf16[16,144,384]{2,1,0:T(8,128)(2,1)S(1)} async-done(((bf16[16,144,384]{2,1,0:T(8,128)(2,1)}), bf16[16,144,384]{2,1,0:T(8,128)(2,1)S(1)}, u32[]{:S(2)}, u32[]{:S(2)}) %all-to-all-start.2) | async-done | bytes 1769504 | tf_op jit(solution)/shard_map/all_to_all | solution.py:141
  170.4 0.8 copy-done.2
  171.3 2.1 collective-permute-start.12
  174.1 3.8 %all-to-all-start.3 = ((f32[8,8,384]{2,1,0:T(8,128)}), f32[8,8,384]{2,1,0:T(8,128)S(1)}, u32[]{:S(2)}, u32[]{:S(2)}) async-start(f32[8,8,384]{2,1,0:T(8,128)} %broadcast_in_dim.25), calls=%async_computation.3 | async-start | bytes 196608 | tf_op jit(solution)/shard_map/all_to_all | solution.py:22
  177.9 5.3 %all-to-all-done.3.moments_ref = f32[8,8,384]{2,1,0:T(8,128)S(1)} async-done(((f32[8,8,384]{2,1,0:T(8,128)}), f32[8,8,384]{2,1,0:T(8,128)S(1)}, u32[]{:S(2)}, u32[]{:S(2)}) %all-to-all-start.3) | async-done | bytes 98336 | tf_op jit(solution)/shard_map/all_to_all | solution.py:22
  183.2 0.7 broadcast_in_dim.26
  183.9 10.0 %all-to-all-start.4 = ((f32[32,8,128]{2,1,0:T(8,128)}), f32[32,8,128]{2,1,0:T(8,128)S(1)}, u32[]{:S(2)}, u32[]{:S(2)}) async-start(f32[32,8,128]{2,1,0:T(8,128)} %broadcast_in_dim.26), calls=%async_computation.4 | async-start | bytes 262144 | tf_op jit(solution)/shard_map/all_to_all | solution.py:22
  193.9 1.1 copy-done.3
  195.0 1.0 shard_map.69
  196.0 9.2 %all-to-all-done.4 = f32[32,8,128]{2,1,0:T(8,128)S(1)} async-done(((f32[32,8,128]{2,1,0:T(8,128)}), f32[32,8,128]{2,1,0:T(8,128)S(1)}, u32[]{:S(2)}, u32[]{:S(2)}) %all-to-all-start.4) | async-done | bytes 131104 | tf_op jit(solution)/shard_map/all_to_all | solution.py:22
  (53 shorter events, 3.5 us)
Async XLA Ops:
  7.2 29.6 %copy-start.12 = (bf16[384,1536]{1,0:T(8,128)(2,1)S(1)}, bf16[384,1536]{1,0:T(8,128)(2,1)}, u32[]{:S(2)}) copy-start(bf16[384,1536]{1,0:T(8,128)(2,1)} %param.9) | copy-start | bytes 3538948
  7.2 82.2 %all-gather.2.cloned.1.call-start = ((), (), s32[]{:S(2)}) async-start(), calls=%async_computation.5 | async-start | bytes 1327104 | tf_op jit(solution)/shard_map/all_gather | solution.py:115
  7.2 17.8 %collective-permute-start = (bf16[48,1536]{1,0:T(8,128)(2,1)}, bf16[48,1536]{1,0:T(8,128)(2,1)S(1)}, u32[]{:S(2)}, u32[]{:S(2)}) collective-permute-start(bf16[48,1536]{1,0:T(8,128)(2,1)} %param.8), channel_id=1, source_target_pairs={{0,48},{16,0},{32,16},{48,32},{1,49},{17,1},{33,17},{49,33},{2,50}... | collective-permute-start | bytes 442376 | tf_op jit(solution)/shard_map/ppermute | solution.py:26
  18.8 8.6 %collective-permute-start.1 = (bf16[48,1536]{1,0:T(8,128)(2,1)}, bf16[48,1536]{1,0:T(8,128)(2,1)S(1)}, u32[]{:S(2)}, u32[]{:S(2)}) collective-permute-start(bf16[48,1536]{1,0:T(8,128)(2,1)} %param.8), channel_id=1, source_target_pairs={{0,16},{16,32},{32,48},{48,0},{1,17},{17,33},{33,49},{49,1},{2,18}... | collective-permute-start | bytes 442376 | tf_op jit(solution)/shard_map/ppermute | solution.py:26
  20.8 14.2 %collective-permute-start.2 = (bf16[48,1536]{1,0:T(8,128)(2,1)}, bf16[48,1536]{1,0:T(8,128)(2,1)S(1)}, u32[]{:S(2)}, u32[]{:S(2)}) collective-permute-start(bf16[48,1536]{1,0:T(8,128)(2,1)} %param.8), channel_id=1, source_target_pairs={{0,32},{16,48},{32,0},{48,16},{1,33},{17,49},{33,1},{49,17},{2,34}... | collective-permute-start | bytes 442376 | tf_op jit(solution)/shard_map/ppermute | solution.py:26
  44.9 27.6 %collective-permute-start.7 = (bf16[1536,384]{1,0:T(8,128)(2,1)S(1)}, bf16[1536,384]{1,0:T(8,128)(2,1)}, u32[]{:S(2)}, u32[]{:S(2)}) collective-permute-start(bf16[1536,384]{1,0:T(8,128)(2,1)S(1)} %fusion.36), channel_id=1, source_target_pairs={{0,8},{8,0},{1,9},{9,1},{2,10},{10,2},{3,11},{11,3},{4,12},{12,4},... | collective-permute-start | bytes 3538952 | tf_op jit(solution)/shard_map/ppermute | solution.py:137
  48.8 15.6 %collective-permute-start.3 = (bf16[144,1536]{1,0:T(8,128)(2,1)S(1)}, bf16[144,1536]{1,0:T(8,128)(2,1)S(1)}, u32[]{:S(2)}, u32[]{:S(2)}) collective-permute-start(bf16[144,1536]{1,0:T(8,128)(2,1)S(1)} %pad_maximum_fusion.1.refs_0_), channel_id=1, source_target_pairs={{0,64},{64,128},{128,192},{192,256},{256,320},{320,384},{384,448},... | collective-permute-start | bytes 1327112 | tf_op jit(solution)/shard_map/ppermute | solution.py:26
  52.0 15.1 %collective-permute-start.5 = (bf16[144,1536]{1,0:T(8,128)(2,1)S(1)}, bf16[144,1536]{1,0:T(8,128)(2,1)}, u32[]{:S(2)}, u32[]{:S(2)}) collective-permute-start(bf16[144,1536]{1,0:T(8,128)(2,1)S(1)} %pad_maximum_fusion.1.refs_0_), channel_id=1, source_target_pairs={{0,448},{64,0},{128,64},{192,128},{256,192},{320,256},{384,320},{4... | collective-permute-start | bytes 1327112 | tf_op jit(solution)/shard_map/ppermute | solution.py:26
  57.0 17.1 %copy-start.10 = (bf16[384,384]{0,1:T(8,128)(2,1)}, bf16[384,384]{0,1:T(8,128)(2,1)S(1)}, u32[]{:S(2)}) copy-start(bf16[384,384]{0,1:T(8,128)(2,1)S(1)} %copy.20) | copy-start | bytes 884740
  57.9 35.0 %all-to-all-start = ((f32[8,8,384]{2,1,0:T(8,128)}), f32[8,8,384]{2,1,0:T(8,128)S(1)}, u32[]{:S(2)}, u32[]{:S(2)}) async-start(f32[8,8,384]{2,1,0:T(8,128)} %broadcast_in_dim.22), calls=%async_computation | async-start | bytes 196608 | tf_op jit(solution)/shard_map/all_to_all | solution.py:22
  64.4 9.7 %copy-start.8 = (bf16[144,1536]{1,0:T(8,128)(2,1)}, bf16[144,1536]{1,0:T(8,128)(2,1)S(1)}, u32[]{:S(2)}) copy-start(bf16[144,1536]{1,0:T(8,128)(2,1)S(1)} %collective-permute-done.3.refs_1_) | copy-start | bytes 1327108
  64.4 28.5 %collective-permute-start.4 = (bf16[144,1536]{1,0:T(8,128)(2,1)S(1)}, bf16[144,1536]{1,0:T(8,128)(2,1)}, u32[]{:S(2)}, u32[]{:S(2)}) collective-permute-start(bf16[144,1536]{1,0:T(8,128)(2,1)S(1)} %collective-permute-done.3.refs_1_), channel_id=1, source_target_pairs={{0,64},{64,128},{128,192},{192,256},{256,320},{320,384},{384,448},... | collective-permute-start | bytes 1327112 | tf_op jit(solution)/shard_map/ppermute | solution.py:26
  67.1 25.8 %collective-permute-start.6 = (bf16[144,1536]{1,0:T(8,128)(2,1)}, bf16[144,1536]{1,0:T(8,128)(2,1)}, u32[]{:S(2)}, u32[]{:S(2)}) collective-permute-start(bf16[144,1536]{1,0:T(8,128)(2,1)} %collective-permute-done.5.refs_2_), channel_id=1, source_target_pairs={{0,448},{64,0},{128,64},{192,128},{256,192},{320,256},{384,320},{4... | collective-permute-start | bytes 1327112 | tf_op jit(solution)/shard_map/ppermute | solution.py:26
  89.4 1.3 copy-start.1
  92.9 45.7 %all-to-all-start.1 = ((bf16[16,48,384]{2,1,0:T(8,128)(2,1)}), bf16[16,48,384]{2,1,0:T(8,128)(2,1)S(1)}, u32[]{:S(2)}, u32[]{:S(2)}) async-start(bf16[16,48,384]{2,1,0:T(8,128)(2,1)} %bitcast.5), calls=%async_computation.1 | async-start | bytes 1179648 | tf_op jit(solution)/shard_map/all_to_all | solution.py:141
  101.0 15.0 %collective-permute-start.8 = (bf16[144,1536]{1,0:T(8,128)(2,1)}, bf16[144,1536]{1,0:T(8,128)(2,1)S(1)}, u32[]{:S(2)}, u32[]{:S(2)}) collective-permute-start(bf16[144,1536]{1,0:T(8,128)(2,1)} %collective-permute-done.4.refs_3_), channel_id=1, source_target_pairs={{0,64},{64,128},{128,192},{192,256},{256,320},{320,384},{384,448},... | collective-permute-start | bytes 1327112 | tf_op jit(solution)/shard_map/ppermute | solution.py:26
  104.1 15.4 %collective-permute-start.9 = (bf16[144,1536]{1,0:T(8,128)(2,1)}, bf16[144,1536]{1,0:T(8,128)(2,1)S(1)}, u32[]{:S(2)}, u32[]{:S(2)}) collective-permute-start(bf16[144,1536]{1,0:T(8,128)(2,1)} %collective-permute-done.6.refs_4_), channel_id=1, source_target_pairs={{0,448},{64,0},{128,64},{192,128},{256,192},{320,256},{384,320},{4... | collective-permute-start | bytes 1327112 | tf_op jit(solution)/shard_map/ppermute | solution.py:26
  116.8 0.8 copy-start.4
  117.5 11.3 %collective-permute-start.10 = (bf16[80,1536]{1,0:T(8,128)(2,1)}, bf16[80,1536]{1,0:T(8,128)(2,1)}, u32[]{:S(2)}, u32[]{:S(2)}) collective-permute-start(bf16[80,1536]{1,0:T(8,128)(2,1)} %slice.22), channel_id=1, source_target_pairs={{0,64},{64,128},{128,192},{192,256},{256,320},{320,384},{384,448},... | collective-permute-start | bytes 737288 | tf_op jit(solution)/shard_map/ppermute | solution.py:26
  120.1 0.8 copy-start.6
  120.9 7.9 %collective-permute-start.11 = (bf16[64,1536]{1,0:T(8,128)(2,1)}, bf16[64,1536]{1,0:T(8,128)(2,1)}, u32[]{:S(2)}, u32[]{:S(2)}) collective-permute-start(bf16[64,1536]{1,0:T(8,128)(2,1)} %slice.23), channel_id=1, source_target_pairs={{0,448},{64,0},{128,64},{192,128},{256,192},{320,256},{384,320},{4... | collective-permute-start | bytes 589832 | tf_op jit(solution)/shard_map/ppermute | solution.py:26
  128.8 1.0 copy-start.5
  129.8 1.0 copy-start.7
  130.8 1.0 copy-start.9
  137.3 1.2 copy-start
  138.6 7.2 %copy-start.13 = (bf16[384]{0:T(512)(128)(2,1)S(1)}, bf16[384]{0:T(512)(128)(2,1)}, u32[]{:S(2)}) copy-start(bf16[384]{0:T(512)(128)(2,1)} %param.6) | copy-start | bytes 2308
  138.6 7.4 %copy-start.11 = (bf16[384,384]{0,1:T(8,128)(2,1)S(1)}, bf16[384,384]{0,1:T(8,128)(2,1)}, u32[]{:S(2)}) copy-start(bf16[384,384]{0,1:T(8,128)(2,1)} %copy-done.10) | copy-start | bytes 884740
  138.6 31.3 %all-to-all-start.2 = ((bf16[16,144,384]{2,1,0:T(8,128)(2,1)}), bf16[16,144,384]{2,1,0:T(8,128)(2,1)S(1)}, u32[]{:S(2)}, u32[]{:S(2)}) async-start(bf16[16,144,384]{2,1,0:T(8,128)(2,1)} %bitcast.21), calls=%async_computation.2 | async-start | bytes 3538944 | tf_op jit(solution)/shard_map/all_to_all | solution.py:141
  170.4 0.8 copy-start.2
  171.3 6.6 %collective-permute-start.12 = (f32[8,128]{1,0:T(8,128)S(1)}, f32[8,128]{1,0:T(8,128)S(1)}, u32[]{:S(2)}, u32[]{:S(2)}) collective-permute-start(f32[8,128]{1,0:T(8,128)S(1)} %pad.4), channel_id=1, source_target_pairs={{0,8},{8,0},{1,9},{9,1},{2,10},{10,2},{3,11},{11,3},{4,12},{12,4},... | collective-permute-start | bytes 12296 | tf_op jit(solution)/shard_map/ppermute | solution.py:26
  174.1 9.1 %all-to-all-start.3 = ((f32[8,8,384]{2,1,0:T(8,128)}), f32[8,8,384]{2,1,0:T(8,128)S(1)}, u32[]{:S(2)}, u32[]{:S(2)}) async-start(f32[8,8,384]{2,1,0:T(8,128)} %broadcast_in_dim.25), calls=%async_computation.3 | async-start | bytes 196608 | tf_op jit(solution)/shard_map/all_to_all | solution.py:22
  183.9 21.4 %all-to-all-start.4 = ((f32[32,8,128]{2,1,0:T(8,128)}), f32[32,8,128]{2,1,0:T(8,128)S(1)}, u32[]{:S(2)}, u32[]{:S(2)}) async-start(f32[32,8,128]{2,1,0:T(8,128)} %broadcast_in_dim.26), calls=%async_computation.4 | async-start | bytes 262144 | tf_op jit(solution)/shard_map/all_to_all | solution.py:22
  193.9 1.1 copy-start.3
Sparse Core Ops, SparseCore 0:
  48.9 40.4 all-gather.1

commit v3 on v1

v3 whole, which is shorter than its diff:
```python
import jax
import jax.numpy as jnp
from jax import lax
from jax.experimental import pallas as pl
from jax.experimental.pallas import tpu as pltpu
from jax.sharding import Mesh, PartitionSpec as P

NAMES = ("y", "zh", "c", "zl", "x")
SIZES = (8, 4, 2, 2, 4)
DP, MP = ("y", "zh", "c"), ("zl", "x")
F32, BF16 = jnp.float32, jnp.bfloat16
SHARD = 48
PARAMS = pltpu.CompilerParams(vmem_limit_bytes=40 * 1024 * 1024)
together = lax.optimization_barrier


def gelu_exact(value):
    return jax.nn.gelu(value, approximate=False)


def spread(row, axes, n):
    return lax.all_to_all(jnp.broadcast_to(row, (n,) + row.shape), axes, 0, 0)


def shift(array, axis, n, by):
    return lax.ppermute(array, axis, [(i, (i - by) % n) for i in range(n)])


def both_ways(behind, ahead):
    return shift(behind, "y", 8, -1), shift(ahead, "y", 8, 1)


def product(pieces, offset, d_pair, y, parts):
    _, hidden, tokens = d_pair.shape
    rows = sum(p.shape[0] for p in pieces)
    shape = jax.ShapeDtypeStruct((2, 8, rows, tokens), BF16)

    def kernel(y_ref, d_ref, *refs):
        w_refs, out_ref = refs[: len(pieces)], refs[-1]
        w = jnp.concatenate([r[...] for r in w_refs], axis=0)
        out_ref[0, 0] = jnp.dot(w, d_ref[0], preferred_element_type=F32).astype(BF16)

    return pl.pallas_call(
        kernel,
        grid_spec=pltpu.PrefetchScalarGridSpec(
            num_scalar_prefetch=1,
            grid=(2,),
            in_specs=[pl.BlockSpec((1, hidden, tokens), lambda t, _: (t, 0, 0))]
            + [pl.BlockSpec(p.shape, lambda t, _: (0, 0)) for p in pieces]
            + [pl.BlockSpec(memory_space=pl.ANY)] * (parts is not None),
            out_specs=pl.BlockSpec(
                (1, 1, rows, tokens), lambda t, y: (t, lax.rem(y[0] + offset, 8), 0, 0)
            ),
        ),
        out_shape=shape,
        input_output_aliases={} if parts is None else {2 + len(pieces): 0},
        compiler_params=PARAMS,
        cost_estimate=pl.CostEstimate(
            flops=rows * hidden * tokens, bytes_accessed=1 << 18, transcendentals=0
        ),
    )(y, d_pair, *pieces, *([] if parts is None else [parts]))


def sum_kernel(parts_ref, xhat_ref, gain_ref, d_ref, moments_ref, share_ref):
    first, second = 0.0, 0.0
    for z in range(4):
        for c in range(2):
            total = parts_ref[c * 8, pl.ds(z * SHARD, SHARD), :].astype(F32)
            for m in range(1, 8):
                total += parts_ref[c * 8 + m, pl.ds(z * SHARD, SHARD), :].astype(F32)
            at = pl.ds((z * 2 + c) * SHARD, SHARD)
            d_ref[at, :] = total
            xhat = xhat_ref[at, :]
            product = total * xhat
            share_ref[at, :] = jnp.sum(product, axis=1, keepdims=True)
            first += jnp.sum(total * gain_ref[at, :], axis=0, keepdims=True)
            second += jnp.sum(product * gain_ref[at, :], axis=0, keepdims=True)
    moments_ref[...] = jnp.concatenate([first, second, jnp.zeros((6, first.shape[1]), F32)], axis=0)


def final_kernel(d_ref, xhat_ref, gain_ref, moments_ref, rstd_ref, out_ref):
    both = moments_ref[...] * (1.0 / 3072)
    g = d_ref[...] * gain_ref[...]
    value = rstd_ref[...] * (g - both[0:1] - xhat_ref[...] * both[1:2])
    out_ref[...] = value.T.astype(BF16)


def on_device(tokens, gain, pre_act, w_in, act_cotangent):
    rows, share = tokens.shape
    core = lax.axis_index("c")
    y = lax.axis_index("y").astype(jnp.int32).reshape(1)

    w0 = lax.all_gather(w_in, "zh", axis=0, tiled=True)
    w0, tokens, pre_act, act_cotangent = together((w0, tokens, pre_act, act_cotangent))
    step1 = both_ways(w0, w0)

    _, gelu_back = jax.vjp(gelu_exact, pre_act.astype(F32))
    d_pre = gelu_back(act_cotangent.astype(F32))[0].astype(BF16).T
    x = tokens.astype(F32).T
    local_mean = jnp.mean(x, axis=0, keepdims=True)
    local_square = jnp.sum((x - local_mean) ** 2, axis=0, keepdims=True)
    stats = jnp.concatenate([local_mean, local_square] * 4, axis=0)

    step1, d_pre, stats = together((step1, d_pre, stats))
    step2 = both_ways(*step1)
    other = shift(d_pre, "c", 2, 1)
    stats = spread(stats, MP, 8)

    step2, other, stats = together((step2, other, stats))
    step3 = both_ways(*step2)
    d_pair = jnp.stack([jnp.where(core == 0, d_pre, other), jnp.where(core == 0, other, d_pre)])
    parts = product([w0], 0, d_pair, y, None)
    parts = product([step1[0]], 7, d_pair, y, parts)
    parts = product([step1[1]], 1, d_pair, y, parts)
    parts = product([step2[0]], 6, d_pair, y, parts)
    parts = product([step2[1]], 2, d_pair, y, parts)

    step3, parts = together((step3, parts))
    half = w0.shape[0] // 2
    step4 = both_ways(step3[0][:half], step3[1][half:])
    parts = product([step3[0]], 5, d_pair, y, parts)
    parts = product([step3[1]], 3, d_pair, y, parts)
    means, squares = stats[:, 0], stats[:, 1]
    mean = jnp.mean(means, axis=0, keepdims=True)
    variance = (
        jnp.sum(squares, axis=0, keepdims=True)
        + share * jnp.sum((means - mean) ** 2, axis=0, keepdims=True)
    ) / (8 * share)
    rstd = 1.0 / jnp.sqrt(variance + 1e-06)
    xhat = (x - mean) * rstd

    step4, parts, xhat = together((step4, parts, xhat))
    parts = product(step4, 4, d_pair, y, parts)
    parts = lax.all_to_all(parts.reshape(16, -1, rows), ("c", "zl", "x"), 0, 0)

    gain_column = gain.astype(F32)[:, None]
    d_normed, moments, gain_share = pl.pallas_call(
        sum_kernel,
        out_shape=[
            jax.ShapeDtypeStruct((share, rows), F32),
            jax.ShapeDtypeStruct((8, rows), F32),
            jax.ShapeDtypeStruct((share, 1), F32),
        ],
        compiler_params=PARAMS,
    )(parts, xhat, gain_column)

    gain_share = jnp.pad(gain_share.reshape(3, 128), ((0, 5), (0, 0)))
    gain_gradient = jnp.sum(spread(gain_share, DP, 64), axis=0)[:3].reshape(share)

    moments = lax.psum(moments, MP)
    token_gradient = pl.pallas_call(
        final_kernel,
        out_shape=jax.ShapeDtypeStruct((rows, share), BF16),
        compiler_params=PARAMS,
    )(d_normed, xhat, gain_column, moments, rstd)
    return (token_gradient, gain_gradient)


def solution(mesh):
    fine = Mesh(mesh.devices.reshape(SIZES), NAMES)
    placed = (P(DP, MP), P(MP), P(DP, MP), P(DP, MP), P(DP, MP))
    return jax.shard_map(
        on_device, mesh=fine, in_specs=placed, out_specs=(P(DP, MP), P(MP)), check_vma=False
    )
```

time: 190 us -> 193 us (1.016)
  the two profiles are of different devices: /device:TPU:1 before, /device:TPU:32 now
where the time goes in v3:
time: 193 us; the launch traced here: 192 us
  blocking collectives  57.2 us (30%)
  starting transfers between devices  55.4 us (29%)
  waiting for transfers between devices  45.8 us (24%)
  Pallas kernels  14.5 us (8%)
  other arithmetic  10.2 us (5%)
  local copies, waits for them, and re-layouts  8.33 us (4%)
    psum x1, blocking collectives, on_device(): moments = lax.psum(moments, MP)  34.6 us
    ppermute x9, starting transfers between devices, shift(): return lax.ppermute(array, axis, [(i, (i - by) % n) for i in range(n)])  31 us
    all_to_all x1, waiting for transfers between devices, on_device(): parts = lax.all_to_all(parts.reshape(16, -1, rows), ('c', 'zl', 'x'), 0, 0)  30.3 us
    all_gather x1, blocking collectives, on_device(): w0 = lax.all_gather(w_in, 'zh', axis=0, tiled=True)  22.6 us
    all_to_all x2, starting transfers between devices, spread(): return lax.all_to_all(jnp.broadcast_to(row, (n,) + row.shape), axes, 0, 0)  17.6 us
    pallas_call x8, Pallas kernels, product(): pl.pallas_call(kernel, grid_spec=pltpu.PrefetchScalarGridSpec(num_scalar_...  13 us
    ppermute x9, waiting for transfers between devices, shift(): return lax.ppermute(array, axis, [(i, (i - by) % n) for i in range(n)])  8.97 us
    transpose x1, other arithmetic, on_device(): d_pre = gelu_back(act_cotangent.astype(F32))[0].astype(BF16).T  7.54 us
  transfers between devices with their start and end apart: 12, of which 7 were waited for; matrix products, arithmetic and copies ran while one was open for 7% of the time, Pallas kernels for 5%

profile of v3, /device:TPU:32, one launch (start us, length us, event | category | flops | bytes accessed | tf_op | source)
XLA Modules:
  0.0 192.2 jit_solution(6119220551554363791)
XLA Ops:
  0.6 22.6 %all_gather.3.refs_0_ = bf16[192,1536]{1,0:T(8,128)(2,1)S(1)} all-gather(bf16[48,1536]{1,0:T(8,128)(2,1)} %param.8), channel_id=1, replica_groups=mesh['y'=8,'zh'=4,'c'=2,'zl'=2,'x'=4] {'zh'}, dimensions={0}, use_global_device_ids=true | all-gather | bytes 737280 | tf_op jit(solution)/shard_map/all_gather | solution.py:93
  23.2 2.6 %collective-permute-start = (bf16[192,1536]{1,0:T(8,128)(2,1)S(1)}, bf16[192,1536]{1,0:T(8,128)(2,1)S(1)}, u32[]{:S(2)}, u32[]{:S(2)}) collective-permute-start(bf16[192,1536]{1,0:T(8,128)(2,1)S(1)} %all_gather.3.refs_0_), channel_id=1, source_target_pairs={{0,64},{64,128},{128,192},{192,256},{256,320},{320,384},{384,448},... | collective-permute-start | bytes 1769480 | tf_op jit(solution)/shard_map/ppermute | solution.py:26
  25.8 4.5 %collective-permute-start.1 = (bf16[192,1536]{1,0:T(8,128)(2,1)S(1)}, bf16[192,1536]{1,0:T(8,128)(2,1)S(1)}, u32[]{:S(2)}, u32[]{:S(2)}) collective-permute-start(bf16[192,1536]{1,0:T(8,128)(2,1)S(1)} %all_gather.3.refs_0_), channel_id=1, source_target_pairs={{0,448},{64,0},{128,64},{192,128},{256,192},{320,256},{384,320},{4... | collective-permute-start | bytes 1769480 | tf_op jit(solution)/shard_map/ppermute | solution.py:26
  30.3 1.7 copy.27
  32.0 2.4 %copy.28 = bf16[384,1536]{0,1:T(8,128)(2,1)} copy(bf16[384,1536]{1,0:T(8,128)(2,1)} %param.9) | data formatting | bytes 2359296 | tf_op jit(solution)/shard_map/optimization_barrier | solution.py:94
  34.4 7.5 %fusion.36 = bf16[1536,384]{1,0:T(8,128)(2,1)} fusion(bf16[384,1536]{0,1:T(8,128)(2,1)} %copy.28, bf16[384,1536]{0,1:T(8,128)(2,1)S(1)} %copy.27), kind=kLoop, calls=%fused_computation.44 | loop fusion | flops 43646976 | bytes 3538944 | tf_op jit(solution)/shard_map/transpose | solution.py:98
  41.9 0.2 copy.29
  42.1 0.1 convert_reduce_fusion
  42.2 0.1 fusion.38
  42.4 1.9 collective-permute-start.4
  44.3 1.9 collective-permute-start.2
  46.2 5.1 %collective-permute-start.3 = (bf16[192,1536]{1,0:T(8,128)(2,1)S(1)}, bf16[192,1536]{1,0:T(8,128)(2,1)S(1)}, u32[]{:S(2)}, u32[]{:S(2)}) collective-permute-start(bf16[192,1536]{1,0:T(8,128)(2,1)S(1)} %collective-permute-done.1.refs_0_), channel_id=1, source_target_pairs={{0,448},{64,0},{128,64},{192,128},{256,192},{320,256},{384,320},{4... | collective-permute-start | bytes 1769480 | tf_op jit(solution)/shard_map/ppermute | solution.py:26
  51.4 0.6 broadcast_in_dim.19
  52.0 5.6 %all-to-all-start = ((f32[8,8,384]{2,1,0:T(8,128)}), f32[8,8,384]{2,1,0:T(8,128)S(1)}, u32[]{:S(2)}, u32[]{:S(2)}) async-start(f32[8,8,384]{2,1,0:T(8,128)} %broadcast_in_dim.19), calls=%async_computation | async-start | bytes 196608 | tf_op jit(solution)/shard_map/all_to_all | solution.py:22
  57.7 6.4 %all-to-all-done = f32[8,8,384]{2,1,0:T(8,128)S(1)} async-done(((f32[8,8,384]{2,1,0:T(8,128)}), f32[8,8,384]{2,1,0:T(8,128)S(1)}, u32[]{:S(2)}, u32[]{:S(2)}) %all-to-all-start) | async-done | bytes 98336 | tf_op jit(solution)/shard_map/all_to_all | solution.py:22
  64.1 0.2 collective-permute-done.3.refs_0_
  64.3 1.8 select_bitcast_fusion.1
  66.2 0.3 pad_maximum_fusion.d_ref
  66.5 1.6 shard_map.68.refs_1_
  68.1 1.6 shard_map.69.refs_1_
  69.7 1.9 collective-permute-start.5
  71.6 5.6 %collective-permute-start.6 = (bf16[192,1536]{1,0:T(8,128)(2,1)S(1)}, bf16[192,1536]{1,0:T(8,128)(2,1)S(1)}, u32[]{:S(2)}, u32[]{:S(2)}) collective-permute-start(bf16[192,1536]{1,0:T(8,128)(2,1)S(1)} %collective-permute-done.3.refs_0_), channel_id=1, source_target_pairs={{0,448},{64,0},{128,64},{192,128},{256,192},{320,256},{384,320},{4... | collective-permute-start | bytes 1769480 | tf_op jit(solution)/shard_map/ppermute | solution.py:26
  77.2 1.6 shard_map.70.refs_1_
  78.9 1.6 shard_map.71.refs_1_
  80.5 1.6 shard_map.72.refs_1_
  82.2 6.0 %collective-permute-done.5.refs_0_ = bf16[192,1536]{1,0:T(8,128)(2,1)S(1)} collective-permute-done((bf16[192,1536]{1,0:T(8,128)(2,1)S(1)}, bf16[192,1536]{1,0:T(8,128)(2,1)S(1)}, u32[]{:S(2)}, u32[]{:S(2)}) %collective-permute-start.5) | collective-permute-done | bytes 589856 | tf_op jit(solution)/shard_map/ppermute | solution.py:26
  88.2 1.2 collective-permute-done.6.refs_0_
  89.4 1.9 collective-permute-start.7
  91.3 5.6 %collective-permute-start.8 = (bf16[96,1536]{1,0:T(8,128)(2,1)S(1)}, bf16[96,1536]{1,0:T(8,128)(2,1)S(1)}, u32[]{:S(2)}, u32[]{:S(2)}) collective-permute-start(bf16[96,1536]{1,0:T(8,128)(2,1)S(1)} %slice.16), channel_id=1, source_target_pairs={{0,448},{64,0},{128,64},{192,128},{256,192},{320,256},{384,320},{4... | collective-permute-start | bytes 884744 | tf_op jit(solution)/shard_map/ppermute | solution.py:26
  97.0 0.1 fusion.40.xhat_ref
  97.0 1.6 shard_map.73.refs_1_
  98.7 1.6 shard_map.74.refs_2_
  100.3 0.3 collective-permute-done.7.refs_0_
  100.6 1.2 collective-permute-done.8.refs_1_
  101.8 1.6 shard_map.75
  103.5 6.8 %all-to-all-start.1 = ((bf16[16,192,384]{2,1,0:T(8,128)(2,1)}), bf16[16,192,384]{2,1,0:T(8,128)(2,1)S(1)}, u32[]{:S(2)}, u32[]{:S(2)}) async-start(bf16[16,192,384]{2,1,0:T(8,128)(2,1)} %bitcast.5), calls=%async_computation.1 | async-start | bytes 4718592 | tf_op jit(solution)/shard_map/all_to_all | solution.py:134
  110.3 0.1 reshape.72.gain_ref
  110.4 30.3 %all-to-all-done.1.parts_ref = bf16[16,192,384]{2,1,0:T(8,128)(2,1)S(1)} async-done(((bf16[16,192,384]{2,1,0:T(8,128)(2,1)}), bf16[16,192,384]{2,1,0:T(8,128)(2,1)S(1)}, u32[]{:S(2)}, u32[]{:S(2)}) %all-to-all-start.1) | async-done | bytes 2359328 | tf_op jit(solution)/shard_map/all_to_all | solution.py:134
  140.8 0.5 shard_map.76
  141.3 0.8 copy-done
  142.1 0.1 reduce.4
  142.2 0.7 broadcast_in_dim.22
  142.9 12.0 %all-to-all-start.2 = ((f32[64,8,128]{2,1,0:T(8,128)}), f32[64,8,128]{2,1,0:T(8,128)S(1)}, u32[]{:S(2)}, u32[]{:S(2)}) async-start(f32[64,8,128]{2,1,0:T(8,128)} %broadcast_in_dim.22), calls=%async_computation.2 | async-start | bytes 524288 | tf_op jit(solution)/shard_map/all_to_all | solution.py:22
  154.9 34.6 %psum.7.moments_ref = f32[8,384]{1,0:T(8,128)S(1)} all-reduce(f32[8,384]{1,0:T(8,128)S(1)} %get-tuple-element.44), channel_id=1, replica_groups=mesh['y'=8,'zh'=4,'c'=2,'zl'=2,'x'=4] {'zl','x'}, use_global_device_ids=true, to_apply=%region_5.6 | all-reduce | flops 3072 | bytes 24576 | tf_op jit(solution)/shard_map/psum | solution.py:150
  189.5 1.1 copy-done.1
  190.6 1.0 shard_map.77
  191.6 0.1 reduce_sum.59
  191.7 0.6 slice_bitcast_fusion
  (23 shorter events, 0.2 us)
Async XLA Ops:
  23.2 19.2 %collective-permute-start = (bf16[192,1536]{1,0:T(8,128)(2,1)S(1)}, bf16[192,1536]{1,0:T(8,128)(2,1)S(1)}, u32[]{:S(2)}, u32[]{:S(2)}) collective-permute-start(bf16[192,1536]{1,0:T(8,128)(2,1)S(1)} %all_gather.3.refs_0_), channel_id=1, source_target_pairs={{0,64},{64,128},{128,192},{192,256},{256,320},{320,384},{384,448},... | collective-permute-start | bytes 1769480 | tf_op jit(solution)/shard_map/ppermute | solution.py:26
  25.8 16.6 %collective-permute-start.1 = (bf16[192,1536]{1,0:T(8,128)(2,1)S(1)}, bf16[192,1536]{1,0:T(8,128)(2,1)S(1)}, u32[]{:S(2)}, u32[]{:S(2)}) collective-permute-start(bf16[192,1536]{1,0:T(8,128)(2,1)S(1)} %all_gather.3.refs_0_), channel_id=1, source_target_pairs={{0,448},{64,0},{128,64},{192,128},{256,192},{320,256},{384,320},{4... | collective-permute-start | bytes 1769480 | tf_op jit(solution)/shard_map/ppermute | solution.py:26
  34.4 7.5 %copy-start.2 = (bf16[384,384]{1,0:T(8,128)(2,1)S(1)}, bf16[384,384]{1,0:T(8,128)(2,1)}, u32[]{:S(2)}) copy-start(bf16[384,384]{1,0:T(8,128)(2,1)} %param.5) | copy-start | bytes 884740
  42.4 21.9 %collective-permute-start.4 = (bf16[1536,384]{1,0:T(8,128)(2,1)}, bf16[1536,384]{1,0:T(8,128)(2,1)}, u32[]{:S(2)}, u32[]{:S(2)}) collective-permute-start(bf16[1536,384]{1,0:T(8,128)(2,1)} %fusion.36), channel_id=1, source_target_pairs={{0,8},{8,0},{1,9},{9,1},{2,10},{10,2},{3,11},{11,3},{4,12},{12,4},... | collective-permute-start | bytes 3538952 | tf_op jit(solution)/shard_map/ppermute | solution.py:26
  44.3 19.8 %collective-permute-start.2 = (bf16[192,1536]{1,0:T(8,128)(2,1)S(1)}, bf16[192,1536]{1,0:T(8,128)(2,1)S(1)}, u32[]{:S(2)}, u32[]{:S(2)}) collective-permute-start(bf16[192,1536]{1,0:T(8,128)(2,1)S(1)} %collective-permute-done.refs_0_), channel_id=1, source_target_pairs={{0,64},{64,128},{128,192},{192,256},{256,320},{320,384},{384,448},... | collective-permute-start | bytes 1769480 | tf_op jit(solution)/shard_map/ppermute | solution.py:26
  46.2 18.1 %collective-permute-start.3 = (bf16[192,1536]{1,0:T(8,128)(2,1)S(1)}, bf16[192,1536]{1,0:T(8,128)(2,1)S(1)}, u32[]{:S(2)}, u32[]{:S(2)}) collective-permute-start(bf16[192,1536]{1,0:T(8,128)(2,1)S(1)} %collective-permute-done.1.refs_0_), channel_id=1, source_target_pairs={{0,448},{64,0},{128,64},{192,128},{256,192},{320,256},{384,320},{4... | collective-permute-start | bytes 1769480 | tf_op jit(solution)/shard_map/ppermute | solution.py:26
  52.0 12.1 %all-to-all-start = ((f32[8,8,384]{2,1,0:T(8,128)}), f32[8,8,384]{2,1,0:T(8,128)S(1)}, u32[]{:S(2)}, u32[]{:S(2)}) async-start(f32[8,8,384]{2,1,0:T(8,128)} %broadcast_in_dim.19), calls=%async_computation | async-start | bytes 196608 | tf_op jit(solution)/shard_map/all_to_all | solution.py:22
  69.7 18.5 %collective-permute-start.5 = (bf16[192,1536]{1,0:T(8,128)(2,1)S(1)}, bf16[192,1536]{1,0:T(8,128)(2,1)S(1)}, u32[]{:S(2)}, u32[]{:S(2)}) collective-permute-start(bf16[192,1536]{1,0:T(8,128)(2,1)S(1)} %collective-permute-done.2.refs_0_), channel_id=1, source_target_pairs={{0,64},{64,128},{128,192},{192,256},{256,320},{320,384},{384,448},... | collective-permute-start | bytes 1769480 | tf_op jit(solution)/shard_map/ppermute | solution.py:26
  71.6 17.7 %collective-permute-start.6 = (bf16[192,1536]{1,0:T(8,128)(2,1)S(1)}, bf16[192,1536]{1,0:T(8,128)(2,1)S(1)}, u32[]{:S(2)}, u32[]{:S(2)}) collective-permute-start(bf16[192,1536]{1,0:T(8,128)(2,1)S(1)} %collective-permute-done.3.refs_0_), channel_id=1, source_target_pairs={{0,448},{64,0},{128,64},{192,128},{256,192},{320,256},{384,320},{4... | collective-permute-start | bytes 1769480 | tf_op jit(solution)/shard_map/ppermute | solution.py:26
  89.4 11.2 %collective-permute-start.7 = (bf16[96,1536]{1,0:T(8,128)(2,1)S(1)}, bf16[96,1536]{1,0:T(8,128)(2,1)S(1)}, u32[]{:S(2)}, u32[]{:S(2)}) collective-permute-start(bf16[96,1536]{1,0:T(8,128)(2,1)S(1)} %slice.15), channel_id=1, source_target_pairs={{0,64},{64,128},{128,192},{192,256},{256,320},{320,384},{384,448},... | collective-permute-start | bytes 884744 | tf_op jit(solution)/shard_map/ppermute | solution.py:26
  91.3 10.5 %collective-permute-start.8 = (bf16[96,1536]{1,0:T(8,128)(2,1)S(1)}, bf16[96,1536]{1,0:T(8,128)(2,1)S(1)}, u32[]{:S(2)}, u32[]{:S(2)}) collective-permute-start(bf16[96,1536]{1,0:T(8,128)(2,1)S(1)} %slice.16), channel_id=1, source_target_pairs={{0,448},{64,0},{128,64},{192,128},{256,192},{320,256},{384,320},{4... | collective-permute-start | bytes 884744 | tf_op jit(solution)/shard_map/ppermute | solution.py:26
  103.5 6.8 %copy-start.3 = (bf16[384]{0:T(512)(128)(2,1)S(1)}, bf16[384]{0:T(512)(128)(2,1)}, u32[]{:S(2)}) copy-start(bf16[384]{0:T(512)(128)(2,1)} %param.6) | copy-start | bytes 2308
  103.5 37.3 %all-to-all-start.1 = ((bf16[16,192,384]{2,1,0:T(8,128)(2,1)}), bf16[16,192,384]{2,1,0:T(8,128)(2,1)S(1)}, u32[]{:S(2)}, u32[]{:S(2)}) async-start(bf16[16,192,384]{2,1,0:T(8,128)(2,1)} %bitcast.5), calls=%async_computation.1 | async-start | bytes 4718592 | tf_op jit(solution)/shard_map/all_to_all | solution.py:134
  141.2 0.8 copy-start
  142.9 48.7 %all-to-all-start.2 = ((f32[64,8,128]{2,1,0:T(8,128)}), f32[64,8,128]{2,1,0:T(8,128)S(1)}, u32[]{:S(2)}, u32[]{:S(2)}) async-start(f32[64,8,128]{2,1,0:T(8,128)} %broadcast_in_dim.22), calls=%async_computation.2 | async-start | bytes 524288 | tf_op jit(solution)/shard_map/all_to_all | solution.py:22
  189.5 1.1 copy-start.1

commit v4 on v1

v4 whole, which is shorter than its diff:
```python
import jax
import jax.numpy as jnp
from jax import lax
from jax.experimental import pallas as pl
from jax.experimental.pallas import tpu as pltpu
from jax.sharding import Mesh, PartitionSpec as P

NAMES = ("y", "zh", "c", "zl", "x")
SIZES = (8, 4, 2, 2, 4)
DP, MP, CHIPS = ("y", "zh", "c"), ("zl", "x"), ("c", "zl", "x")
F32, BF16 = jnp.float32, jnp.bfloat16
SHARD = 48
WIDTH = 3072
PARAMS = pltpu.CompilerParams(vmem_limit_bytes=20 * 1024 * 1024)
together = lax.optimization_barrier


def gelu_exact(value):
    return jax.nn.gelu(value, approximate=False)


def shift(array, axis, n, by):
    return lax.ppermute(array, axis, [(i, (i - by) % n) for i in range(n)])


def partner(array, axis, n, bit):
    return lax.ppermute(array, axis, [(i, i ^ bit) for i in range(n)])


def products(groups, d_own, d_other, place, parts):
    tokens, hidden = d_own.shape
    flat = [p for _, pieces in groups for p in pieces]
    rows, n = sum(p.shape[0] for p in groups[0][1]), len(groups)

    def kernel(place_ref, own_ref, other_ref, *refs):
        w_refs, (out_ref, held, sem) = refs[: len(flat)], refs[-3:]
        w = jnp.concatenate([r[...] for r in w_refs], axis=0)
        copies = []
        for k, d_ref in enumerate((own_ref, other_ref)):
            half = lax.rem(place_ref[1] + k, 2)
            out = lax.dot_general(
                w, d_ref[...], (((1,), (1,)), ((), ())), preferred_element_type=F32
            ).astype(BF16)
            for g, (offset, _) in enumerate(groups):
                held[k, g] = out[g * rows : (g + 1) * rows]
                block = lax.rem(place_ref[0] + offset, 8)
                copies.append(
                    pltpu.make_async_copy(held.at[k, g], out_ref.at[half, block], sem.at[k, g])
                )
                copies[-1].start()
        for copy in copies:
            copy.wait()

    whole = pl.BlockSpec(memory_space=pltpu.VMEM)
    return pl.pallas_call(
        kernel,
        in_specs=[pl.BlockSpec(memory_space=pltpu.SMEM)]
        + [whole] * (2 + len(flat))
        + [pl.BlockSpec(memory_space=pl.ANY)] * (parts is not None),
        out_specs=pl.BlockSpec(memory_space=pl.ANY),
        out_shape=jax.ShapeDtypeStruct((2, 8, rows, tokens), BF16),
        scratch_shapes=[pltpu.VMEM((2, n, rows, tokens), BF16), pltpu.SemaphoreType.DMA((2, n))],
        input_output_aliases={} if parts is None else {3 + len(flat): 0},
        compiler_params=PARAMS,
        cost_estimate=pl.CostEstimate(
            flops=n * rows * hidden * tokens, bytes_accessed=1 << 18, transcendentals=0
        ),
    )(place, d_own, d_other, *flat, *([] if parts is None else [parts]))


def sum_kernel(parts_ref, xhat_ref, gain_ref, d_ref, moments_ref, share_ref):
    first, second = 0.0, 0.0
    for z in range(4):
        for c in range(2):
            total = parts_ref[c * 8, pl.ds(z * SHARD, SHARD), :].astype(F32)
            for m in range(1, 8):
                total += parts_ref[c * 8 + m, pl.ds(z * SHARD, SHARD), :].astype(F32)
            at = pl.ds((z * 2 + c) * SHARD, SHARD)
            xhat, g = xhat_ref[at, :], total * gain_ref[at, :]
            d_ref[at, :] = g
            value = total * xhat
            share_ref[at, :] = value[:, :128] + value[:, 128:256] + value[:, 256:]
            first += jnp.sum(g, axis=0, keepdims=True)
            second += jnp.sum(g * xhat, axis=0, keepdims=True)
    moments_ref[...] = jnp.concatenate([first, second, jnp.zeros((6, first.shape[1]), F32)], axis=0)
    row = jnp.sum(share_ref[...].T, axis=0, keepdims=True)
    share_ref[0:8, :] = jnp.concatenate(
        [row[:, i * 128 : (i + 1) * 128] for i in range(3)] + [jnp.zeros((5, 128), F32)], axis=0
    )


def final_kernel(d_ref, xhat_ref, moments_ref, rstd_ref, out_ref):
    both = moments_ref[...] * (1.0 / WIDTH)
    value = rstd_ref[...] * (d_ref[...] - both[0:1] - xhat_ref[...] * both[1:2])
    out_ref[...] = value.T.astype(BF16)


def on_device(tokens, gain, pre_act, w_in, act_cotangent):
    rows, share = tokens.shape
    here = [lax.axis_index(a).astype(jnp.int32).reshape(1) for a in ("y", "c")]
    place = jnp.concatenate(here)

    def tie(behind, ahead, done, *later):
        (behind_next, _), (ahead_next, _) = together((behind, done)), together((ahead, done))
        return behind_next, ahead_next, *together((behind, ahead, done, *later))[2:]

    w0 = lax.all_gather(w_in, "zh", axis=0, tiled=True)
    w0, pre_act, act_cotangent = together((w0, pre_act, act_cotangent))
    behind1, ahead1 = shift(w0, "y", 8, -1), shift(w0, "y", 8, 1)
    _, gelu_back = jax.vjp(gelu_exact, pre_act.astype(F32))
    d_own = gelu_back(act_cotangent.astype(F32))[0].astype(BF16)

    behind, ahead, d_own = tie(behind1, ahead1, d_own)
    behind2, ahead2 = shift(behind, "y", 8, -1), shift(ahead, "y", 8, 1)
    d_other = partner(d_own, "c", 2, 1)
    parts = products([(0, [w0]), (7, [behind1]), (1, [ahead1])], d_own, d_other, place, None)

    behind, ahead, parts = tie(behind2, ahead2, parts)
    behind3, ahead3 = shift(behind, "y", 8, -1), shift(ahead, "y", 8, 1)
    parts = products([(6, [behind2]), (2, [ahead2])], d_own, d_other, place, parts)

    behind, ahead, parts = tie(behind3, ahead3, parts)
    half = w0.shape[0] // 2
    behind4, ahead4 = shift(behind[:half], "y", 8, -1), shift(ahead[half:], "y", 8, 1)
    parts = products([(5, [behind3]), (3, [ahead3])], d_own, d_other, place, parts)

    behind4, parts, tokens = together((behind4, parts, tokens))
    parts = products([(4, [behind4, ahead4])], d_own, d_other, place, parts)
    parts = lax.all_to_all(parts.reshape(16, share // 2, rows), CHIPS, 0, 0)

    x = tokens.astype(F32).T
    mean = jnp.mean(x, axis=0, keepdims=True)
    square = jnp.sum((x - mean) ** 2, axis=0, keepdims=True)
    for axis, n, bit, count in (("x", 4, 1, 1), ("x", 4, 2, 2), ("zl", 2, 1, 4)):
        other = partner(jnp.concatenate([mean, square] * 4, axis=0), axis, n, bit)
        mean_too, square_too = other[0:1], other[1:2]
        square = square + square_too + (share * count / 2) * (mean - mean_too) ** 2
        mean = (mean + mean_too) * 0.5
    rstd = 1.0 / jnp.sqrt(square * (1.0 / WIDTH) + 1e-06)
    xhat = (x - mean) * rstd

    d_scaled, moments, gain_share = pl.pallas_call(
        sum_kernel,
        out_shape=[
            jax.ShapeDtypeStruct((share, rows), F32),
            jax.ShapeDtypeStruct((8, rows), F32),
            jax.ShapeDtypeStruct((share, 128), F32),
        ],
        compiler_params=PARAMS,
    )(parts, xhat, gain.astype(F32)[:, None])

    gain_share = jnp.broadcast_to(gain_share[:8], (64, 8, 128))
    gain_gradient = jnp.sum(lax.all_to_all(gain_share, DP, 0, 0), axis=0)[:3].reshape(share)

    for axis, n, bit in (("x", 4, 1), ("x", 4, 2), ("zl", 2, 1)):
        moments += partner(moments, axis, n, bit)
    token_gradient = pl.pallas_call(
        final_kernel,
        out_shape=jax.ShapeDtypeStruct((rows, share), BF16),
        compiler_params=PARAMS,
    )(d_scaled, xhat, moments, rstd)
    return (token_gradient, gain_gradient)


def solution(mesh):
    fine = Mesh(mesh.devices.reshape(SIZES), NAMES)
    placed = (P(DP, MP), P(MP), P(DP, MP), P(DP, MP), P(DP, MP))
    return jax.shard_map(
        on_device, mesh=fine, in_specs=placed, out_specs=(P(DP, MP), P(MP)), check_vma=False
    )
```

time: 190 us -> 181 us (0.953)
  starting transfers between devices: 32.8 us -> 71.4 us
  waiting for transfers between devices: 93.8 us -> 60.1 us
  between operations: 14.2 us -> 0.9 us
  local copies, waits for them, and re-layouts: 8.57 us -> 3.68 us
  Pallas kernels: 10.4 us -> 13.3 us
    ppermute x1 -> x15, waiting for transfers between devices: 0.01 us -> 60.1 us  [the longest x7 37.8 us: partner(): return lax.ppermute(array, axis, [(i, i ^ bit) for i in range(n)])]
    all_to_all x4 -> x2, waiting for transfers between devices: 48.7 us -> 0.01 us  [the longest x1 0.01 us: on_device(): parts = lax.all_to_all(parts.reshape(16, share // 2, rows), CHIPS, 0, 0)]
    all_gather x1 -> x0, waiting for transfers between devices: 45 us -> none  [on_device(): w_half = lax.all_gather(w_half, 'y', axis=0, tiled=True)]
    ppermute x1 -> x15, starting transfers between devices: 4.75 us -> 48.1 us  [the longest x8 26.7 us: shift(): return lax.ppermute(array, axis, [(i, (i - by) % n) for i in range(n)])]
    all_to_all x4 -> x2, starting transfers between devices: 28 us -> 23.3 us  [the longest x1 14.4 us: on_device(): lax.all_to_all(gain_share, DP, 0, 0)]
    unnamed x13 -> x8, local copies, waits for them, and re-layouts: 5.82 us -> 1.9 us
    pallas_call x1 -> x4, Pallas kernels: 8.9 us -> 11.9 us  [products(): pl.pallas_call(kernel, in_specs=[pl.BlockSpec(memory_space=pltpu.SMEM)] +...]
  transfers between devices with their start and end apart: 6 -> 17, of which waited for: 4 -> 14; matrix products, arithmetic and copies ran while one was open for 5% -> 4% of each run, Pallas kernels for 5% -> 6%
where the time goes in v4:
time: 181 us; the launch traced here: 179 us
  starting transfers between devices  71.4 us (39%)
  waiting for transfers between devices  60.1 us (33%)
  blocking collectives  22.2 us (12%)
  Pallas kernels  13.3 us (7%)
  other arithmetic  7.27 us (4%)
  local copies, waits for them, and re-layouts  3.68 us (2%)
    ppermute x7, waiting for transfers between devices, partner(): return lax.ppermute(array, axis, [(i, i ^ bit) for i in range(n)])  37.8 us
    ppermute x8, starting transfers between devices, shift(): return lax.ppermute(array, axis, [(i, (i - by) % n) for i in range(n)])  26.7 us
    ppermute x8, waiting for transfers between devices, shift(): return lax.ppermute(array, axis, [(i, (i - by) % n) for i in range(n)])  22.3 us
    all_gather x1, blocking collectives, on_device(): w0 = lax.all_gather(w_in, 'zh', axis=0, tiled=True)  22.2 us
    ppermute x7, starting transfers between devices, partner(): return lax.ppermute(array, axis, [(i, i ^ bit) for i in range(n)])  21.5 us
    all_to_all x1, starting transfers between devices, on_device(): lax.all_to_all(gain_share, DP, 0, 0)  14.4 us
    pallas_call x4, Pallas kernels, products(): pl.pallas_call(kernel, in_specs=[pl.BlockSpec(memory_space=pltpu.SMEM)] +...  11.9 us
    all_to_all x1, starting transfers between devices, on_device(): parts = lax.all_to_all(parts.reshape(16, share // 2, rows), CHIPS, 0, 0)  8.91 us
  transfers between devices with their start and end apart: 17, of which 14 were waited for; matrix products, arithmetic and copies ran while one was open for 4% of the time, Pallas kernels for 6%

profile of v4, /device:TPU:1, one launch (start us, length us, event | category | flops | bytes accessed | tf_op | source)
XLA Modules:
  0.0 178.9 jit_solution(7047712387682774188)
XLA Ops:
  0.6 22.2 %all_gather.3.refs_0_ = bf16[192,1536]{1,0:T(8,128)(2,1)S(1)} all-gather(bf16[48,1536]{1,0:T(8,128)(2,1)} %param.8), channel_id=1, replica_groups=mesh['y'=8,'zh'=4,'c'=2,'zl'=2,'x'=4] {'zh'}, dimensions={0}, use_global_device_ids=true | all-gather | bytes 737280 | tf_op jit(solution)/shard_map/all_gather | solution.py:107
  22.9 3.2 %collective-permute-start = (bf16[192,1536]{1,0:T(8,128)(2,1)S(1)}, bf16[192,1536]{1,0:T(8,128)(2,1)}, u32[]{:S(2)}, u32[]{:S(2)}) collective-permute-start(bf16[192,1536]{1,0:T(8,128)(2,1)S(1)} %all_gather.3.refs_0_), channel_id=1, source_target_pairs={{0,64},{64,128},{128,192},{192,256},{256,320},{320,384},{384,448},... | collective-permute-start | bytes 1769480 | tf_op jit(solution)/shard_map/ppermute | solution.py:23
  26.1 3.8 %collective-permute-start.1 = (bf16[192,1536]{1,0:T(8,128)(2,1)S(1)}, bf16[192,1536]{1,0:T(8,128)(2,1)S(1)}, u32[]{:S(2)}, u32[]{:S(2)}) collective-permute-start(bf16[192,1536]{1,0:T(8,128)(2,1)S(1)} %all_gather.3.refs_0_), channel_id=1, source_target_pairs={{0,448},{64,0},{128,64},{192,128},{256,192},{320,256},{384,320},{4... | collective-permute-start | bytes 1769480 | tf_op jit(solution)/shard_map/ppermute | solution.py:23
  29.9 6.8 %fusion.34.own_ref = bf16[384,1536]{1,0:T(8,128)(2,1)S(1)} fusion(bf16[384,1536]{1,0:T(8,128)(2,1)} %param.9, bf16[384,1536]{1,0:T(8,128)(2,1)} %param.7), kind=kLoop, calls=%fused_computation.39 | loop fusion | flops 43646976 | bytes 3538944 | tf_op jit(solution)/shard_map/convert_element_type | solution.py:111
  36.7 3.2 %collective-permute-done.refs_1_ = bf16[192,1536]{1,0:T(8,128)(2,1)} collective-permute-done((bf16[192,1536]{1,0:T(8,128)(2,1)S(1)}, bf16[192,1536]{1,0:T(8,128)(2,1)}, u32[]{:S(2)}, u32[]{:S(2)}) %collective-permute-start) | collective-permute-done | bytes 589856 | tf_op jit(solution)/shard_map/ppermute | solution.py:23
  39.9 0.9 collective-permute-done.1.refs_2_
  40.8 4.8 %collective-permute-start.2 = (bf16[384,1536]{1,0:T(8,128)(2,1)S(1)}, bf16[384,1536]{1,0:T(8,128)(2,1)S(1)}, u32[]{:S(2)}, u32[]{:S(2)}) collective-permute-start(bf16[384,1536]{1,0:T(8,128)(2,1)S(1)} %fusion.34.own_ref), channel_id=1, source_target_pairs={{0,8},{8,0},{1,9},{9,1},{2,10},{10,2},{3,11},{11,3},{4,12},{12,4},... | collective-permute-start | bytes 3538952 | tf_op jit(solution)/shard_map/ppermute | solution.py:27
  45.6 3.2 %collective-permute-start.3 = (bf16[192,1536]{1,0:T(8,128)(2,1)}, bf16[192,1536]{1,0:T(8,128)(2,1)}, u32[]{:S(2)}, u32[]{:S(2)}) collective-permute-start(bf16[192,1536]{1,0:T(8,128)(2,1)} %collective-permute-done.refs_1_), channel_id=1, source_target_pairs={{0,64},{64,128},{128,192},{192,256},{256,320},{320,384},{384,448},... | collective-permute-start | bytes 1769480 | tf_op jit(solution)/shard_map/ppermute | solution.py:23
  48.8 3.7 %collective-permute-start.5 = (bf16[192,1536]{1,0:T(8,128)(2,1)S(1)}, bf16[192,1536]{1,0:T(8,128)(2,1)}, u32[]{:S(2)}, u32[]{:S(2)}) collective-permute-start(bf16[192,1536]{1,0:T(8,128)(2,1)S(1)} %collective-permute-done.1.refs_2_), channel_id=1, source_target_pairs={{0,448},{64,0},{128,64},{192,128},{256,192},{320,256},{384,320},{4... | collective-permute-start | bytes 1769480 | tf_op jit(solution)/shard_map/ppermute | solution.py:23
  52.6 0.1 pad_add_fusion.place_ref
  52.7 3.8 %shard_map.68.refs_2_ = bf16[2,8,192,384]{3,2,1,0:T(8,128)(2,1)} custom-call(s32[2]{0:T(128)S(1)} %pad_add_fusion.place_ref, bf16[384,1536]{1,0:T(8,128)(2,1)S(1)} %fusion.34.own_ref, bf16[384,1536]{1,0:T(8,128)(2,1)S(1)} %collective-permute-done.2.other_ref, bf16[192,1536]{1,0:T(8,128)(2,1)S(1)} %all_gather.3.refs_0_, ...), custom_call_target="tpu_custom_call" | custom-call | flops 339738624 | bytes 262144 | tf_op jit(solution)/shard_map/pallas_call | solution.py:55
  56.5 8.2 %collective-permute-done.3.refs_0_ = bf16[192,1536]{1,0:T(8,128)(2,1)} collective-permute-done((bf16[192,1536]{1,0:T(8,128)(2,1)}, bf16[192,1536]{1,0:T(8,128)(2,1)}, u32[]{:S(2)}, u32[]{:S(2)}) %collective-permute-start.3) | collective-permute-done | bytes 589856 | tf_op jit(solution)/shard_map/ppermute | solution.py:23
  64.6 1.9 %collective-permute-start.4 = (bf16[192,1536]{1,0:T(8,128)(2,1)}, bf16[192,1536]{1,0:T(8,128)(2,1)S(1)}, u32[]{:S(2)}, u32[]{:S(2)}) collective-permute-start(bf16[192,1536]{1,0:T(8,128)(2,1)} %collective-permute-done.3.refs_0_), channel_id=1, source_target_pairs={{0,64},{64,128},{128,192},{192,256},{256,320},{320,384},{384,448},... | collective-permute-start | bytes 1769480 | tf_op jit(solution)/shard_map/ppermute | solution.py:23
  66.6 0.1 collective-permute-done.5.refs_1_
  66.7 4.5 %collective-permute-start.7 = (bf16[192,1536]{1,0:T(8,128)(2,1)}, bf16[192,1536]{1,0:T(8,128)(2,1)S(1)}, u32[]{:S(2)}, u32[]{:S(2)}) collective-permute-start(bf16[192,1536]{1,0:T(8,128)(2,1)} %collective-permute-done.5.refs_1_), channel_id=1, source_target_pairs={{0,448},{64,0},{128,64},{192,128},{256,192},{320,256},{384,320},{4... | collective-permute-start | bytes 1769480 | tf_op jit(solution)/shard_map/ppermute | solution.py:23
  71.2 3.3 %shard_map.69.refs_2_ = bf16[2,8,192,384]{3,2,1,0:T(8,128)(2,1)} custom-call(s32[2]{0:T(128)S(1)} %pad_add_fusion.place_ref, bf16[384,1536]{1,0:T(8,128)(2,1)S(1)} %fusion.34.own_ref, bf16[384,1536]{1,0:T(8,128)(2,1)S(1)} %collective-permute-done.2.other_ref, bf16[192,1536]{1,0:T(8,128)(2,1)} %collective-permute-done.3.refs_0_, ...), custom_call_target="tpu_custom_call", output_to_operand_aliasing={{}: (5, {})} | custom-call | flops 226492416 | bytes 262144 | tf_op jit(solution)/shard_map/pallas_call | solution.py:55
  74.5 7.7 %collective-permute-done.4.refs_0_ = bf16[192,1536]{1,0:T(8,128)(2,1)S(1)} collective-permute-done((bf16[192,1536]{1,0:T(8,128)(2,1)}, bf16[192,1536]{1,0:T(8,128)(2,1)S(1)}, u32[]{:S(2)}, u32[]{:S(2)}) %collective-permute-start.4) | collective-permute-done | bytes 589856 | tf_op jit(solution)/shard_map/ppermute | solution.py:23
  82.3 1.9 %collective-permute-start.6 = (bf16[96,1536]{1,0:T(8,128)(2,1)S(1)}, bf16[96,1536]{1,0:T(8,128)(2,1)S(1)}, u32[]{:S(2)}, u32[]{:S(2)}) collective-permute-start(bf16[96,1536]{1,0:T(8,128)(2,1)S(1)} %slice.30), channel_id=1, source_target_pairs={{0,64},{64,128},{128,192},{192,256},{256,320},{320,384},{384,448},... | collective-permute-start | bytes 884744 | tf_op jit(solution)/shard_map/ppermute | solution.py:23
  84.2 0.2 collective-permute-done.7.refs_1_
  84.4 4.4 %collective-permute-start.8 = (bf16[96,1536]{1,0:T(8,128)(2,1)S(1)}, bf16[96,1536]{1,0:T(8,128)(2,1)S(1)}, u32[]{:S(2)}, u32[]{:S(2)}) collective-permute-start(bf16[96,1536]{1,0:T(8,128)(2,1)S(1)} %slice.31), channel_id=1, source_target_pairs={{0,448},{64,0},{128,64},{192,128},{256,192},{320,256},{384,320},{4... | collective-permute-start | bytes 884744 | tf_op jit(solution)/shard_map/ppermute | solution.py:23
  88.8 2.6 %shard_map.70.refs_2_ = bf16[2,8,192,384]{3,2,1,0:T(8,128)(2,1)} custom-call(s32[2]{0:T(128)S(1)} %pad_add_fusion.place_ref, bf16[384,1536]{1,0:T(8,128)(2,1)S(1)} %fusion.34.own_ref, bf16[384,1536]{1,0:T(8,128)(2,1)S(1)} %collective-permute-done.2.other_ref, bf16[192,1536]{1,0:T(8,128)(2,1)S(1)} %collective-permute-done.4.refs_0_, ...), custom_call_target="tpu_custom_call", output_to_operand_aliasing={{}: (5, {})} | custom-call | flops 226492416 | bytes 262144 | tf_op jit(solution)/shard_map/pallas_call | solution.py:55
  91.5 1.0 collective-permute-done.6.refs_0_
  92.4 1.0 collective-permute-done.8.refs_1_
  93.4 2.1 %shard_map.71 = bf16[2,8,192,384]{3,2,1,0:T(8,128)(2,1)} custom-call(s32[2]{0:T(128)S(1)} %pad_add_fusion.place_ref, bf16[384,1536]{1,0:T(8,128)(2,1)S(1)} %fusion.34.own_ref, bf16[384,1536]{1,0:T(8,128)(2,1)S(1)} %collective-permute-done.2.other_ref, bf16[96,1536]{1,0:T(8,128)(2,1)S(1)} %collective-permute-done.6.refs_0_, ...), custom_call_target="tpu_custom_call", output_to_operand_aliasing={{}: (5, {})} | custom-call | flops 113246208 | bytes 262144 | tf_op jit(solution)/shard_map/pallas_call | solution.py:55
  95.6 8.9 %all-to-all-start = ((bf16[16,192,384]{2,1,0:T(8,128)(2,1)}), bf16[16,192,384]{2,1,0:T(8,128)(2,1)S(1)}, u32[]{:S(2)}, u32[]{:S(2)}) async-start(bf16[16,192,384]{2,1,0:T(8,128)(2,1)} %bitcast.2), calls=%async_computation | async-start | bytes 4718592 | tf_op jit(solution)/shard_map/all_to_all | solution.py:129
  104.5 0.2 copy.13
  104.7 0.1 convert_reduce_fusion
  104.8 0.1 fusion.37
  105.0 3.3 %collective-permute-start.9 = (f32[8,384]{1,0:T(8,128)S(1)}, f32[8,384]{1,0:T(8,128)S(1)}, u32[]{:S(2)}, u32[]{:S(2)}) collective-permute-start(f32[8,384]{1,0:T(8,128)S(1)} %concatenate.13), channel_id=1, source_target_pairs={{0,1},{1,0},{2,3},{3,2},{4,5},{5,4},{6,7},{7,6},{8,9},{9,8},{10,11... | collective-permute-start | bytes 36872 | tf_op jit(solution)/shard_map/ppermute | solution.py:27
  108.3 24.8 %collective-permute-done.9 = f32[8,384]{1,0:T(8,128)S(1)} collective-permute-done((f32[8,384]{1,0:T(8,128)S(1)}, f32[8,384]{1,0:T(8,128)S(1)}, u32[]{:S(2)}, u32[]{:S(2)}) %collective-permute-start.9) | collective-permute-done | bytes 12320 | tf_op jit(solution)/shard_map/ppermute | solution.py:27
  133.1 1.9 %collective-permute-start.10 = (f32[8,384]{1,0:T(8,128)S(1)}, f32[8,384]{1,0:T(8,128)S(1)}, u32[]{:S(2)}, u32[]{:S(2)}) collective-permute-start(f32[8,384]{1,0:T(8,128)S(1)} %concatenate.14), channel_id=1, source_target_pairs={{0,2},{1,3},{2,0},{3,1},{4,6},{5,7},{6,4},{7,5},{8,10},{9,11},{10,... | collective-permute-start | bytes 36872 | tf_op jit(solution)/shard_map/ppermute | solution.py:27
  135.0 4.0 %collective-permute-done.10 = f32[8,384]{1,0:T(8,128)S(1)} collective-permute-done((f32[8,384]{1,0:T(8,128)S(1)}, f32[8,384]{1,0:T(8,128)S(1)}, u32[]{:S(2)}, u32[]{:S(2)}) %collective-permute-start.10) | collective-permute-done | bytes 12320 | tf_op jit(solution)/shard_map/ppermute | solution.py:27
  139.1 3.8 %collective-permute-start.11 = (f32[8,384]{1,0:T(8,128)S(1)}, f32[8,384]{1,0:T(8,128)S(1)}, u32[]{:S(2)}, u32[]{:S(2)}) collective-permute-start(f32[8,384]{1,0:T(8,128)S(1)} %concatenate.15), channel_id=1, source_target_pairs={{0,4},{4,0},{1,5},{5,1},{2,6},{6,2},{3,7},{7,3},{8,12},{12,8},{9,1... | collective-permute-start | bytes 36872 | tf_op jit(solution)/shard_map/ppermute | solution.py:27
  142.9 0.1 reshape.31.gain_ref
  143.1 0.9 collective-permute-done.11
  144.1 0.5 shard_map.72
  144.6 0.8 copy-done
  145.5 0.7 broadcast_in_dim.15
  146.2 14.4 %all-to-all-start.1 = ((f32[64,8,128]{2,1,0:T(8,128)}), f32[64,8,128]{2,1,0:T(8,128)S(1)}, u32[]{:S(2)}, u32[]{:S(2)}) async-start(f32[64,8,128]{2,1,0:T(8,128)} %broadcast_in_dim.15), calls=%async_computation.1 | async-start | bytes 524288 | tf_op jit(solution)/shard_map/all_to_all | solution.py:153
  160.6 2.0 %collective-permute-start.12 = (f32[8,384]{1,0:T(8,128)S(1)}, f32[8,384]{1,0:T(8,128)S(1)}, u32[]{:S(2)}, u32[]{:S(2)}) collective-permute-start(f32[8,384]{1,0:T(8,128)S(1)} %get-tuple-element.36), channel_id=1, source_target_pairs={{0,1},{1,0},{2,3},{3,2},{4,5},{5,4},{6,7},{7,6},{8,9},{9,8},{10,11... | collective-permute-start | bytes 36872 | tf_op jit(solution)/shard_map/ppermute | solution.py:27
  162.6 2.7 %collective-permute-done.12 = f32[8,384]{1,0:T(8,128)S(1)} collective-permute-done((f32[8,384]{1,0:T(8,128)S(1)}, f32[8,384]{1,0:T(8,128)S(1)}, u32[]{:S(2)}, u32[]{:S(2)}) %collective-permute-start.12) | collective-permute-done | bytes 12320 | tf_op jit(solution)/shard_map/ppermute | solution.py:27
  165.3 1.9 %collective-permute-start.13 = (f32[8,384]{1,0:T(8,128)S(1)}, f32[8,384]{1,0:T(8,128)S(1)}, u32[]{:S(2)}, u32[]{:S(2)}) collective-permute-start(f32[8,384]{1,0:T(8,128)S(1)} %add.53), channel_id=1, source_target_pairs={{0,2},{1,3},{2,0},{3,1},{4,6},{5,7},{6,4},{7,5},{8,10},{9,11},{10,... | collective-permute-start | bytes 36872 | tf_op jit(solution)/shard_map/ppermute | solution.py:27
  167.2 4.3 %collective-permute-done.13 = f32[8,384]{1,0:T(8,128)S(1)} collective-permute-done((f32[8,384]{1,0:T(8,128)S(1)}, f32[8,384]{1,0:T(8,128)S(1)}, u32[]{:S(2)}, u32[]{:S(2)}) %collective-permute-start.13) | collective-permute-done | bytes 12320 | tf_op jit(solution)/shard_map/ppermute | solution.py:27
  171.5 3.6 %collective-permute-start.14 = (f32[8,384]{1,0:T(8,128)S(1)}, f32[8,384]{1,0:T(8,128)S(1)}, u32[]{:S(2)}, u32[]{:S(2)}) collective-permute-start(f32[8,384]{1,0:T(8,128)S(1)} %add.54), channel_id=1, source_target_pairs={{0,4},{4,0},{1,5},{5,1},{2,6},{6,2},{3,7},{7,3},{8,12},{12,8},{9,1... | collective-permute-start | bytes 36872 | tf_op jit(solution)/shard_map/ppermute | solution.py:27
  175.2 1.1 collective-permute-done.14
  176.2 1.1 copy-done.1
  177.3 0.9 shard_map.73
  178.3 0.6 slice_bitcast_fusion
  (26 shorter events, 0.4 us)
Async XLA Ops:
  22.9 17.0 %collective-permute-start = (bf16[192,1536]{1,0:T(8,128)(2,1)S(1)}, bf16[192,1536]{1,0:T(8,128)(2,1)}, u32[]{:S(2)}, u32[]{:S(2)}) collective-permute-start(bf16[192,1536]{1,0:T(8,128)(2,1)S(1)} %all_gather.3.refs_0_), channel_id=1, source_target_pairs={{0,64},{64,128},{128,192},{192,256},{256,320},{320,384},{384,448},... | collective-permute-start | bytes 1769480 | tf_op jit(solution)/shard_map/ppermute | solution.py:23
  26.1 14.7 %collective-permute-start.1 = (bf16[192,1536]{1,0:T(8,128)(2,1)S(1)}, bf16[192,1536]{1,0:T(8,128)(2,1)S(1)}, u32[]{:S(2)}, u32[]{:S(2)}) collective-permute-start(bf16[192,1536]{1,0:T(8,128)(2,1)S(1)} %all_gather.3.refs_0_), channel_id=1, source_target_pairs={{0,448},{64,0},{128,64},{192,128},{256,192},{320,256},{384,320},{4... | collective-permute-start | bytes 1769480 | tf_op jit(solution)/shard_map/ppermute | solution.py:23
  40.8 11.9 %collective-permute-start.2 = (bf16[384,1536]{1,0:T(8,128)(2,1)S(1)}, bf16[384,1536]{1,0:T(8,128)(2,1)S(1)}, u32[]{:S(2)}, u32[]{:S(2)}) collective-permute-start(bf16[384,1536]{1,0:T(8,128)(2,1)S(1)} %fusion.34.own_ref), channel_id=1, source_target_pairs={{0,8},{8,0},{1,9},{9,1},{2,10},{10,2},{3,11},{11,3},{4,12},{12,4},... | collective-permute-start | bytes 3538952 | tf_op jit(solution)/shard_map/ppermute | solution.py:27
  45.6 19.0 %collective-permute-start.3 = (bf16[192,1536]{1,0:T(8,128)(2,1)}, bf16[192,1536]{1,0:T(8,128)(2,1)}, u32[]{:S(2)}, u32[]{:S(2)}) collective-permute-start(bf16[192,1536]{1,0:T(8,128)(2,1)} %collective-permute-done.refs_1_), channel_id=1, source_target_pairs={{0,64},{64,128},{128,192},{192,256},{256,320},{320,384},{384,448},... | collective-permute-start | bytes 1769480 | tf_op jit(solution)/shard_map/ppermute | solution.py:23
  48.8 17.8 %collective-permute-start.5 = (bf16[192,1536]{1,0:T(8,128)(2,1)S(1)}, bf16[192,1536]{1,0:T(8,128)(2,1)}, u32[]{:S(2)}, u32[]{:S(2)}) collective-permute-start(bf16[192,1536]{1,0:T(8,128)(2,1)S(1)} %collective-permute-done.1.refs_2_), channel_id=1, source_target_pairs={{0,448},{64,0},{128,64},{192,128},{256,192},{320,256},{384,320},{4... | collective-permute-start | bytes 1769480 | tf_op jit(solution)/shard_map/ppermute | solution.py:23
  64.6 17.6 %collective-permute-start.4 = (bf16[192,1536]{1,0:T(8,128)(2,1)}, bf16[192,1536]{1,0:T(8,128)(2,1)S(1)}, u32[]{:S(2)}, u32[]{:S(2)}) collective-permute-start(bf16[192,1536]{1,0:T(8,128)(2,1)} %collective-permute-done.3.refs_0_), channel_id=1, source_target_pairs={{0,64},{64,128},{128,192},{192,256},{256,320},{320,384},{384,448},... | collective-permute-start | bytes 1769480 | tf_op jit(solution)/shard_map/ppermute | solution.py:23
  66.7 17.7 %collective-permute-start.7 = (bf16[192,1536]{1,0:T(8,128)(2,1)}, bf16[192,1536]{1,0:T(8,128)(2,1)S(1)}, u32[]{:S(2)}, u32[]{:S(2)}) collective-permute-start(bf16[192,1536]{1,0:T(8,128)(2,1)} %collective-permute-done.5.refs_1_), channel_id=1, source_target_pairs={{0,448},{64,0},{128,64},{192,128},{256,192},{320,256},{384,320},{4... | collective-permute-start | bytes 1769480 | tf_op jit(solution)/shard_map/ppermute | solution.py:23
  82.3 10.2 %collective-permute-start.6 = (bf16[96,1536]{1,0:T(8,128)(2,1)S(1)}, bf16[96,1536]{1,0:T(8,128)(2,1)S(1)}, u32[]{:S(2)}, u32[]{:S(2)}) collective-permute-start(bf16[96,1536]{1,0:T(8,128)(2,1)S(1)} %slice.30), channel_id=1, source_target_pairs={{0,64},{64,128},{128,192},{192,256},{256,320},{320,384},{384,448},... | collective-permute-start | bytes 884744 | tf_op jit(solution)/shard_map/ppermute | solution.py:23
  84.4 9.0 %collective-permute-start.8 = (bf16[96,1536]{1,0:T(8,128)(2,1)S(1)}, bf16[96,1536]{1,0:T(8,128)(2,1)S(1)}, u32[]{:S(2)}, u32[]{:S(2)}) collective-permute-start(bf16[96,1536]{1,0:T(8,128)(2,1)S(1)} %slice.31), channel_id=1, source_target_pairs={{0,448},{64,0},{128,64},{192,128},{256,192},{320,256},{384,320},{4... | collective-permute-start | bytes 884744 | tf_op jit(solution)/shard_map/ppermute | solution.py:23
  95.5 8.9 %copy-start.2 = (bf16[384,384]{1,0:T(8,128)(2,1)S(1)}, bf16[384,384]{1,0:T(8,128)(2,1)}, u32[]{:S(2)}) copy-start(bf16[384,384]{1,0:T(8,128)(2,1)} %param.5) | copy-start | bytes 884740
  95.6 47.4 %copy-start.3 = (bf16[384]{0:T(512)(128)(2,1)S(1)}, bf16[384]{0:T(512)(128)(2,1)}, u32[]{:S(2)}) copy-start(bf16[384]{0:T(512)(128)(2,1)} %param.6) | copy-start | bytes 2308
  95.6 48.5 %all-to-all-start = ((bf16[16,192,384]{2,1,0:T(8,128)(2,1)}), bf16[16,192,384]{2,1,0:T(8,128)(2,1)S(1)}, u32[]{:S(2)}, u32[]{:S(2)}) async-start(bf16[16,192,384]{2,1,0:T(8,128)(2,1)} %bitcast.2), calls=%async_computation | async-start | bytes 4718592 | tf_op jit(solution)/shard_map/all_to_all | solution.py:129
  105.0 28.1 %collective-permute-start.9 = (f32[8,384]{1,0:T(8,128)S(1)}, f32[8,384]{1,0:T(8,128)S(1)}, u32[]{:S(2)}, u32[]{:S(2)}) collective-permute-start(f32[8,384]{1,0:T(8,128)S(1)} %concatenate.13), channel_id=1, source_target_pairs={{0,1},{1,0},{2,3},{3,2},{4,5},{5,4},{6,7},{7,6},{8,9},{9,8},{10,11... | collective-permute-start | bytes 36872 | tf_op jit(solution)/shard_map/ppermute | solution.py:27
  133.1 5.9 %collective-permute-start.10 = (f32[8,384]{1,0:T(8,128)S(1)}, f32[8,384]{1,0:T(8,128)S(1)}, u32[]{:S(2)}, u32[]{:S(2)}) collective-permute-start(f32[8,384]{1,0:T(8,128)S(1)} %concatenate.14), channel_id=1, source_target_pairs={{0,2},{1,3},{2,0},{3,1},{4,6},{5,7},{6,4},{7,5},{8,10},{9,11},{10,... | collective-permute-start | bytes 36872 | tf_op jit(solution)/shard_map/ppermute | solution.py:27
  139.1 4.9 %collective-permute-start.11 = (f32[8,384]{1,0:T(8,128)S(1)}, f32[8,384]{1,0:T(8,128)S(1)}, u32[]{:S(2)}, u32[]{:S(2)}) collective-permute-start(f32[8,384]{1,0:T(8,128)S(1)} %concatenate.15), channel_id=1, source_target_pairs={{0,4},{4,0},{1,5},{5,1},{2,6},{6,2},{3,7},{7,3},{8,12},{12,8},{9,1... | collective-permute-start | bytes 36872 | tf_op jit(solution)/shard_map/ppermute | solution.py:27
  144.6 0.8 copy-start
  146.2 32.0 %all-to-all-start.1 = ((f32[64,8,128]{2,1,0:T(8,128)}), f32[64,8,128]{2,1,0:T(8,128)S(1)}, u32[]{:S(2)}, u32[]{:S(2)}) async-start(f32[64,8,128]{2,1,0:T(8,128)} %broadcast_in_dim.15), calls=%async_computation.1 | async-start | bytes 524288 | tf_op jit(solution)/shard_map/all_to_all | solution.py:153
  160.6 4.7 %collective-permute-start.12 = (f32[8,384]{1,0:T(8,128)S(1)}, f32[8,384]{1,0:T(8,128)S(1)}, u32[]{:S(2)}, u32[]{:S(2)}) collective-permute-start(f32[8,384]{1,0:T(8,128)S(1)} %get-tuple-element.36), channel_id=1, source_target_pairs={{0,1},{1,0},{2,3},{3,2},{4,5},{5,4},{6,7},{7,6},{8,9},{9,8},{10,11... | collective-permute-start | bytes 36872 | tf_op jit(solution)/shard_map/ppermute | solution.py:27
  165.3 6.2 %collective-permute-start.13 = (f32[8,384]{1,0:T(8,128)S(1)}, f32[8,384]{1,0:T(8,128)S(1)}, u32[]{:S(2)}, u32[]{:S(2)}) collective-permute-start(f32[8,384]{1,0:T(8,128)S(1)} %add.53), channel_id=1, source_target_pairs={{0,2},{1,3},{2,0},{3,1},{4,6},{5,7},{6,4},{7,5},{8,10},{9,11},{10,... | collective-permute-start | bytes 36872 | tf_op jit(solution)/shard_map/ppermute | solution.py:27
  171.5 4.7 %collective-permute-start.14 = (f32[8,384]{1,0:T(8,128)S(1)}, f32[8,384]{1,0:T(8,128)S(1)}, u32[]{:S(2)}, u32[]{:S(2)}) collective-permute-start(f32[8,384]{1,0:T(8,128)S(1)} %add.54), channel_id=1, source_target_pairs={{0,4},{4,0},{1,5},{5,1},{2,6},{6,2},{3,7},{7,3},{8,12},{12,8},{9,1... | collective-permute-start | bytes 36872 | tf_op jit(solution)/shard_map/ppermute | solution.py:27
  176.2 1.1 copy-start.1

commit v5 on v4

--- a/solution.py
+++ b/solution.py
@@ -17,10 +17,6 @@
 
 def gelu_exact(value):
     return jax.nn.gelu(value, approximate=False)
-
-
-def shift(array, axis, n, by):
-    return lax.ppermute(array, axis, [(i, (i - by) % n) for i in range(n)])
 
 
 def partner(array, axis, n, bit):
@@ -43,7 +39,7 @@
             ).astype(BF16)
             for g, (offset, _) in enumerate(groups):
                 held[k, g] = out[g * rows : (g + 1) * rows]
-                block = lax.rem(place_ref[0] + offset, 8)
+                block = lax.rem(place_ref[0] + offset + place_ref[1] * ((8 - 2 * offset) % 8), 8)
                 copies.append(
                     pltpu.make_async_copy(held.at[k, g], out_ref.at[half, block], sem.at[k, g])
                 )
@@ -100,44 +96,55 @@
     here = [lax.axis_index(a).astype(jnp.int32).reshape(1) for a in ("y", "c")]
     place = jnp.concatenate(here)
 
-    def tie(behind, ahead, done, *later):
-        (behind_next, _), (ahead_next, _) = together((behind, done)), together((ahead, done))
-        return behind_next, ahead_next, *together((behind, ahead, done, *later))[2:]
+    def step(array, way):
+        moves = [((i + way) % 8, i, 0) for i in range(8)] + [((i - way) % 8, i, 1) for i in range(8)]
+        return lax.ppermute(array, ("y", "c"), [(a * 2 + c, b * 2 + c) for a, b, c in moves])
+
+    def tie(first, second, done, *later):
+        (first_next, _), (second_next, _) = together((first, done)), together((second, done))
+        return first_next, second_next, *together((first, second, done, *later))[2:]
+
+    def merge(stats, other, count):
+        mean, square = (stats[0:1] + other[0:1]) * 0.5, stats[1:2] + other[1:2]
+        square = square + (share * count / 2) * (stats[0:1] - other[0:1]) ** 2
+        return jnp.concatenate([mean, square] * 4, axis=0)
 
     w0 = lax.all_gather(w_in, "zh", axis=0, tiled=True)
     w0, pre_act, act_cotangent = together((w0, pre_act, act_cotangent))
-    behind1, ahead1 = shift(w0, "y", 8, -1), shift(w0, "y", 8, 1)
+    first1, second1 = step(w0, 1), step(w0, -1)
     _, gelu_back = jax.vjp(gelu_exact, pre_act.astype(F32))
     d_own = gelu_back(act_cotangent.astype(F32))[0].astype(BF16)
 
-    behind, ahead, d_own = tie(behind1, ahead1, d_own)
-    behind2, ahead2 = shift(behind, "y", 8, -1), shift(ahead, "y", 8, 1)
+    first, second, d_own, tokens = tie(first1, second1, d_own, tokens)
+    first2, second2 = step(first, 1), step(second, -1)
     d_other = partner(d_own, "c", 2, 1)
-    parts = products([(0, [w0]), (7, [behind1]), (1, [ahead1])], d_own, d_other, place, None)
-
-    behind, ahead, parts = tie(behind2, ahead2, parts)
-    behind3, ahead3 = shift(behind, "y", 8, -1), shift(ahead, "y", 8, 1)
-    parts = products([(6, [behind2]), (2, [ahead2])], d_own, d_other, place, parts)
-
-    behind, ahead, parts = tie(behind3, ahead3, parts)
-    half = w0.shape[0] // 2
-    behind4, ahead4 = shift(behind[:half], "y", 8, -1), shift(ahead[half:], "y", 8, 1)
-    parts = products([(5, [behind3]), (3, [ahead3])], d_own, d_other, place, parts)
-
-    behind4, parts, tokens = together((behind4, parts, tokens))
-    parts = products([(4, [behind4, ahead4])], d_own, d_other, place, parts)
-    parts = lax.all_to_all(parts.reshape(16, share // 2, rows), CHIPS, 0, 0)
-
     x = tokens.astype(F32).T
     mean = jnp.mean(x, axis=0, keepdims=True)
     square = jnp.sum((x - mean) ** 2, axis=0, keepdims=True)
-    for axis, n, bit, count in (("x", 4, 1, 1), ("x", 4, 2, 2), ("zl", 2, 1, 4)):
-        other = partner(jnp.concatenate([mean, square] * 4, axis=0), axis, n, bit)
-        mean_too, square_too = other[0:1], other[1:2]
-        square = square + square_too + (share * count / 2) * (mean - mean_too) ** 2
-        mean = (mean + mean_too) * 0.5
-    rstd = 1.0 / jnp.sqrt(square * (1.0 / WIDTH) + 1e-06)
-    xhat = (x - mean) * rstd
+    stats = jnp.concatenate([mean, square] * 4, axis=0)
+    other = partner(stats, "x", 4, 1)
+
+    first, second, (d_other, stats, other) = tie(first2, second2, (d_other, stats, other))
+    first3, second3 = step(first, 1), step(second, -1)
+    groups = [(0, [w0]), (1, [first1]), (7, [second1]), (2, [first2]), (6, [second2])]
+    parts = products(groups, d_own, d_other, place, None)
+    stats = merge(stats, other, 1)
+    other = partner(stats, "x", 4, 2)
+
+    first, second, (parts, stats, other) = tie(first3, second3, (parts, stats, other))
+    half = w0.shape[0] // 2
+    first4, second4 = step(first[:half], 1), step(second[half:], -1)
+    parts = products([(3, [first3]), (5, [second3])], d_own, d_other, place, parts)
+    stats = merge(stats, other, 2)
+    other = partner(stats, "zl", 2, 1)
+
+    first4, parts, stats, other = together((first4, parts, stats, other))
+    parts = products([(4, [first4, second4])], d_own, d_other, place, parts)
+    parts = lax.all_to_all(parts.reshape(16, share // 2, rows), CHIPS, 0, 0)
+
+    stats = merge(stats, other, 4)
+    rstd = 1.0 / jnp.sqrt(stats[1:2] * (1.0 / WIDTH) + 1e-06)
+    xhat = (x - stats[0:1]) * rstd
 
     d_scaled, moments, gain_share = pl.pallas_call(
         sum_kernel,

time: 181 us -> 171 us (0.945)
  waiting for transfers between devices: 60.1 us -> 43.7 us
  local copies, waits for them, and re-layouts: 3.68 us -> 11.1 us
  starting transfers between devices: 71.4 us -> 66.3 us
  other arithmetic: 7.27 us -> 11.5 us
    ppermute x7, waiting for transfers between devices: 37.8 us -> 7.67 us  [partner(): return lax.ppermute(array, axis, [(i, i ^ bit) for i in range(n)])]
    all_to_all x1, waiting for transfers between devices: 0.01 us -> 29.3 us  [on_device(): parts = lax.all_to_all(parts.reshape(16, share // 2, rows), CHIPS, 0, 0)]
    ppermute x8, waiting for transfers between devices: 22.3 us -> 6.64 us  [step(): lax.ppermute(array, ('y', 'c'), [(a * 2 + c, b * 2 + c) for a, b, c in mo...]
    all_to_all x1, starting transfers between devices: 14.4 us -> 8.54 us  [on_device(): lax.all_to_all(gain_share, DP, 0, 0)]
    all_to_all x1, starting transfers between devices: 8.91 us -> 6.44 us  [on_device(): parts = lax.all_to_all(parts.reshape(16, share // 2, rows), CHIPS, 0, 0)]
    slice x2, local copies, waits for them, and re-layouts: 0.04 us -> 2.42 us  [on_device(): first4, second4 = (step(first[:half], 1), step(second[half:], -1))]
    ppermute x7, starting transfers between devices: 21.5 us -> 23.6 us  [partner(): return lax.ppermute(array, axis, [(i, i ^ bit) for i in range(n)])]
    pallas_call x4 -> x3, Pallas kernels: 11.9 us -> 10.7 us  [products(): pl.pallas_call(kernel, in_specs=[pl.BlockSpec(memory_space=pltpu.SMEM)] +...]
  transfers between devices with their start and end apart: 17 -> 17, of which waited for: 14 -> 7; matrix products, arithmetic and copies ran while one was open for 4% -> 10% of each run, Pallas kernels for 6% -> 6%
where the time goes in v5:
time: 171 us; the launch traced here: 168 us
  starting transfers between devices  66.3 us (39%)
  waiting for transfers between devices  43.7 us (26%)
  blocking collectives  22.2 us (13%)
  Pallas kernels  12.1 us (7%)
  other arithmetic  11.5 us (7%)
  local copies, waits for them, and re-layouts  11.1 us (6%)
    all_to_all x1, waiting for transfers between devices, on_device(): parts = lax.all_to_all(parts.reshape(16, share // 2, rows), CHIPS, 0, 0)  29.3 us
    ppermute x8, starting transfers between devices, step(): lax.ppermute(array, ('y', 'c'), [(a * 2 + c, b * 2 + c) for a, b, c in mo...  27.7 us
    ppermute x7, starting transfers between devices, partner(): return lax.ppermute(array, axis, [(i, i ^ bit) for i in range(n)])  23.6 us
    all_gather x1, blocking collectives, on_device(): w0 = lax.all_gather(w_in, 'zh', axis=0, tiled=True)  22.2 us
    pallas_call x3, Pallas kernels, products(): pl.pallas_call(kernel, in_specs=[pl.BlockSpec(memory_space=pltpu.SMEM)] +...  10.7 us
    all_to_all x1, starting transfers between devices, on_device(): lax.all_to_all(gain_share, DP, 0, 0)  8.54 us
    ppermute x7, waiting for transfers between devices, partner(): return lax.ppermute(array, axis, [(i, i ^ bit) for i in range(n)])  7.67 us
    convert_element_type x1, other arithmetic, on_device(): d_own = gelu_back(act_cotangent.astype(F32))[0].astype(BF16)  6.81 us
  transfers between devices with their start and end apart: 17, of which 7 were waited for; matrix products, arithmetic and copies ran while one was open for 10% of the time, Pallas kernels for 6%

profile of v5, /device:TPU:1, one launch (start us, length us, event | category | flops | bytes accessed | tf_op | source)
XLA Modules:
  0.0 167.9 jit_solution(6610317690551950795)
XLA Ops:
  0.6 22.2 %all_gather.3.refs_0_ = bf16[192,1536]{1,0:T(8,128)(2,1)S(1)} all-gather(bf16[48,1536]{1,0:T(8,128)(2,1)} %param.8), channel_id=1, replica_groups=mesh['y'=8,'zh'=4,'c'=2,'zl'=2,'x'=4] {'zh'}, dimensions={0}, use_global_device_ids=true | all-gather | bytes 737280 | tf_op jit(solution)/shard_map/all_gather | solution.py:112
  22.9 3.2 %collective-permute-start = (bf16[192,1536]{1,0:T(8,128)(2,1)S(1)}, bf16[192,1536]{1,0:T(8,128)(2,1)S(1)}, u32[]{:S(2)}, u32[]{:S(2)}) collective-permute-start(bf16[192,1536]{1,0:T(8,128)(2,1)S(1)} %all_gather.3.refs_0_), channel_id=1, source_target_pairs={{64,0},{128,64},{192,128},{256,192},{320,256},{384,320},{448,384},... | collective-permute-start | bytes 1769480 | tf_op jit(solution)/shard_map/ppermute | solution.py:101
  26.1 3.8 %collective-permute-start.1 = (bf16[192,1536]{1,0:T(8,128)(2,1)S(1)}, bf16[192,1536]{1,0:T(8,128)(2,1)}, u32[]{:S(2)}, u32[]{:S(2)}) collective-permute-start(bf16[192,1536]{1,0:T(8,128)(2,1)S(1)} %all_gather.3.refs_0_), channel_id=1, source_target_pairs={{448,0},{0,64},{64,128},{128,192},{192,256},{256,320},{320,384},{3... | collective-permute-start | bytes 1769480 | tf_op jit(solution)/shard_map/ppermute | solution.py:101
  29.9 6.8 %fusion.34.own_ref = bf16[384,1536]{1,0:T(8,128)(2,1)S(1)} fusion(bf16[384,1536]{1,0:T(8,128)(2,1)} %param.9, bf16[384,1536]{1,0:T(8,128)(2,1)} %param.7), kind=kLoop, calls=%fused_computation.39 | loop fusion | flops 43646976 | bytes 3538944 | tf_op jit(solution)/shard_map/convert_element_type | solution.py:116
  36.7 6.0 %collective-permute-done.1.refs_2_ = bf16[192,1536]{1,0:T(8,128)(2,1)} collective-permute-done((bf16[192,1536]{1,0:T(8,128)(2,1)S(1)}, bf16[192,1536]{1,0:T(8,128)(2,1)}, u32[]{:S(2)}, u32[]{:S(2)}) %collective-permute-start.1) | collective-permute-done | bytes 589856 | tf_op jit(solution)/shard_map/ppermute | solution.py:101
  42.8 2.6 %collective-permute-start.4 = (bf16[384,1536]{1,0:T(8,128)(2,1)S(1)}, bf16[384,1536]{1,0:T(8,128)(2,1)S(1)}, u32[]{:S(2)}, u32[]{:S(2)}) collective-permute-start(bf16[384,1536]{1,0:T(8,128)(2,1)S(1)} %fusion.34.own_ref), channel_id=1, source_target_pairs={{0,8},{8,0},{1,9},{9,1},{2,10},{10,2},{3,11},{11,3},{4,12},{12,4},... | collective-permute-start | bytes 3538952 | tf_op jit(solution)/shard_map/ppermute | solution.py:23
  45.3 2.0 %collective-permute-start.2 = (bf16[192,1536]{1,0:T(8,128)(2,1)S(1)}, bf16[192,1536]{1,0:T(8,128)(2,1)}, u32[]{:S(2)}, u32[]{:S(2)}) collective-permute-start(bf16[192,1536]{1,0:T(8,128)(2,1)S(1)} %collective-permute-done.refs_1_), channel_id=1, source_target_pairs={{64,0},{128,64},{192,128},{256,192},{320,256},{384,320},{448,384},... | collective-permute-start | bytes 1769480 | tf_op jit(solution)/shard_map/ppermute | solution.py:101
  47.3 5.3 %collective-permute-start.3 = (bf16[192,1536]{1,0:T(8,128)(2,1)}, bf16[192,1536]{1,0:T(8,128)(2,1)}, u32[]{:S(2)}, u32[]{:S(2)}) collective-permute-start(bf16[192,1536]{1,0:T(8,128)(2,1)} %collective-permute-done.1.refs_2_), channel_id=1, source_target_pairs={{448,0},{0,64},{64,128},{128,192},{192,256},{256,320},{320,384},{3... | collective-permute-start | bytes 1769480 | tf_op jit(solution)/shard_map/ppermute | solution.py:101
  52.6 1.9 %copy.12 = bf16[384,384]{0,1:T(8,128)(2,1)} copy(bf16[384,384]{1,0:T(8,128)(2,1)} %param.5) | data formatting | bytes 589824 | tf_op jit(solution)/shard_map/optimization_barrier | solution.py:105
  54.4 1.0 convert_reduce_fusion
  55.5 1.1 fusion.37
  56.6 0.6 concatenate.13
  57.2 3.1 %collective-permute-start.5 = (f32[8,384]{1,0:T(8,128)}, f32[8,384]{1,0:T(8,128)S(1)}, u32[]{:S(2)}, u32[]{:S(2)}) collective-permute-start(f32[8,384]{1,0:T(8,128)} %concatenate.13), channel_id=1, source_target_pairs={{0,1},{1,0},{2,3},{3,2},{4,5},{5,4},{6,7},{7,6},{8,9},{9,8},{10,11... | collective-permute-start | bytes 36872 | tf_op jit(solution)/shard_map/ppermute | solution.py:23
  60.3 1.9 %collective-permute-done.5 = f32[8,384]{1,0:T(8,128)S(1)} collective-permute-done((f32[8,384]{1,0:T(8,128)}, f32[8,384]{1,0:T(8,128)S(1)}, u32[]{:S(2)}, u32[]{:S(2)}) %collective-permute-start.5) | collective-permute-done | bytes 12320 | tf_op jit(solution)/shard_map/ppermute | solution.py:23
  62.3 0.6 copy-done.6
  62.8 1.9 %collective-permute-start.6 = (bf16[192,1536]{1,0:T(8,128)(2,1)}, bf16[192,1536]{1,0:T(8,128)(2,1)S(1)}, u32[]{:S(2)}, u32[]{:S(2)}) collective-permute-start(bf16[192,1536]{1,0:T(8,128)(2,1)} %collective-permute-done.2.refs_3_), channel_id=1, source_target_pairs={{64,0},{128,64},{192,128},{256,192},{320,256},{384,320},{448,384},... | collective-permute-start | bytes 1769480 | tf_op jit(solution)/shard_map/ppermute | solution.py:101
  64.8 4.6 %collective-permute-start.9 = (bf16[192,1536]{1,0:T(8,128)(2,1)}, bf16[192,1536]{1,0:T(8,128)(2,1)}, u32[]{:S(2)}, u32[]{:S(2)}) collective-permute-start(bf16[192,1536]{1,0:T(8,128)(2,1)} %collective-permute-done.3.refs_4_), channel_id=1, source_target_pairs={{448,0},{0,64},{64,128},{128,192},{192,256},{256,320},{320,384},{3... | collective-permute-start | bytes 1769480 | tf_op jit(solution)/shard_map/ppermute | solution.py:101
  69.5 0.8 multiply_add_fusion.1
  70.3 0.6 concatenate.14
  70.9 4.6 %collective-permute-start.7 = (f32[8,384]{1,0:T(8,128)}, f32[8,384]{1,0:T(8,128)S(1)}, u32[]{:S(2)}, u32[]{:S(2)}) collective-permute-start(f32[8,384]{1,0:T(8,128)} %concatenate.14), channel_id=1, source_target_pairs={{0,2},{1,3},{2,0},{3,1},{4,6},{5,7},{6,4},{7,5},{8,10},{9,11},{10,... | collective-permute-start | bytes 36872 | tf_op jit(solution)/shard_map/ppermute | solution.py:23
  75.5 1.1 copy-done.3
  76.6 5.4 %shard_map.68.refs_2_ = bf16[2,8,192,384]{3,2,1,0:T(8,128)(2,1)} custom-call(s32[2]{0:T(128)S(1)} %pad_add_fusion.place_ref, bf16[384,1536]{1,0:T(8,128)(2,1)S(1)} %fusion.34.own_ref, bf16[384,1536]{1,0:T(8,128)(2,1)S(1)} %collective-permute-done.4.other_ref, bf16[192,1536]{1,0:T(8,128)(2,1)S(1)} %all_gather.3.refs_0_, bf16[192,1536]{1,0:T(8,128)(2,1)S(1)} %copy-done.3, ...), custom_call_target="tpu_custom_call" | custom-call | flops 566231040 | bytes 262144 | tf_op jit(solution)/shard_map/pallas_call | solution.py:51
  82.0 0.6 collective-permute-done.9.refs_1_
  82.6 0.7 slice.58
  83.4 1.9 %collective-permute-start.8 = (bf16[96,1536]{1,0:T(8,128)(2,1)}, bf16[96,1536]{1,0:T(8,128)(2,1)S(1)}, u32[]{:S(2)}, u32[]{:S(2)}) collective-permute-start(bf16[96,1536]{1,0:T(8,128)(2,1)} %slice.58), channel_id=1, source_target_pairs={{64,0},{128,64},{192,128},{256,192},{320,256},{384,320},{448,384},... | collective-permute-start | bytes 884744 | tf_op jit(solution)/shard_map/ppermute | solution.py:101
  85.3 1.7 %slice.63 = bf16[96,1536]{1,0:T(8,128)(2,1)} slice(bf16[192,1536]{1,0:T(8,128)(2,1)} %collective-permute-done.9.refs_1_), slice={[96:192], [0:1536]} | slice | bytes 589824 | tf_op jit(solution)/shard_map/slice | solution.py:136
  87.0 5.0 %collective-permute-start.11 = (bf16[96,1536]{1,0:T(8,128)(2,1)}, bf16[96,1536]{1,0:T(8,128)(2,1)S(1)}, u32[]{:S(2)}, u32[]{:S(2)}) collective-permute-start(bf16[96,1536]{1,0:T(8,128)(2,1)} %slice.63), channel_id=1, source_target_pairs={{448,0},{0,64},{64,128},{128,192},{192,256},{256,320},{320,384},{3... | collective-permute-start | bytes 884744 | tf_op jit(solution)/shard_map/ppermute | solution.py:101
  92.0 0.8 multiply_add_fusion
  92.8 0.6 concatenate.15
  93.4 3.7 %collective-permute-start.10 = (f32[8,384]{1,0:T(8,128)}, f32[8,384]{1,0:T(8,128)S(1)}, u32[]{:S(2)}, u32[]{:S(2)}) collective-permute-start(f32[8,384]{1,0:T(8,128)} %concatenate.15), channel_id=1, source_target_pairs={{0,4},{4,0},{1,5},{5,1},{2,6},{6,2},{3,7},{7,3},{8,12},{12,8},{9,1... | collective-permute-start | bytes 36872 | tf_op jit(solution)/shard_map/ppermute | solution.py:23
  97.1 3.2 %shard_map.69.refs_2_ = bf16[2,8,192,384]{3,2,1,0:T(8,128)(2,1)} custom-call(s32[2]{0:T(128)S(1)} %pad_add_fusion.place_ref, bf16[384,1536]{1,0:T(8,128)(2,1)S(1)} %fusion.34.own_ref, bf16[384,1536]{1,0:T(8,128)(2,1)S(1)} %collective-permute-done.4.other_ref, bf16[192,1536]{1,0:T(8,128)(2,1)S(1)} %collective-permute-done.6.refs_0_, ...), custom_call_target="tpu_custom_call", output_to_operand_aliasing={{}: (5, {})} | custom-call | flops 226492416 | bytes 262144 | tf_op jit(solution)/shard_map/pallas_call | solution.py:51
  100.3 2.1 %shard_map.70 = bf16[2,8,192,384]{3,2,1,0:T(8,128)(2,1)} custom-call(s32[2]{0:T(128)S(1)} %pad_add_fusion.place_ref, bf16[384,1536]{1,0:T(8,128)(2,1)S(1)} %fusion.34.own_ref, bf16[384,1536]{1,0:T(8,128)(2,1)S(1)} %collective-permute-done.4.other_ref, bf16[96,1536]{1,0:T(8,128)(2,1)S(1)} %collective-permute-done.8.refs_0_, ...), custom_call_target="tpu_custom_call", output_to_operand_aliasing={{}: (5, {})} | custom-call | flops 113246208 | bytes 262144 | tf_op jit(solution)/shard_map/pallas_call | solution.py:51
  102.4 6.4 %all-to-all-start = ((bf16[16,192,384]{2,1,0:T(8,128)(2,1)}), bf16[16,192,384]{2,1,0:T(8,128)(2,1)S(1)}, u32[]{:S(2)}, u32[]{:S(2)}) async-start(bf16[16,192,384]{2,1,0:T(8,128)(2,1)} %bitcast.2), calls=%async_computation | async-start | bytes 4718592 | tf_op jit(solution)/shard_map/all_to_all | solution.py:143
  109.0 0.8 fusion.40
  109.9 29.3 %all-to-all-done.parts_ref = bf16[16,192,384]{2,1,0:T(8,128)(2,1)S(1)} async-done(((bf16[16,192,384]{2,1,0:T(8,128)(2,1)}), bf16[16,192,384]{2,1,0:T(8,128)(2,1)S(1)}, u32[]{:S(2)}, u32[]{:S(2)}) %all-to-all-start) | async-done | bytes 2359328 | tf_op jit(solution)/shard_map/all_to_all | solution.py:143
  139.2 0.5 shard_map.71
  139.7 0.8 copy-done
  140.6 0.7 broadcast_in_dim.15
  141.3 8.5 %all-to-all-start.1 = ((f32[64,8,128]{2,1,0:T(8,128)}), f32[64,8,128]{2,1,0:T(8,128)S(1)}, u32[]{:S(2)}, u32[]{:S(2)}) async-start(f32[64,8,128]{2,1,0:T(8,128)} %broadcast_in_dim.15), calls=%async_computation.1 | async-start | bytes 524288 | tf_op jit(solution)/shard_map/all_to_all | solution.py:160
  149.8 2.2 %collective-permute-start.12 = (f32[8,384]{1,0:T(8,128)S(1)}, f32[8,384]{1,0:T(8,128)S(1)}, u32[]{:S(2)}, u32[]{:S(2)}) collective-permute-start(f32[8,384]{1,0:T(8,128)S(1)} %get-tuple-element.48), channel_id=1, source_target_pairs={{0,1},{1,0},{2,3},{3,2},{4,5},{5,4},{6,7},{7,6},{8,9},{9,8},{10,11... | collective-permute-start | bytes 36872 | tf_op jit(solution)/shard_map/ppermute | solution.py:23
  152.0 2.5 %collective-permute-done.12 = f32[8,384]{1,0:T(8,128)S(1)} collective-permute-done((f32[8,384]{1,0:T(8,128)S(1)}, f32[8,384]{1,0:T(8,128)S(1)}, u32[]{:S(2)}, u32[]{:S(2)}) %collective-permute-start.12) | collective-permute-done | bytes 12320 | tf_op jit(solution)/shard_map/ppermute | solution.py:23
  154.6 4.2 %collective-permute-start.13 = (f32[8,384]{1,0:T(8,128)S(1)}, f32[8,384]{1,0:T(8,128)S(1)}, u32[]{:S(2)}, u32[]{:S(2)}) collective-permute-start(f32[8,384]{1,0:T(8,128)S(1)} %add.53), channel_id=1, source_target_pairs={{0,2},{1,3},{2,0},{3,1},{4,6},{5,7},{6,4},{7,5},{8,10},{9,11},{10,... | collective-permute-start | bytes 36872 | tf_op jit(solution)/shard_map/ppermute | solution.py:23
  158.8 2.0 %collective-permute-done.13 = f32[8,384]{1,0:T(8,128)S(1)} collective-permute-done((f32[8,384]{1,0:T(8,128)S(1)}, f32[8,384]{1,0:T(8,128)S(1)}, u32[]{:S(2)}, u32[]{:S(2)}) %collective-permute-start.13) | collective-permute-done | bytes 12320 | tf_op jit(solution)/shard_map/ppermute | solution.py:23
  160.8 3.3 %collective-permute-start.14 = (f32[8,384]{1,0:T(8,128)S(1)}, f32[8,384]{1,0:T(8,128)S(1)}, u32[]{:S(2)}, u32[]{:S(2)}) collective-permute-start(f32[8,384]{1,0:T(8,128)S(1)} %add.54), channel_id=1, source_target_pairs={{0,4},{4,0},{1,5},{5,1},{2,6},{6,2},{3,7},{7,3},{8,12},{12,8},{9,1... | collective-permute-start | bytes 36872 | tf_op jit(solution)/shard_map/ppermute | solution.py:23
  164.1 1.2 collective-permute-done.14
  165.3 1.1 copy-done.1
  166.3 0.9 shard_map.72
  167.3 0.6 slice_bitcast_fusion
  (31 shorter events, 0.4 us)
Async XLA Ops:
  22.9 13.8 %collective-permute-start = (bf16[192,1536]{1,0:T(8,128)(2,1)S(1)}, bf16[192,1536]{1,0:T(8,128)(2,1)S(1)}, u32[]{:S(2)}, u32[]{:S(2)}) collective-permute-start(bf16[192,1536]{1,0:T(8,128)(2,1)S(1)} %all_gather.3.refs_0_), channel_id=1, source_target_pairs={{64,0},{128,64},{192,128},{256,192},{320,256},{384,320},{448,384},... | collective-permute-start | bytes 1769480 | tf_op jit(solution)/shard_map/ppermute | solution.py:101
  26.1 16.7 %collective-permute-start.1 = (bf16[192,1536]{1,0:T(8,128)(2,1)S(1)}, bf16[192,1536]{1,0:T(8,128)(2,1)}, u32[]{:S(2)}, u32[]{:S(2)}) collective-permute-start(bf16[192,1536]{1,0:T(8,128)(2,1)S(1)} %all_gather.3.refs_0_), channel_id=1, source_target_pairs={{448,0},{0,64},{64,128},{128,192},{192,256},{256,320},{320,384},{3... | collective-permute-start | bytes 1769480 | tf_op jit(solution)/shard_map/ppermute | solution.py:101
  36.7 25.5 %copy-start.2 = (bf16[192,1536]{1,0:T(8,128)(2,1)}, bf16[192,1536]{1,0:T(8,128)(2,1)S(1)}, u32[]{:S(2)}) copy-start(bf16[192,1536]{1,0:T(8,128)(2,1)S(1)} %collective-permute-done.refs_1_) | copy-start | bytes 1769476
  42.8 19.5 %collective-permute-start.4 = (bf16[384,1536]{1,0:T(8,128)(2,1)S(1)}, bf16[384,1536]{1,0:T(8,128)(2,1)S(1)}, u32[]{:S(2)}, u32[]{:S(2)}) collective-permute-start(bf16[384,1536]{1,0:T(8,128)(2,1)S(1)} %fusion.34.own_ref), channel_id=1, source_target_pairs={{0,8},{8,0},{1,9},{9,1},{2,10},{10,2},{3,11},{11,3},{4,12},{12,4},... | collective-permute-start | bytes 3538952 | tf_op jit(solution)/shard_map/ppermute | solution.py:23
  45.3 16.9 %collective-permute-start.2 = (bf16[192,1536]{1,0:T(8,128)(2,1)S(1)}, bf16[192,1536]{1,0:T(8,128)(2,1)}, u32[]{:S(2)}, u32[]{:S(2)}) collective-permute-start(bf16[192,1536]{1,0:T(8,128)(2,1)S(1)} %collective-permute-done.refs_1_), channel_id=1, source_target_pairs={{64,0},{128,64},{192,128},{256,192},{320,256},{384,320},{448,384},... | collective-permute-start | bytes 1769480 | tf_op jit(solution)/shard_map/ppermute | solution.py:101
  47.3 17.4 %collective-permute-start.3 = (bf16[192,1536]{1,0:T(8,128)(2,1)}, bf16[192,1536]{1,0:T(8,128)(2,1)}, u32[]{:S(2)}, u32[]{:S(2)}) collective-permute-start(bf16[192,1536]{1,0:T(8,128)(2,1)} %collective-permute-done.1.refs_2_), channel_id=1, source_target_pairs={{448,0},{0,64},{64,128},{128,192},{192,256},{256,320},{320,384},{3... | collective-permute-start | bytes 1769480 | tf_op jit(solution)/shard_map/ppermute | solution.py:101
  57.2 5.0 %collective-permute-start.5 = (f32[8,384]{1,0:T(8,128)}, f32[8,384]{1,0:T(8,128)S(1)}, u32[]{:S(2)}, u32[]{:S(2)}) collective-permute-start(f32[8,384]{1,0:T(8,128)} %concatenate.13), channel_id=1, source_target_pairs={{0,1},{1,0},{2,3},{3,2},{4,5},{5,4},{6,7},{7,6},{8,9},{9,8},{10,11... | collective-permute-start | bytes 36872 | tf_op jit(solution)/shard_map/ppermute | solution.py:23
  62.2 0.6 copy-start.6
  62.8 19.2 %collective-permute-start.6 = (bf16[192,1536]{1,0:T(8,128)(2,1)}, bf16[192,1536]{1,0:T(8,128)(2,1)S(1)}, u32[]{:S(2)}, u32[]{:S(2)}) collective-permute-start(bf16[192,1536]{1,0:T(8,128)(2,1)} %collective-permute-done.2.refs_3_), channel_id=1, source_target_pairs={{64,0},{128,64},{192,128},{256,192},{320,256},{384,320},{448,384},... | collective-permute-start | bytes 1769480 | tf_op jit(solution)/shard_map/ppermute | solution.py:101
  64.8 17.9 %collective-permute-start.9 = (bf16[192,1536]{1,0:T(8,128)(2,1)}, bf16[192,1536]{1,0:T(8,128)(2,1)}, u32[]{:S(2)}, u32[]{:S(2)}) collective-permute-start(bf16[192,1536]{1,0:T(8,128)(2,1)} %collective-permute-done.3.refs_4_), channel_id=1, source_target_pairs={{448,0},{0,64},{64,128},{128,192},{192,256},{256,320},{320,384},{3... | collective-permute-start | bytes 1769480 | tf_op jit(solution)/shard_map/ppermute | solution.py:101
  70.9 11.1 %collective-permute-start.7 = (f32[8,384]{1,0:T(8,128)}, f32[8,384]{1,0:T(8,128)S(1)}, u32[]{:S(2)}, u32[]{:S(2)}) collective-permute-start(f32[8,384]{1,0:T(8,128)} %concatenate.14), channel_id=1, source_target_pairs={{0,2},{1,3},{2,0},{3,1},{4,6},{5,7},{6,4},{7,5},{8,10},{9,11},{10,... | collective-permute-start | bytes 36872 | tf_op jit(solution)/shard_map/ppermute | solution.py:23
  75.5 1.1 copy-start.3
  83.4 16.9 %collective-permute-start.8 = (bf16[96,1536]{1,0:T(8,128)(2,1)}, bf16[96,1536]{1,0:T(8,128)(2,1)S(1)}, u32[]{:S(2)}, u32[]{:S(2)}) collective-permute-start(bf16[96,1536]{1,0:T(8,128)(2,1)} %slice.58), channel_id=1, source_target_pairs={{64,0},{128,64},{192,128},{256,192},{320,256},{384,320},{448,384},... | collective-permute-start | bytes 884744 | tf_op jit(solution)/shard_map/ppermute | solution.py:101
  87.0 13.3 %collective-permute-start.11 = (bf16[96,1536]{1,0:T(8,128)(2,1)}, bf16[96,1536]{1,0:T(8,128)(2,1)S(1)}, u32[]{:S(2)}, u32[]{:S(2)}) collective-permute-start(bf16[96,1536]{1,0:T(8,128)(2,1)} %slice.63), channel_id=1, source_target_pairs={{448,0},{0,64},{64,128},{128,192},{192,256},{256,320},{320,384},{3... | collective-permute-start | bytes 884744 | tf_op jit(solution)/shard_map/ppermute | solution.py:101
  93.4 6.8 %collective-permute-start.10 = (f32[8,384]{1,0:T(8,128)}, f32[8,384]{1,0:T(8,128)S(1)}, u32[]{:S(2)}, u32[]{:S(2)}) collective-permute-start(f32[8,384]{1,0:T(8,128)} %concatenate.15), channel_id=1, source_target_pairs={{0,4},{4,0},{1,5},{5,1},{2,6},{6,2},{3,7},{7,3},{8,12},{12,8},{9,1... | collective-permute-start | bytes 36872 | tf_op jit(solution)/shard_map/ppermute | solution.py:23
  102.4 6.5 %copy-start.5 = (bf16[384]{0:T(512)(128)(2,1)S(1)}, bf16[384]{0:T(512)(128)(2,1)}, u32[]{:S(2)}) copy-start(bf16[384]{0:T(512)(128)(2,1)} %param.6) | copy-start | bytes 2308
  102.4 7.4 %copy-start.4 = (bf16[384,384]{0,1:T(8,128)(2,1)S(1)}, bf16[384,384]{0,1:T(8,128)(2,1)}, u32[]{:S(2)}) copy-start(bf16[384,384]{0,1:T(8,128)(2,1)} %copy.12) | copy-start | bytes 884740
  102.4 36.8 %all-to-all-start = ((bf16[16,192,384]{2,1,0:T(8,128)(2,1)}), bf16[16,192,384]{2,1,0:T(8,128)(2,1)S(1)}, u32[]{:S(2)}, u32[]{:S(2)}) async-start(bf16[16,192,384]{2,1,0:T(8,128)(2,1)} %bitcast.2), calls=%async_computation | async-start | bytes 4718592 | tf_op jit(solution)/shard_map/all_to_all | solution.py:143
  139.7 0.8 copy-start
  141.3 25.9 %all-to-all-start.1 = ((f32[64,8,128]{2,1,0:T(8,128)}), f32[64,8,128]{2,1,0:T(8,128)S(1)}, u32[]{:S(2)}, u32[]{:S(2)}) async-start(f32[64,8,128]{2,1,0:T(8,128)} %broadcast_in_dim.15), calls=%async_computation.1 | async-start | bytes 524288 | tf_op jit(solution)/shard_map/all_to_all | solution.py:160
  149.8 4.7 %collective-permute-start.12 = (f32[8,384]{1,0:T(8,128)S(1)}, f32[8,384]{1,0:T(8,128)S(1)}, u32[]{:S(2)}, u32[]{:S(2)}) collective-permute-start(f32[8,384]{1,0:T(8,128)S(1)} %get-tuple-element.48), channel_id=1, source_target_pairs={{0,1},{1,0},{2,3},{3,2},{4,5},{5,4},{6,7},{7,6},{8,9},{9,8},{10,11... | collective-permute-start | bytes 36872 | tf_op jit(solution)/shard_map/ppermute | solution.py:23
  154.6 6.2 %collective-permute-start.13 = (f32[8,384]{1,0:T(8,128)S(1)}, f32[8,384]{1,0:T(8,128)S(1)}, u32[]{:S(2)}, u32[]{:S(2)}) collective-permute-start(f32[8,384]{1,0:T(8,128)S(1)} %add.53), channel_id=1, source_target_pairs={{0,2},{1,3},{2,0},{3,1},{4,6},{5,7},{6,4},{7,5},{8,10},{9,11},{10,... | collective-permute-start | bytes 36872 | tf_op jit(solution)/shard_map/ppermute | solution.py:23
  160.8 4.5 %collective-permute-start.14 = (f32[8,384]{1,0:T(8,128)S(1)}, f32[8,384]{1,0:T(8,128)S(1)}, u32[]{:S(2)}, u32[]{:S(2)}) collective-permute-start(f32[8,384]{1,0:T(8,128)S(1)} %add.54), channel_id=1, source_target_pairs={{0,4},{4,0},{1,5},{5,1},{2,6},{6,2},{3,7},{7,3},{8,12},{12,8},{9,1... | collective-permute-start | bytes 36872 | tf_op jit(solution)/shard_map/ppermute | solution.py:23
  165.3 1.1 copy-start.1

commit v6 on v5

v6 whole, which is shorter than its diff:
```python
import jax
import jax.numpy as jnp
from jax import lax
from jax.experimental import pallas as pl
from jax.experimental.pallas import tpu as pltpu
from jax.sharding import Mesh, PartitionSpec as P

NAMES = ("y", "zh", "c", "zl", "x")
SIZES = (8, 4, 2, 2, 4)
DP, MP, CHIPS = ("y", "zh", "c"), ("zl", "x"), ("c", "zl", "x")
F32, BF16 = jnp.float32, jnp.bfloat16
SHARD = 48
WIDTH = 3072
EXTRA = 16
PARAMS = pltpu.CompilerParams(vmem_limit_bytes=20 * 1024 * 1024)
together = lax.optimization_barrier


def gelu_exact(value):
    return jax.nn.gelu(value, approximate=False)


def partner(array, axis, n, bit):
    return lax.ppermute(array, axis, [(i, i ^ bit) for i in range(n)])


def products(groups, d_own, d_other, place, parts, extra=None):
    tokens, hidden = d_own.shape
    weights = [w for _, w in groups]
    rows, n = weights[0].shape[0], len(groups)

    def kernel(place_ref, own_ref, other_ref, *refs):
        w_refs, (out_ref, held, sem, extra_sem) = refs[:n], refs[-4:]
        copies = []
        if extra is not None:
            for t in range(2):
                for m in range(8):
                    to = out_ref.at[t, m, pl.ds(rows, EXTRA)]
                    copies.append(pltpu.make_async_copy(refs[n], to, extra_sem.at[t, m]))
                    copies[-1].start()
        w = jnp.concatenate([r[...] for r in w_refs], axis=0)
        for k, d_ref in enumerate((own_ref, other_ref)):
            half = lax.rem(place_ref[1] + k, 2)
            out = lax.dot_general(
                w, d_ref[...], (((1,), (1,)), ((), ())), preferred_element_type=F32
            ).astype(BF16)
            for g, (offset, _) in enumerate(groups):
                held[k, g] = out[g * rows : (g + 1) * rows]
                block = lax.rem(place_ref[0] + offset + place_ref[1] * ((8 - 2 * offset) % 8), 8)
                to = out_ref.at[half, block, pl.ds(0, rows)]
                copies.append(pltpu.make_async_copy(held.at[k, g], to, sem.at[k, g]))
                copies[-1].start()
        for copy in copies:
            copy.wait()

    whole = pl.BlockSpec(memory_space=pltpu.VMEM)
    more = [] if extra is None else [extra]
    return pl.pallas_call(
        kernel,
        in_specs=[pl.BlockSpec(memory_space=pltpu.SMEM)]
        + [whole] * (2 + n + len(more))
        + [pl.BlockSpec(memory_space=pl.ANY)] * (parts is not None),
        out_specs=pl.BlockSpec(memory_space=pl.ANY),
        out_shape=jax.ShapeDtypeStruct((2, 8, rows + EXTRA, tokens), BF16),
        scratch_shapes=[
            pltpu.VMEM((2, n, rows, tokens), BF16),
            pltpu.SemaphoreType.DMA((2, n)),
            pltpu.SemaphoreType.DMA((2, 8)),
        ],
        input_output_aliases={} if parts is None else {3 + n + len(more): 0},
        compiler_params=PARAMS,
        cost_estimate=pl.CostEstimate(
            flops=n * rows * hidden * tokens, bytes_accessed=1 << 18, transcendentals=0
        ),
    )(place, d_own, d_other, *weights, *more, *([] if parts is None else [parts]))


def tokens_kernel(tokens_ref, x_ref, stats_ref):
    x = tokens_ref[...].astype(F32).T
    x_ref[...] = x
    mean = jnp.sum(x, axis=0, keepdims=True) * (1.0 / x.shape[0])
    square = jnp.sum((x - mean) ** 2, axis=0, keepdims=True)
    rows = []
    for rest in (mean, square):
        for _ in range(3):
            rows.append(rest.astype(BF16).astype(F32))
            rest = rest - rows[-1]
    rows.append(jnp.zeros((EXTRA - 6, x.shape[1]), F32))
    stats_ref[...] = jnp.concatenate(rows, axis=0).astype(BF16)


def sum_kernel(core_ref, parts_ref, x_ref, gain_ref, d_out, xhat_out, moments_ref, share_ref, d_ref, xhat_ref, sem):
    copies = []
    rows, share = parts_ref.shape[1] - EXTRA, x_ref.shape[0]
    means, squares = [], []
    for m in range(8):
        stat = parts_ref[core_ref[0] * 8 + m, pl.ds(rows, EXTRA), :].astype(F32)
        means.append(stat[0:1] + stat[1:2] + stat[2:3])
        squares.append(stat[3:4] + stat[4:5] + stat[5:6])
    mean = sum(means) * 0.125
    variance = (sum(squares) + share * sum((m - mean) ** 2 for m in means)) * (1.0 / WIDTH)
    rstd = 1.0 / jnp.sqrt(variance + 1e-06)
    first, second = 0.0, 0.0
    for z in range(4):
        for c in range(2):
            total = parts_ref[c * 8, pl.ds(z * SHARD, SHARD), :].astype(F32)
            for m in range(1, 8):
                total += parts_ref[c * 8 + m, pl.ds(z * SHARD, SHARD), :].astype(F32)
            at = pl.ds((z * 2 + c) * SHARD, SHARD)
            xhat, g = (x_ref[at, :] - mean) * rstd, total * gain_ref[at, :]
            xhat_ref[at, :] = xhat
            d_ref[at, :] = g
            for k, (held, out) in enumerate(((d_ref, d_out), (xhat_ref, xhat_out))):
                copies.append(pltpu.make_async_copy(held.at[at], out.at[at], sem.at[k, z, c]))
                copies[-1].start()
            value = total * xhat
            share_ref[at, :] = value[:, :128] + value[:, 128:256] + value[:, 256:]
            first += jnp.sum(g, axis=0, keepdims=True)
            second += jnp.sum(g * xhat, axis=0, keepdims=True)
    moments_ref[...] = jnp.concatenate(
        [first, second, rstd * 0.125, jnp.zeros((5, rstd.shape[1]), F32)], axis=0
    )
    row = jnp.sum(share_ref[...].T, axis=0, keepdims=True)
    share_ref[0:8, :] = jnp.concatenate(
        [row[:, i * 128 : (i + 1) * 128] for i in range(3)] + [jnp.zeros((5, 128), F32)], axis=0
    )
    for copy in copies:
        copy.wait()


def final_kernel(d_in, xhat_in, moments_ref, out_ref, d_ref, xhat_ref, sem):
    copies = [
        pltpu.make_async_copy(d_in, d_ref, sem.at[0]),
        pltpu.make_async_copy(xhat_in, xhat_ref, sem.at[1]),
    ]
    for copy in copies:
        copy.start()
    for copy in copies:
        copy.wait()
    both = moments_ref[0:2, :] * (1.0 / WIDTH)
    value = moments_ref[2:3, :] * (d_ref[...] - both[0:1] - xhat_ref[...] * both[1:2])
    out_ref[...] = value.T.astype(BF16)


def on_device(tokens, gain, pre_act, w_in, act_cotangent):
    rows, share = tokens.shape
    here = [lax.axis_index(a).astype(jnp.int32).reshape(1) for a in ("y", "c")]
    place = jnp.concatenate(here)

    def step(array, way):
        moves = [((i + way) % 8, i, 0) for i in range(8)] + [((i - way) % 8, i, 1) for i in range(8)]
        return lax.ppermute(array, ("y", "c"), [(a * 2 + c, b * 2 + c) for a, b, c in moves])

    def tie(first, second, done, *later):
        (first_next, _), (second_next, _) = together((first, done)), together((second, done))
        return first_next, second_next, *together((first, second, done, *later))[2:]

    w0 = lax.all_gather(w_in, "zh", axis=0, tiled=True)
    w0, pre_act, act_cotangent = together((w0, pre_act, act_cotangent))
    first1, second1 = step(w0, 1), step(w0, -1)
    _, gelu_back = jax.vjp(gelu_exact, pre_act.astype(F32))
    d_own = gelu_back(act_cotangent.astype(F32))[0].astype(BF16)

    first, second, d_own, tokens = tie(first1, second1, d_own, tokens)
    first2, second2 = step(first, 1), step(second, -1)
    d_other = partner(d_own, "c", 2, 1)
    x, stats = pl.pallas_call(
        tokens_kernel,
        out_shape=[
            jax.ShapeDtypeStruct((share, rows), F32),
            jax.ShapeDtypeStruct((EXTRA, rows), BF16),
        ],
        compiler_params=PARAMS,
    )(tokens)

    first, second, (d_other, stats) = tie(first2, second2, (d_other, stats))
    first3, second3 = step(first, 1), step(second, -1)
    groups = [(0, w0), (1, first1), (7, second1), (2, first2), (6, second2)]
    parts = products(groups, d_own, d_other, place, None, stats)

    first, second, parts = tie(first3, second3, parts)
    first4 = step(first, 1)
    parts = products([(3, first3), (5, second)], d_own, d_other, place, parts)

    first4, parts = together((first4, parts))
    parts = products([(4, first4)], d_own, d_other, place, parts)
    parts = lax.all_to_all(parts.reshape(16, -1, rows), CHIPS, 0, 0)

    vmem, hbm = pl.BlockSpec(memory_space=pltpu.VMEM), pl.BlockSpec(memory_space=pltpu.HBM)
    d_scaled, xhat, moments, gain_share = pl.pallas_call(
        sum_kernel,
        in_specs=[pl.BlockSpec(memory_space=pltpu.SMEM), vmem, vmem, vmem],
        out_specs=[hbm, hbm, vmem, vmem],
        scratch_shapes=[pltpu.VMEM((share, rows), F32)] * 2 + [pltpu.SemaphoreType.DMA((2, 4, 2))],
        out_shape=[
            jax.ShapeDtypeStruct((share, rows), F32),
            jax.ShapeDtypeStruct((share, rows), F32),
            jax.ShapeDtypeStruct((8, rows), F32),
            jax.ShapeDtypeStruct((share, 128), F32),
        ],
        compiler_params=PARAMS,
    )(here[1], parts, x, gain.astype(F32)[:, None])

    gain_share = jnp.broadcast_to(gain_share[:8], (64, 8, 128))
    gain_gradient = jnp.sum(lax.all_to_all(gain_share, DP, 0, 0), axis=0)[:3].reshape(share)

    for axis, n, bit in (("x", 4, 1), ("x", 4, 2), ("zl", 2, 1)):
        moments += partner(moments, axis, n, bit)
    token_gradient = pl.pallas_call(
        final_kernel,
        in_specs=[hbm, hbm, vmem],
        scratch_shapes=[pltpu.VMEM((share, rows), F32)] * 2 + [pltpu.SemaphoreType.DMA((2,))],
        out_shape=jax.ShapeDtypeStruct((rows, share), BF16),
        compiler_params=pltpu.CompilerParams(vmem_limit_bytes=60 * 1024 * 1024),
    )(d_scaled, xhat, moments)
    return (token_gradient, gain_gradient)


def solution(mesh):
    fine = Mesh(mesh.devices.reshape(SIZES), NAMES)
    placed = (P(DP, MP), P(MP), P(DP, MP), P(DP, MP), P(DP, MP))
    return jax.shard_map(
        on_device, mesh=fine, in_specs=placed, out_specs=(P(DP, MP), P(MP)), check_vma=False
    )
```

time: 171 us -> 173 us (1.012)
  waiting for transfers between devices: 43.7 us -> 59.9 us
  starting transfers between devices: 66.3 us -> 58.8 us
  local copies, waits for them, and re-layouts: 11.1 us -> 3.91 us
  Pallas kernels: 12.1 us -> 16.6 us
  other arithmetic: 11.5 us -> 7.56 us
    ppermute x8 -> x7, waiting for transfers between devices: 6.64 us -> 22 us  [step(): lax.ppermute(array, ('y', 'c'), [(a * 2 + c, b * 2 + c) for a, b, c in mo...]
    ppermute x7 -> x4, starting transfers between devices: 23.6 us -> 12.5 us  [partner(): return lax.ppermute(array, axis, [(i, i ^ bit) for i in range(n)])]
    all_to_all x1, starting transfers between devices: 6.44 us -> 14.2 us  [on_device(): parts = lax.all_to_all(parts.reshape(16, -1, rows), CHIPS, 0, 0)]
    ppermute x8 -> x7, starting transfers between devices: 27.7 us -> 23.1 us  [step(): lax.ppermute(array, ('y', 'c'), [(a * 2 + c, b * 2 + c) for a, b, c in mo...]
    pallas_call x2 -> x3, Pallas kernels: 1.41 us -> 5.53 us  [the longest x1 2.86 us: on_device(): pl.pallas_call(final_kernel, in_specs=[hbm, hbm, vmem], scratch_shapes=[p...]
    all_to_all x1, waiting for transfers between devices: 29.3 us -> 32.3 us  [on_device(): parts = lax.all_to_all(parts.reshape(16, -1, rows), CHIPS, 0, 0)]
    slice x2 -> x0, local copies, waits for them, and re-layouts: 2.42 us -> none  [on_device(): first4, second4 = (step(first[:half], 1), step(second[half:], -1))]
    ppermute x7 -> x4, waiting for transfers between devices: 7.67 us -> 5.48 us  [partner(): return lax.ppermute(array, axis, [(i, i ^ bit) for i in range(n)])]
  transfers between devices with their start and end apart: 17 -> 13, of which waited for: 7 -> 9; matrix products, arithmetic and copies ran while one was open for 10% -> 4% of each run, Pallas kernels for 6% -> 7%
where the time goes in v6:
time: 173 us; the launch traced here: 170 us
  waiting for transfers between devices  59.9 us (35%)
  starting transfers between devices  58.8 us (34%)
  blocking collectives  22.4 us (13%)
  Pallas kernels  16.6 us (10%)
  other arithmetic  7.56 us (4%)
  local copies, waits for them, and re-layouts  3.91 us (2%)
    all_to_all x1, waiting for transfers between devices, on_device(): parts = lax.all_to_all(parts.reshape(16, -1, rows), CHIPS, 0, 0)  32.3 us
    ppermute x7, starting transfers between devices, step(): lax.ppermute(array, ('y', 'c'), [(a * 2 + c, b * 2 + c) for a, b, c in mo...  23.1 us
    all_gather x1, blocking collectives, on_device(): w0 = lax.all_gather(w_in, 'zh', axis=0, tiled=True)  22.4 us
    ppermute x7, waiting for transfers between devices, step(): lax.ppermute(array, ('y', 'c'), [(a * 2 + c, b * 2 + c) for a, b, c in mo...  22 us
    all_to_all x1, starting transfers between devices, on_device(): parts = lax.all_to_all(parts.reshape(16, -1, rows), CHIPS, 0, 0)  14.2 us
    ppermute x4, starting transfers between devices, partner(): return lax.ppermute(array, axis, [(i, i ^ bit) for i in range(n)])  12.5 us
    pallas_call x3, Pallas kernels, products(): pl.pallas_call(kernel, in_specs=[pl.BlockSpec(memory_space=pltpu.SMEM)] +...  11.1 us
    all_to_all x1, starting transfers between devices, on_device(): lax.all_to_all(gain_share, DP, 0, 0)  9.03 us
  transfers between devices with their start and end apart: 13, of which 9 were waited for; matrix products, arithmetic and copies ran while one was open for 4% of the time, Pallas kernels for 7%

profile of v6, /device:TPU:1, one launch (start us, length us, event | category | flops | bytes accessed | tf_op | source)
XLA Modules:
  0.0 170.1 jit_solution(8167569245866107026)
XLA Ops:
  0.6 0.0 copy-start.4
  0.6 22.4 %all_gather.3.refs_0_ = bf16[192,1536]{1,0:T(8,128)(2,1)S(1)} all-gather(bf16[48,1536]{1,0:T(8,128)(2,1)} %param.8), channel_id=1, replica_groups=mesh['y'=8,'zh'=4,'c'=2,'zl'=2,'x'=4] {'zh'}, dimensions={0}, use_global_device_ids=true | all-gather | bytes 737280 | tf_op jit(solution)/shard_map/all_gather | solution.py:158
  23.0 3.2 %collective-permute-start = (bf16[192,1536]{1,0:T(8,128)(2,1)S(1)}, bf16[192,1536]{1,0:T(8,128)(2,1)S(1)}, u32[]{:S(2)}, u32[]{:S(2)}) collective-permute-start(bf16[192,1536]{1,0:T(8,128)(2,1)S(1)} %all_gather.3.refs_0_), channel_id=1, source_target_pairs={{64,0},{128,64},{192,128},{256,192},{320,256},{384,320},{448,384},... | collective-permute-start | bytes 1769480 | tf_op jit(solution)/shard_map/ppermute | solution.py:152
  26.2 3.8 %collective-permute-start.1 = (bf16[192,1536]{1,0:T(8,128)(2,1)S(1)}, bf16[192,1536]{1,0:T(8,128)(2,1)}, u32[]{:S(2)}, u32[]{:S(2)}) collective-permute-start(bf16[192,1536]{1,0:T(8,128)(2,1)S(1)} %all_gather.3.refs_0_), channel_id=1, source_target_pairs={{448,0},{0,64},{64,128},{128,192},{192,256},{256,320},{320,384},{3... | collective-permute-start | bytes 1769480 | tf_op jit(solution)/shard_map/ppermute | solution.py:152
  30.0 6.8 %fusion.34.own_ref = bf16[384,1536]{1,0:T(8,128)(2,1)S(1)} fusion(bf16[384,1536]{1,0:T(8,128)(2,1)} %param.9, bf16[384,1536]{1,0:T(8,128)(2,1)} %param.7), kind=kLoop, calls=%fused_computation.39 | loop fusion | flops 43646976 | bytes 3538944 | tf_op jit(solution)/shard_map/convert_element_type | solution.py:162
  36.9 0.0 collective-permute-done.refs_1_
  36.9 6.0 %collective-permute-done.1.refs_2_ = bf16[192,1536]{1,0:T(8,128)(2,1)} collective-permute-done((bf16[192,1536]{1,0:T(8,128)(2,1)S(1)}, bf16[192,1536]{1,0:T(8,128)(2,1)}, u32[]{:S(2)}, u32[]{:S(2)}) %collective-permute-start.1) | collective-permute-done | bytes 589856 | tf_op jit(solution)/shard_map/ppermute | solution.py:152
  42.9 2.6 %collective-permute-start.4 = (bf16[384,1536]{1,0:T(8,128)(2,1)S(1)}, bf16[384,1536]{1,0:T(8,128)(2,1)S(1)}, u32[]{:S(2)}, u32[]{:S(2)}) collective-permute-start(bf16[384,1536]{1,0:T(8,128)(2,1)S(1)} %fusion.34.own_ref), channel_id=1, source_target_pairs={{0,8},{8,0},{1,9},{9,1},{2,10},{10,2},{3,11},{11,3},{4,12},{12,4},... | collective-permute-start | bytes 3538952 | tf_op jit(solution)/shard_map/ppermute | solution.py:24
  45.5 2.0 %collective-permute-start.2 = (bf16[192,1536]{1,0:T(8,128)(2,1)S(1)}, bf16[192,1536]{1,0:T(8,128)(2,1)}, u32[]{:S(2)}, u32[]{:S(2)}) collective-permute-start(bf16[192,1536]{1,0:T(8,128)(2,1)S(1)} %collective-permute-done.refs_1_), channel_id=1, source_target_pairs={{64,0},{128,64},{192,128},{256,192},{320,256},{384,320},{448,384},... | collective-permute-start | bytes 1769480 | tf_op jit(solution)/shard_map/ppermute | solution.py:152
  47.5 5.3 %collective-permute-start.3 = (bf16[192,1536]{1,0:T(8,128)(2,1)}, bf16[192,1536]{1,0:T(8,128)(2,1)}, u32[]{:S(2)}, u32[]{:S(2)}) collective-permute-start(bf16[192,1536]{1,0:T(8,128)(2,1)} %collective-permute-done.1.refs_2_), channel_id=1, source_target_pairs={{448,0},{0,64},{64,128},{128,192},{192,256},{256,320},{320,384},{3... | collective-permute-start | bytes 1769480 | tf_op jit(solution)/shard_map/ppermute | solution.py:152
  52.7 0.0 copy-done.4
  52.7 0.3 shard_map.68
  53.0 0.8 copy-done
  53.8 5.3 %collective-permute-done.2.refs_3_ = bf16[192,1536]{1,0:T(8,128)(2,1)} collective-permute-done((bf16[192,1536]{1,0:T(8,128)(2,1)S(1)}, bf16[192,1536]{1,0:T(8,128)(2,1)}, u32[]{:S(2)}, u32[]{:S(2)}) %collective-permute-start.2) | collective-permute-done | bytes 589856 | tf_op jit(solution)/shard_map/ppermute | solution.py:152
  59.2 0.0 collective-permute-done.4.other_ref
  59.2 1.9 %collective-permute-start.5 = (bf16[192,1536]{1,0:T(8,128)(2,1)}, bf16[192,1536]{1,0:T(8,128)(2,1)}, u32[]{:S(2)}, u32[]{:S(2)}) collective-permute-start(bf16[192,1536]{1,0:T(8,128)(2,1)} %collective-permute-done.2.refs_3_), channel_id=1, source_target_pairs={{64,0},{128,64},{192,128},{256,192},{320,256},{384,320},{448,384},... | collective-permute-start | bytes 1769480 | tf_op jit(solution)/shard_map/ppermute | solution.py:152
  61.1 0.1 pad_add_fusion.place_ref
  61.2 3.3 %collective-permute-done.3.refs_4_ = bf16[192,1536]{1,0:T(8,128)(2,1)} collective-permute-done((bf16[192,1536]{1,0:T(8,128)(2,1)}, bf16[192,1536]{1,0:T(8,128)(2,1)}, u32[]{:S(2)}, u32[]{:S(2)}) %collective-permute-start.3) | collective-permute-done | bytes 589856 | tf_op jit(solution)/shard_map/ppermute | solution.py:152
  64.5 5.0 %collective-permute-start.7 = (bf16[192,1536]{1,0:T(8,128)(2,1)}, bf16[192,1536]{1,0:T(8,128)(2,1)S(1)}, u32[]{:S(2)}, u32[]{:S(2)}) collective-permute-start(bf16[192,1536]{1,0:T(8,128)(2,1)} %collective-permute-done.3.refs_4_), channel_id=1, source_target_pairs={{448,0},{0,64},{64,128},{128,192},{192,256},{256,320},{320,384},{3... | collective-permute-start | bytes 1769480 | tf_op jit(solution)/shard_map/ppermute | solution.py:152
  69.5 5.5 %shard_map.69.refs_2_ = bf16[2,8,208,384]{3,2,1,0:T(8,128)(2,1)} custom-call(s32[2]{0:T(128)S(1)} %pad_add_fusion.place_ref, bf16[384,1536]{1,0:T(8,128)(2,1)S(1)} %fusion.34.own_ref, bf16[384,1536]{1,0:T(8,128)(2,1)S(1)} %collective-permute-done.4.other_ref, bf16[192,1536]{1,0:T(8,128)(2,1)S(1)} %all_gather.3.refs_0_, ...), custom_call_target="tpu_custom_call" | custom-call | flops 566231040 | bytes 262144 | tf_op jit(solution)/shard_map/pallas_call | solution.py:58
  75.1 0.0 collective-permute-done.5.refs_0_
  75.1 1.9 %collective-permute-start.6 = (bf16[192,1536]{1,0:T(8,128)(2,1)}, bf16[192,1536]{1,0:T(8,128)(2,1)S(1)}, u32[]{:S(2)}, u32[]{:S(2)}) collective-permute-start(bf16[192,1536]{1,0:T(8,128)(2,1)} %collective-permute-done.5.refs_0_), channel_id=1, source_target_pairs={{64,0},{128,64},{192,128},{256,192},{320,256},{384,320},{448,384},... | collective-permute-start | bytes 1769480 | tf_op jit(solution)/shard_map/ppermute | solution.py:152
  77.0 5.4 %collective-permute-done.7.refs_1_ = bf16[192,1536]{1,0:T(8,128)(2,1)S(1)} collective-permute-done((bf16[192,1536]{1,0:T(8,128)(2,1)}, bf16[192,1536]{1,0:T(8,128)(2,1)S(1)}, u32[]{:S(2)}, u32[]{:S(2)}) %collective-permute-start.7) | collective-permute-done | bytes 589856 | tf_op jit(solution)/shard_map/ppermute | solution.py:152
  82.4 3.3 %shard_map.70.refs_1_ = bf16[2,8,208,384]{3,2,1,0:T(8,128)(2,1)} custom-call(s32[2]{0:T(128)S(1)} %pad_add_fusion.place_ref, bf16[384,1536]{1,0:T(8,128)(2,1)S(1)} %fusion.34.own_ref, bf16[384,1536]{1,0:T(8,128)(2,1)S(1)} %collective-permute-done.4.other_ref, bf16[192,1536]{1,0:T(8,128)(2,1)} %collective-permute-done.5.refs_0_, ...), custom_call_target="tpu_custom_call", output_to_operand_aliasing={{}: (5, {})} | custom-call | flops 226492416 | bytes 262144 | tf_op jit(solution)/shard_map/pallas_call | solution.py:58
  85.7 2.0 %collective-permute-done.6.refs_0_ = bf16[192,1536]{1,0:T(8,128)(2,1)S(1)} collective-permute-done((bf16[192,1536]{1,0:T(8,128)(2,1)}, bf16[192,1536]{1,0:T(8,128)(2,1)S(1)}, u32[]{:S(2)}, u32[]{:S(2)}) %collective-permute-start.6) | collective-permute-done | bytes 589856 | tf_op jit(solution)/shard_map/ppermute | solution.py:152
  87.7 2.3 %shard_map.71 = bf16[2,8,208,384]{3,2,1,0:T(8,128)(2,1)} custom-call(s32[2]{0:T(128)S(1)} %pad_add_fusion.place_ref, bf16[384,1536]{1,0:T(8,128)(2,1)S(1)} %fusion.34.own_ref, bf16[384,1536]{1,0:T(8,128)(2,1)S(1)} %collective-permute-done.4.other_ref, bf16[192,1536]{1,0:T(8,128)(2,1)S(1)} %collective-permute-done.6.refs_0_, ...), custom_call_target="tpu_custom_call", output_to_operand_aliasing={{}: (4, {})} | custom-call | flops 113246208 | bytes 262144 | tf_op jit(solution)/shard_map/pallas_call | solution.py:58
  89.9 0.0 copy-start.5
  89.9 0.0 copy-start.1
  90.0 14.2 %all-to-all-start = ((bf16[16,208,384]{2,1,0:T(8,128)(2,1)}), bf16[16,208,384]{2,1,0:T(8,128)(2,1)S(1)}, u32[]{:S(2)}, u32[]{:S(2)}) async-start(bf16[16,208,384]{2,1,0:T(8,128)(2,1)} %bitcast.2), calls=%async_computation | async-start | bytes 5111808 | tf_op jit(solution)/shard_map/all_to_all | solution.py:187
  104.2 0.1 reshape.21.gain_ref
  104.3 32.3 %all-to-all-done.parts_ref = bf16[16,208,384]{2,1,0:T(8,128)(2,1)S(1)} async-done(((bf16[16,208,384]{2,1,0:T(8,128)(2,1)}), bf16[16,208,384]{2,1,0:T(8,128)(2,1)S(1)}, u32[]{:S(2)}, u32[]{:S(2)}) %all-to-all-start) | async-done | bytes 2555936 | tf_op jit(solution)/shard_map/all_to_all | solution.py:187
  136.7 0.0 copy-done.1
  136.7 2.4 %shard_map.72 = (f32[384,384]{1,0:T(8,128)S(1)}, f32[384,384]{1,0:T(8,128)S(1)}, f32[8,384]{1,0:T(8,128)S(1)}, f32[384,128]{1,0:T(8,128)S(1)}) custom-call(s32[1]{0:T(128)} %bitcast.core_ref, bf16[16,208,384]{2,1,0:T(8,128)(2,1)S(1)} %all-to-all-done.parts_ref, f32[384,384]{1,0:T(8,128)S(1)} %copy-done.1, f32[384,1]{1,0:T(8,128)S(1)} %reshape.21.gain_ref), custom_call_target="tpu_custom_call" | custom-call | tf_op jit(solution)/shard_map/pallas_call | solution.py:190
  139.1 0.8 copy-done.2
  139.9 0.8 copy-done.3
  140.8 0.7 broadcast_in_dim.10
  141.5 9.0 %all-to-all-start.1 = ((f32[64,8,128]{2,1,0:T(8,128)}), f32[64,8,128]{2,1,0:T(8,128)S(1)}, u32[]{:S(2)}, u32[]{:S(2)}) async-start(f32[64,8,128]{2,1,0:T(8,128)} %broadcast_in_dim.10), calls=%async_computation.1 | async-start | bytes 524288 | tf_op jit(solution)/shard_map/all_to_all | solution.py:205
  150.5 2.2 %collective-permute-start.8 = (f32[8,384]{1,0:T(8,128)S(1)}, f32[8,384]{1,0:T(8,128)S(1)}, u32[]{:S(2)}, u32[]{:S(2)}) collective-permute-start(f32[8,384]{1,0:T(8,128)S(1)} %get-tuple-element.44), channel_id=1, source_target_pairs={{0,1},{1,0},{2,3},{3,2},{4,5},{5,4},{6,7},{7,6},{8,9},{9,8},{10,11... | collective-permute-start | bytes 36872 | tf_op jit(solution)/shard_map/ppermute | solution.py:24
  152.7 2.5 %collective-permute-done.8 = f32[8,384]{1,0:T(8,128)S(1)} collective-permute-done((f32[8,384]{1,0:T(8,128)S(1)}, f32[8,384]{1,0:T(8,128)S(1)}, u32[]{:S(2)}, u32[]{:S(2)}) %collective-permute-start.8) | collective-permute-done | bytes 12320 | tf_op jit(solution)/shard_map/ppermute | solution.py:24
  155.3 4.5 %collective-permute-start.9 = (f32[8,384]{1,0:T(8,128)S(1)}, f32[8,384]{1,0:T(8,128)S(1)}, u32[]{:S(2)}, u32[]{:S(2)}) collective-permute-start(f32[8,384]{1,0:T(8,128)S(1)} %add.9), channel_id=1, source_target_pairs={{0,2},{1,3},{2,0},{3,1},{4,6},{5,7},{6,4},{7,5},{8,10},{9,11},{10,... | collective-permute-start | bytes 36872 | tf_op jit(solution)/shard_map/ppermute | solution.py:24
  159.7 1.8 %collective-permute-done.9 = f32[8,384]{1,0:T(8,128)S(1)} collective-permute-done((f32[8,384]{1,0:T(8,128)S(1)}, f32[8,384]{1,0:T(8,128)S(1)}, u32[]{:S(2)}, u32[]{:S(2)}) %collective-permute-start.9) | collective-permute-done | bytes 12320 | tf_op jit(solution)/shard_map/ppermute | solution.py:24
  161.5 3.3 %collective-permute-start.10 = (f32[8,384]{1,0:T(8,128)S(1)}, f32[8,384]{1,0:T(8,128)S(1)}, u32[]{:S(2)}, u32[]{:S(2)}) collective-permute-start(f32[8,384]{1,0:T(8,128)S(1)} %add.10), channel_id=1, source_target_pairs={{0,4},{4,0},{1,5},{5,1},{2,6},{6,2},{3,7},{7,3},{8,12},{12,8},{9,1... | collective-permute-start | bytes 36872 | tf_op jit(solution)/shard_map/ppermute | solution.py:24
  164.8 1.2 collective-permute-done.10
  166.0 0.6 add.11.moments_ref
  166.6 2.9 %shard_map.73 = bf16[384,384]{1,0:T(8,128)(2,1)} custom-call(f32[384,384]{1,0:T(8,128)} %copy-done.2, f32[384,384]{1,0:T(8,128)} %copy-done.3, f32[8,384]{1,0:T(8,128)} %add.11.moments_ref), custom_call_target="tpu_custom_call" | custom-call | tf_op jit(solution)/shard_map/pallas_call | solution.py:209
  169.4 0.0 all-to-all-done.1
  169.4 0.1 reduce_sum.9
  169.5 0.6 slice_bitcast_fusion
  (7 shorter events, 0.0 us)
Async XLA Ops:
  0.6 52.1 %copy-start.4 = (bf16[384,384]{1,0:T(8,128)(2,1)S(1)}, bf16[384,384]{1,0:T(8,128)(2,1)}, u32[]{:S(2)}) copy-start(bf16[384,384]{1,0:T(8,128)(2,1)} %tokens_ref) | copy-start | bytes 884740
  23.0 13.8 %collective-permute-start = (bf16[192,1536]{1,0:T(8,128)(2,1)S(1)}, bf16[192,1536]{1,0:T(8,128)(2,1)S(1)}, u32[]{:S(2)}, u32[]{:S(2)}) collective-permute-start(bf16[192,1536]{1,0:T(8,128)(2,1)S(1)} %all_gather.3.refs_0_), channel_id=1, source_target_pairs={{64,0},{128,64},{192,128},{256,192},{320,256},{384,320},{448,384},... | collective-permute-start | bytes 1769480 | tf_op jit(solution)/shard_map/ppermute | solution.py:152
  26.2 16.7 %collective-permute-start.1 = (bf16[192,1536]{1,0:T(8,128)(2,1)S(1)}, bf16[192,1536]{1,0:T(8,128)(2,1)}, u32[]{:S(2)}, u32[]{:S(2)}) collective-permute-start(bf16[192,1536]{1,0:T(8,128)(2,1)S(1)} %all_gather.3.refs_0_), channel_id=1, source_target_pairs={{448,0},{0,64},{64,128},{128,192},{192,256},{256,320},{320,384},{3... | collective-permute-start | bytes 1769480 | tf_op jit(solution)/shard_map/ppermute | solution.py:152
  42.9 16.3 %collective-permute-start.4 = (bf16[384,1536]{1,0:T(8,128)(2,1)S(1)}, bf16[384,1536]{1,0:T(8,128)(2,1)S(1)}, u32[]{:S(2)}, u32[]{:S(2)}) collective-permute-start(bf16[384,1536]{1,0:T(8,128)(2,1)S(1)} %fusion.34.own_ref), channel_id=1, source_target_pairs={{0,8},{8,0},{1,9},{9,1},{2,10},{10,2},{3,11},{11,3},{4,12},{12,4},... | collective-permute-start | bytes 3538952 | tf_op jit(solution)/shard_map/ppermute | solution.py:24
  45.5 13.7 %collective-permute-start.2 = (bf16[192,1536]{1,0:T(8,128)(2,1)S(1)}, bf16[192,1536]{1,0:T(8,128)(2,1)}, u32[]{:S(2)}, u32[]{:S(2)}) collective-permute-start(bf16[192,1536]{1,0:T(8,128)(2,1)S(1)} %collective-permute-done.refs_1_), channel_id=1, source_target_pairs={{64,0},{128,64},{192,128},{256,192},{320,256},{384,320},{448,384},... | collective-permute-start | bytes 1769480 | tf_op jit(solution)/shard_map/ppermute | solution.py:152
  47.5 17.0 %collective-permute-start.3 = (bf16[192,1536]{1,0:T(8,128)(2,1)}, bf16[192,1536]{1,0:T(8,128)(2,1)}, u32[]{:S(2)}, u32[]{:S(2)}) collective-permute-start(bf16[192,1536]{1,0:T(8,128)(2,1)} %collective-permute-done.1.refs_2_), channel_id=1, source_target_pairs={{448,0},{0,64},{64,128},{128,192},{192,256},{256,320},{320,384},{3... | collective-permute-start | bytes 1769480 | tf_op jit(solution)/shard_map/ppermute | solution.py:152
  53.0 0.8 copy-start
  59.2 15.9 %collective-permute-start.5 = (bf16[192,1536]{1,0:T(8,128)(2,1)}, bf16[192,1536]{1,0:T(8,128)(2,1)}, u32[]{:S(2)}, u32[]{:S(2)}) collective-permute-start(bf16[192,1536]{1,0:T(8,128)(2,1)} %collective-permute-done.2.refs_3_), channel_id=1, source_target_pairs={{64,0},{128,64},{192,128},{256,192},{320,256},{384,320},{448,384},... | collective-permute-start | bytes 1769480 | tf_op jit(solution)/shard_map/ppermute | solution.py:152
  64.5 17.9 %collective-permute-start.7 = (bf16[192,1536]{1,0:T(8,128)(2,1)}, bf16[192,1536]{1,0:T(8,128)(2,1)S(1)}, u32[]{:S(2)}, u32[]{:S(2)}) collective-permute-start(bf16[192,1536]{1,0:T(8,128)(2,1)} %collective-permute-done.3.refs_4_), channel_id=1, source_target_pairs={{448,0},{0,64},{64,128},{128,192},{192,256},{256,320},{320,384},{3... | collective-permute-start | bytes 1769480 | tf_op jit(solution)/shard_map/ppermute | solution.py:152
  75.1 12.6 %collective-permute-start.6 = (bf16[192,1536]{1,0:T(8,128)(2,1)}, bf16[192,1536]{1,0:T(8,128)(2,1)S(1)}, u32[]{:S(2)}, u32[]{:S(2)}) collective-permute-start(bf16[192,1536]{1,0:T(8,128)(2,1)} %collective-permute-done.5.refs_0_), channel_id=1, source_target_pairs={{64,0},{128,64},{192,128},{256,192},{320,256},{384,320},{448,384},... | collective-permute-start | bytes 1769480 | tf_op jit(solution)/shard_map/ppermute | solution.py:152
  89.9 14.3 %copy-start.5 = (bf16[384]{0:T(512)(128)(2,1)S(1)}, bf16[384]{0:T(512)(128)(2,1)}, u32[]{:S(2)}) copy-start(bf16[384]{0:T(512)(128)(2,1)} %param.6) | copy-start | bytes 2308
  89.9 46.7 %copy-start.1 = (f32[384,384]{1,0:T(8,128)S(1)}, f32[384,384]{1,0:T(8,128)}, u32[]{:S(2)}) copy-start(f32[384,384]{1,0:T(8,128)} %copy-done) | copy-start | bytes 1769476
  90.0 46.7 %all-to-all-start = ((bf16[16,208,384]{2,1,0:T(8,128)(2,1)}), bf16[16,208,384]{2,1,0:T(8,128)(2,1)S(1)}, u32[]{:S(2)}, u32[]{:S(2)}) async-start(bf16[16,208,384]{2,1,0:T(8,128)(2,1)} %bitcast.2), calls=%async_computation | async-start | bytes 5111808 | tf_op jit(solution)/shard_map/all_to_all | solution.py:187
  139.1 0.8 copy-start.2
  139.9 0.8 copy-start.3
  141.5 27.9 %all-to-all-start.1 = ((f32[64,8,128]{2,1,0:T(8,128)}), f32[64,8,128]{2,1,0:T(8,128)S(1)}, u32[]{:S(2)}, u32[]{:S(2)}) async-start(f32[64,8,128]{2,1,0:T(8,128)} %broadcast_in_dim.10), calls=%async_computation.1 | async-start | bytes 524288 | tf_op jit(solution)/shard_map/all_to_all | solution.py:205
  150.5 4.7 %collective-permute-start.8 = (f32[8,384]{1,0:T(8,128)S(1)}, f32[8,384]{1,0:T(8,128)S(1)}, u32[]{:S(2)}, u32[]{:S(2)}) collective-permute-start(f32[8,384]{1,0:T(8,128)S(1)} %get-tuple-element.44), channel_id=1, source_target_pairs={{0,1},{1,0},{2,3},{3,2},{4,5},{5,4},{6,7},{7,6},{8,9},{9,8},{10,11... | collective-permute-start | bytes 36872 | tf_op jit(solution)/shard_map/ppermute | solution.py:24
  155.3 6.2 %collective-permute-start.9 = (f32[8,384]{1,0:T(8,128)S(1)}, f32[8,384]{1,0:T(8,128)S(1)}, u32[]{:S(2)}, u32[]{:S(2)}) collective-permute-start(f32[8,384]{1,0:T(8,128)S(1)} %add.9), channel_id=1, source_target_pairs={{0,2},{1,3},{2,0},{3,1},{4,6},{5,7},{6,4},{7,5},{8,10},{9,11},{10,... | collective-permute-start | bytes 36872 | tf_op jit(solution)/shard_map/ppermute | solution.py:24
  161.5 4.5 %collective-permute-start.10 = (f32[8,384]{1,0:T(8,128)S(1)}, f32[8,384]{1,0:T(8,128)S(1)}, u32[]{:S(2)}, u32[]{:S(2)}) collective-permute-start(f32[8,384]{1,0:T(8,128)S(1)} %add.10), channel_id=1, source_target_pairs={{0,4},{4,0},{1,5},{5,1},{2,6},{6,2},{3,7},{7,3},{8,12},{12,8},{9,1... | collective-permute-start | bytes 36872 | tf_op jit(solution)/shard_map/ppermute | solution.py:24

commit v7 on v5

v7 whole, which is shorter than its diff:
```python
import jax
import jax.numpy as jnp
from jax import lax
from jax.experimental import pallas as pl
from jax.experimental.pallas import tpu as pltpu
from jax.sharding import Mesh, PartitionSpec as P

NAMES = ("y", "zh", "c", "zl", "x")
SIZES = (8, 4, 2, 2, 4)
DP, MP, CHIPS = ("y", "zh", "c"), ("zl", "x"), ("c", "zl", "x")
F32, BF16 = jnp.float32, jnp.bfloat16
SHARD = 48
HALF = 1536
PARAMS = pltpu.CompilerParams(vmem_limit_bytes=20 * 1024 * 1024)
together = lax.optimization_barrier


def gelu_exact(value):
    return jax.nn.gelu(value, approximate=False)


def partner(array, axis, n, bit):
    return lax.ppermute(array, axis, [(i, i ^ bit) for i in range(n)])


def products(groups, d_own, d_other, place, parts):
    tokens, hidden = d_own.shape
    weights = [w for _, w in groups]
    rows, n = weights[0].shape[0], len(groups)

    def kernel(place_ref, own_ref, other_ref, *refs):
        w_refs, (out_ref, held, sem) = refs[:n], refs[-3:]
        copies = []
        w = jnp.concatenate([r[...] for r in w_refs], axis=0)
        for k, d_ref in enumerate((own_ref, other_ref)):
            half = lax.rem(place_ref[1] + k, 2)
            out = lax.dot_general(
                w, d_ref[...], (((1,), (1,)), ((), ())), preferred_element_type=F32
            ).astype(BF16)
            for g, (offset, _) in enumerate(groups):
                held[k, g] = out[g * rows : (g + 1) * rows]
                block = lax.rem(place_ref[0] + offset + place_ref[1] * ((8 - 2 * offset) % 8), 8)
                to = out_ref.at[half, block]
                copies.append(pltpu.make_async_copy(held.at[k, g], to, sem.at[k, g]))
                copies[-1].start()
        for copy in copies:
            copy.wait()

    whole = pl.BlockSpec(memory_space=pltpu.VMEM)
    return pl.pallas_call(
        kernel,
        in_specs=[pl.BlockSpec(memory_space=pltpu.SMEM)]
        + [whole] * (2 + n)
        + [pl.BlockSpec(memory_space=pl.ANY)] * (parts is not None),
        out_specs=pl.BlockSpec(memory_space=pl.ANY),
        out_shape=jax.ShapeDtypeStruct((2, 8, rows, tokens), BF16),
        scratch_shapes=[
            pltpu.VMEM((2, n, rows, tokens), BF16),
            pltpu.SemaphoreType.DMA((2, n)),
        ],
        input_output_aliases={} if parts is None else {3 + n: 0},
        compiler_params=PARAMS,
        cost_estimate=pl.CostEstimate(
            flops=1 << 38, bytes_accessed=64 << 20, transcendentals=0
        ),
    )(place, d_own, d_other, *weights, *([] if parts is None else [parts]))


def stats_kernel(x_ref, out_ref):
    for t in range(2):
        total = 0.0
        for m in range(8):
            total += jnp.sum(x_ref[t * 8 + m].astype(F32), axis=0, keepdims=True)
        mean = total * (1.0 / HALF)
        square = 0.0
        for m in range(8):
            centred = x_ref[t * 8 + m].astype(F32) - mean
            square += jnp.sum(centred * centred, axis=0, keepdims=True)
        out_ref[t] = jnp.concatenate([mean, square] * 4, axis=0)


def mean_and_rstd(one, two):
    mean = (one[0:1] + two[0:1]) * 0.5
    between = (one[0:1] - mean) ** 2 + (two[0:1] - mean) ** 2
    variance = (one[1:2] + two[1:2] + HALF * between) * (1.0 / (2 * HALF))
    return mean, 1.0 / jnp.sqrt(variance + 1e-06)


def gain_kernel(parts_ref, x_ref, one_ref, two_ref, out_ref):
    total = 0.0
    for t in range(2):
        mean, rstd = mean_and_rstd(one_ref[t], two_ref[t])
        xhat = (x_ref[t, 0].astype(F32) - mean) * rstd
        value = parts_ref[t, 0].astype(F32) * xhat
        total += value[:, :128] + value[:, 128:256] + value[:, 256:]
    total = jnp.concatenate([total, jnp.zeros((64, 128), F32)], axis=0)
    out_ref[pl.ds(pl.program_id(0), 1), :] = jnp.sum(total.T, axis=0, keepdims=True)


def gain_share(parts, x_all, one, two):
    _, _, rows, tokens = parts.shape
    block = pl.BlockSpec((2, 1, rows, tokens), lambda m: (0, m, 0, 0))
    stat = pl.BlockSpec((2, 8, tokens), lambda m: (0, 0, 0))
    return pl.pallas_call(
        gain_kernel,
        grid=(8,),
        in_specs=[block, block, stat, stat],
        out_specs=pl.BlockSpec((8, 256), lambda m: (0, 0)),
        out_shape=jax.ShapeDtypeStruct((8, 256), F32),
        compiler_params=PARAMS,
    )(parts, x_all.reshape(parts.shape), one, two)


def sum_kernel(core_ref, parts_ref, x_ref, gain_ref, one_ref, two_ref, d_ref, moments_ref):
    mean, rstd = mean_and_rstd(one_ref[core_ref[0]], two_ref[core_ref[0]])
    first, second = 0.0, 0.0
    for z in range(4):
        for c in range(2):
            total = parts_ref[c * 8, pl.ds(z * SHARD, SHARD), :].astype(F32)
            for m in range(1, 8):
                total += parts_ref[c * 8 + m, pl.ds(z * SHARD, SHARD), :].astype(F32)
            at = pl.ds((z * 2 + c) * SHARD, SHARD)
            g = total * gain_ref[at, :]
            d_ref[at, :] = g
            xhat = (x_ref[at, :].astype(F32) - mean) * rstd
            first += jnp.sum(g, axis=0, keepdims=True)
            second += jnp.sum(g * xhat, axis=0, keepdims=True)
    moments_ref[...] = jnp.concatenate([first, second, jnp.zeros((6, first.shape[1]), F32)], axis=0)


def final_kernel(core_ref, d_ref, x_ref, one_ref, two_ref, small_ref, out_ref, gain_ref):
    core = core_ref[0]
    mean, rstd = mean_and_rstd(one_ref[core], two_ref[core])
    both = small_ref[core * 8]
    for m in range(1, 8):
        both += small_ref[core * 8 + m]
    both = both * (1.0 / (2 * HALF))
    xhat = (x_ref[...].astype(F32) - mean) * rstd
    value = rstd * (d_ref[...] - both[0:1] - xhat * both[1:2])
    out_ref[...] = value.T.astype(BF16)
    rows = []
    for c in range(2):
        row = small_ref[c * 8, 2:3]
        for m in range(1, 8):
            row += small_ref[c * 8 + m, 2:3]
        rows.append(row)
    gain_ref[...] = jnp.concatenate(rows + [jnp.zeros((6, row.shape[1]), F32)], axis=0)


def on_device(tokens, gain, pre_act, w_in, act_cotangent):
    rows, share = tokens.shape
    here = [lax.axis_index(a).astype(jnp.int32).reshape(1) for a in ("y", "c")]
    place = jnp.concatenate(here)

    def step(array, way):
        moves = [((i + way) % 8, i, 0) for i in range(8)] + [((i - way) % 8, i, 1) for i in range(8)]
        return lax.ppermute(array, ("y", "c"), [(a * 2 + c, b * 2 + c) for a, b, c in moves])

    def tie(first, second, done, *later):
        (first_next, _), (second_next, _) = together((first, done)), together((second, done))
        return first_next, second_next, *together((first, second, done, *later))[2:]

    w0 = lax.all_gather(w_in, "zh", axis=0, tiled=True)
    w0, pre_act, act_cotangent = together((w0, pre_act, act_cotangent))
    first1, second1 = step(w0, 1), step(w0, -1)
    _, gelu_back = jax.vjp(gelu_exact, pre_act.astype(F32))
    d_own = gelu_back(act_cotangent.astype(F32))[0].astype(BF16)

    first, second, d_own, tokens = tie(first1, second1, d_own, tokens)
    first2, second2 = step(first, 1), step(second, -1)
    d_other = partner(d_own, "c", 2, 1)
    x = tokens.T
    x_all = jnp.swapaxes(x.reshape(4, 2, SHARD, rows), 0, 1).reshape(2, 1, share // 2, rows)
    x_all = jnp.broadcast_to(x_all, (2, 8, share // 2, rows)).reshape(16, share // 2, rows)
    x_all = lax.all_to_all(x_all, CHIPS, 0, 0)
    parts = products([(0, w0), (1, first1), (7, second1)], d_own, d_other, place, None)

    first, second, parts = tie(first2, second2, parts)
    first3, second3 = step(first, 1), step(second, -1)
    parts = products([(2, first2), (6, second2)], d_own, d_other, place, parts)

    first, second, parts = tie(first3, second3, parts)
    first4 = step(first, 1)
    parts = products([(3, first3), (5, second)], d_own, d_other, place, parts)

    first4, parts = together((first4, parts))
    parts = products([(4, first4)], d_own, d_other, place, parts)
    received = lax.all_to_all(parts.reshape(16, share // 2, rows), CHIPS, 0, 0)

    one = pl.pallas_call(
        stats_kernel,
        out_shape=jax.ShapeDtypeStruct((2, 8, rows), F32),
        compiler_params=PARAMS,
    )(x_all)
    two = partner(one, "c", 2, 1)
    shares = gain_share(parts, x_all, one, two)
    for axis, n, bit in (("y", 8, 1), ("y", 8, 2), ("y", 8, 4), ("zh", 4, 1), ("zh", 4, 2)):
        shares += partner(shares, axis, n, bit)

    gain_column = gain.astype(F32)[:, None]
    vmem = pl.BlockSpec(memory_space=pltpu.VMEM)
    smem = pl.BlockSpec(memory_space=pltpu.SMEM)
    d_scaled, moments = pl.pallas_call(
        sum_kernel,
        in_specs=[smem] + [vmem] * 5,
        out_shape=[
            jax.ShapeDtypeStruct((share, rows), F32),
            jax.ShapeDtypeStruct((8, rows), F32),
        ],
        compiler_params=PARAMS,
    )(here[1], received, x, gain_column, one, two)

    small = jnp.concatenate(
        [
            jnp.broadcast_to(moments[None, :2], (8, 2, rows)),
            jnp.pad(shares, ((0, 0), (0, rows - 256)))[:, None],
            jnp.zeros((8, 5, rows), F32),
        ],
        axis=1,
    )
    small = lax.all_to_all(jnp.concatenate([small, small], axis=0), CHIPS, 0, 0)
    token_gradient, gain_rows = pl.pallas_call(
        final_kernel,
        in_specs=[smem] + [vmem] * 5,
        out_shape=[
            jax.ShapeDtypeStruct((rows, share), BF16),
            jax.ShapeDtypeStruct((8, rows), F32),
        ],
        compiler_params=PARAMS,
    )(here[1], d_scaled, x, one, two, small)
    gain_gradient = jnp.swapaxes(gain_rows[:2, : share // 2].reshape(2, 4, SHARD), 0, 1).reshape(share)
    return (token_gradient, gain_gradient)


def solution(mesh):
    fine = Mesh(mesh.devices.reshape(SIZES), NAMES)
    placed = (P(DP, MP), P(MP), P(DP, MP), P(DP, MP), P(DP, MP))
    return jax.shard_map(
        on_device, mesh=fine, in_specs=placed, out_specs=(P(DP, MP), P(MP)), check_vma=False
    )
```

time: 171 us -> 175 us (1.023); the launches traced: 168 us -> 174 us
  blocking collectives: 22.2 us -> 39.5 us
  Pallas kernels: 12.1 us -> 24.2 us
  waiting for transfers between devices: 43.7 us -> 35.8 us
  starting transfers between devices: 66.3 us -> 58.9 us
  other arithmetic: 11.5 us -> 6.94 us
  local copies, waits for them, and re-layouts: 11.1 us -> 7.74 us
    all_to_all x2, waiting for transfers between devices: 29.3 us -> 0.01 us  [the longest x1 0.01 us: on_device(): x_all = lax.all_to_all(x_all, CHIPS, 0, 0)]
    all_to_all x0 -> x1, blocking collectives: none -> 17.1 us  [on_device(): small = lax.all_to_all(jnp.concatenate([small, small], axis=0), CHIPS, 0, 0)]
    ppermute x8 -> x7, waiting for transfers between devices: 6.64 us -> 21.8 us  [step(): lax.ppermute(array, ('y', 'c'), [(a * 2 + c, b * 2 + c) for a, b, c in mo...]
    pallas_call x2 -> x4, Pallas kernels: 1.41 us -> 9.54 us  [the longest x1 5.22 us: gain_share(): pl.pallas_call(gain_kernel, grid=(8,), in_specs=[block, block, stat, stat...]
    ppermute x7, waiting for transfers between devices: 7.67 us -> 14 us  [partner(): return lax.ppermute(array, axis, [(i, i ^ bit) for i in range(n)])]
    ppermute x8 -> x7, starting transfers between devices: 27.7 us -> 23 us  [step(): lax.ppermute(array, ('y', 'c'), [(a * 2 + c, b * 2 + c) for a, b, c in mo...]
    pallas_call x3 -> x4, Pallas kernels: 10.7 us -> 14.6 us  [products(): pl.pallas_call(kernel, in_specs=[pl.BlockSpec(memory_space=pltpu.SMEM)] +...]
    all_to_all x2, starting transfers between devices: 15 us -> 11.5 us  [the longest x1 6 us: on_device(): x_all = lax.all_to_all(x_all, CHIPS, 0, 0)]
  transfers between devices with their start and end apart: 17 -> 16, of which waited for: 7 -> 10; matrix products, arithmetic and copies ran while one was open for 10% -> 5% of each run, Pallas kernels for 6% -> 13%
where the time goes in v7:
time: 175 us; the launch traced here: 174 us
  starting transfers between devices  58.9 us (34%)
  blocking collectives  39.5 us (23%)
  waiting for transfers between devices  35.8 us (20%)
  Pallas kernels  24.2 us (14%)
  local copies, waits for them, and re-layouts  7.74 us (4%)
  other arithmetic  6.94 us (4%)
    ppermute x7, starting transfers between devices, partner(): return lax.ppermute(array, axis, [(i, i ^ bit) for i in range(n)])  24.3 us
    ppermute x7, starting transfers between devices, step(): lax.ppermute(array, ('y', 'c'), [(a * 2 + c, b * 2 + c) for a, b, c in mo...  23 us
    all_gather x1, blocking collectives, on_device(): w0 = lax.all_gather(w_in, 'zh', axis=0, tiled=True)  22.4 us
    ppermute x7, waiting for transfers between devices, step(): lax.ppermute(array, ('y', 'c'), [(a * 2 + c, b * 2 + c) for a, b, c in mo...  21.8 us
    all_to_all x1, blocking collectives, on_device(): small = lax.all_to_all(jnp.concatenate([small, small], axis=0), CHIPS, 0, 0)  17.1 us
    pallas_call x4, Pallas kernels, products(): pl.pallas_call(kernel, in_specs=[pl.BlockSpec(memory_space=pltpu.SMEM)] +...  14.6 us
    ppermute x7, waiting for transfers between devices, partner(): return lax.ppermute(array, axis, [(i, i ^ bit) for i in range(n)])  14 us
    convert_element_type x1, other arithmetic, on_device(): d_own = gelu_back(act_cotangent.astype(F32))[0].astype(BF16)  6.81 us
  transfers between devices with their start and end apart: 16, of which 10 were waited for; matrix products, arithmetic and copies ran while one was open for 5% of the time, Pallas kernels for 13%

profile of v7, /device:TPU:1, one launch (start us, length us, event | category | flops | bytes accessed | tf_op | source)
XLA Modules:
  0.0 174.1 jit_solution(9964466106924142929)
XLA Ops:
  0.6 22.4 %all_gather.3.refs_0_ = bf16[192,1536]{1,0:T(8,128)(2,1)S(1)} all-gather(bf16[48,1536]{1,0:T(8,128)(2,1)} %param.8), channel_id=1, replica_groups=mesh['y'=8,'zh'=4,'c'=2,'zl'=2,'x'=4] {'zh'}, dimensions={0}, use_global_device_ids=true | all-gather | bytes 737280 | tf_op jit(solution)/shard_map/all_gather | solution.py:163
  23.0 3.2 %collective-permute-start = (bf16[192,1536]{1,0:T(8,128)(2,1)S(1)}, bf16[192,1536]{1,0:T(8,128)(2,1)}, u32[]{:S(2)}, u32[]{:S(2)}) collective-permute-start(bf16[192,1536]{1,0:T(8,128)(2,1)S(1)} %all_gather.3.refs_0_), channel_id=1, source_target_pairs={{64,0},{128,64},{192,128},{256,192},{320,256},{384,320},{448,384},... | collective-permute-start | bytes 1769480 | tf_op jit(solution)/shard_map/ppermute | solution.py:157
  26.2 3.8 %collective-permute-start.1 = (bf16[192,1536]{1,0:T(8,128)(2,1)S(1)}, bf16[192,1536]{1,0:T(8,128)(2,1)}, u32[]{:S(2)}, u32[]{:S(2)}) collective-permute-start(bf16[192,1536]{1,0:T(8,128)(2,1)S(1)} %all_gather.3.refs_0_), channel_id=1, source_target_pairs={{448,0},{0,64},{64,128},{128,192},{192,256},{256,320},{320,384},{3... | collective-permute-start | bytes 1769480 | tf_op jit(solution)/shard_map/ppermute | solution.py:157
  30.0 6.8 %fusion.34.own_ref = bf16[384,1536]{1,0:T(8,128)(2,1)S(1)} fusion(bf16[384,1536]{1,0:T(8,128)(2,1)} %param.9, bf16[384,1536]{1,0:T(8,128)(2,1)} %param.7), kind=kLoop, calls=%fused_computation.39 | loop fusion | flops 43646976 | bytes 3538944 | tf_op jit(solution)/shard_map/convert_element_type | solution.py:167
  36.9 6.0 %collective-permute-done.1.refs_2_ = bf16[192,1536]{1,0:T(8,128)(2,1)} collective-permute-done((bf16[192,1536]{1,0:T(8,128)(2,1)S(1)}, bf16[192,1536]{1,0:T(8,128)(2,1)}, u32[]{:S(2)}, u32[]{:S(2)}) %collective-permute-start.1) | collective-permute-done | bytes 589856 | tf_op jit(solution)/shard_map/ppermute | solution.py:157
  42.9 2.6 %collective-permute-start.2 = (bf16[384,1536]{1,0:T(8,128)(2,1)S(1)}, bf16[384,1536]{1,0:T(8,128)(2,1)S(1)}, u32[]{:S(2)}, u32[]{:S(2)}) collective-permute-start(bf16[384,1536]{1,0:T(8,128)(2,1)S(1)} %fusion.34.own_ref), channel_id=1, source_target_pairs={{0,8},{8,0},{1,9},{9,1},{2,10},{10,2},{3,11},{11,3},{4,12},{12,4},... | collective-permute-start | bytes 3538952 | tf_op jit(solution)/shard_map/ppermute | solution.py:23
  45.5 0.1 pad_add_fusion.place_ref
  45.6 2.0 %collective-permute-start.3 = (bf16[192,1536]{1,0:T(8,128)(2,1)}, bf16[192,1536]{1,0:T(8,128)(2,1)}, u32[]{:S(2)}, u32[]{:S(2)}) collective-permute-start(bf16[192,1536]{1,0:T(8,128)(2,1)} %collective-permute-done.refs_1_), channel_id=1, source_target_pairs={{64,0},{128,64},{192,128},{256,192},{320,256},{384,320},{448,384},... | collective-permute-start | bytes 1769480 | tf_op jit(solution)/shard_map/ppermute | solution.py:157
  47.5 5.4 %collective-permute-start.5 = (bf16[192,1536]{1,0:T(8,128)(2,1)}, bf16[192,1536]{1,0:T(8,128)(2,1)}, u32[]{:S(2)}, u32[]{:S(2)}) collective-permute-start(bf16[192,1536]{1,0:T(8,128)(2,1)} %collective-permute-done.1.refs_2_), channel_id=1, source_target_pairs={{448,0},{0,64},{64,128},{128,192},{192,256},{256,320},{320,384},{3... | collective-permute-start | bytes 1769480 | tf_op jit(solution)/shard_map/ppermute | solution.py:157
  52.9 0.2 copy.11
  53.1 0.0 copy-start.2
  53.2 1.7 %broadcast_in_dim.27 = bf16[2,8,192,384]{3,2,1,0:T(8,128)(2,1)} broadcast(bf16[2,192,384]{2,1,0:T(8,128)(2,1)S(1)} %bitcast.19), dimensions={0,2,3} | broadcast | bytes 2654208 | tf_op jit(solution)/shard_map/broadcast_in_dim | solution.py:174
  55.0 6.0 %all-to-all-start.1 = ((bf16[16,192,384]{2,1,0:T(8,128)(2,1)}), bf16[16,192,384]{2,1,0:T(8,128)(2,1)}, u32[]{:S(2)}, u32[]{:S(2)}) async-start(bf16[16,192,384]{2,1,0:T(8,128)(2,1)} %bitcast.18), calls=%async_computation.1 | async-start | bytes 4718592 | tf_op jit(solution)/shard_map/all_to_all | solution.py:175
  61.0 1.0 copy-done.6
  62.0 1.1 copy-done.5
  63.1 1.3 copy-done.7
  64.3 4.7 %shard_map.68.refs_2_ = bf16[2,8,192,384]{3,2,1,0:T(8,128)(2,1)S(1)} custom-call(s32[2]{0:T(128)S(1)} %pad_add_fusion.place_ref, bf16[384,1536]{1,0:T(8,128)(2,1)S(1)} %fusion.34.own_ref, bf16[384,1536]{1,0:T(8,128)(2,1)S(1)} %copy-done.7, bf16[192,1536]{1,0:T(8,128)(2,1)S(1)} %copy-done.5, bf16[192,1536]{1,0:T(8,128)(2,1)} %collective-permute-done.refs_1_, ...), custom_call_target="tpu_custom_call" | custom-call | flops 274877906944 | bytes 67108864 | tf_op jit(solution)/shard_map/pallas_call | solution.py:50
  69.1 1.9 %collective-permute-start.4 = (bf16[192,1536]{1,0:T(8,128)(2,1)}, bf16[192,1536]{1,0:T(8,128)(2,1)}, u32[]{:S(2)}, u32[]{:S(2)}) collective-permute-start(bf16[192,1536]{1,0:T(8,128)(2,1)} %collective-permute-done.3.refs_0_), channel_id=1, source_target_pairs={{64,0},{128,64},{192,128},{256,192},{320,256},{384,320},{448,384},... | collective-permute-start | bytes 1769480 | tf_op jit(solution)/shard_map/ppermute | solution.py:157
  71.0 4.9 %collective-permute-start.7 = (bf16[192,1536]{1,0:T(8,128)(2,1)}, bf16[192,1536]{1,0:T(8,128)(2,1)}, u32[]{:S(2)}, u32[]{:S(2)}) collective-permute-start(bf16[192,1536]{1,0:T(8,128)(2,1)} %collective-permute-done.5.refs_1_), channel_id=1, source_target_pairs={{448,0},{0,64},{64,128},{128,192},{192,256},{256,320},{320,384},{3... | collective-permute-start | bytes 1769480 | tf_op jit(solution)/shard_map/ppermute | solution.py:157
  75.9 3.7 %shard_map.69.refs_2_ = bf16[2,8,192,384]{3,2,1,0:T(8,128)(2,1)S(1)} custom-call(s32[2]{0:T(128)S(1)} %pad_add_fusion.place_ref, bf16[384,1536]{1,0:T(8,128)(2,1)S(1)} %fusion.34.own_ref, bf16[384,1536]{1,0:T(8,128)(2,1)S(1)} %copy-done.7, bf16[192,1536]{1,0:T(8,128)(2,1)} %collective-permute-done.3.refs_0_, ...), custom_call_target="tpu_custom_call", output_to_operand_aliasing={{}: (5, {})} | custom-call | flops 274877906944 | bytes 67108864 | tf_op jit(solution)/shard_map/pallas_call | solution.py:50
  79.5 3.1 %collective-permute-done.4.refs_0_ = bf16[192,1536]{1,0:T(8,128)(2,1)} collective-permute-done((bf16[192,1536]{1,0:T(8,128)(2,1)}, bf16[192,1536]{1,0:T(8,128)(2,1)}, u32[]{:S(2)}, u32[]{:S(2)}) %collective-permute-start.4) | collective-permute-done | bytes 589856 | tf_op jit(solution)/shard_map/ppermute | solution.py:157
  82.6 5.4 %collective-permute-done.7.refs_1_ = bf16[192,1536]{1,0:T(8,128)(2,1)} collective-permute-done((bf16[192,1536]{1,0:T(8,128)(2,1)}, bf16[192,1536]{1,0:T(8,128)(2,1)}, u32[]{:S(2)}, u32[]{:S(2)}) %collective-permute-start.7) | collective-permute-done | bytes 589856 | tf_op jit(solution)/shard_map/ppermute | solution.py:157
  88.0 1.9 %collective-permute-start.6 = (bf16[192,1536]{1,0:T(8,128)(2,1)}, bf16[192,1536]{1,0:T(8,128)(2,1)}, u32[]{:S(2)}, u32[]{:S(2)}) collective-permute-start(bf16[192,1536]{1,0:T(8,128)(2,1)} %collective-permute-done.4.refs_0_), channel_id=1, source_target_pairs={{64,0},{128,64},{192,128},{256,192},{320,256},{384,320},{448,384},... | collective-permute-start | bytes 1769480 | tf_op jit(solution)/shard_map/ppermute | solution.py:157
  89.9 3.7 %shard_map.70.refs_1_ = bf16[2,8,192,384]{3,2,1,0:T(8,128)(2,1)S(1)} custom-call(s32[2]{0:T(128)S(1)} %pad_add_fusion.place_ref, bf16[384,1536]{1,0:T(8,128)(2,1)S(1)} %fusion.34.own_ref, bf16[384,1536]{1,0:T(8,128)(2,1)S(1)} %copy-done.7, bf16[192,1536]{1,0:T(8,128)(2,1)} %collective-permute-done.4.refs_0_, ...), custom_call_target="tpu_custom_call", output_to_operand_aliasing={{}: (5, {})} | custom-call | flops 274877906944 | bytes 67108864 | tf_op jit(solution)/shard_map/pallas_call | solution.py:50
  93.6 7.3 %collective-permute-done.6.refs_0_ = bf16[192,1536]{1,0:T(8,128)(2,1)} collective-permute-done((bf16[192,1536]{1,0:T(8,128)(2,1)}, bf16[192,1536]{1,0:T(8,128)(2,1)}, u32[]{:S(2)}, u32[]{:S(2)}) %collective-permute-start.6) | collective-permute-done | bytes 589856 | tf_op jit(solution)/shard_map/ppermute | solution.py:157
  100.9 2.6 %shard_map.71.parts_ref = bf16[2,8,192,384]{3,2,1,0:T(8,128)(2,1)S(1)} custom-call(s32[2]{0:T(128)S(1)} %pad_add_fusion.place_ref, bf16[384,1536]{1,0:T(8,128)(2,1)S(1)} %fusion.34.own_ref, bf16[384,1536]{1,0:T(8,128)(2,1)S(1)} %copy-done.7, bf16[192,1536]{1,0:T(8,128)(2,1)} %collective-permute-done.6.refs_0_, ...), custom_call_target="tpu_custom_call", output_to_operand_aliasing={{}: (4, {})} | custom-call | flops 274877906944 | bytes 67108864 | tf_op jit(solution)/shard_map/pallas_call | solution.py:50
  103.5 1.4 copy-done
  105.0 5.5 %all-to-all-start = ((bf16[16,192,384]{2,1,0:T(8,128)(2,1)}), bf16[16,192,384]{2,1,0:T(8,128)(2,1)S(1)}, u32[]{:S(2)}, u32[]{:S(2)}) async-start(bf16[16,192,384]{2,1,0:T(8,128)(2,1)} %bitcast.14), calls=%async_computation | async-start | bytes 4718592 | tf_op jit(solution)/shard_map/all_to_all | solution.py:188
  110.5 2.9 %shard_map.72.one_ref = f32[2,8,384]{2,1,0:T(8,128)S(1)} custom-call(bf16[16,192,384]{2,1,0:T(8,128)(2,1)} %all-to-all-done.1.x_ref), custom_call_target="tpu_custom_call" | custom-call | tf_op jit(solution)/shard_map/pallas_call | solution.py:190
  113.4 2.0 %collective-permute-start.8 = (f32[2,8,384]{2,1,0:T(8,128)S(1)}, f32[2,8,384]{2,1,0:T(8,128)S(1)}, u32[]{:S(2)}, u32[]{:S(2)}) collective-permute-start(f32[2,8,384]{2,1,0:T(8,128)S(1)} %shard_map.72.one_ref), channel_id=1, source_target_pairs={{0,8},{8,0},{1,9},{9,1},{2,10},{10,2},{3,11},{11,3},{4,12},{12,4},... | collective-permute-start | bytes 73736 | tf_op jit(solution)/shard_map/ppermute | solution.py:23
  115.4 1.1 collective-permute-done.8.two_ref
  116.5 5.2 %shard_map.74 = f32[8,256]{1,0:T(8,128)S(1)} custom-call(bf16[2,8,192,384]{3,2,1,0:T(8,128)(2,1)S(1)} %copy-done.1, bf16[2,8,192,384]{3,2,1,0:T(8,128)(2,1)} %bitcast.8.x_ref, f32[2,8,384]{2,1,0:T(8,128)S(1)} %shard_map.72.one_ref, f32[2,8,384]{2,1,0:T(8,128)S(1)} %collective-permute-done.8.two_ref), custom_call_target="tpu_custom_call" | custom-call | tf_op jit(solution)/shard_map/pallas_call | solution.py:104
  121.7 1.9 %collective-permute-start.9 = (f32[8,256]{1,0:T(8,128)S(1)}, f32[8,256]{1,0:T(8,128)S(1)}, u32[]{:S(2)}, u32[]{:S(2)}) collective-permute-start(f32[8,256]{1,0:T(8,128)S(1)} %shard_map.74), channel_id=1, source_target_pairs={{0,64},{64,0},{128,192},{192,128},{256,320},{320,256},{384,448},{4... | collective-permute-start | bytes 24584 | tf_op jit(solution)/shard_map/ppermute | solution.py:23
  123.6 2.8 %collective-permute-done.9 = f32[8,256]{1,0:T(8,128)S(1)} collective-permute-done((f32[8,256]{1,0:T(8,128)S(1)}, f32[8,256]{1,0:T(8,128)S(1)}, u32[]{:S(2)}, u32[]{:S(2)}) %collective-permute-start.9) | collective-permute-done | bytes 8224 | tf_op jit(solution)/shard_map/ppermute | solution.py:23
  126.4 3.3 %collective-permute-start.10 = (f32[8,256]{1,0:T(8,128)S(1)}, f32[8,256]{1,0:T(8,128)S(1)}, u32[]{:S(2)}, u32[]{:S(2)}) collective-permute-start(f32[8,256]{1,0:T(8,128)S(1)} %add.17), channel_id=1, source_target_pairs={{0,128},{64,192},{128,0},{192,64},{256,384},{320,448},{384,256},{4... | collective-permute-start | bytes 24584 | tf_op jit(solution)/shard_map/ppermute | solution.py:23
  129.7 2.2 %collective-permute-done.10 = f32[8,256]{1,0:T(8,128)S(1)} collective-permute-done((f32[8,256]{1,0:T(8,128)S(1)}, f32[8,256]{1,0:T(8,128)S(1)}, u32[]{:S(2)}, u32[]{:S(2)}) %collective-permute-start.10) | collective-permute-done | bytes 8224 | tf_op jit(solution)/shard_map/ppermute | solution.py:23
  132.0 4.5 %collective-permute-start.11 = (f32[8,256]{1,0:T(8,128)S(1)}, f32[8,256]{1,0:T(8,128)S(1)}, u32[]{:S(2)}, u32[]{:S(2)}) collective-permute-start(f32[8,256]{1,0:T(8,128)S(1)} %add.18), channel_id=1, source_target_pairs={{0,256},{64,320},{128,384},{192,448},{256,0},{320,64},{384,128},{4... | collective-permute-start | bytes 24584 | tf_op jit(solution)/shard_map/ppermute | solution.py:23
  136.5 3.7 %collective-permute-done.11 = f32[8,256]{1,0:T(8,128)S(1)} collective-permute-done((f32[8,256]{1,0:T(8,128)S(1)}, f32[8,256]{1,0:T(8,128)S(1)}, u32[]{:S(2)}, u32[]{:S(2)}) %collective-permute-start.11) | collective-permute-done | bytes 8224 | tf_op jit(solution)/shard_map/ppermute | solution.py:23
  140.3 5.0 %collective-permute-start.12 = (f32[8,256]{1,0:T(8,128)S(1)}, f32[8,256]{1,0:T(8,128)S(1)}, u32[]{:S(2)}, u32[]{:S(2)}) collective-permute-start(f32[8,256]{1,0:T(8,128)S(1)} %add.19), channel_id=1, source_target_pairs={{0,16},{16,0},{32,48},{48,32},{1,17},{17,1},{33,49},{49,33},{2,18}... | collective-permute-start | bytes 24584 | tf_op jit(solution)/shard_map/ppermute | solution.py:23
  145.3 1.0 collective-permute-done.12
  146.3 5.0 %collective-permute-start.13 = (f32[8,256]{1,0:T(8,128)S(1)}, f32[8,256]{1,0:T(8,128)S(1)}, u32[]{:S(2)}, u32[]{:S(2)}) collective-permute-start(f32[8,256]{1,0:T(8,128)S(1)} %add.20), channel_id=1, source_target_pairs={{0,32},{16,48},{32,0},{48,16},{1,33},{17,49},{33,1},{49,17},{2,34}... | collective-permute-start | bytes 24584 | tf_op jit(solution)/shard_map/ppermute | solution.py:23
  151.3 0.1 reshape.40.gain_ref
  151.4 3.2 %collective-permute-done.13 = f32[8,256]{1,0:T(8,128)S(1)} collective-permute-done((f32[8,256]{1,0:T(8,128)S(1)}, f32[8,256]{1,0:T(8,128)S(1)}, u32[]{:S(2)}, u32[]{:S(2)}) %collective-permute-start.13) | collective-permute-done | bytes 8224 | tf_op jit(solution)/shard_map/ppermute | solution.py:23
  154.7 0.5 shard_map.73
  155.2 17.1 %all_to_all.15.small_ref = f32[16,8,384]{2,1,0:T(8,128)S(1)} all-to-all(f32[16,8,384]{2,1,0:T(8,128)S(1)} %maximum_maximum_fusion), channel_id=1, replica_groups=mesh['y'=8,'zh'=4,'c'=2,'zl'=2,'x'=4] {'c','zl','x'}, dimensions={0} | all-to-all | bytes 393216 | tf_op jit(solution)/shard_map/all_to_all | solution.py:221
  172.3 1.0 shard_map.75
  173.3 0.1 reshape.37
  173.4 0.7 reshape.38
  (35 shorter events, 0.2 us)
Async XLA Ops:
  0.6 52.3 %copy-start.8 = (bf16[384,384]{1,0:T(8,128)(2,1)S(1)}, bf16[384,384]{1,0:T(8,128)(2,1)}, u32[]{:S(2)}) copy-start(bf16[384,384]{1,0:T(8,128)(2,1)} %param.5) | copy-start | bytes 884740
  23.0 13.9 %copy-start.4 = (bf16[192,1536]{1,0:T(8,128)(2,1)}, bf16[192,1536]{1,0:T(8,128)(2,1)S(1)}, u32[]{:S(2)}) copy-start(bf16[192,1536]{1,0:T(8,128)(2,1)S(1)} %all_gather.3.refs_0_) | copy-start | bytes 1769476
  23.0 13.8 %collective-permute-start = (bf16[192,1536]{1,0:T(8,128)(2,1)S(1)}, bf16[192,1536]{1,0:T(8,128)(2,1)}, u32[]{:S(2)}, u32[]{:S(2)}) collective-permute-start(bf16[192,1536]{1,0:T(8,128)(2,1)S(1)} %all_gather.3.refs_0_), channel_id=1, source_target_pairs={{64,0},{128,64},{192,128},{256,192},{320,256},{384,320},{448,384},... | collective-permute-start | bytes 1769480 | tf_op jit(solution)/shard_map/ppermute | solution.py:157
  26.2 16.7 %collective-permute-start.1 = (bf16[192,1536]{1,0:T(8,128)(2,1)S(1)}, bf16[192,1536]{1,0:T(8,128)(2,1)}, u32[]{:S(2)}, u32[]{:S(2)}) collective-permute-start(bf16[192,1536]{1,0:T(8,128)(2,1)S(1)} %all_gather.3.refs_0_), channel_id=1, source_target_pairs={{448,0},{0,64},{64,128},{128,192},{192,256},{256,320},{320,384},{3... | collective-permute-start | bytes 1769480 | tf_op jit(solution)/shard_map/ppermute | solution.py:157
  42.9 18.0 %collective-permute-start.2 = (bf16[384,1536]{1,0:T(8,128)(2,1)S(1)}, bf16[384,1536]{1,0:T(8,128)(2,1)S(1)}, u32[]{:S(2)}, u32[]{:S(2)}) collective-permute-start(bf16[384,1536]{1,0:T(8,128)(2,1)S(1)} %fusion.34.own_ref), channel_id=1, source_target_pairs={{0,8},{8,0},{1,9},{9,1},{2,10},{10,2},{3,11},{11,3},{4,12},{12,4},... | collective-permute-start | bytes 3538952 | tf_op jit(solution)/shard_map/ppermute | solution.py:23
  45.6 23.5 %collective-permute-start.3 = (bf16[192,1536]{1,0:T(8,128)(2,1)}, bf16[192,1536]{1,0:T(8,128)(2,1)}, u32[]{:S(2)}, u32[]{:S(2)}) collective-permute-start(bf16[192,1536]{1,0:T(8,128)(2,1)} %collective-permute-done.refs_1_), channel_id=1, source_target_pairs={{64,0},{128,64},{192,128},{256,192},{320,256},{384,320},{448,384},... | collective-permute-start | bytes 1769480 | tf_op jit(solution)/shard_map/ppermute | solution.py:157
  47.5 21.5 %collective-permute-start.5 = (bf16[192,1536]{1,0:T(8,128)(2,1)}, bf16[192,1536]{1,0:T(8,128)(2,1)}, u32[]{:S(2)}, u32[]{:S(2)}) collective-permute-start(bf16[192,1536]{1,0:T(8,128)(2,1)} %collective-permute-done.1.refs_2_), channel_id=1, source_target_pairs={{448,0},{0,64},{64,128},{128,192},{192,256},{256,320},{320,384},{3... | collective-permute-start | bytes 1769480 | tf_op jit(solution)/shard_map/ppermute | solution.py:157
  53.1 1.8 %copy-start.2 = (bf16[384,384]{0,1:T(8,128)(2,1)}, bf16[384,384]{0,1:T(8,128)(2,1)S(1)}, u32[]{:S(2)}) copy-start(bf16[384,384]{0,1:T(8,128)(2,1)S(1)} %copy.11) | copy-start | bytes 884740
  55.0 50.0 %all-to-all-start.1 = ((bf16[16,192,384]{2,1,0:T(8,128)(2,1)}), bf16[16,192,384]{2,1,0:T(8,128)(2,1)}, u32[]{:S(2)}, u32[]{:S(2)}) async-start(bf16[16,192,384]{2,1,0:T(8,128)(2,1)} %bitcast.18), calls=%async_computation.1 | async-start | bytes 4718592 | tf_op jit(solution)/shard_map/all_to_all | solution.py:175
  61.0 1.0 copy-start.6
  62.0 1.1 copy-start.5
  63.1 1.3 copy-start.7
  69.1 13.5 %collective-permute-start.4 = (bf16[192,1536]{1,0:T(8,128)(2,1)}, bf16[192,1536]{1,0:T(8,128)(2,1)}, u32[]{:S(2)}, u32[]{:S(2)}) collective-permute-start(bf16[192,1536]{1,0:T(8,128)(2,1)} %collective-permute-done.3.refs_0_), channel_id=1, source_target_pairs={{64,0},{128,64},{192,128},{256,192},{320,256},{384,320},{448,384},... | collective-permute-start | bytes 1769480 | tf_op jit(solution)/shard_map/ppermute | solution.py:157
  71.0 17.0 %collective-permute-start.7 = (bf16[192,1536]{1,0:T(8,128)(2,1)}, bf16[192,1536]{1,0:T(8,128)(2,1)}, u32[]{:S(2)}, u32[]{:S(2)}) collective-permute-start(bf16[192,1536]{1,0:T(8,128)(2,1)} %collective-permute-done.5.refs_1_), channel_id=1, source_target_pairs={{448,0},{0,64},{64,128},{128,192},{192,256},{256,320},{320,384},{3... | collective-permute-start | bytes 1769480 | tf_op jit(solution)/shard_map/ppermute | solution.py:157
  88.0 12.9 %collective-permute-start.6 = (bf16[192,1536]{1,0:T(8,128)(2,1)}, bf16[192,1536]{1,0:T(8,128)(2,1)}, u32[]{:S(2)}, u32[]{:S(2)}) collective-permute-start(bf16[192,1536]{1,0:T(8,128)(2,1)} %collective-permute-done.4.refs_0_), channel_id=1, source_target_pairs={{64,0},{128,64},{192,128},{256,192},{320,256},{384,320},{448,384},... | collective-permute-start | bytes 1769480 | tf_op jit(solution)/shard_map/ppermute | solution.py:157
  103.5 1.4 copy-start
  105.0 49.7 %all-to-all-start = ((bf16[16,192,384]{2,1,0:T(8,128)(2,1)}), bf16[16,192,384]{2,1,0:T(8,128)(2,1)S(1)}, u32[]{:S(2)}, u32[]{:S(2)}) async-start(bf16[16,192,384]{2,1,0:T(8,128)(2,1)} %bitcast.14), calls=%async_computation | async-start | bytes 4718592 | tf_op jit(solution)/shard_map/all_to_all | solution.py:188
  110.5 6.0 %copy-start.1 = (bf16[2,8,192,384]{3,2,1,0:T(8,128)(2,1)S(1)}, bf16[2,8,192,384]{3,2,1,0:T(8,128)(2,1)}, u32[]{:S(2)}) copy-start(bf16[2,8,192,384]{3,2,1,0:T(8,128)(2,1)} %copy-done) | copy-start | bytes 7077892
  113.4 3.1 %collective-permute-start.8 = (f32[2,8,384]{2,1,0:T(8,128)S(1)}, f32[2,8,384]{2,1,0:T(8,128)S(1)}, u32[]{:S(2)}, u32[]{:S(2)}) collective-permute-start(f32[2,8,384]{2,1,0:T(8,128)S(1)} %shard_map.72.one_ref), channel_id=1, source_target_pairs={{0,8},{8,0},{1,9},{9,1},{2,10},{10,2},{3,11},{11,3},{4,12},{12,4},... | collective-permute-start | bytes 73736 | tf_op jit(solution)/shard_map/ppermute | solution.py:23
  116.5 34.8 %copy-start.9 = (bf16[384]{0:T(512)(128)(2,1)S(1)}, bf16[384]{0:T(512)(128)(2,1)}, u32[]{:S(2)}) copy-start(bf16[384]{0:T(512)(128)(2,1)} %param.6) | copy-start | bytes 2308
  116.5 38.2 %copy-start.3 = (bf16[384,384]{0,1:T(8,128)(2,1)S(1)}, bf16[384,384]{0,1:T(8,128)(2,1)}, u32[]{:S(2)}) copy-start(bf16[384,384]{0,1:T(8,128)(2,1)} %copy-done.2) | copy-start | bytes 884740
  121.7 4.7 %collective-permute-start.9 = (f32[8,256]{1,0:T(8,128)S(1)}, f32[8,256]{1,0:T(8,128)S(1)}, u32[]{:S(2)}, u32[]{:S(2)}) collective-permute-start(f32[8,256]{1,0:T(8,128)S(1)} %shard_map.74), channel_id=1, source_target_pairs={{0,64},{64,0},{128,192},{192,128},{256,320},{320,256},{384,448},{4... | collective-permute-start | bytes 24584 | tf_op jit(solution)/shard_map/ppermute | solution.py:23
  126.4 5.6 %collective-permute-start.10 = (f32[8,256]{1,0:T(8,128)S(1)}, f32[8,256]{1,0:T(8,128)S(1)}, u32[]{:S(2)}, u32[]{:S(2)}) collective-permute-start(f32[8,256]{1,0:T(8,128)S(1)} %add.17), channel_id=1, source_target_pairs={{0,128},{64,192},{128,0},{192,64},{256,384},{320,448},{384,256},{4... | collective-permute-start | bytes 24584 | tf_op jit(solution)/shard_map/ppermute | solution.py:23
  132.0 8.3 %collective-permute-start.11 = (f32[8,256]{1,0:T(8,128)S(1)}, f32[8,256]{1,0:T(8,128)S(1)}, u32[]{:S(2)}, u32[]{:S(2)}) collective-permute-start(f32[8,256]{1,0:T(8,128)S(1)} %add.18), channel_id=1, source_target_pairs={{0,256},{64,320},{128,384},{192,448},{256,0},{320,64},{384,128},{4... | collective-permute-start | bytes 24584 | tf_op jit(solution)/shard_map/ppermute | solution.py:23
  140.3 6.0 %collective-permute-start.12 = (f32[8,256]{1,0:T(8,128)S(1)}, f32[8,256]{1,0:T(8,128)S(1)}, u32[]{:S(2)}, u32[]{:S(2)}) collective-permute-start(f32[8,256]{1,0:T(8,128)S(1)} %add.19), channel_id=1, source_target_pairs={{0,16},{16,0},{32,48},{48,32},{1,17},{17,1},{33,49},{49,33},{2,18}... | collective-permute-start | bytes 24584 | tf_op jit(solution)/shard_map/ppermute | solution.py:23
  146.3 8.3 %collective-permute-start.13 = (f32[8,256]{1,0:T(8,128)S(1)}, f32[8,256]{1,0:T(8,128)S(1)}, u32[]{:S(2)}, u32[]{:S(2)}) collective-permute-start(f32[8,256]{1,0:T(8,128)S(1)} %add.20), channel_id=1, source_target_pairs={{0,32},{16,48},{32,0},{48,16},{1,33},{17,49},{33,1},{49,17},{2,34}... | collective-permute-start | bytes 24584 | tf_op jit(solution)/shard_map/ppermute | solution.py:23

commit v8 on v7

--- a/solution.py
+++ b/solution.py
@@ -125,26 +125,29 @@
             xhat = (x_ref[at, :].astype(F32) - mean) * rstd
             first += jnp.sum(g, axis=0, keepdims=True)
             second += jnp.sum(g * xhat, axis=0, keepdims=True)
-    moments_ref[...] = jnp.concatenate([first, second, jnp.zeros((6, first.shape[1]), F32)], axis=0)
-
-
-def final_kernel(core_ref, d_ref, x_ref, one_ref, two_ref, small_ref, out_ref, gain_ref):
-    core = core_ref[0]
+    rows = [m[:, i * 128 : (i + 1) * 128] for m in (first, second) for i in range(3)]
+    moments_ref[...] = jnp.concatenate(rows + [jnp.zeros((2, 128), F32)], axis=0)
+
+
+def final_kernel(here_ref, d_ref, x_ref, one_ref, two_ref, small_ref, out_ref, gain_ref):
+    core, zh = here_ref[0], here_ref[1]
     mean, rstd = mean_and_rstd(one_ref[core], two_ref[core])
-    both = small_ref[core * 8]
+    total = small_ref[zh * 16 + core * 8]
     for m in range(1, 8):
-        both += small_ref[core * 8 + m]
-    both = both * (1.0 / (2 * HALF))
+        total += small_ref[zh * 16 + core * 8 + m]
+    total = total * (1.0 / (2 * HALF))
+    first, second = (jnp.concatenate([total[k + i : k + i + 1] for i in range(3)], axis=1) for k in (0, 3))
     xhat = (x_ref[...].astype(F32) - mean) * rstd
-    value = rstd * (d_ref[...] - both[0:1] - xhat * both[1:2])
+    value = rstd * (d_ref[...] - first - xhat * second)
     out_ref[...] = value.T.astype(BF16)
     rows = []
     for c in range(2):
-        row = small_ref[c * 8, 2:3]
-        for m in range(1, 8):
-            row += small_ref[c * 8 + m, 2:3]
-        rows.append(row)
-    gain_ref[...] = jnp.concatenate(rows + [jnp.zeros((6, row.shape[1]), F32)], axis=0)
+        both = jnp.zeros((8, 128), F32)
+        for z in range(4):
+            for m in range(8):
+                both += small_ref[z * 16 + c * 8 + m]
+        rows.append(jnp.concatenate([both[6:7], both[7:8]], axis=1))
+    gain_ref[...] = jnp.concatenate(rows + [jnp.zeros((6, 256), F32)], axis=0)
 
 
 def on_device(tokens, gain, pre_act, w_in, act_cotangent):
@@ -173,61 +176,57 @@
     x_all = jnp.swapaxes(x.reshape(4, 2, SHARD, rows), 0, 1).reshape(2, 1, share // 2, rows)
     x_all = jnp.broadcast_to(x_all, (2, 8, share // 2, rows)).reshape(16, share // 2, rows)
     x_all = lax.all_to_all(x_all, CHIPS, 0, 0)
-    parts = products([(0, w0), (1, first1), (7, second1)], d_own, d_other, place, None)
+    parts = products([(0, w0)], d_own, d_other, place, None)
 
     first, second, parts = tie(first2, second2, parts)
     first3, second3 = step(first, 1), step(second, -1)
-    parts = products([(2, first2), (6, second2)], d_own, d_other, place, parts)
+    groups = [(1, first1), (7, second1), (2, first2), (6, second2)]
+    parts = products(groups, d_own, d_other, place, parts)
 
     first, second, parts = tie(first3, second3, parts)
     first4 = step(first, 1)
     parts = products([(3, first3), (5, second)], d_own, d_other, place, parts)
 
-    first4, parts = together((first4, parts))
-    parts = products([(4, first4)], d_own, d_other, place, parts)
-    received = lax.all_to_all(parts.reshape(16, share // 2, rows), CHIPS, 0, 0)
-
     one = pl.pallas_call(
         stats_kernel,
         out_shape=jax.ShapeDtypeStruct((2, 8, rows), F32),
         compiler_params=PARAMS,
     )(x_all)
     two = partner(one, "c", 2, 1)
+
+    first4, parts, one, two = together((first4, parts, one, two))
+    parts = products([(4, first4)], d_own, d_other, place, parts)
+    received = lax.all_to_all(parts.reshape(16, share // 2, rows), CHIPS, 0, 0)
+
     shares = gain_share(parts, x_all, one, two)
-    for axis, n, bit in (("y", 8, 1), ("y", 8, 2), ("y", 8, 4), ("zh", 4, 1), ("zh", 4, 2)):
-        shares += partner(shares, axis, n, bit)
-
-    gain_column = gain.astype(F32)[:, None]
-    vmem = pl.BlockSpec(memory_space=pltpu.VMEM)
-    smem = pl.BlockSpec(memory_space=pltpu.SMEM)
+    for bit in (1, 2, 4):
+        shares += partner(shares, "y", 8, bit)
+
+    vmem, smem = pl.BlockSpec(memory_space=pltpu.VMEM), pl.BlockSpec(memory_space=pltpu.SMEM)
     d_scaled, moments = pl.pallas_call(
         sum_kernel,
         in_specs=[smem] + [vmem] * 5,
         out_shape=[
             jax.ShapeDtypeStruct((share, rows), F32),
-            jax.ShapeDtypeStruct((8, rows), F32),
+            jax.ShapeDtypeStruct((8, 128), F32),
         ],
         compiler_params=PARAMS,
-    )(here[1], received, x, gain_column, one, two)
+    )(here[1], received, x, gain.astype(F32)[:, None], one, two)
 
     small = jnp.concatenate(
-        [
-            jnp.broadcast_to(moments[None, :2], (8, 2, rows)),
-            jnp.pad(shares, ((0, 0), (0, rows - 256)))[:, None],
-            jnp.zeros((8, 5, rows), F32),
-        ],
-        axis=1,
+        [jnp.broadcast_to(moments[None, :6], (8, 6, 128)), shares.reshape(8, 2, 128)], axis=1
     )
-    small = lax.all_to_all(jnp.concatenate([small, small], axis=0), CHIPS, 0, 0)
+    small = jnp.broadcast_to(small, (8, 8, 8, 128)).reshape(64, 8, 128)
+    small = lax.all_to_all(small, ("zh",) + CHIPS, 0, 0)
     token_gradient, gain_rows = pl.pallas_call(
         final_kernel,
         in_specs=[smem] + [vmem] * 5,
         out_shape=[
             jax.ShapeDtypeStruct((rows, share), BF16),
-            jax.ShapeDtypeStruct((8, rows), F32),
+            jax.ShapeDtypeStruct((8, 256), F32),
         ],
         compiler_params=PARAMS,
-    )(here[1], d_scaled, x, one, two, small)
+    )(jnp.concatenate([here[1], lax.axis_index("zh").astype(jnp.int32).reshape(1)]), d_scaled, x, one, two, small)
     gain_gradient = jnp.swapaxes(gain_rows[:2, : share // 2].reshape(2, 4, SHARD), 0, 1).reshape(share)
     return (token_gradient, gain_gradient)
 

time: 175 us -> 167 us (0.954)
  blocking collectives: 39.5 us -> 22.4 us
  waiting for transfers between devices: 35.8 us -> 40.5 us
  local copies, waits for them, and re-layouts: 7.74 us -> 10.1 us
  Pallas kernels: 24.2 us -> 26.1 us
    all_to_all x1 -> x0, blocking collectives: 17.1 us -> none  [on_device(): small = lax.all_to_all(jnp.concatenate([small, small], axis=0), CHIPS, 0, 0)]
    all_to_all x0 -> x1, waiting for transfers between devices: none -> 12.1 us  [on_device(): small = lax.all_to_all(small, ('zh',) + CHIPS, 0, 0)]
    ppermute x7, waiting for transfers between devices: 21.8 us -> 12 us  [step(): lax.ppermute(array, ('y', 'c'), [(a * 2 + c, b * 2 + c) for a, b, c in mo...]
    ppermute x7 -> x5, starting transfers between devices: 24.3 us -> 15.7 us  [partner(): return lax.ppermute(array, axis, [(i, i ^ bit) for i in range(n)])]
    all_to_all x0 -> x1, starting transfers between devices: none -> 8.44 us  [on_device(): small = lax.all_to_all(small, ('zh',) + CHIPS, 0, 0)]
    ppermute x7 -> x5, waiting for transfers between devices: 14 us -> 7.44 us  [partner(): return lax.ppermute(array, axis, [(i, i ^ bit) for i in range(n)])]
    all_to_all x1, waiting for transfers between devices: 0.01 us -> 4.82 us  [on_device(): received = lax.all_to_all(parts.reshape(16, share // 2, rows), CHIPS, 0, 0)]
    all_to_all x1, waiting for transfers between devices: 0.01 us -> 4.12 us  [on_device(): x_all = lax.all_to_all(x_all, CHIPS, 0, 0)]
  transfers between devices with their start and end apart: 16 -> 15, of which waited for: 10 -> 9; matrix products, arithmetic and copies ran while one was open for 5% -> 6% of each run, Pallas kernels for 13% -> 12%
where the time goes in v8:
time: 167 us; the launch traced here: 165 us
  starting transfers between devices  58.1 us (35%)
  waiting for transfers between devices  40.5 us (24%)
  Pallas kernels  26.1 us (16%)
  blocking collectives  22.4 us (13%)
  local copies, waits for them, and re-layouts  10.1 us (6%)
  other arithmetic  6.98 us (4%)
    ppermute x7, starting transfers between devices, step(): lax.ppermute(array, ('y', 'c'), [(a * 2 + c, b * 2 + c) for a, b, c in mo...  23 us
    all_gather x1, blocking collectives, on_device(): w0 = lax.all_gather(w_in, 'zh', axis=0, tiled=True)  22.4 us
    ppermute x5, starting transfers between devices, partner(): return lax.ppermute(array, axis, [(i, i ^ bit) for i in range(n)])  15.7 us
    pallas_call x4, Pallas kernels, products(): pl.pallas_call(kernel, in_specs=[pl.BlockSpec(memory_space=pltpu.SMEM)] +...  14.5 us
    all_to_all x1, waiting for transfers between devices, on_device(): small = lax.all_to_all(small, ('zh',) + CHIPS, 0, 0)  12.1 us
    ppermute x7, waiting for transfers between devices, step(): lax.ppermute(array, ('y', 'c'), [(a * 2 + c, b * 2 + c) for a, b, c in mo...  12 us
    all_to_all x1, starting transfers between devices, on_device(): small = lax.all_to_all(small, ('zh',) + CHIPS, 0, 0)  8.44 us
    ppermute x5, waiting for transfers between devices, partner(): return lax.ppermute(array, axis, [(i, i ^ bit) for i in range(n)])  7.44 us
  transfers between devices with their start and end apart: 15, of which 9 were waited for; matrix products, arithmetic and copies ran while one was open for 6% of the time, Pallas kernels for 12%

profile of v8, /device:TPU:1, one launch (start us, length us, event | category | flops | bytes accessed | tf_op | source)
XLA Modules:
  0.0 165.2 jit_solution(16269059976242901964)
XLA Ops:
  0.6 22.4 %all_gather.3.refs_0_ = bf16[192,1536]{1,0:T(8,128)(2,1)S(1)} all-gather(bf16[48,1536]{1,0:T(8,128)(2,1)} %param.8), channel_id=1, replica_groups=mesh['y'=8,'zh'=4,'c'=2,'zl'=2,'x'=4] {'zh'}, dimensions={0}, use_global_device_ids=true | all-gather | bytes 737280 | tf_op jit(solution)/shard_map/all_gather | solution.py:166
  23.0 3.2 %collective-permute-start = (bf16[192,1536]{1,0:T(8,128)(2,1)S(1)}, bf16[192,1536]{1,0:T(8,128)(2,1)}, u32[]{:S(2)}, u32[]{:S(2)}) collective-permute-start(bf16[192,1536]{1,0:T(8,128)(2,1)S(1)} %all_gather.3.refs_0_), channel_id=1, source_target_pairs={{64,0},{128,64},{192,128},{256,192},{320,256},{384,320},{448,384},... | collective-permute-start | bytes 1769480 | tf_op jit(solution)/shard_map/ppermute | solution.py:160
  26.2 3.8 %collective-permute-start.1 = (bf16[192,1536]{1,0:T(8,128)(2,1)S(1)}, bf16[192,1536]{1,0:T(8,128)(2,1)}, u32[]{:S(2)}, u32[]{:S(2)}) collective-permute-start(bf16[192,1536]{1,0:T(8,128)(2,1)S(1)} %all_gather.3.refs_0_), channel_id=1, source_target_pairs={{448,0},{0,64},{64,128},{128,192},{192,256},{256,320},{320,384},{3... | collective-permute-start | bytes 1769480 | tf_op jit(solution)/shard_map/ppermute | solution.py:160
  30.0 6.8 %fusion.34.own_ref = bf16[384,1536]{1,0:T(8,128)(2,1)S(1)} fusion(bf16[384,1536]{1,0:T(8,128)(2,1)} %param.9, bf16[384,1536]{1,0:T(8,128)(2,1)} %param.7), kind=kLoop, calls=%fused_computation.39 | loop fusion | flops 43646976 | bytes 3538944 | tf_op jit(solution)/shard_map/convert_element_type | solution.py:170
  36.9 6.0 %collective-permute-done.1.refs_1_ = bf16[192,1536]{1,0:T(8,128)(2,1)} collective-permute-done((bf16[192,1536]{1,0:T(8,128)(2,1)S(1)}, bf16[192,1536]{1,0:T(8,128)(2,1)}, u32[]{:S(2)}, u32[]{:S(2)}) %collective-permute-start.1) | collective-permute-done | bytes 589856 | tf_op jit(solution)/shard_map/ppermute | solution.py:160
  42.9 2.6 %collective-permute-start.2 = (bf16[384,1536]{1,0:T(8,128)(2,1)S(1)}, bf16[384,1536]{1,0:T(8,128)(2,1)S(1)}, u32[]{:S(2)}, u32[]{:S(2)}) collective-permute-start(bf16[384,1536]{1,0:T(8,128)(2,1)S(1)} %fusion.34.own_ref), channel_id=1, source_target_pairs={{0,8},{8,0},{1,9},{9,1},{2,10},{10,2},{3,11},{11,3},{4,12},{12,4},... | collective-permute-start | bytes 3538952 | tf_op jit(solution)/shard_map/ppermute | solution.py:23
  45.5 0.1 pad_add_fusion.1.place_ref
  45.6 2.0 %collective-permute-start.3 = (bf16[192,1536]{1,0:T(8,128)(2,1)}, bf16[192,1536]{1,0:T(8,128)(2,1)}, u32[]{:S(2)}, u32[]{:S(2)}) collective-permute-start(bf16[192,1536]{1,0:T(8,128)(2,1)} %collective-permute-done.refs_0_), channel_id=1, source_target_pairs={{64,0},{128,64},{192,128},{256,192},{320,256},{384,320},{448,384},... | collective-permute-start | bytes 1769480 | tf_op jit(solution)/shard_map/ppermute | solution.py:160
  47.5 5.4 %collective-permute-start.5 = (bf16[192,1536]{1,0:T(8,128)(2,1)}, bf16[192,1536]{1,0:T(8,128)(2,1)}, u32[]{:S(2)}, u32[]{:S(2)}) collective-permute-start(bf16[192,1536]{1,0:T(8,128)(2,1)} %collective-permute-done.1.refs_1_), channel_id=1, source_target_pairs={{448,0},{0,64},{64,128},{128,192},{192,256},{256,320},{320,384},{3... | collective-permute-start | bytes 1769480 | tf_op jit(solution)/shard_map/ppermute | solution.py:160
  52.9 0.2 copy.12
  53.1 0.0 copy-start.2
  53.2 1.8 %broadcast_in_dim.22 = bf16[2,8,192,384]{3,2,1,0:T(8,128)(2,1)} broadcast(bf16[2,192,384]{2,1,0:T(8,128)(2,1)S(1)} %bitcast.25), dimensions={0,2,3} | broadcast | bytes 2654208 | tf_op jit(solution)/shard_map/broadcast_in_dim | solution.py:177
  55.0 6.0 %all-to-all-start = ((bf16[16,192,384]{2,1,0:T(8,128)(2,1)}), bf16[16,192,384]{2,1,0:T(8,128)(2,1)}, u32[]{:S(2)}, u32[]{:S(2)}) async-start(bf16[16,192,384]{2,1,0:T(8,128)(2,1)} %bitcast.24), calls=%async_computation | async-start | bytes 4718592 | tf_op jit(solution)/shard_map/all_to_all | solution.py:178
  61.0 1.0 copy-done.6
  62.0 1.1 copy-done.5
  63.1 1.3 copy-done.7
  64.4 2.1 %shard_map.68.refs_4_ = bf16[2,8,192,384]{3,2,1,0:T(8,128)(2,1)S(1)} custom-call(s32[2]{0:T(128)S(1)} %pad_add_fusion.1.place_ref, bf16[384,1536]{1,0:T(8,128)(2,1)S(1)} %fusion.34.own_ref, bf16[384,1536]{1,0:T(8,128)(2,1)S(1)} %copy-done.7, bf16[192,1536]{1,0:T(8,128)(2,1)S(1)} %copy-done.5), custom_call_target="tpu_custom_call" | custom-call | flops 274877906944 | bytes 67108864 | tf_op jit(solution)/shard_map/pallas_call | solution.py:50
  66.5 1.9 %collective-permute-start.4 = (bf16[192,1536]{1,0:T(8,128)(2,1)}, bf16[192,1536]{1,0:T(8,128)(2,1)}, u32[]{:S(2)}, u32[]{:S(2)}) collective-permute-start(bf16[192,1536]{1,0:T(8,128)(2,1)} %collective-permute-done.3.refs_2_), channel_id=1, source_target_pairs={{64,0},{128,64},{192,128},{256,192},{320,256},{384,320},{448,384},... | collective-permute-start | bytes 1769480 | tf_op jit(solution)/shard_map/ppermute | solution.py:160
  68.4 4.9 %collective-permute-start.7 = (bf16[192,1536]{1,0:T(8,128)(2,1)}, bf16[192,1536]{1,0:T(8,128)(2,1)}, u32[]{:S(2)}, u32[]{:S(2)}) collective-permute-start(bf16[192,1536]{1,0:T(8,128)(2,1)} %collective-permute-done.5.refs_3_), channel_id=1, source_target_pairs={{448,0},{0,64},{64,128},{128,192},{192,256},{256,320},{320,384},{3... | collective-permute-start | bytes 1769480 | tf_op jit(solution)/shard_map/ppermute | solution.py:160
  73.3 6.1 %shard_map.69.refs_2_ = bf16[2,8,192,384]{3,2,1,0:T(8,128)(2,1)S(1)} custom-call(s32[2]{0:T(128)S(1)} %pad_add_fusion.1.place_ref, bf16[384,1536]{1,0:T(8,128)(2,1)S(1)} %fusion.34.own_ref, bf16[384,1536]{1,0:T(8,128)(2,1)S(1)} %copy-done.7, bf16[192,1536]{1,0:T(8,128)(2,1)} %collective-permute-done.refs_0_, ...), custom_call_target="tpu_custom_call", output_to_operand_aliasing={{}: (7, {})} | custom-call | flops 274877906944 | bytes 67108864 | tf_op jit(solution)/shard_map/pallas_call | solution.py:50
  79.4 0.6 collective-permute-done.4.refs_0_
  80.0 5.4 %collective-permute-done.7.refs_1_ = bf16[192,1536]{1,0:T(8,128)(2,1)} collective-permute-done((bf16[192,1536]{1,0:T(8,128)(2,1)}, bf16[192,1536]{1,0:T(8,128)(2,1)}, u32[]{:S(2)}, u32[]{:S(2)}) %collective-permute-start.7) | collective-permute-done | bytes 589856 | tf_op jit(solution)/shard_map/ppermute | solution.py:160
  85.4 1.9 %collective-permute-start.6 = (bf16[192,1536]{1,0:T(8,128)(2,1)}, bf16[192,1536]{1,0:T(8,128)(2,1)}, u32[]{:S(2)}, u32[]{:S(2)}) collective-permute-start(bf16[192,1536]{1,0:T(8,128)(2,1)} %collective-permute-done.4.refs_0_), channel_id=1, source_target_pairs={{64,0},{128,64},{192,128},{256,192},{320,256},{384,320},{448,384},... | collective-permute-start | bytes 1769480 | tf_op jit(solution)/shard_map/ppermute | solution.py:160
  87.3 4.1 %all-to-all-done.x_ref = bf16[16,192,384]{2,1,0:T(8,128)(2,1)} async-done(((bf16[16,192,384]{2,1,0:T(8,128)(2,1)}), bf16[16,192,384]{2,1,0:T(8,128)(2,1)}, u32[]{:S(2)}, u32[]{:S(2)}) %all-to-all-start) | async-done | bytes 2359328 | tf_op jit(solution)/shard_map/all_to_all | solution.py:178
  91.4 3.4 %shard_map.71.one_ref = f32[2,8,384]{2,1,0:T(8,128)} custom-call(bf16[16,192,384]{2,1,0:T(8,128)(2,1)} %all-to-all-done.x_ref), custom_call_target="tpu_custom_call" | custom-call | tf_op jit(solution)/shard_map/pallas_call | solution.py:190
  94.9 2.1 %collective-permute-start.8 = (f32[2,8,384]{2,1,0:T(8,128)}, f32[2,8,384]{2,1,0:T(8,128)}, u32[]{:S(2)}, u32[]{:S(2)}) collective-permute-start(f32[2,8,384]{2,1,0:T(8,128)} %shard_map.71.one_ref), channel_id=1, source_target_pairs={{0,8},{8,0},{1,9},{9,1},{2,10},{10,2},{3,11},{11,3},{4,12},{12,4},... | collective-permute-start | bytes 73736 | tf_op jit(solution)/shard_map/ppermute | solution.py:23
  97.0 3.7 %shard_map.70.refs_1_ = bf16[2,8,192,384]{3,2,1,0:T(8,128)(2,1)S(1)} custom-call(s32[2]{0:T(128)S(1)} %pad_add_fusion.1.place_ref, bf16[384,1536]{1,0:T(8,128)(2,1)S(1)} %fusion.34.own_ref, bf16[384,1536]{1,0:T(8,128)(2,1)S(1)} %copy-done.8, bf16[192,1536]{1,0:T(8,128)(2,1)} %collective-permute-done.4.refs_0_, ...), custom_call_target="tpu_custom_call", output_to_operand_aliasing={{}: (5, {})} | custom-call | flops 274877906944 | bytes 67108864 | tf_op jit(solution)/shard_map/pallas_call | solution.py:50
  100.7 2.6 %shard_map.72.parts_ref = bf16[2,8,192,384]{3,2,1,0:T(8,128)(2,1)S(1)} custom-call(s32[2]{0:T(128)S(1)} %pad_add_fusion.1.place_ref, bf16[384,1536]{1,0:T(8,128)(2,1)S(1)} %fusion.34.own_ref, bf16[384,1536]{1,0:T(8,128)(2,1)S(1)} %copy-done.8, bf16[192,1536]{1,0:T(8,128)(2,1)} %collective-permute-done.6.refs_0_, ...), custom_call_target="tpu_custom_call", output_to_operand_aliasing={{}: (4, {})} | custom-call | flops 274877906944 | bytes 67108864 | tf_op jit(solution)/shard_map/pallas_call | solution.py:50
  103.3 1.4 copy-done
  104.8 5.0 %all-to-all-start.1 = ((bf16[16,192,384]{2,1,0:T(8,128)(2,1)}), bf16[16,192,384]{2,1,0:T(8,128)(2,1)S(1)}, u32[]{:S(2)}, u32[]{:S(2)}) async-start(bf16[16,192,384]{2,1,0:T(8,128)(2,1)} %bitcast.19), calls=%async_computation.1 | async-start | bytes 4718592 | tf_op jit(solution)/shard_map/all_to_all | solution.py:199
  109.8 1.7 %copy-done.1 = bf16[2,8,192,384]{3,2,1,0:T(8,128)(2,1)S(1)} copy-done((bf16[2,8,192,384]{3,2,1,0:T(8,128)(2,1)S(1)}, bf16[2,8,192,384]{3,2,1,0:T(8,128)(2,1)}, u32[]{:S(2)}) %copy-start.1) | copy-done | bytes 2359320
  111.5 5.2 %shard_map.74 = f32[8,256]{1,0:T(8,128)S(1)} custom-call(bf16[2,8,192,384]{3,2,1,0:T(8,128)(2,1)S(1)} %copy-done.1, bf16[2,8,192,384]{3,2,1,0:T(8,128)(2,1)} %bitcast.9.x_ref, f32[2,8,384]{2,1,0:T(8,128)} %shard_map.71.one_ref, f32[2,8,384]{2,1,0:T(8,128)} %collective-permute-done.8.two_ref), custom_call_target="tpu_custom_call" | custom-call | tf_op jit(solution)/shard_map/pallas_call | solution.py:104
  116.7 1.9 %collective-permute-start.9 = (f32[8,256]{1,0:T(8,128)S(1)}, f32[8,256]{1,0:T(8,128)S(1)}, u32[]{:S(2)}, u32[]{:S(2)}) collective-permute-start(f32[8,256]{1,0:T(8,128)S(1)} %shard_map.74), channel_id=1, source_target_pairs={{0,64},{64,0},{128,192},{192,128},{256,320},{320,256},{384,448},{4... | collective-permute-start | bytes 24584 | tf_op jit(solution)/shard_map/ppermute | solution.py:23
  118.7 2.8 %collective-permute-done.9 = f32[8,256]{1,0:T(8,128)S(1)} collective-permute-done((f32[8,256]{1,0:T(8,128)S(1)}, f32[8,256]{1,0:T(8,128)S(1)}, u32[]{:S(2)}, u32[]{:S(2)}) %collective-permute-start.9) | collective-permute-done | bytes 8224 | tf_op jit(solution)/shard_map/ppermute | solution.py:23
  121.4 3.8 %collective-permute-start.10 = (f32[8,256]{1,0:T(8,128)S(1)}, f32[8,256]{1,0:T(8,128)S(1)}, u32[]{:S(2)}, u32[]{:S(2)}) collective-permute-start(f32[8,256]{1,0:T(8,128)S(1)} %add.9), channel_id=1, source_target_pairs={{0,128},{64,192},{128,0},{192,64},{256,384},{320,448},{384,256},{4... | collective-permute-start | bytes 24584 | tf_op jit(solution)/shard_map/ppermute | solution.py:23
  125.2 1.8 %collective-permute-done.10 = f32[8,256]{1,0:T(8,128)S(1)} collective-permute-done((f32[8,256]{1,0:T(8,128)S(1)}, f32[8,256]{1,0:T(8,128)S(1)}, u32[]{:S(2)}, u32[]{:S(2)}) %collective-permute-start.10) | collective-permute-done | bytes 8224 | tf_op jit(solution)/shard_map/ppermute | solution.py:23
  127.0 5.3 %collective-permute-start.11 = (f32[8,256]{1,0:T(8,128)S(1)}, f32[8,256]{1,0:T(8,128)S(1)}, u32[]{:S(2)}, u32[]{:S(2)}) collective-permute-start(f32[8,256]{1,0:T(8,128)S(1)} %add.10), channel_id=1, source_target_pairs={{0,256},{64,320},{128,384},{192,448},{256,0},{320,64},{384,128},{4... | collective-permute-start | bytes 24584 | tf_op jit(solution)/shard_map/ppermute | solution.py:23
  132.3 0.1 reshape.52.gain_ref
  132.4 2.9 %collective-permute-done.11 = f32[8,256]{1,0:T(8,128)S(1)} collective-permute-done((f32[8,256]{1,0:T(8,128)S(1)}, f32[8,256]{1,0:T(8,128)S(1)}, u32[]{:S(2)}, u32[]{:S(2)}) %collective-permute-start.11) | collective-permute-done | bytes 8224 | tf_op jit(solution)/shard_map/ppermute | solution.py:23
  135.3 4.8 %all-to-all-done.1.parts_ref = bf16[16,192,384]{2,1,0:T(8,128)(2,1)S(1)} async-done(((bf16[16,192,384]{2,1,0:T(8,128)(2,1)}), bf16[16,192,384]{2,1,0:T(8,128)(2,1)S(1)}, u32[]{:S(2)}, u32[]{:S(2)}) %all-to-all-start.1) | async-done | bytes 2359328 | tf_op jit(solution)/shard_map/all_to_all | solution.py:199
  140.1 1.2 shard_map.73
  141.4 0.7 broadcast_in_dim.26
  142.1 8.4 %all-to-all-start.2 = ((f32[64,8,128]{2,1,0:T(8,128)}), f32[64,8,128]{2,1,0:T(8,128)S(1)}, u32[]{:S(2)}, u32[]{:S(2)}) async-start(f32[64,8,128]{2,1,0:T(8,128)} %bitcast.11), calls=%async_computation.2 | async-start | bytes 524288 | tf_op jit(solution)/shard_map/all_to_all | solution.py:220
  150.6 0.1 pad_add_fusion.here_ref
  150.7 12.1 %all-to-all-done.2.small_ref = f32[64,8,128]{2,1,0:T(8,128)S(1)} async-done(((f32[64,8,128]{2,1,0:T(8,128)}), f32[64,8,128]{2,1,0:T(8,128)S(1)}, u32[]{:S(2)}, u32[]{:S(2)}) %all-to-all-start.2) | async-done | bytes 262176 | tf_op jit(solution)/shard_map/all_to_all | solution.py:220
  162.7 1.7 %shard_map.75 = (bf16[384,384]{1,0:T(8,128)(2,1)}, f32[8,256]{1,0:T(8,128)S(1)}) custom-call(s32[2]{0:T(128)S(1)} %pad_add_fusion.here_ref, f32[384,384]{1,0:T(8,128)S(1)} %get-tuple-element.40.d_ref, bf16[384,384]{1,0:T(8,128)(2,1)S(1)} %bitcast.22, f32[2,8,384]{2,1,0:T(8,128)} %shard_map.71.one_ref, f32[2,8,384]{2,1,0:T(8,128)} %collective-permute-done.8.two_ref, ...), custom_call_target="tpu_custom_call" | custom-call | tf_op jit(solution)/shard_map/pallas_call | solution.py:221
  164.5 0.1 reshape.49
  164.5 0.7 reshape.50
  (31 shorter events, 0.1 us)
Async XLA Ops:
  0.6 52.3 %copy-start.9 = (bf16[384,384]{1,0:T(8,128)(2,1)S(1)}, bf16[384,384]{1,0:T(8,128)(2,1)}, u32[]{:S(2)}) copy-start(bf16[384,384]{1,0:T(8,128)(2,1)} %param.5) | copy-start | bytes 884740
  23.0 13.9 %copy-start.4 = (bf16[192,1536]{1,0:T(8,128)(2,1)}, bf16[192,1536]{1,0:T(8,128)(2,1)S(1)}, u32[]{:S(2)}) copy-start(bf16[192,1536]{1,0:T(8,128)(2,1)S(1)} %all_gather.3.refs_0_) | copy-start | bytes 1769476
  23.0 13.8 %collective-permute-start = (bf16[192,1536]{1,0:T(8,128)(2,1)S(1)}, bf16[192,1536]{1,0:T(8,128)(2,1)}, u32[]{:S(2)}, u32[]{:S(2)}) collective-permute-start(bf16[192,1536]{1,0:T(8,128)(2,1)S(1)} %all_gather.3.refs_0_), channel_id=1, source_target_pairs={{64,0},{128,64},{192,128},{256,192},{320,256},{384,320},{448,384},... | collective-permute-start | bytes 1769480 | tf_op jit(solution)/shard_map/ppermute | solution.py:160
  26.2 16.7 %collective-permute-start.1 = (bf16[192,1536]{1,0:T(8,128)(2,1)S(1)}, bf16[192,1536]{1,0:T(8,128)(2,1)}, u32[]{:S(2)}, u32[]{:S(2)}) collective-permute-start(bf16[192,1536]{1,0:T(8,128)(2,1)S(1)} %all_gather.3.refs_0_), channel_id=1, source_target_pairs={{448,0},{0,64},{64,128},{128,192},{192,256},{256,320},{320,384},{3... | collective-permute-start | bytes 1769480 | tf_op jit(solution)/shard_map/ppermute | solution.py:160
  42.9 18.1 %collective-permute-start.2 = (bf16[384,1536]{1,0:T(8,128)(2,1)S(1)}, bf16[384,1536]{1,0:T(8,128)(2,1)S(1)}, u32[]{:S(2)}, u32[]{:S(2)}) collective-permute-start(bf16[384,1536]{1,0:T(8,128)(2,1)S(1)} %fusion.34.own_ref), channel_id=1, source_target_pairs={{0,8},{8,0},{1,9},{9,1},{2,10},{10,2},{3,11},{11,3},{4,12},{12,4},... | collective-permute-start | bytes 3538952 | tf_op jit(solution)/shard_map/ppermute | solution.py:23
  45.6 20.9 %collective-permute-start.3 = (bf16[192,1536]{1,0:T(8,128)(2,1)}, bf16[192,1536]{1,0:T(8,128)(2,1)}, u32[]{:S(2)}, u32[]{:S(2)}) collective-permute-start(bf16[192,1536]{1,0:T(8,128)(2,1)} %collective-permute-done.refs_0_), channel_id=1, source_target_pairs={{64,0},{128,64},{192,128},{256,192},{320,256},{384,320},{448,384},... | collective-permute-start | bytes 1769480 | tf_op jit(solution)/shard_map/ppermute | solution.py:160
  47.5 18.9 %collective-permute-start.5 = (bf16[192,1536]{1,0:T(8,128)(2,1)}, bf16[192,1536]{1,0:T(8,128)(2,1)}, u32[]{:S(2)}, u32[]{:S(2)}) collective-permute-start(bf16[192,1536]{1,0:T(8,128)(2,1)} %collective-permute-done.1.refs_1_), channel_id=1, source_target_pairs={{448,0},{0,64},{64,128},{128,192},{192,256},{256,320},{320,384},{3... | collective-permute-start | bytes 1769480 | tf_op jit(solution)/shard_map/ppermute | solution.py:160
  53.1 1.8 %copy-start.2 = (bf16[384,384]{0,1:T(8,128)(2,1)}, bf16[384,384]{0,1:T(8,128)(2,1)S(1)}, u32[]{:S(2)}) copy-start(bf16[384,384]{0,1:T(8,128)(2,1)S(1)} %copy.12) | copy-start | bytes 884740
  55.0 36.5 %all-to-all-start = ((bf16[16,192,384]{2,1,0:T(8,128)(2,1)}), bf16[16,192,384]{2,1,0:T(8,128)(2,1)}, u32[]{:S(2)}, u32[]{:S(2)}) async-start(bf16[16,192,384]{2,1,0:T(8,128)(2,1)} %bitcast.24), calls=%async_computation | async-start | bytes 4718592 | tf_op jit(solution)/shard_map/all_to_all | solution.py:178
  61.0 1.0 copy-start.6
  62.0 1.1 copy-start.5
  63.1 1.3 copy-start.7
  66.5 13.5 %collective-permute-start.4 = (bf16[192,1536]{1,0:T(8,128)(2,1)}, bf16[192,1536]{1,0:T(8,128)(2,1)}, u32[]{:S(2)}, u32[]{:S(2)}) collective-permute-start(bf16[192,1536]{1,0:T(8,128)(2,1)} %collective-permute-done.3.refs_2_), channel_id=1, source_target_pairs={{64,0},{128,64},{192,128},{256,192},{320,256},{384,320},{448,384},... | collective-permute-start | bytes 1769480 | tf_op jit(solution)/shard_map/ppermute | solution.py:160
  68.4 17.0 %collective-permute-start.7 = (bf16[192,1536]{1,0:T(8,128)(2,1)}, bf16[192,1536]{1,0:T(8,128)(2,1)}, u32[]{:S(2)}, u32[]{:S(2)}) collective-permute-start(bf16[192,1536]{1,0:T(8,128)(2,1)} %collective-permute-done.5.refs_3_), channel_id=1, source_target_pairs={{448,0},{0,64},{64,128},{128,192},{192,256},{256,320},{320,384},{3... | collective-permute-start | bytes 1769480 | tf_op jit(solution)/shard_map/ppermute | solution.py:160
  85.4 15.3 %collective-permute-start.6 = (bf16[192,1536]{1,0:T(8,128)(2,1)}, bf16[192,1536]{1,0:T(8,128)(2,1)}, u32[]{:S(2)}, u32[]{:S(2)}) collective-permute-start(bf16[192,1536]{1,0:T(8,128)(2,1)} %collective-permute-done.4.refs_0_), channel_id=1, source_target_pairs={{64,0},{128,64},{192,128},{256,192},{320,256},{384,320},{448,384},... | collective-permute-start | bytes 1769480 | tf_op jit(solution)/shard_map/ppermute | solution.py:160
  91.4 5.6 %copy-start.8 = (bf16[384,1536]{1,0:T(8,128)(2,1)S(1)}, bf16[384,1536]{1,0:T(8,128)(2,1)}, u32[]{:S(2)}) copy-start(bf16[384,1536]{1,0:T(8,128)(2,1)} %copy-done.6) | copy-start | bytes 3538948
  94.9 5.8 %collective-permute-start.8 = (f32[2,8,384]{2,1,0:T(8,128)}, f32[2,8,384]{2,1,0:T(8,128)}, u32[]{:S(2)}, u32[]{:S(2)}) collective-permute-start(f32[2,8,384]{2,1,0:T(8,128)} %shard_map.71.one_ref), channel_id=1, source_target_pairs={{0,8},{8,0},{1,9},{9,1},{2,10},{10,2},{3,11},{11,3},{4,12},{12,4},... | collective-permute-start | bytes 73736 | tf_op jit(solution)/shard_map/ppermute | solution.py:23
  103.3 1.5 copy-start
  104.8 35.4 %all-to-all-start.1 = ((bf16[16,192,384]{2,1,0:T(8,128)(2,1)}), bf16[16,192,384]{2,1,0:T(8,128)(2,1)S(1)}, u32[]{:S(2)}, u32[]{:S(2)}) async-start(bf16[16,192,384]{2,1,0:T(8,128)(2,1)} %bitcast.19), calls=%async_computation.1 | async-start | bytes 4718592 | tf_op jit(solution)/shard_map/all_to_all | solution.py:199
  109.8 1.7 %copy-start.1 = (bf16[2,8,192,384]{3,2,1,0:T(8,128)(2,1)S(1)}, bf16[2,8,192,384]{3,2,1,0:T(8,128)(2,1)}, u32[]{:S(2)}) copy-start(bf16[2,8,192,384]{3,2,1,0:T(8,128)(2,1)} %copy-done) | copy-start | bytes 7077892
  111.5 20.8 %copy-start.10 = (bf16[384]{0:T(512)(128)(2,1)S(1)}, bf16[384]{0:T(512)(128)(2,1)}, u32[]{:S(2)}) copy-start(bf16[384]{0:T(512)(128)(2,1)} %param.6) | copy-start | bytes 2308
  111.5 28.7 %copy-start.3 = (bf16[384,384]{0,1:T(8,128)(2,1)S(1)}, bf16[384,384]{0,1:T(8,128)(2,1)}, u32[]{:S(2)}) copy-start(bf16[384,384]{0,1:T(8,128)(2,1)} %copy-done.2) | copy-start | bytes 884740
  116.7 4.7 %collective-permute-start.9 = (f32[8,256]{1,0:T(8,128)S(1)}, f32[8,256]{1,0:T(8,128)S(1)}, u32[]{:S(2)}, u32[]{:S(2)}) collective-permute-start(f32[8,256]{1,0:T(8,128)S(1)} %shard_map.74), channel_id=1, source_target_pairs={{0,64},{64,0},{128,192},{192,128},{256,320},{320,256},{384,448},{4... | collective-permute-start | bytes 24584 | tf_op jit(solution)/shard_map/ppermute | solution.py:23
  121.4 5.6 %collective-permute-start.10 = (f32[8,256]{1,0:T(8,128)S(1)}, f32[8,256]{1,0:T(8,128)S(1)}, u32[]{:S(2)}, u32[]{:S(2)}) collective-permute-start(f32[8,256]{1,0:T(8,128)S(1)} %add.9), channel_id=1, source_target_pairs={{0,128},{64,192},{128,0},{192,64},{256,384},{320,448},{384,256},{4... | collective-permute-start | bytes 24584 | tf_op jit(solution)/shard_map/ppermute | solution.py:23
  127.0 8.3 %collective-permute-start.11 = (f32[8,256]{1,0:T(8,128)S(1)}, f32[8,256]{1,0:T(8,128)S(1)}, u32[]{:S(2)}, u32[]{:S(2)}) collective-permute-start(f32[8,256]{1,0:T(8,128)S(1)} %add.10), channel_id=1, source_target_pairs={{0,256},{64,320},{128,384},{192,448},{256,0},{320,64},{384,128},{4... | collective-permute-start | bytes 24584 | tf_op jit(solution)/shard_map/ppermute | solution.py:23
  142.1 20.6 %all-to-all-start.2 = ((f32[64,8,128]{2,1,0:T(8,128)}), f32[64,8,128]{2,1,0:T(8,128)S(1)}, u32[]{:S(2)}, u32[]{:S(2)}) async-start(f32[64,8,128]{2,1,0:T(8,128)} %bitcast.11), calls=%async_computation.2 | async-start | bytes 524288 | tf_op jit(solution)/shard_map/all_to_all | solution.py:220

commit v9 on v8

--- a/solution.py
+++ b/solution.py
@@ -12,6 +12,7 @@
 SHARD = 48
 HALF = 1536
 PARAMS = pltpu.CompilerParams(vmem_limit_bytes=20 * 1024 * 1024)
+WIDE = pltpu.CompilerParams(vmem_limit_bytes=52 * 1024 * 1024)
 together = lax.optimization_barrier
 
 
@@ -59,11 +60,42 @@
             pltpu.SemaphoreType.DMA((2, n)),
         ],
         input_output_aliases={} if parts is None else {3 + n: 0},
-        compiler_params=PARAMS,
+        compiler_params=WIDE,
         cost_estimate=pl.CostEstimate(
             flops=1 << 38, bytes_accessed=64 << 20, transcendentals=0
         ),
     )(place, d_own, d_other, *weights, *([] if parts is None else [parts]))
+
+
+def tokens_kernel(tokens_ref, x_ref, send_ref, held, sem):
+    x = tokens_ref[...].astype(F32).T.astype(BF16)
+    x_ref[...] = x
+    copies = []
+    for c in range(2):
+        for z in range(4):
+            held[c, pl.ds(z * SHARD, SHARD)] = x[(z * 2 + c) * SHARD : (z * 2 + c + 1) * SHARD]
+        for m in range(8):
+            copies.append(pltpu.make_async_copy(held.at[c], send_ref.at[c, m], sem.at[c, m]))
+            copies[-1].start()
+    for copy in copies:
+        copy.wait()
+
+
+def transposed(tokens):
+    rows, share = tokens.shape
+    return pl.pallas_call(
+        tokens_kernel,
+        out_specs=[pl.BlockSpec(memory_space=pltpu.VMEM), pl.BlockSpec(memory_space=pl.ANY)],
+        out_shape=[
+            jax.ShapeDtypeStruct((share, rows), BF16),
+            jax.ShapeDtypeStruct((2, 8, share // 2, rows), BF16),
+        ],
+        scratch_shapes=[
+            pltpu.VMEM((2, share // 2, rows), BF16),
+            pltpu.SemaphoreType.DMA((2, 8)),
+        ],
+        compiler_params=PARAMS,
+    )(tokens)
 
 
 def stats_kernel(x_ref, out_ref):
@@ -86,11 +118,16 @@
     return mean, 1.0 / jnp.sqrt(variance + 1e-06)
 
 
-def gain_kernel(parts_ref, x_ref, one_ref, two_ref, out_ref):
+def gain_kernel(parts_ref, x_ref, one_ref, two_ref, out_ref, stat_ref):
+    @pl.when(pl.program_id(0) == 0)
+    def _():
+        for t in range(2):
+            mean, rstd = mean_and_rstd(one_ref[t], two_ref[t])
+            stat_ref[t] = jnp.concatenate([mean, rstd] * 4, axis=0)
+
     total = 0.0
     for t in range(2):
-        mean, rstd = mean_and_rstd(one_ref[t], two_ref[t])
-        xhat = (x_ref[t, 0].astype(F32) - mean) * rstd
+        xhat = (x_ref[t, 0].astype(F32) - stat_ref[t, 0:1]) * stat_ref[t, 1:2]
         value = parts_ref[t, 0].astype(F32) * xhat
         total += value[:, :128] + value[:, 128:256] + value[:, 256:]
     total = jnp.concatenate([total, jnp.zeros((64, 128), F32)], axis=0)
@@ -106,8 +143,9 @@
         grid=(8,),
         in_specs=[block, block, stat, stat],
         out_specs=pl.BlockSpec((8, 256), lambda m: (0, 0)),
+        scratch_shapes=[pltpu.VMEM((2, 8, tokens), F32)],
         out_shape=jax.ShapeDtypeStruct((8, 256), F32),
-        compiler_params=PARAMS,
+        compiler_params=WIDE,
     )(parts, x_all.reshape(parts.shape), one, two)
 
 
@@ -163,19 +201,18 @@
         (first_next, _), (second_next, _) = together((first, done)), together((second, done))
         return first_next, second_next, *together((first, second, done, *later))[2:]
 
-    w0 = lax.all_gather(w_in, "zh", axis=0, tiled=True)
-    w0, pre_act, act_cotangent = together((w0, pre_act, act_cotangent))
+    w0 = lax.all_to_all(jnp.broadcast_to(w_in, (4,) + w_in.shape), "zh", 0, 0).reshape(-1, w_in.shape[1])
+    w0, pre_act, act_cotangent, tokens = together((w0, pre_act, act_cotangent, tokens))
     first1, second1 = step(w0, 1), step(w0, -1)
     _, gelu_back = jax.vjp(gelu_exact, pre_act.astype(F32))
     d_own = gelu_back(act_cotangent.astype(F32))[0].astype(BF16)
 
-    first, second, d_own, tokens = tie(first1, second1, d_own, tokens)
+    x, x_all = transposed(tokens)
+
+    first, second, (d_own, x_all) = tie(first1, second1, (d_own, x_all))
     first2, second2 = step(first, 1), step(second, -1)
     d_other = partner(d_own, "c", 2, 1)
-    x = tokens.T
-    x_all = jnp.swapaxes(x.reshape(4, 2, SHARD, rows), 0, 1).reshape(2, 1, share // 2, rows)
-    x_all = jnp.broadcast_to(x_all, (2, 8, share // 2, rows)).reshape(16, share // 2, rows)
-    x_all = lax.all_to_all(x_all, CHIPS, 0, 0)
+    x_all = lax.all_to_all(x_all.reshape(16, share // 2, rows), CHIPS, 0, 0)
     parts = products([(0, w0)], d_own, d_other, place, None)
 
     first, second, parts = tie(first2, second2, parts)

time: 167 us -> 167 us (level)
  local copies, waits for them, and re-layouts: 10.1 us -> 3.78 us
  Pallas kernels: 26.1 us -> 29.3 us
  blocking collectives: 22.4 us -> 24.8 us
  starting transfers between devices: 58.1 us -> 60.3 us
    all_to_all x0 -> x1, blocking collectives: none -> 24.8 us  [on_device(): lax.all_to_all(jnp.broadcast_to(w_in, (4,) + w_in.shape), 'zh', 0, 0)]
    all_gather x1 -> x0, blocking collectives: 22.4 us -> none  [on_device(): w0 = lax.all_gather(w_in, 'zh', axis=0, tiled=True)]
    ppermute x5, starting transfers between devices: 15.7 us -> 21.5 us  [partner(): return lax.ppermute(array, axis, [(i, i ^ bit) for i in range(n)])]
    unnamed x22 -> x12, local copies, waits for them, and re-layouts: 6.54 us -> 1.13 us
    all_to_all x1, starting transfers between devices: 8.44 us -> 5.71 us  [on_device(): small = lax.all_to_all(small, ('zh',) + CHIPS, 0, 0)]
    pallas_call x0 -> x1, Pallas kernels: none -> 1.85 us  [transposed(): pl.pallas_call(tokens_kernel, out_specs=[pl.BlockSpec(memory_space=pltpu....]
    ppermute x7, waiting for transfers between devices: 12 us -> 10.3 us  [step(): lax.ppermute(array, ('y', 'c'), [(a * 2 + c, b * 2 + c) for a, b, c in mo...]
  transfers between devices with their start and end apart: 15 -> 15, of which waited for: 9 -> 10; matrix products, arithmetic and copies ran while one was open for 6% -> 4% of each run, Pallas kernels for 12% -> 14%
where the time goes in v9:
time: 167 us; the launch traced here: 166 us
  starting transfers between devices  60.3 us (36%)
  waiting for transfers between devices  40.2 us (24%)
  Pallas kernels  29.3 us (18%)
  blocking collectives  24.8 us (15%)
  other arithmetic  6.83 us (4%)
  local copies, waits for them, and re-layouts  3.78 us (2%)
    all_to_all x1, blocking collectives, on_device(): lax.all_to_all(jnp.broadcast_to(w_in, (4,) + w_in.shape), 'zh', 0, 0)  24.8 us
    ppermute x7, starting transfers between devices, step(): lax.ppermute(array, ('y', 'c'), [(a * 2 + c, b * 2 + c) for a, b, c in mo...  21.9 us
    ppermute x5, starting transfers between devices, partner(): return lax.ppermute(array, axis, [(i, i ^ bit) for i in range(n)])  21.5 us
    pallas_call x4, Pallas kernels, products(): pl.pallas_call(kernel, in_specs=[pl.BlockSpec(memory_space=pltpu.SMEM)] +...  15.7 us
    all_to_all x1, waiting for transfers between devices, on_device(): small = lax.all_to_all(small, ('zh',) + CHIPS, 0, 0)  12.1 us
    ppermute x7, waiting for transfers between devices, step(): lax.ppermute(array, ('y', 'c'), [(a * 2 + c, b * 2 + c) for a, b, c in mo...  10.3 us
    ppermute x5, waiting for transfers between devices, partner(): return lax.ppermute(array, axis, [(i, i ^ bit) for i in range(n)])  7.5 us
    convert_element_type x1, other arithmetic, on_device(): d_own = gelu_back(act_cotangent.astype(F32))[0].astype(BF16)  6.65 us
  transfers between devices with their start and end apart: 15, of which 10 were waited for; matrix products, arithmetic and copies ran while one was open for 4% of the time, Pallas kernels for 14%

profile of v9, /device:TPU:1, one launch (start us, length us, event | category | flops | bytes accessed | tf_op | source)
XLA Modules:
  0.0 166.1 jit_solution(18411797790672320728)
XLA Ops:
  0.6 1.0 broadcast_in_dim.17
  1.7 0.0 copy-start.2
  1.7 24.8 %all_to_all.20 = bf16[4,48,1536]{2,1,0:T(8,128)(2,1)S(1)} all-to-all(bf16[4,48,1536]{2,1,0:T(8,128)(2,1)S(1)} %broadcast_in_dim.17), channel_id=1, replica_groups=mesh['y'=8,'zh'=4,'c'=2,'zl'=2,'x'=4] {'zh'}, dimensions={0} | all-to-all | bytes 1179648 | tf_op jit(solution)/shard_map/all_to_all | solution.py:204
  26.5 3.2 %collective-permute-start = (bf16[192,1536]{1,0:T(8,128)(2,1)S(1)}, bf16[192,1536]{1,0:T(8,128)(2,1)}, u32[]{:S(2)}, u32[]{:S(2)}) collective-permute-start(bf16[192,1536]{1,0:T(8,128)(2,1)S(1)} %bitcast.14), channel_id=1, source_target_pairs={{64,0},{128,64},{192,128},{256,192},{320,256},{384,320},{448,384},... | collective-permute-start | bytes 1769480 | tf_op jit(solution)/shard_map/ppermute | solution.py:198
  29.7 3.8 %collective-permute-start.1 = (bf16[192,1536]{1,0:T(8,128)(2,1)S(1)}, bf16[192,1536]{1,0:T(8,128)(2,1)}, u32[]{:S(2)}, u32[]{:S(2)}) collective-permute-start(bf16[192,1536]{1,0:T(8,128)(2,1)S(1)} %bitcast.15), channel_id=1, source_target_pairs={{448,0},{0,64},{64,128},{128,192},{192,256},{256,320},{320,384},{3... | collective-permute-start | bytes 1769480 | tf_op jit(solution)/shard_map/ppermute | solution.py:198
  33.5 6.7 %fusion.34.own_ref = bf16[384,1536]{1,0:T(8,128)(2,1)S(1)} fusion(bf16[384,1536]{1,0:T(8,128)(2,1)S(1)} %copy-done.3, bf16[384,1536]{1,0:T(8,128)(2,1)} %param.7), kind=kLoop, calls=%fused_computation.39 | loop fusion | flops 43646976 | bytes 3538944 | tf_op jit(solution)/shard_map/convert_element_type | solution.py:208
  40.2 1.8 %shard_map.68 = (bf16[384,384]{1,0:T(8,128)(2,1)S(1)}, bf16[2,8,192,384]{3,2,1,0:T(8,128)(2,1)}) custom-call(bf16[384,384]{1,0:T(8,128)(2,1)S(1)} %copy-done.2), custom_call_target="tpu_custom_call" | custom-call | tf_op jit(solution)/shard_map/pallas_call | solution.py:86
  42.0 0.0 collective-permute-done.refs_0_
  42.1 2.0 %collective-permute-done.1.refs_1_ = bf16[192,1536]{1,0:T(8,128)(2,1)} collective-permute-done((bf16[192,1536]{1,0:T(8,128)(2,1)S(1)}, bf16[192,1536]{1,0:T(8,128)(2,1)}, u32[]{:S(2)}, u32[]{:S(2)}) %collective-permute-start.1) | collective-permute-done | bytes 589856 | tf_op jit(solution)/shard_map/ppermute | solution.py:198
  44.0 8.5 %collective-permute-start.2 = (bf16[384,1536]{1,0:T(8,128)(2,1)S(1)}, bf16[384,1536]{1,0:T(8,128)(2,1)S(1)}, u32[]{:S(2)}, u32[]{:S(2)}) collective-permute-start(bf16[384,1536]{1,0:T(8,128)(2,1)S(1)} %fusion.34.own_ref), channel_id=1, source_target_pairs={{0,8},{8,0},{1,9},{9,1},{2,10},{10,2},{3,11},{11,3},{4,12},{12,4},... | collective-permute-start | bytes 3538952 | tf_op jit(solution)/shard_map/ppermute | solution.py:24
  52.5 0.1 pad_add_fusion.1.place_ref
  52.6 1.9 %collective-permute-start.3 = (bf16[192,1536]{1,0:T(8,128)(2,1)}, bf16[192,1536]{1,0:T(8,128)(2,1)}, u32[]{:S(2)}, u32[]{:S(2)}) collective-permute-start(bf16[192,1536]{1,0:T(8,128)(2,1)} %collective-permute-done.refs_0_), channel_id=1, source_target_pairs={{64,0},{128,64},{192,128},{256,192},{320,256},{384,320},{448,384},... | collective-permute-start | bytes 1769480 | tf_op jit(solution)/shard_map/ppermute | solution.py:198
  54.5 4.6 %collective-permute-start.5 = (bf16[192,1536]{1,0:T(8,128)(2,1)}, bf16[192,1536]{1,0:T(8,128)(2,1)}, u32[]{:S(2)}, u32[]{:S(2)}) collective-permute-start(bf16[192,1536]{1,0:T(8,128)(2,1)} %collective-permute-done.1.refs_1_), channel_id=1, source_target_pairs={{448,0},{0,64},{64,128},{128,192},{192,256},{256,320},{320,384},{3... | collective-permute-start | bytes 1769480 | tf_op jit(solution)/shard_map/ppermute | solution.py:198
  59.1 6.2 %all-to-all-start.1 = ((bf16[16,192,384]{2,1,0:T(8,128)(2,1)}), bf16[16,192,384]{2,1,0:T(8,128)(2,1)}, u32[]{:S(2)}, u32[]{:S(2)}) async-start(bf16[16,192,384]{2,1,0:T(8,128)(2,1)} %bitcast.4), calls=%async_computation.1 | async-start | bytes 4718592 | tf_op jit(solution)/shard_map/all_to_all | solution.py:215
  65.3 0.0 collective-permute-done.2.other_ref
  65.3 1.1 copy-done.5
  66.4 2.9 %shard_map.69.refs_4_ = bf16[2,8,192,384]{3,2,1,0:T(8,128)(2,1)} custom-call(s32[2]{0:T(128)S(1)} %pad_add_fusion.1.place_ref, bf16[384,1536]{1,0:T(8,128)(2,1)S(1)} %fusion.34.own_ref, bf16[384,1536]{1,0:T(8,128)(2,1)} %copy-done.5, bf16[192,1536]{1,0:T(8,128)(2,1)S(1)} %bitcast.16), custom_call_target="tpu_custom_call" | custom-call | flops 274877906944 | bytes 67108864 | tf_op jit(solution)/shard_map/pallas_call | solution.py:51
  69.3 0.0 collective-permute-done.3.refs_2_
  69.3 1.3 collective-permute-done.5.refs_3_
  70.6 1.9 %collective-permute-start.4 = (bf16[192,1536]{1,0:T(8,128)(2,1)}, bf16[192,1536]{1,0:T(8,128)(2,1)}, u32[]{:S(2)}, u32[]{:S(2)}) collective-permute-start(bf16[192,1536]{1,0:T(8,128)(2,1)} %collective-permute-done.3.refs_2_), channel_id=1, source_target_pairs={{64,0},{128,64},{192,128},{256,192},{320,256},{384,320},{448,384},... | collective-permute-start | bytes 1769480 | tf_op jit(solution)/shard_map/ppermute | solution.py:198
  72.5 4.6 %collective-permute-start.7 = (bf16[192,1536]{1,0:T(8,128)(2,1)}, bf16[192,1536]{1,0:T(8,128)(2,1)}, u32[]{:S(2)}, u32[]{:S(2)}) collective-permute-start(bf16[192,1536]{1,0:T(8,128)(2,1)} %collective-permute-done.5.refs_3_), channel_id=1, source_target_pairs={{448,0},{0,64},{64,128},{128,192},{192,256},{256,320},{320,384},{3... | collective-permute-start | bytes 1769480 | tf_op jit(solution)/shard_map/ppermute | solution.py:198
  77.1 5.7 %shard_map.70.refs_2_ = bf16[2,8,192,384]{3,2,1,0:T(8,128)(2,1)} custom-call(s32[2]{0:T(128)S(1)} %pad_add_fusion.1.place_ref, bf16[384,1536]{1,0:T(8,128)(2,1)} %copy-done, bf16[384,1536]{1,0:T(8,128)(2,1)} %copy-done.5, bf16[192,1536]{1,0:T(8,128)(2,1)} %collective-permute-done.refs_0_, ...), custom_call_target="tpu_custom_call", output_to_operand_aliasing={{}: (7, {})} | custom-call | flops 274877906944 | bytes 67108864 | tf_op jit(solution)/shard_map/pallas_call | solution.py:51
  82.8 2.1 %collective-permute-done.4.refs_0_ = bf16[192,1536]{1,0:T(8,128)(2,1)} collective-permute-done((bf16[192,1536]{1,0:T(8,128)(2,1)}, bf16[192,1536]{1,0:T(8,128)(2,1)}, u32[]{:S(2)}, u32[]{:S(2)}) %collective-permute-start.4) | collective-permute-done | bytes 589856 | tf_op jit(solution)/shard_map/ppermute | solution.py:198
  84.9 4.9 %collective-permute-done.7.refs_1_ = bf16[192,1536]{1,0:T(8,128)(2,1)} collective-permute-done((bf16[192,1536]{1,0:T(8,128)(2,1)}, bf16[192,1536]{1,0:T(8,128)(2,1)}, u32[]{:S(2)}, u32[]{:S(2)}) %collective-permute-start.7) | collective-permute-done | bytes 589856 | tf_op jit(solution)/shard_map/ppermute | solution.py:198
  89.8 1.9 %collective-permute-start.6 = (bf16[192,1536]{1,0:T(8,128)(2,1)}, bf16[192,1536]{1,0:T(8,128)(2,1)}, u32[]{:S(2)}, u32[]{:S(2)}) collective-permute-start(bf16[192,1536]{1,0:T(8,128)(2,1)} %collective-permute-done.4.refs_0_), channel_id=1, source_target_pairs={{64,0},{128,64},{192,128},{256,192},{320,256},{384,320},{448,384},... | collective-permute-start | bytes 1769480 | tf_op jit(solution)/shard_map/ppermute | solution.py:198
  91.7 4.1 %all-to-all-done.1.x_ref = bf16[16,192,384]{2,1,0:T(8,128)(2,1)} async-done(((bf16[16,192,384]{2,1,0:T(8,128)(2,1)}), bf16[16,192,384]{2,1,0:T(8,128)(2,1)}, u32[]{:S(2)}, u32[]{:S(2)}) %all-to-all-start.1) | async-done | bytes 2359328 | tf_op jit(solution)/shard_map/all_to_all | solution.py:215
  95.7 3.3 %shard_map.72.one_ref = f32[2,8,384]{2,1,0:T(8,128)} custom-call(bf16[16,192,384]{2,1,0:T(8,128)(2,1)} %all-to-all-done.1.x_ref), custom_call_target="tpu_custom_call" | custom-call | tf_op jit(solution)/shard_map/pallas_call | solution.py:227
  99.1 2.1 %collective-permute-start.8 = (f32[2,8,384]{2,1,0:T(8,128)}, f32[2,8,384]{2,1,0:T(8,128)}, u32[]{:S(2)}, u32[]{:S(2)}) collective-permute-start(f32[2,8,384]{2,1,0:T(8,128)} %shard_map.72.one_ref), channel_id=1, source_target_pairs={{0,8},{8,0},{1,9},{9,1},{2,10},{10,2},{3,11},{11,3},{4,12},{12,4},... | collective-permute-start | bytes 73736 | tf_op jit(solution)/shard_map/ppermute | solution.py:24
  101.2 4.2 %shard_map.71.refs_1_ = bf16[2,8,192,384]{3,2,1,0:T(8,128)(2,1)} custom-call(s32[2]{0:T(128)S(1)} %pad_add_fusion.1.place_ref, bf16[384,1536]{1,0:T(8,128)(2,1)} %copy-done, bf16[384,1536]{1,0:T(8,128)(2,1)} %copy-done.5, bf16[192,1536]{1,0:T(8,128)(2,1)} %collective-permute-done.4.refs_0_, ...), custom_call_target="tpu_custom_call", output_to_operand_aliasing={{}: (5, {})} | custom-call | flops 274877906944 | bytes 67108864 | tf_op jit(solution)/shard_map/pallas_call | solution.py:51
  105.4 3.0 %shard_map.73.parts_ref = bf16[2,8,192,384]{3,2,1,0:T(8,128)(2,1)} custom-call(s32[2]{0:T(128)S(1)} %pad_add_fusion.1.place_ref, bf16[384,1536]{1,0:T(8,128)(2,1)S(1)} %copy-done.1, bf16[384,1536]{1,0:T(8,128)(2,1)} %copy-done.5, bf16[192,1536]{1,0:T(8,128)(2,1)} %collective-permute-done.6.refs_0_, ...), custom_call_target="tpu_custom_call", output_to_operand_aliasing={{}: (4, {})} | custom-call | flops 274877906944 | bytes 67108864 | tf_op jit(solution)/shard_map/pallas_call | solution.py:51
  108.4 5.0 %all-to-all-start.2 = ((bf16[16,192,384]{2,1,0:T(8,128)(2,1)}), bf16[16,192,384]{2,1,0:T(8,128)(2,1)S(1)}, u32[]{:S(2)}, u32[]{:S(2)}) async-start(bf16[16,192,384]{2,1,0:T(8,128)(2,1)} %bitcast.18), calls=%async_computation.2 | async-start | bytes 4718592 | tf_op jit(solution)/shard_map/all_to_all | solution.py:236
  113.4 5.4 %shard_map.75 = f32[8,256]{1,0:T(8,128)S(1)} custom-call(bf16[2,8,192,384]{3,2,1,0:T(8,128)(2,1)} %shard_map.73.parts_ref, bf16[2,8,192,384]{3,2,1,0:T(8,128)(2,1)} %bitcast.6.x_ref, f32[2,8,384]{2,1,0:T(8,128)} %shard_map.72.one_ref, f32[2,8,384]{2,1,0:T(8,128)} %collective-permute-done.8.two_ref), custom_call_target="tpu_custom_call" | custom-call | tf_op jit(solution)/shard_map/pallas_call | solution.py:141
  118.9 1.9 %collective-permute-start.9 = (f32[8,256]{1,0:T(8,128)S(1)}, f32[8,256]{1,0:T(8,128)S(1)}, u32[]{:S(2)}, u32[]{:S(2)}) collective-permute-start(f32[8,256]{1,0:T(8,128)S(1)} %shard_map.75), channel_id=1, source_target_pairs={{0,64},{64,0},{128,192},{192,128},{256,320},{320,256},{384,448},{4... | collective-permute-start | bytes 24584 | tf_op jit(solution)/shard_map/ppermute | solution.py:24
  120.8 2.8 %collective-permute-done.9 = f32[8,256]{1,0:T(8,128)S(1)} collective-permute-done((f32[8,256]{1,0:T(8,128)S(1)}, f32[8,256]{1,0:T(8,128)S(1)}, u32[]{:S(2)}, u32[]{:S(2)}) %collective-permute-start.9) | collective-permute-done | bytes 8224 | tf_op jit(solution)/shard_map/ppermute | solution.py:24
  123.6 3.7 %collective-permute-start.10 = (f32[8,256]{1,0:T(8,128)S(1)}, f32[8,256]{1,0:T(8,128)S(1)}, u32[]{:S(2)}, u32[]{:S(2)}) collective-permute-start(f32[8,256]{1,0:T(8,128)S(1)} %add.9), channel_id=1, source_target_pairs={{0,128},{64,192},{128,0},{192,64},{256,384},{320,448},{384,256},{4... | collective-permute-start | bytes 24584 | tf_op jit(solution)/shard_map/ppermute | solution.py:24
  127.3 1.9 %collective-permute-done.10 = f32[8,256]{1,0:T(8,128)S(1)} collective-permute-done((f32[8,256]{1,0:T(8,128)S(1)}, f32[8,256]{1,0:T(8,128)S(1)}, u32[]{:S(2)}, u32[]{:S(2)}) %collective-permute-start.10) | collective-permute-done | bytes 8224 | tf_op jit(solution)/shard_map/ppermute | solution.py:24
  129.2 5.3 %collective-permute-start.11 = (f32[8,256]{1,0:T(8,128)S(1)}, f32[8,256]{1,0:T(8,128)S(1)}, u32[]{:S(2)}, u32[]{:S(2)}) collective-permute-start(f32[8,256]{1,0:T(8,128)S(1)} %add.10), channel_id=1, source_target_pairs={{0,256},{64,320},{128,384},{192,448},{256,0},{320,64},{384,128},{4... | collective-permute-start | bytes 24584 | tf_op jit(solution)/shard_map/ppermute | solution.py:24
  134.5 0.1 reshape.50.gain_ref
  134.6 2.8 %collective-permute-done.11 = f32[8,256]{1,0:T(8,128)S(1)} collective-permute-done((f32[8,256]{1,0:T(8,128)S(1)}, f32[8,256]{1,0:T(8,128)S(1)}, u32[]{:S(2)}, u32[]{:S(2)}) %collective-permute-start.11) | collective-permute-done | bytes 8224 | tf_op jit(solution)/shard_map/ppermute | solution.py:24
  137.5 6.3 %all-to-all-done.2.parts_ref = bf16[16,192,384]{2,1,0:T(8,128)(2,1)S(1)} async-done(((bf16[16,192,384]{2,1,0:T(8,128)(2,1)}), bf16[16,192,384]{2,1,0:T(8,128)(2,1)S(1)}, u32[]{:S(2)}, u32[]{:S(2)}) %all-to-all-start.2) | async-done | bytes 2359328 | tf_op jit(solution)/shard_map/all_to_all | solution.py:236
  143.8 1.2 shard_map.74
  145.1 0.7 broadcast_in_dim.21
  145.8 5.7 %all-to-all-start.3 = ((f32[64,8,128]{2,1,0:T(8,128)}), f32[64,8,128]{2,1,0:T(8,128)S(1)}, u32[]{:S(2)}, u32[]{:S(2)}) async-start(f32[64,8,128]{2,1,0:T(8,128)} %bitcast.8), calls=%async_computation.3 | async-start | bytes 524288 | tf_op jit(solution)/shard_map/all_to_all | solution.py:257
  151.5 0.1 pad_add_fusion.here_ref
  151.6 12.1 %all-to-all-done.3.small_ref = f32[64,8,128]{2,1,0:T(8,128)S(1)} async-done(((f32[64,8,128]{2,1,0:T(8,128)}), f32[64,8,128]{2,1,0:T(8,128)S(1)}, u32[]{:S(2)}, u32[]{:S(2)}) %all-to-all-start.3) | async-done | bytes 262176 | tf_op jit(solution)/shard_map/all_to_all | solution.py:257
  163.6 1.7 %shard_map.76 = (bf16[384,384]{1,0:T(8,128)(2,1)}, f32[8,256]{1,0:T(8,128)S(1)}) custom-call(s32[2]{0:T(128)S(1)} %pad_add_fusion.here_ref, f32[384,384]{1,0:T(8,128)S(1)} %get-tuple-element.46.d_ref, bf16[384,384]{1,0:T(8,128)(2,1)S(1)} %get-tuple-element.43.x_ref, f32[2,8,384]{2,1,0:T(8,128)} %shard_map.72.one_ref, ...), custom_call_target="tpu_custom_call" | custom-call | tf_op jit(solution)/shard_map/pallas_call | solution.py:258
  165.4 0.1 reshape.47
  165.5 0.7 reshape.48
  (20 shorter events, 0.1 us)
Async XLA Ops:
  0.6 32.9 %copy-start.3 = (bf16[384,1536]{1,0:T(8,128)(2,1)S(1)}, bf16[384,1536]{1,0:T(8,128)(2,1)}, u32[]{:S(2)}) copy-start(bf16[384,1536]{1,0:T(8,128)(2,1)} %param.9) | copy-start | bytes 3538948
  1.7 38.5 %copy-start.2 = (bf16[384,384]{1,0:T(8,128)(2,1)S(1)}, bf16[384,384]{1,0:T(8,128)(2,1)}, u32[]{:S(2)}) copy-start(bf16[384,384]{1,0:T(8,128)(2,1)} %tokens_ref) | copy-start | bytes 884740
  26.5 15.6 %collective-permute-start = (bf16[192,1536]{1,0:T(8,128)(2,1)S(1)}, bf16[192,1536]{1,0:T(8,128)(2,1)}, u32[]{:S(2)}, u32[]{:S(2)}) collective-permute-start(bf16[192,1536]{1,0:T(8,128)(2,1)S(1)} %bitcast.14), channel_id=1, source_target_pairs={{64,0},{128,64},{192,128},{256,192},{320,256},{384,320},{448,384},... | collective-permute-start | bytes 1769480 | tf_op jit(solution)/shard_map/ppermute | solution.py:198
  29.7 14.4 %collective-permute-start.1 = (bf16[192,1536]{1,0:T(8,128)(2,1)S(1)}, bf16[192,1536]{1,0:T(8,128)(2,1)}, u32[]{:S(2)}, u32[]{:S(2)}) collective-permute-start(bf16[192,1536]{1,0:T(8,128)(2,1)S(1)} %bitcast.15), channel_id=1, source_target_pairs={{448,0},{0,64},{64,128},{128,192},{192,256},{256,320},{320,384},{3... | collective-permute-start | bytes 1769480 | tf_op jit(solution)/shard_map/ppermute | solution.py:198
  40.2 25.1 %copy-start = (bf16[384,1536]{1,0:T(8,128)(2,1)}, bf16[384,1536]{1,0:T(8,128)(2,1)S(1)}, u32[]{:S(2)}) copy-start(bf16[384,1536]{1,0:T(8,128)(2,1)S(1)} %fusion.34.own_ref) | copy-start | bytes 3538948
  44.0 21.2 %collective-permute-start.2 = (bf16[384,1536]{1,0:T(8,128)(2,1)S(1)}, bf16[384,1536]{1,0:T(8,128)(2,1)S(1)}, u32[]{:S(2)}, u32[]{:S(2)}) collective-permute-start(bf16[384,1536]{1,0:T(8,128)(2,1)S(1)} %fusion.34.own_ref), channel_id=1, source_target_pairs={{0,8},{8,0},{1,9},{9,1},{2,10},{10,2},{3,11},{11,3},{4,12},{12,4},... | collective-permute-start | bytes 3538952 | tf_op jit(solution)/shard_map/ppermute | solution.py:24
  52.6 16.7 %collective-permute-start.3 = (bf16[192,1536]{1,0:T(8,128)(2,1)}, bf16[192,1536]{1,0:T(8,128)(2,1)}, u32[]{:S(2)}, u32[]{:S(2)}) collective-permute-start(bf16[192,1536]{1,0:T(8,128)(2,1)} %collective-permute-done.refs_0_), channel_id=1, source_target_pairs={{64,0},{128,64},{192,128},{256,192},{320,256},{384,320},{448,384},... | collective-permute-start | bytes 1769480 | tf_op jit(solution)/shard_map/ppermute | solution.py:198
  54.5 16.1 %collective-permute-start.5 = (bf16[192,1536]{1,0:T(8,128)(2,1)}, bf16[192,1536]{1,0:T(8,128)(2,1)}, u32[]{:S(2)}, u32[]{:S(2)}) collective-permute-start(bf16[192,1536]{1,0:T(8,128)(2,1)} %collective-permute-done.1.refs_1_), channel_id=1, source_target_pairs={{448,0},{0,64},{64,128},{128,192},{192,256},{256,320},{320,384},{3... | collective-permute-start | bytes 1769480 | tf_op jit(solution)/shard_map/ppermute | solution.py:198
  59.1 36.6 %all-to-all-start.1 = ((bf16[16,192,384]{2,1,0:T(8,128)(2,1)}), bf16[16,192,384]{2,1,0:T(8,128)(2,1)}, u32[]{:S(2)}, u32[]{:S(2)}) async-start(bf16[16,192,384]{2,1,0:T(8,128)(2,1)} %bitcast.4), calls=%async_computation.1 | async-start | bytes 4718592 | tf_op jit(solution)/shard_map/all_to_all | solution.py:215
  65.3 1.1 copy-start.5
  70.6 14.3 %collective-permute-start.4 = (bf16[192,1536]{1,0:T(8,128)(2,1)}, bf16[192,1536]{1,0:T(8,128)(2,1)}, u32[]{:S(2)}, u32[]{:S(2)}) collective-permute-start(bf16[192,1536]{1,0:T(8,128)(2,1)} %collective-permute-done.3.refs_2_), channel_id=1, source_target_pairs={{64,0},{128,64},{192,128},{256,192},{320,256},{384,320},{448,384},... | collective-permute-start | bytes 1769480 | tf_op jit(solution)/shard_map/ppermute | solution.py:198
  72.5 17.2 %collective-permute-start.7 = (bf16[192,1536]{1,0:T(8,128)(2,1)}, bf16[192,1536]{1,0:T(8,128)(2,1)}, u32[]{:S(2)}, u32[]{:S(2)}) collective-permute-start(bf16[192,1536]{1,0:T(8,128)(2,1)} %collective-permute-done.5.refs_3_), channel_id=1, source_target_pairs={{448,0},{0,64},{64,128},{128,192},{192,256},{256,320},{320,384},{3... | collective-permute-start | bytes 1769480 | tf_op jit(solution)/shard_map/ppermute | solution.py:198
  89.8 15.6 %collective-permute-start.6 = (bf16[192,1536]{1,0:T(8,128)(2,1)}, bf16[192,1536]{1,0:T(8,128)(2,1)}, u32[]{:S(2)}, u32[]{:S(2)}) collective-permute-start(bf16[192,1536]{1,0:T(8,128)(2,1)} %collective-permute-done.4.refs_0_), channel_id=1, source_target_pairs={{64,0},{128,64},{192,128},{256,192},{320,256},{384,320},{448,384},... | collective-permute-start | bytes 1769480 | tf_op jit(solution)/shard_map/ppermute | solution.py:198
  99.1 6.3 %collective-permute-start.8 = (f32[2,8,384]{2,1,0:T(8,128)}, f32[2,8,384]{2,1,0:T(8,128)}, u32[]{:S(2)}, u32[]{:S(2)}) collective-permute-start(f32[2,8,384]{2,1,0:T(8,128)} %shard_map.72.one_ref), channel_id=1, source_target_pairs={{0,8},{8,0},{1,9},{9,1},{2,10},{10,2},{3,11},{11,3},{4,12},{12,4},... | collective-permute-start | bytes 73736 | tf_op jit(solution)/shard_map/ppermute | solution.py:24
  101.2 4.2 %copy-start.1 = (bf16[384,1536]{1,0:T(8,128)(2,1)S(1)}, bf16[384,1536]{1,0:T(8,128)(2,1)}, u32[]{:S(2)}) copy-start(bf16[384,1536]{1,0:T(8,128)(2,1)} %copy-done) | copy-start | bytes 3538948
  108.4 35.4 %all-to-all-start.2 = ((bf16[16,192,384]{2,1,0:T(8,128)(2,1)}), bf16[16,192,384]{2,1,0:T(8,128)(2,1)S(1)}, u32[]{:S(2)}, u32[]{:S(2)}) async-start(bf16[16,192,384]{2,1,0:T(8,128)(2,1)} %bitcast.18), calls=%async_computation.2 | async-start | bytes 4718592 | tf_op jit(solution)/shard_map/all_to_all | solution.py:236
  113.4 21.1 %copy-start.4 = (bf16[384]{0:T(512)(128)(2,1)S(1)}, bf16[384]{0:T(512)(128)(2,1)}, u32[]{:S(2)}) copy-start(bf16[384]{0:T(512)(128)(2,1)} %param.6) | copy-start | bytes 2308
  118.9 4.7 %collective-permute-start.9 = (f32[8,256]{1,0:T(8,128)S(1)}, f32[8,256]{1,0:T(8,128)S(1)}, u32[]{:S(2)}, u32[]{:S(2)}) collective-permute-start(f32[8,256]{1,0:T(8,128)S(1)} %shard_map.75), channel_id=1, source_target_pairs={{0,64},{64,0},{128,192},{192,128},{256,320},{320,256},{384,448},{4... | collective-permute-start | bytes 24584 | tf_op jit(solution)/shard_map/ppermute | solution.py:24
  123.6 5.6 %collective-permute-start.10 = (f32[8,256]{1,0:T(8,128)S(1)}, f32[8,256]{1,0:T(8,128)S(1)}, u32[]{:S(2)}, u32[]{:S(2)}) collective-permute-start(f32[8,256]{1,0:T(8,128)S(1)} %add.9), channel_id=1, source_target_pairs={{0,128},{64,192},{128,0},{192,64},{256,384},{320,448},{384,256},{4... | collective-permute-start | bytes 24584 | tf_op jit(solution)/shard_map/ppermute | solution.py:24
  129.2 8.3 %collective-permute-start.11 = (f32[8,256]{1,0:T(8,128)S(1)}, f32[8,256]{1,0:T(8,128)S(1)}, u32[]{:S(2)}, u32[]{:S(2)}) collective-permute-start(f32[8,256]{1,0:T(8,128)S(1)} %add.10), channel_id=1, source_target_pairs={{0,256},{64,320},{128,384},{192,448},{256,0},{320,64},{384,128},{4... | collective-permute-start | bytes 24584 | tf_op jit(solution)/shard_map/ppermute | solution.py:24
  145.8 17.9 %all-to-all-start.3 = ((f32[64,8,128]{2,1,0:T(8,128)}), f32[64,8,128]{2,1,0:T(8,128)S(1)}, u32[]{:S(2)}, u32[]{:S(2)}) async-start(f32[64,8,128]{2,1,0:T(8,128)} %bitcast.8), calls=%async_computation.3 | async-start | bytes 524288 | tf_op jit(solution)/shard_map/all_to_all | solution.py:257

commit v10 on v9

--- a/solution.py
+++ b/solution.py
@@ -125,22 +125,25 @@
             mean, rstd = mean_and_rstd(one_ref[t], two_ref[t])
             stat_ref[t] = jnp.concatenate([mean, rstd] * 4, axis=0)
 
-    total = 0.0
-    for t in range(2):
-        xhat = (x_ref[t, 0].astype(F32) - stat_ref[t, 0:1]) * stat_ref[t, 1:2]
-        value = parts_ref[t, 0].astype(F32) * xhat
-        total += value[:, :128] + value[:, 128:256] + value[:, 256:]
-    total = jnp.concatenate([total, jnp.zeros((64, 128), F32)], axis=0)
-    out_ref[pl.ds(pl.program_id(0), 1), :] = jnp.sum(total.T, axis=0, keepdims=True)
+    per_step = x_ref.shape[1]
+    for k in range(per_step):
+        total = jnp.zeros((x_ref.shape[2], 128), F32)
+        for t in range(2):
+            xhat = (x_ref[t, k].astype(F32) - stat_ref[t, 0:1]) * stat_ref[t, 1:2]
+            value = parts_ref[t, k].astype(F32) * xhat
+            total += value[:, :128] + value[:, 128:256] + value[:, 256:]
+        total = jnp.concatenate([total, jnp.zeros((64, 128), F32)], axis=0)
+        row = jnp.sum(total.T, axis=0, keepdims=True)
+        out_ref[pl.ds(pl.program_id(0) * per_step + k, 1), :] = row
 
 
 def gain_share(parts, x_all, one, two):
     _, _, rows, tokens = parts.shape
-    block = pl.BlockSpec((2, 1, rows, tokens), lambda m: (0, m, 0, 0))
+    block = pl.BlockSpec((2, 2, rows, tokens), lambda m: (0, m, 0, 0))
     stat = pl.BlockSpec((2, 8, tokens), lambda m: (0, 0, 0))
     return pl.pallas_call(
         gain_kernel,
-        grid=(8,),
+        grid=(4,),
         in_specs=[block, block, stat, stat],
         out_specs=pl.BlockSpec((8, 256), lambda m: (0, 0)),
         scratch_shapes=[pltpu.VMEM((2, 8, tokens), F32)],
@@ -201,7 +204,7 @@
         (first_next, _), (second_next, _) = together((first, done)), together((second, done))
         return first_next, second_next, *together((first, second, done, *later))[2:]
 
-    w0 = lax.all_to_all(jnp.broadcast_to(w_in, (4,) + w_in.shape), "zh", 0, 0).reshape(-1, w_in.shape[1])
+    w0 = lax.all_gather(w_in, "zh", axis=0, tiled=True)
     w0, pre_act, act_cotangent, tokens = together((w0, pre_act, act_cotangent, tokens))
     first1, second1 = step(w0, 1), step(w0, -1)
     _, gelu_back = jax.vjp(gelu_exact, pre_act.astype(F32))
@@ -224,20 +227,17 @@
     first4 = step(first, 1)
     parts = products([(3, first3), (5, second)], d_own, d_other, place, parts)
 
+    first4, parts = together((first4, parts))
+    parts = products([(4, first4)], d_own, d_other, place, parts)
+    received = lax.all_to_all(parts.reshape(16, share // 2, rows), CHIPS, 0, 0)
+
     one = pl.pallas_call(
         stats_kernel,
         out_shape=jax.ShapeDtypeStruct((2, 8, rows), F32),
         compiler_params=PARAMS,
     )(x_all)
     two = partner(one, "c", 2, 1)
-
-    first4, parts, one, two = together((first4, parts, one, two))
-    parts = products([(4, first4)], d_own, d_other, place, parts)
-    received = lax.all_to_all(parts.reshape(16, share // 2, rows), CHIPS, 0, 0)
-
-    shares = gain_share(parts, x_all, one, two)
-    for bit in (1, 2, 4):
-        shares += partner(shares, "y", 8, bit)
+    shares = lax.psum(gain_share(parts, x_all, one, two), "y")
 
     vmem, smem = pl.BlockSpec(memory_space=pltpu.VMEM), pl.BlockSpec(memory_space=pltpu.SMEM)
     d_scaled, moments = pl.pallas_call(

time: 167 us -> 161 us (0.964)
  blocking collectives: 24.8 us -> 36.9 us
  starting transfers between devices: 60.3 us -> 49.2 us
  Pallas kernels: 29.3 us -> 25.9 us
  waiting for transfers between devices: 40.2 us -> 37.5 us
    all_to_all x1 -> x0, blocking collectives: 24.8 us -> none  [on_device(): lax.all_to_all(jnp.broadcast_to(w_in, (4,) + w_in.shape), 'zh', 0, 0)]
    all_gather x0 -> x1, blocking collectives: none -> 22.4 us  [on_device(): w0 = lax.all_gather(w_in, 'zh', axis=0, tiled=True)]
    ppermute x5 -> x2, starting transfers between devices: 21.5 us -> 4.56 us  [partner(): return lax.ppermute(array, axis, [(i, i ^ bit) for i in range(n)])]
    psum x0 -> x1, blocking collectives: none -> 14.5 us  [on_device(): shares = lax.psum(gain_share(parts, x_all, one, two), 'y')]
    ppermute x7, waiting for transfers between devices: 10.3 us -> 18 us  [step(): lax.ppermute(array, ('y', 'c'), [(a * 2 + c, b * 2 + c) for a, b, c in mo...]
    ppermute x5 -> x2, waiting for transfers between devices: 7.5 us -> 0.95 us  [partner(): return lax.ppermute(array, axis, [(i, i ^ bit) for i in range(n)])]
    all_to_all x1, waiting for transfers between devices: 4.06 us -> 0.01 us  [on_device(): x_all = lax.all_to_all(x_all.reshape(16, share // 2, rows), CHIPS, 0, 0)]
    all_to_all x1, starting transfers between devices: 5.71 us -> 8.43 us  [on_device(): small = lax.all_to_all(small, ('zh',) + CHIPS, 0, 0)]
  transfers between devices with their start and end apart: 15 -> 12, of which waited for: 10 -> 8; matrix products, arithmetic and copies ran while one was open for 4% -> 4% of each run, Pallas kernels for 14% -> 15%
where the time goes in v10:
time: 161 us; the launch traced here: 160 us
  starting transfers between devices  49.2 us (31%)
  waiting for transfers between devices  37.5 us (23%)
  blocking collectives  36.9 us (23%)
  Pallas kernels  25.9 us (16%)
  other arithmetic  6.97 us (4%)
  local copies, waits for them, and re-layouts  2.72 us (2%)
    ppermute x7, starting transfers between devices, step(): lax.ppermute(array, ('y', 'c'), [(a * 2 + c, b * 2 + c) for a, b, c in mo...  23.5 us
    all_gather x1, blocking collectives, on_device(): w0 = lax.all_gather(w_in, 'zh', axis=0, tiled=True)  22.4 us
    ppermute x7, waiting for transfers between devices, step(): lax.ppermute(array, ('y', 'c'), [(a * 2 + c, b * 2 + c) for a, b, c in mo...  18 us
    pallas_call x4, Pallas kernels, products(): pl.pallas_call(kernel, in_specs=[pl.BlockSpec(memory_space=pltpu.SMEM)] +...  15.7 us
    psum x1, blocking collectives, on_device(): shares = lax.psum(gain_share(parts, x_all, one, two), 'y')  14.5 us
    all_to_all x1, waiting for transfers between devices, on_device(): small = lax.all_to_all(small, ('zh',) + CHIPS, 0, 0)  12.1 us
    all_to_all x1, starting transfers between devices, on_device(): small = lax.all_to_all(small, ('zh',) + CHIPS, 0, 0)  8.43 us
    convert_element_type x1, other arithmetic, on_device(): d_own = gelu_back(act_cotangent.astype(F32))[0].astype(BF16)  6.81 us
  transfers between devices with their start and end apart: 12, of which 8 were waited for; matrix products, arithmetic and copies ran while one was open for 4% of the time, Pallas kernels for 15%

profile of v10, /device:TPU:1, one launch (start us, length us, event | category | flops | bytes accessed | tf_op | source)
XLA Modules:
  0.0 160.1 jit_solution(5806205475714660213)
XLA Ops:
  0.6 0.0 copy-start.2
  0.6 22.4 %all_gather.3.refs_0_ = bf16[192,1536]{1,0:T(8,128)(2,1)S(1)} all-gather(bf16[48,1536]{1,0:T(8,128)(2,1)} %param.8), channel_id=1, replica_groups=mesh['y'=8,'zh'=4,'c'=2,'zl'=2,'x'=4] {'zh'}, dimensions={0}, use_global_device_ids=true | all-gather | bytes 737280 | tf_op jit(solution)/shard_map/all_gather | solution.py:207
  23.0 3.2 %collective-permute-start = (bf16[192,1536]{1,0:T(8,128)(2,1)S(1)}, bf16[192,1536]{1,0:T(8,128)(2,1)}, u32[]{:S(2)}, u32[]{:S(2)}) collective-permute-start(bf16[192,1536]{1,0:T(8,128)(2,1)S(1)} %all_gather.3.refs_0_), channel_id=1, source_target_pairs={{64,0},{128,64},{192,128},{256,192},{320,256},{384,320},{448,384},... | collective-permute-start | bytes 1769480 | tf_op jit(solution)/shard_map/ppermute | solution.py:201
  26.2 3.8 %collective-permute-start.1 = (bf16[192,1536]{1,0:T(8,128)(2,1)S(1)}, bf16[192,1536]{1,0:T(8,128)(2,1)}, u32[]{:S(2)}, u32[]{:S(2)}) collective-permute-start(bf16[192,1536]{1,0:T(8,128)(2,1)S(1)} %all_gather.3.refs_0_), channel_id=1, source_target_pairs={{448,0},{0,64},{64,128},{128,192},{192,256},{256,320},{320,384},{3... | collective-permute-start | bytes 1769480 | tf_op jit(solution)/shard_map/ppermute | solution.py:201
  30.0 6.8 %fusion.34.own_ref = bf16[384,1536]{1,0:T(8,128)(2,1)S(1)} fusion(bf16[384,1536]{1,0:T(8,128)(2,1)} %param.9, bf16[384,1536]{1,0:T(8,128)(2,1)} %param.7), kind=kLoop, calls=%fused_computation.39 | loop fusion | flops 43646976 | bytes 3538944 | tf_op jit(solution)/shard_map/convert_element_type | solution.py:211
  36.9 0.0 copy-done.2
  36.9 0.0 copy-start
  36.9 1.9 %shard_map.68 = (bf16[384,384]{1,0:T(8,128)(2,1)S(1)}, bf16[2,8,192,384]{3,2,1,0:T(8,128)(2,1)}) custom-call(bf16[384,384]{1,0:T(8,128)(2,1)S(1)} %copy-done.2), custom_call_target="tpu_custom_call" | custom-call | tf_op jit(solution)/shard_map/pallas_call | solution.py:86
  38.7 0.0 collective-permute-done.refs_0_
  38.8 4.2 %collective-permute-done.1.refs_1_ = bf16[192,1536]{1,0:T(8,128)(2,1)} collective-permute-done((bf16[192,1536]{1,0:T(8,128)(2,1)S(1)}, bf16[192,1536]{1,0:T(8,128)(2,1)}, u32[]{:S(2)}, u32[]{:S(2)}) %collective-permute-start.1) | collective-permute-done | bytes 589856 | tf_op jit(solution)/shard_map/ppermute | solution.py:201
  42.9 2.6 %collective-permute-start.2 = (bf16[384,1536]{1,0:T(8,128)(2,1)S(1)}, bf16[384,1536]{1,0:T(8,128)(2,1)S(1)}, u32[]{:S(2)}, u32[]{:S(2)}) collective-permute-start(bf16[384,1536]{1,0:T(8,128)(2,1)S(1)} %fusion.34.own_ref), channel_id=1, source_target_pairs={{0,8},{8,0},{1,9},{9,1},{2,10},{10,2},{3,11},{11,3},{4,12},{12,4},... | collective-permute-start | bytes 3538952 | tf_op jit(solution)/shard_map/ppermute | solution.py:24
  45.5 0.1 pad_add_fusion.1.place_ref
  45.6 2.0 %collective-permute-start.3 = (bf16[192,1536]{1,0:T(8,128)(2,1)}, bf16[192,1536]{1,0:T(8,128)(2,1)}, u32[]{:S(2)}, u32[]{:S(2)}) collective-permute-start(bf16[192,1536]{1,0:T(8,128)(2,1)} %collective-permute-done.refs_0_), channel_id=1, source_target_pairs={{64,0},{128,64},{192,128},{256,192},{320,256},{384,320},{448,384},... | collective-permute-start | bytes 1769480 | tf_op jit(solution)/shard_map/ppermute | solution.py:201
  47.5 5.4 %collective-permute-start.5 = (bf16[192,1536]{1,0:T(8,128)(2,1)}, bf16[192,1536]{1,0:T(8,128)(2,1)}, u32[]{:S(2)}, u32[]{:S(2)}) collective-permute-start(bf16[192,1536]{1,0:T(8,128)(2,1)} %collective-permute-done.1.refs_1_), channel_id=1, source_target_pairs={{448,0},{0,64},{64,128},{128,192},{192,256},{256,320},{320,384},{3... | collective-permute-start | bytes 1769480 | tf_op jit(solution)/shard_map/ppermute | solution.py:201
  52.9 6.0 %all-to-all-start.1 = ((bf16[16,192,384]{2,1,0:T(8,128)(2,1)}), bf16[16,192,384]{2,1,0:T(8,128)(2,1)}, u32[]{:S(2)}, u32[]{:S(2)}) async-start(bf16[16,192,384]{2,1,0:T(8,128)(2,1)} %bitcast.4), calls=%async_computation.1 | async-start | bytes 4718592 | tf_op jit(solution)/shard_map/all_to_all | solution.py:218
  58.9 0.0 collective-permute-done.2.other_ref
  58.9 0.0 copy-done
  58.9 0.0 copy-start.4
  59.0 1.1 copy-done.4
  60.1 2.9 %shard_map.69.refs_4_ = bf16[2,8,192,384]{3,2,1,0:T(8,128)(2,1)} custom-call(s32[2]{0:T(128)S(1)} %pad_add_fusion.1.place_ref, bf16[384,1536]{1,0:T(8,128)(2,1)S(1)} %fusion.34.own_ref, bf16[384,1536]{1,0:T(8,128)(2,1)} %copy-done.4, bf16[192,1536]{1,0:T(8,128)(2,1)S(1)} %all_gather.3.refs_0_), custom_call_target="tpu_custom_call" | custom-call | flops 274877906944 | bytes 67108864 | tf_op jit(solution)/shard_map/pallas_call | solution.py:51
  62.9 0.0 collective-permute-done.3.refs_2_
  62.9 2.0 %collective-permute-done.5.refs_3_ = bf16[192,1536]{1,0:T(8,128)(2,1)} collective-permute-done((bf16[192,1536]{1,0:T(8,128)(2,1)}, bf16[192,1536]{1,0:T(8,128)(2,1)}, u32[]{:S(2)}, u32[]{:S(2)}) %collective-permute-start.5) | collective-permute-done | bytes 589856 | tf_op jit(solution)/shard_map/ppermute | solution.py:201
  64.9 1.9 %collective-permute-start.4 = (bf16[192,1536]{1,0:T(8,128)(2,1)}, bf16[192,1536]{1,0:T(8,128)(2,1)}, u32[]{:S(2)}, u32[]{:S(2)}) collective-permute-start(bf16[192,1536]{1,0:T(8,128)(2,1)} %collective-permute-done.3.refs_2_), channel_id=1, source_target_pairs={{64,0},{128,64},{192,128},{256,192},{320,256},{384,320},{448,384},... | collective-permute-start | bytes 1769480 | tf_op jit(solution)/shard_map/ppermute | solution.py:201
  66.8 5.3 %collective-permute-start.7 = (bf16[192,1536]{1,0:T(8,128)(2,1)}, bf16[192,1536]{1,0:T(8,128)(2,1)}, u32[]{:S(2)}, u32[]{:S(2)}) collective-permute-start(bf16[192,1536]{1,0:T(8,128)(2,1)} %collective-permute-done.5.refs_3_), channel_id=1, source_target_pairs={{448,0},{0,64},{64,128},{128,192},{192,256},{256,320},{320,384},{3... | collective-permute-start | bytes 1769480 | tf_op jit(solution)/shard_map/ppermute | solution.py:201
  72.1 5.7 %shard_map.70.refs_2_ = bf16[2,8,192,384]{3,2,1,0:T(8,128)(2,1)} custom-call(s32[2]{0:T(128)S(1)} %pad_add_fusion.1.place_ref, bf16[384,1536]{1,0:T(8,128)(2,1)} %copy-done, bf16[384,1536]{1,0:T(8,128)(2,1)} %copy-done.4, bf16[192,1536]{1,0:T(8,128)(2,1)} %collective-permute-done.refs_0_, ...), custom_call_target="tpu_custom_call", output_to_operand_aliasing={{}: (7, {})} | custom-call | flops 274877906944 | bytes 67108864 | tf_op jit(solution)/shard_map/pallas_call | solution.py:51
  77.9 2.3 %collective-permute-done.4.refs_0_ = bf16[192,1536]{1,0:T(8,128)(2,1)} collective-permute-done((bf16[192,1536]{1,0:T(8,128)(2,1)}, bf16[192,1536]{1,0:T(8,128)(2,1)}, u32[]{:S(2)}, u32[]{:S(2)}) %collective-permute-start.4) | collective-permute-done | bytes 589856 | tf_op jit(solution)/shard_map/ppermute | solution.py:201
  80.1 3.4 %collective-permute-done.7.refs_1_ = bf16[192,1536]{1,0:T(8,128)(2,1)} collective-permute-done((bf16[192,1536]{1,0:T(8,128)(2,1)}, bf16[192,1536]{1,0:T(8,128)(2,1)}, u32[]{:S(2)}, u32[]{:S(2)}) %collective-permute-start.7) | collective-permute-done | bytes 589856 | tf_op jit(solution)/shard_map/ppermute | solution.py:201
  83.6 1.9 %collective-permute-start.6 = (bf16[192,1536]{1,0:T(8,128)(2,1)}, bf16[192,1536]{1,0:T(8,128)(2,1)}, u32[]{:S(2)}, u32[]{:S(2)}) collective-permute-start(bf16[192,1536]{1,0:T(8,128)(2,1)} %collective-permute-done.4.refs_0_), channel_id=1, source_target_pairs={{64,0},{128,64},{192,128},{256,192},{320,256},{384,320},{448,384},... | collective-permute-start | bytes 1769480 | tf_op jit(solution)/shard_map/ppermute | solution.py:201
  85.5 4.2 %shard_map.71.refs_1_ = bf16[2,8,192,384]{3,2,1,0:T(8,128)(2,1)} custom-call(s32[2]{0:T(128)S(1)} %pad_add_fusion.1.place_ref, bf16[384,1536]{1,0:T(8,128)(2,1)} %copy-done, bf16[384,1536]{1,0:T(8,128)(2,1)} %copy-done.4, bf16[192,1536]{1,0:T(8,128)(2,1)} %collective-permute-done.4.refs_0_, ...), custom_call_target="tpu_custom_call", output_to_operand_aliasing={{}: (5, {})} | custom-call | flops 274877906944 | bytes 67108864 | tf_op jit(solution)/shard_map/pallas_call | solution.py:51
  89.7 6.2 %collective-permute-done.6.refs_0_ = bf16[192,1536]{1,0:T(8,128)(2,1)} collective-permute-done((bf16[192,1536]{1,0:T(8,128)(2,1)}, bf16[192,1536]{1,0:T(8,128)(2,1)}, u32[]{:S(2)}, u32[]{:S(2)}) %collective-permute-start.6) | collective-permute-done | bytes 589856 | tf_op jit(solution)/shard_map/ppermute | solution.py:201
  95.9 3.0 %shard_map.72.parts_ref = bf16[2,8,192,384]{3,2,1,0:T(8,128)(2,1)} custom-call(s32[2]{0:T(128)S(1)} %pad_add_fusion.1.place_ref, bf16[384,1536]{1,0:T(8,128)(2,1)S(1)} %copy-done.1, bf16[384,1536]{1,0:T(8,128)(2,1)} %copy-done.4, bf16[192,1536]{1,0:T(8,128)(2,1)} %collective-permute-done.6.refs_0_, ...), custom_call_target="tpu_custom_call", output_to_operand_aliasing={{}: (4, {})} | custom-call | flops 274877906944 | bytes 67108864 | tf_op jit(solution)/shard_map/pallas_call | solution.py:51
  98.9 0.0 all-to-all-done.1.x_ref
  98.9 6.7 %all-to-all-start = ((bf16[16,192,384]{2,1,0:T(8,128)(2,1)}), bf16[16,192,384]{2,1,0:T(8,128)(2,1)S(1)}, u32[]{:S(2)}, u32[]{:S(2)}) async-start(bf16[16,192,384]{2,1,0:T(8,128)(2,1)} %bitcast.14), calls=%async_computation | async-start | bytes 4718592 | tf_op jit(solution)/shard_map/all_to_all | solution.py:232
  105.6 2.7 %shard_map.73.one_ref = f32[2,8,384]{2,1,0:T(8,128)S(1)} custom-call(bf16[16,192,384]{2,1,0:T(8,128)(2,1)} %all-to-all-done.1.x_ref), custom_call_target="tpu_custom_call" | custom-call | tf_op jit(solution)/shard_map/pallas_call | solution.py:234
  108.4 2.0 %collective-permute-start.8 = (f32[2,8,384]{2,1,0:T(8,128)S(1)}, f32[2,8,384]{2,1,0:T(8,128)S(1)}, u32[]{:S(2)}, u32[]{:S(2)}) collective-permute-start(f32[2,8,384]{2,1,0:T(8,128)S(1)} %shard_map.73.one_ref), channel_id=1, source_target_pairs={{0,8},{8,0},{1,9},{9,1},{2,10},{10,2},{3,11},{11,3},{4,12},{12,4},... | collective-permute-start | bytes 73736 | tf_op jit(solution)/shard_map/ppermute | solution.py:24
  110.4 0.1 reshape.46.gain_ref
  110.5 0.9 collective-permute-done.8.two_ref
  111.5 3.6 %shard_map.75 = f32[8,256]{1,0:T(8,128)S(1)} custom-call(bf16[2,8,192,384]{3,2,1,0:T(8,128)(2,1)} %shard_map.72.parts_ref, bf16[2,8,192,384]{3,2,1,0:T(8,128)(2,1)} %bitcast.5.x_ref, f32[2,8,384]{2,1,0:T(8,128)S(1)} %shard_map.73.one_ref, f32[2,8,384]{2,1,0:T(8,128)S(1)} %collective-permute-done.8.two_ref), custom_call_target="tpu_custom_call" | custom-call | tf_op jit(solution)/shard_map/pallas_call | solution.py:144
  115.1 14.5 %psum.7 = f32[8,2,128]{2,0,1:T(8,128)S(1)} all-reduce(f32[8,2,128]{2,0,1:T(8,128)S(1)} %bitcast.12), channel_id=1, replica_groups=mesh['y'=8,'zh'=4,'c'=2,'zl'=2,'x'=4] {'y'}, use_global_device_ids=true, to_apply=%region_0.0 | all-reduce | flops 2048 | bytes 16384 | tf_op jit(solution)/shard_map/psum | solution.py:240
  129.6 6.4 %all-to-all-done.parts_ref = bf16[16,192,384]{2,1,0:T(8,128)(2,1)S(1)} async-done(((bf16[16,192,384]{2,1,0:T(8,128)(2,1)}), bf16[16,192,384]{2,1,0:T(8,128)(2,1)S(1)}, u32[]{:S(2)}, u32[]{:S(2)}) %all-to-all-start) | async-done | bytes 2359328 | tf_op jit(solution)/shard_map/all_to_all | solution.py:232
  136.0 0.5 shard_map.74
  136.5 0.7 broadcast_in_dim.17
  137.2 8.4 %all-to-all-start.2 = ((f32[64,8,128]{2,1,0:T(8,128)}), f32[64,8,128]{2,1,0:T(8,128)S(1)}, u32[]{:S(2)}, u32[]{:S(2)}) async-start(f32[64,8,128]{2,1,0:T(8,128)} %bitcast.7), calls=%async_computation.2 | async-start | bytes 524288 | tf_op jit(solution)/shard_map/all_to_all | solution.py:257
  145.7 0.1 pad_add_fusion.here_ref
  145.7 12.1 %all-to-all-done.2.small_ref = f32[64,8,128]{2,1,0:T(8,128)S(1)} async-done(((f32[64,8,128]{2,1,0:T(8,128)}), f32[64,8,128]{2,1,0:T(8,128)S(1)}, u32[]{:S(2)}, u32[]{:S(2)}) %all-to-all-start.2) | async-done | bytes 262176 | tf_op jit(solution)/shard_map/all_to_all | solution.py:257
  157.8 1.5 shard_map.76
  159.3 0.1 reshape.43
  159.4 0.7 reshape.44
  (9 shorter events, 0.0 us)
Async XLA Ops:
  0.6 36.2 %copy-start.2 = (bf16[384,384]{1,0:T(8,128)(2,1)S(1)}, bf16[384,384]{1,0:T(8,128)(2,1)}, u32[]{:S(2)}) copy-start(bf16[384,384]{1,0:T(8,128)(2,1)} %tokens_ref) | copy-start | bytes 884740
  23.0 15.7 %collective-permute-start = (bf16[192,1536]{1,0:T(8,128)(2,1)S(1)}, bf16[192,1536]{1,0:T(8,128)(2,1)}, u32[]{:S(2)}, u32[]{:S(2)}) collective-permute-start(bf16[192,1536]{1,0:T(8,128)(2,1)S(1)} %all_gather.3.refs_0_), channel_id=1, source_target_pairs={{64,0},{128,64},{192,128},{256,192},{320,256},{384,320},{448,384},... | collective-permute-start | bytes 1769480 | tf_op jit(solution)/shard_map/ppermute | solution.py:201
  26.2 16.7 %collective-permute-start.1 = (bf16[192,1536]{1,0:T(8,128)(2,1)S(1)}, bf16[192,1536]{1,0:T(8,128)(2,1)}, u32[]{:S(2)}, u32[]{:S(2)}) collective-permute-start(bf16[192,1536]{1,0:T(8,128)(2,1)S(1)} %all_gather.3.refs_0_), channel_id=1, source_target_pairs={{448,0},{0,64},{64,128},{128,192},{192,256},{256,320},{320,384},{3... | collective-permute-start | bytes 1769480 | tf_op jit(solution)/shard_map/ppermute | solution.py:201
  36.9 22.1 %copy-start = (bf16[384,1536]{1,0:T(8,128)(2,1)}, bf16[384,1536]{1,0:T(8,128)(2,1)S(1)}, u32[]{:S(2)}) copy-start(bf16[384,1536]{1,0:T(8,128)(2,1)S(1)} %fusion.34.own_ref) | copy-start | bytes 3538948
  42.9 16.0 %collective-permute-start.2 = (bf16[384,1536]{1,0:T(8,128)(2,1)S(1)}, bf16[384,1536]{1,0:T(8,128)(2,1)S(1)}, u32[]{:S(2)}, u32[]{:S(2)}) collective-permute-start(bf16[384,1536]{1,0:T(8,128)(2,1)S(1)} %fusion.34.own_ref), channel_id=1, source_target_pairs={{0,8},{8,0},{1,9},{9,1},{2,10},{10,2},{3,11},{11,3},{4,12},{12,4},... | collective-permute-start | bytes 3538952 | tf_op jit(solution)/shard_map/ppermute | solution.py:24
  45.6 17.4 %collective-permute-start.3 = (bf16[192,1536]{1,0:T(8,128)(2,1)}, bf16[192,1536]{1,0:T(8,128)(2,1)}, u32[]{:S(2)}, u32[]{:S(2)}) collective-permute-start(bf16[192,1536]{1,0:T(8,128)(2,1)} %collective-permute-done.refs_0_), channel_id=1, source_target_pairs={{64,0},{128,64},{192,128},{256,192},{320,256},{384,320},{448,384},... | collective-permute-start | bytes 1769480 | tf_op jit(solution)/shard_map/ppermute | solution.py:201
  47.5 17.3 %collective-permute-start.5 = (bf16[192,1536]{1,0:T(8,128)(2,1)}, bf16[192,1536]{1,0:T(8,128)(2,1)}, u32[]{:S(2)}, u32[]{:S(2)}) collective-permute-start(bf16[192,1536]{1,0:T(8,128)(2,1)} %collective-permute-done.1.refs_1_), channel_id=1, source_target_pairs={{448,0},{0,64},{64,128},{128,192},{192,256},{256,320},{320,384},{3... | collective-permute-start | bytes 1769480 | tf_op jit(solution)/shard_map/ppermute | solution.py:201
  52.9 46.0 %all-to-all-start.1 = ((bf16[16,192,384]{2,1,0:T(8,128)(2,1)}), bf16[16,192,384]{2,1,0:T(8,128)(2,1)}, u32[]{:S(2)}, u32[]{:S(2)}) async-start(bf16[16,192,384]{2,1,0:T(8,128)(2,1)} %bitcast.4), calls=%async_computation.1 | async-start | bytes 4718592 | tf_op jit(solution)/shard_map/all_to_all | solution.py:218
  58.9 1.1 copy-start.4
  64.9 15.2 %collective-permute-start.4 = (bf16[192,1536]{1,0:T(8,128)(2,1)}, bf16[192,1536]{1,0:T(8,128)(2,1)}, u32[]{:S(2)}, u32[]{:S(2)}) collective-permute-start(bf16[192,1536]{1,0:T(8,128)(2,1)} %collective-permute-done.3.refs_2_), channel_id=1, source_target_pairs={{64,0},{128,64},{192,128},{256,192},{320,256},{384,320},{448,384},... | collective-permute-start | bytes 1769480 | tf_op jit(solution)/shard_map/ppermute | solution.py:201
  66.8 16.8 %collective-permute-start.7 = (bf16[192,1536]{1,0:T(8,128)(2,1)}, bf16[192,1536]{1,0:T(8,128)(2,1)}, u32[]{:S(2)}, u32[]{:S(2)}) collective-permute-start(bf16[192,1536]{1,0:T(8,128)(2,1)} %collective-permute-done.5.refs_3_), channel_id=1, source_target_pairs={{448,0},{0,64},{64,128},{128,192},{192,256},{256,320},{320,384},{3... | collective-permute-start | bytes 1769480 | tf_op jit(solution)/shard_map/ppermute | solution.py:201
  83.6 12.3 %collective-permute-start.6 = (bf16[192,1536]{1,0:T(8,128)(2,1)}, bf16[192,1536]{1,0:T(8,128)(2,1)}, u32[]{:S(2)}, u32[]{:S(2)}) collective-permute-start(bf16[192,1536]{1,0:T(8,128)(2,1)} %collective-permute-done.4.refs_0_), channel_id=1, source_target_pairs={{64,0},{128,64},{192,128},{256,192},{320,256},{384,320},{448,384},... | collective-permute-start | bytes 1769480 | tf_op jit(solution)/shard_map/ppermute | solution.py:201
  85.5 10.4 %copy-start.1 = (bf16[384,1536]{1,0:T(8,128)(2,1)S(1)}, bf16[384,1536]{1,0:T(8,128)(2,1)}, u32[]{:S(2)}) copy-start(bf16[384,1536]{1,0:T(8,128)(2,1)} %copy-done) | copy-start | bytes 3538948
  98.9 37.1 %all-to-all-start = ((bf16[16,192,384]{2,1,0:T(8,128)(2,1)}), bf16[16,192,384]{2,1,0:T(8,128)(2,1)S(1)}, u32[]{:S(2)}, u32[]{:S(2)}) async-start(bf16[16,192,384]{2,1,0:T(8,128)(2,1)} %bitcast.14), calls=%async_computation | async-start | bytes 4718592 | tf_op jit(solution)/shard_map/all_to_all | solution.py:232
  105.6 4.8 %copy-start.3 = (bf16[384]{0:T(512)(128)(2,1)S(1)}, bf16[384]{0:T(512)(128)(2,1)}, u32[]{:S(2)}) copy-start(bf16[384]{0:T(512)(128)(2,1)} %param.6) | copy-start | bytes 2308
  108.4 3.1 %collective-permute-start.8 = (f32[2,8,384]{2,1,0:T(8,128)S(1)}, f32[2,8,384]{2,1,0:T(8,128)S(1)}, u32[]{:S(2)}, u32[]{:S(2)}) collective-permute-start(f32[2,8,384]{2,1,0:T(8,128)S(1)} %shard_map.73.one_ref), channel_id=1, source_target_pairs={{0,8},{8,0},{1,9},{9,1},{2,10},{10,2},{3,11},{11,3},{4,12},{12,4},... | collective-permute-start | bytes 73736 | tf_op jit(solution)/shard_map/ppermute | solution.py:24
  137.2 20.6 %all-to-all-start.2 = ((f32[64,8,128]{2,1,0:T(8,128)}), f32[64,8,128]{2,1,0:T(8,128)S(1)}, u32[]{:S(2)}, u32[]{:S(2)}) async-start(f32[64,8,128]{2,1,0:T(8,128)} %bitcast.7), calls=%async_computation.2 | async-start | bytes 524288 | tf_op jit(solution)/shard_map/all_to_all | solution.py:257

commit v11 on v10

--- a/solution.py
+++ b/solution.py
@@ -171,11 +171,11 @@
 
 
 def final_kernel(here_ref, d_ref, x_ref, one_ref, two_ref, small_ref, out_ref, gain_ref):
-    core, zh = here_ref[0], here_ref[1]
+    core = here_ref[0]
     mean, rstd = mean_and_rstd(one_ref[core], two_ref[core])
-    total = small_ref[zh * 16 + core * 8]
+    total = small_ref[core * 8]
     for m in range(1, 8):
-        total += small_ref[zh * 16 + core * 8 + m]
+        total += small_ref[core * 8 + m]
     total = total * (1.0 / (2 * HALF))
     first, second = (jnp.concatenate([total[k + i : k + i + 1] for i in range(3)], axis=1) for k in (0, 3))
     xhat = (x_ref[...].astype(F32) - mean) * rstd
@@ -184,9 +184,8 @@
     rows = []
     for c in range(2):
         both = jnp.zeros((8, 128), F32)
-        for z in range(4):
-            for m in range(8):
-                both += small_ref[z * 16 + c * 8 + m]
+        for m in range(8):
+            both += small_ref[c * 8 + m]
         rows.append(jnp.concatenate([both[6:7], both[7:8]], axis=1))
     gain_ref[...] = jnp.concatenate(rows + [jnp.zeros((6, 256), F32)], axis=0)
 
@@ -227,17 +226,19 @@
     first4 = step(first, 1)
     parts = products([(3, first3), (5, second)], d_own, d_other, place, parts)
 
-    first4, parts = together((first4, parts))
-    parts = products([(4, first4)], d_own, d_other, place, parts)
-    received = lax.all_to_all(parts.reshape(16, share // 2, rows), CHIPS, 0, 0)
-
+    parts, x_all = together((parts, x_all))
     one = pl.pallas_call(
         stats_kernel,
         out_shape=jax.ShapeDtypeStruct((2, 8, rows), F32),
         compiler_params=PARAMS,
     )(x_all)
+
+    first4, parts, one = together((first4, parts, one))
+    parts = products([(4, first4)], d_own, d_other, place, parts)
+    received = lax.all_to_all(parts.reshape(16, share // 2, rows), CHIPS, 0, 0)
+
     two = partner(one, "c", 2, 1)
-    shares = lax.psum(gain_share(parts, x_all, one, two), "y")
+    shares = lax.psum(lax.psum(gain_share(parts, x_all, one, two), "y"), "zh")
 
     vmem, smem = pl.BlockSpec(memory_space=pltpu.VMEM), pl.BlockSpec(memory_space=pltpu.SMEM)
     d_scaled, moments = pl.pallas_call(
@@ -253,8 +254,7 @@
     small = jnp.concatenate(
         [jnp.broadcast_to(moments[None, :6], (8, 6, 128)), shares.reshape(8, 2, 128)], axis=1
     )
-    small = jnp.broadcast_to(small, (8, 8, 8, 128)).reshape(64, 8, 128)
-    small = lax.all_to_all(small, ("zh",) + CHIPS, 0, 0)
+    small = lax.all_to_all(jnp.concatenate([small, small], axis=0), CHIPS, 0, 0)
     token_gradient, gain_rows = pl.pallas_call(
         final_kernel,
         in_specs=[smem] + [vmem] * 5,
@@ -263,7 +263,7 @@
             jax.ShapeDtypeStruct((8, 256), F32),
         ],
         compiler_params=PARAMS,
-    )(jnp.concatenate([here[1], lax.axis_index("zh").astype(jnp.int32).reshape(1)]), d_scaled, x, one, two, small)
+    )(here[1], d_scaled, x, one, two, small)
     gain_gradient = jnp.swapaxes(gain_rows[:2, : share // 2].reshape(2, 4, SHARD), 0, 1).reshape(share)
     return (token_gradient, gain_gradient)
 

time: 161 us -> 155 us (0.963)
  blocking collectives: 36.9 us -> 62.4 us
  waiting for transfers between devices: 37.5 us -> 16.4 us
  starting transfers between devices: 49.2 us -> 40.8 us
    all_to_all x0 -> x1, blocking collectives: none -> 13.7 us  [on_device(): small = lax.all_to_all(jnp.concatenate([small, small], axis=0), CHIPS, 0, 0)]
    all_to_all x1 -> x0, waiting for transfers between devices: 12.1 us -> none  [on_device(): small = lax.all_to_all(small, ('zh',) + CHIPS, 0, 0)]
    psum x1 -> x2, blocking collectives: 14.5 us -> 26.2 us  [on_device(): shares = lax.psum(lax.psum(gain_share(parts, x_all, one, two), 'y'), 'zh')]
    all_to_all x1 -> x0, starting transfers between devices: 8.43 us -> none  [on_device(): small = lax.all_to_all(small, ('zh',) + CHIPS, 0, 0)]
    all_to_all x1, waiting for transfers between devices: 6.42 us -> 0.01 us  [on_device(): received = lax.all_to_all(parts.reshape(16, share // 2, rows), CHIPS, 0, 0)]
    ppermute x7, waiting for transfers between devices: 18 us -> 15.4 us  [step(): lax.ppermute(array, ('y', 'c'), [(a * 2 + c, b * 2 + c) for a, b, c in mo...]
  transfers between devices with their start and end apart: 12 -> 11, of which waited for: 8 -> 6; matrix products, arithmetic and copies ran while one was open for 4% -> 5% of each run, Pallas kernels for 15% -> 13%
where the time goes in v11:
time: 155 us
  blocking collectives  62.4 us (40%)
  starting transfers between devices  40.8 us (26%)
  Pallas kernels  25.2 us (16%)
  waiting for transfers between devices  16.4 us (11%)
  other arithmetic  6.89 us (4%)
  local copies, waits for them, and re-layouts  2 us (1%)
    psum x2, blocking collectives, on_device(): shares = lax.psum(lax.psum(gain_share(parts, x_all, one, two), 'y'), 'zh')  26.2 us
    ppermute x7, starting transfers between devices, step(): lax.ppermute(array, ('y', 'c'), [(a * 2 + c, b * 2 + c) for a, b, c in mo...  23.5 us
    all_gather x1, blocking collectives, on_device(): w0 = lax.all_gather(w_in, 'zh', axis=0, tiled=True)  22.4 us
    pallas_call x4, Pallas kernels, products(): pl.pallas_call(kernel, in_specs=[pl.BlockSpec(memory_space=pltpu.SMEM)] +...  15.6 us
    ppermute x7, waiting for transfers between devices, step(): lax.ppermute(array, ('y', 'c'), [(a * 2 + c, b * 2 + c) for a, b, c in mo...  15.4 us
    all_to_all x1, blocking collectives, on_device(): small = lax.all_to_all(jnp.concatenate([small, small], axis=0), CHIPS, 0, 0)  13.7 us
    convert_element_type x1, other arithmetic, on_device(): d_own = gelu_back(act_cotangent.astype(F32))[0].astype(BF16)  6.81 us
    all_to_all x1, starting transfers between devices, on_device(): received = lax.all_to_all(parts.reshape(16, share // 2, rows), CHIPS, 0, 0)  6.7 us
  transfers between devices with their start and end apart: 11, of which 6 were waited for; matrix products, arithmetic and copies ran while one was open for 5% of the time, Pallas kernels for 13%

profile of v11, /device:TPU:1, one launch (start us, length us, event | category | flops | bytes accessed | tf_op | source)
XLA Modules:
  0.0 154.6 jit_solution(4944826994943982615)
XLA Ops:
  0.6 0.0 copy-start.2
  0.6 22.4 %all_gather.3.refs_0_ = bf16[192,1536]{1,0:T(8,128)(2,1)S(1)} all-gather(bf16[48,1536]{1,0:T(8,128)(2,1)} %param.8), channel_id=1, replica_groups=mesh['y'=8,'zh'=4,'c'=2,'zl'=2,'x'=4] {'zh'}, dimensions={0}, use_global_device_ids=true | all-gather | bytes 737280 | tf_op jit(solution)/shard_map/all_gather | solution.py:206
  23.0 3.2 %collective-permute-start = (bf16[192,1536]{1,0:T(8,128)(2,1)S(1)}, bf16[192,1536]{1,0:T(8,128)(2,1)}, u32[]{:S(2)}, u32[]{:S(2)}) collective-permute-start(bf16[192,1536]{1,0:T(8,128)(2,1)S(1)} %all_gather.3.refs_0_), channel_id=1, source_target_pairs={{64,0},{128,64},{192,128},{256,192},{320,256},{384,320},{448,384},... | collective-permute-start | bytes 1769480 | tf_op jit(solution)/shard_map/ppermute | solution.py:200
  26.2 3.8 %collective-permute-start.1 = (bf16[192,1536]{1,0:T(8,128)(2,1)S(1)}, bf16[192,1536]{1,0:T(8,128)(2,1)}, u32[]{:S(2)}, u32[]{:S(2)}) collective-permute-start(bf16[192,1536]{1,0:T(8,128)(2,1)S(1)} %all_gather.3.refs_0_), channel_id=1, source_target_pairs={{448,0},{0,64},{64,128},{128,192},{192,256},{256,320},{320,384},{3... | collective-permute-start | bytes 1769480 | tf_op jit(solution)/shard_map/ppermute | solution.py:200
  30.0 6.8 %fusion.34.own_ref = bf16[384,1536]{1,0:T(8,128)(2,1)S(1)} fusion(bf16[384,1536]{1,0:T(8,128)(2,1)} %param.9, bf16[384,1536]{1,0:T(8,128)(2,1)} %param.7), kind=kLoop, calls=%fused_computation.39 | loop fusion | flops 43646976 | bytes 3538944 | tf_op jit(solution)/shard_map/convert_element_type | solution.py:210
  36.9 0.0 copy-done.2
  36.9 0.0 copy-start
  36.9 1.8 %shard_map.68 = (bf16[384,384]{1,0:T(8,128)(2,1)S(1)}, bf16[2,8,192,384]{3,2,1,0:T(8,128)(2,1)}) custom-call(bf16[384,384]{1,0:T(8,128)(2,1)S(1)} %copy-done.2), custom_call_target="tpu_custom_call" | custom-call | tf_op jit(solution)/shard_map/pallas_call | solution.py:86
  38.7 0.0 collective-permute-done.refs_0_
  38.7 4.2 %collective-permute-done.1.refs_1_ = bf16[192,1536]{1,0:T(8,128)(2,1)} collective-permute-done((bf16[192,1536]{1,0:T(8,128)(2,1)S(1)}, bf16[192,1536]{1,0:T(8,128)(2,1)}, u32[]{:S(2)}, u32[]{:S(2)}) %collective-permute-start.1) | collective-permute-done | bytes 589856 | tf_op jit(solution)/shard_map/ppermute | solution.py:200
  42.9 2.6 %collective-permute-start.2 = (bf16[384,1536]{1,0:T(8,128)(2,1)S(1)}, bf16[384,1536]{1,0:T(8,128)(2,1)S(1)}, u32[]{:S(2)}, u32[]{:S(2)}) collective-permute-start(bf16[384,1536]{1,0:T(8,128)(2,1)S(1)} %fusion.34.own_ref), channel_id=1, source_target_pairs={{0,8},{8,0},{1,9},{9,1},{2,10},{10,2},{3,11},{11,3},{4,12},{12,4},... | collective-permute-start | bytes 3538952 | tf_op jit(solution)/shard_map/ppermute | solution.py:24
  45.5 0.1 pad_add_fusion.place_ref
  45.6 2.0 %collective-permute-start.3 = (bf16[192,1536]{1,0:T(8,128)(2,1)}, bf16[192,1536]{1,0:T(8,128)(2,1)}, u32[]{:S(2)}, u32[]{:S(2)}) collective-permute-start(bf16[192,1536]{1,0:T(8,128)(2,1)} %collective-permute-done.refs_0_), channel_id=1, source_target_pairs={{64,0},{128,64},{192,128},{256,192},{320,256},{384,320},{448,384},... | collective-permute-start | bytes 1769480 | tf_op jit(solution)/shard_map/ppermute | solution.py:200
  47.5 5.4 %collective-permute-start.5 = (bf16[192,1536]{1,0:T(8,128)(2,1)}, bf16[192,1536]{1,0:T(8,128)(2,1)}, u32[]{:S(2)}, u32[]{:S(2)}) collective-permute-start(bf16[192,1536]{1,0:T(8,128)(2,1)} %collective-permute-done.1.refs_1_), channel_id=1, source_target_pairs={{448,0},{0,64},{64,128},{128,192},{192,256},{256,320},{320,384},{3... | collective-permute-start | bytes 1769480 | tf_op jit(solution)/shard_map/ppermute | solution.py:200
  52.9 6.0 %all-to-all-start = ((bf16[16,192,384]{2,1,0:T(8,128)(2,1)}), bf16[16,192,384]{2,1,0:T(8,128)(2,1)}, u32[]{:S(2)}, u32[]{:S(2)}) async-start(bf16[16,192,384]{2,1,0:T(8,128)(2,1)} %bitcast.2), calls=%async_computation | async-start | bytes 4718592 | tf_op jit(solution)/shard_map/all_to_all | solution.py:217
  58.9 0.0 collective-permute-done.2.other_ref
  58.9 0.0 copy-done
  58.9 0.0 copy-start.4
  59.0 1.1 copy-done.4
  60.0 2.8 %shard_map.69.refs_4_ = bf16[2,8,192,384]{3,2,1,0:T(8,128)(2,1)} custom-call(s32[2]{0:T(128)S(1)} %pad_add_fusion.place_ref, bf16[384,1536]{1,0:T(8,128)(2,1)S(1)} %fusion.34.own_ref, bf16[384,1536]{1,0:T(8,128)(2,1)} %copy-done.4, bf16[192,1536]{1,0:T(8,128)(2,1)S(1)} %all_gather.3.refs_0_), custom_call_target="tpu_custom_call" | custom-call | flops 274877906944 | bytes 67108864 | tf_op jit(solution)/shard_map/pallas_call | solution.py:51
  62.9 0.0 collective-permute-done.3.refs_2_
  62.9 2.0 %collective-permute-done.5.refs_3_ = bf16[192,1536]{1,0:T(8,128)(2,1)} collective-permute-done((bf16[192,1536]{1,0:T(8,128)(2,1)}, bf16[192,1536]{1,0:T(8,128)(2,1)}, u32[]{:S(2)}, u32[]{:S(2)}) %collective-permute-start.5) | collective-permute-done | bytes 589856 | tf_op jit(solution)/shard_map/ppermute | solution.py:200
  64.9 1.9 %collective-permute-start.4 = (bf16[192,1536]{1,0:T(8,128)(2,1)}, bf16[192,1536]{1,0:T(8,128)(2,1)}, u32[]{:S(2)}, u32[]{:S(2)}) collective-permute-start(bf16[192,1536]{1,0:T(8,128)(2,1)} %collective-permute-done.3.refs_2_), channel_id=1, source_target_pairs={{64,0},{128,64},{192,128},{256,192},{320,256},{384,320},{448,384},... | collective-permute-start | bytes 1769480 | tf_op jit(solution)/shard_map/ppermute | solution.py:200
  66.8 5.3 %collective-permute-start.7 = (bf16[192,1536]{1,0:T(8,128)(2,1)}, bf16[192,1536]{1,0:T(8,128)(2,1)}, u32[]{:S(2)}, u32[]{:S(2)}) collective-permute-start(bf16[192,1536]{1,0:T(8,128)(2,1)} %collective-permute-done.5.refs_3_), channel_id=1, source_target_pairs={{448,0},{0,64},{64,128},{128,192},{192,256},{256,320},{320,384},{3... | collective-permute-start | bytes 1769480 | tf_op jit(solution)/shard_map/ppermute | solution.py:200
  72.1 5.7 %shard_map.70.refs_2_ = bf16[2,8,192,384]{3,2,1,0:T(8,128)(2,1)} custom-call(s32[2]{0:T(128)S(1)} %pad_add_fusion.place_ref, bf16[384,1536]{1,0:T(8,128)(2,1)} %copy-done, bf16[384,1536]{1,0:T(8,128)(2,1)} %copy-done.4, bf16[192,1536]{1,0:T(8,128)(2,1)} %collective-permute-done.refs_0_, ...), custom_call_target="tpu_custom_call", output_to_operand_aliasing={{}: (7, {})} | custom-call | flops 274877906944 | bytes 67108864 | tf_op jit(solution)/shard_map/pallas_call | solution.py:51
  77.8 2.3 %collective-permute-done.4.refs_0_ = bf16[192,1536]{1,0:T(8,128)(2,1)} collective-permute-done((bf16[192,1536]{1,0:T(8,128)(2,1)}, bf16[192,1536]{1,0:T(8,128)(2,1)}, u32[]{:S(2)}, u32[]{:S(2)}) %collective-permute-start.4) | collective-permute-done | bytes 589856 | tf_op jit(solution)/shard_map/ppermute | solution.py:200
  80.1 3.4 %collective-permute-done.7.refs_1_ = bf16[192,1536]{1,0:T(8,128)(2,1)} collective-permute-done((bf16[192,1536]{1,0:T(8,128)(2,1)}, bf16[192,1536]{1,0:T(8,128)(2,1)}, u32[]{:S(2)}, u32[]{:S(2)}) %collective-permute-start.7) | collective-permute-done | bytes 589856 | tf_op jit(solution)/shard_map/ppermute | solution.py:200
  83.6 1.9 %collective-permute-start.6 = (bf16[192,1536]{1,0:T(8,128)(2,1)}, bf16[192,1536]{1,0:T(8,128)(2,1)}, u32[]{:S(2)}, u32[]{:S(2)}) collective-permute-start(bf16[192,1536]{1,0:T(8,128)(2,1)} %collective-permute-done.4.refs_0_), channel_id=1, source_target_pairs={{64,0},{128,64},{192,128},{256,192},{320,256},{384,320},{448,384},... | collective-permute-start | bytes 1769480 | tf_op jit(solution)/shard_map/ppermute | solution.py:200
  85.5 4.0 %shard_map.71.refs_1_ = bf16[2,8,192,384]{3,2,1,0:T(8,128)(2,1)} custom-call(s32[2]{0:T(128)S(1)} %pad_add_fusion.place_ref, bf16[384,1536]{1,0:T(8,128)(2,1)} %copy-done, bf16[384,1536]{1,0:T(8,128)(2,1)} %copy-done.4, bf16[192,1536]{1,0:T(8,128)(2,1)} %collective-permute-done.4.refs_0_, ...), custom_call_target="tpu_custom_call", output_to_operand_aliasing={{}: (5, {})} | custom-call | flops 274877906944 | bytes 67108864 | tf_op jit(solution)/shard_map/pallas_call | solution.py:51
  89.5 0.0 copy-start.1
  89.5 0.0 all-to-all-done.x_ref
  89.6 2.8 %shard_map.72.one_ref = f32[2,8,384]{2,1,0:T(8,128)S(1)} custom-call(bf16[16,192,384]{2,1,0:T(8,128)(2,1)} %all-to-all-done.x_ref), custom_call_target="tpu_custom_call" | custom-call | tf_op jit(solution)/shard_map/pallas_call | solution.py:230
  92.4 3.5 %collective-permute-done.6.refs_0_ = bf16[192,1536]{1,0:T(8,128)(2,1)} collective-permute-done((bf16[192,1536]{1,0:T(8,128)(2,1)}, bf16[192,1536]{1,0:T(8,128)(2,1)}, u32[]{:S(2)}, u32[]{:S(2)}) %collective-permute-start.6) | collective-permute-done | bytes 589856 | tf_op jit(solution)/shard_map/ppermute | solution.py:200
  95.9 3.0 %shard_map.73.parts_ref = bf16[2,8,192,384]{3,2,1,0:T(8,128)(2,1)} custom-call(s32[2]{0:T(128)S(1)} %pad_add_fusion.place_ref, bf16[384,1536]{1,0:T(8,128)(2,1)S(1)} %copy-done.1, bf16[384,1536]{1,0:T(8,128)(2,1)} %copy-done.4, bf16[192,1536]{1,0:T(8,128)(2,1)} %collective-permute-done.6.refs_0_, ...), custom_call_target="tpu_custom_call", output_to_operand_aliasing={{}: (4, {})} | custom-call | flops 274877906944 | bytes 67108864 | tf_op jit(solution)/shard_map/pallas_call | solution.py:51
  98.9 0.0 copy-start.3
  98.9 6.7 %all-to-all-start.1 = ((bf16[16,192,384]{2,1,0:T(8,128)(2,1)}), bf16[16,192,384]{2,1,0:T(8,128)(2,1)S(1)}, u32[]{:S(2)}, u32[]{:S(2)}) async-start(bf16[16,192,384]{2,1,0:T(8,128)(2,1)} %bitcast.10), calls=%async_computation.1 | async-start | bytes 4718592 | tf_op jit(solution)/shard_map/all_to_all | solution.py:238
  105.6 2.0 %collective-permute-start.8 = (f32[2,8,384]{2,1,0:T(8,128)S(1)}, f32[2,8,384]{2,1,0:T(8,128)S(1)}, u32[]{:S(2)}, u32[]{:S(2)}) collective-permute-start(f32[2,8,384]{2,1,0:T(8,128)S(1)} %shard_map.72.one_ref), channel_id=1, source_target_pairs={{0,8},{8,0},{1,9},{9,1},{2,10},{10,2},{3,11},{11,3},{4,12},{12,4},... | collective-permute-start | bytes 73736 | tf_op jit(solution)/shard_map/ppermute | solution.py:24
  107.6 0.1 reshape.38.gain_ref
  107.8 0.9 collective-permute-done.8.two_ref
  108.7 3.6 %shard_map.75 = f32[8,256]{1,0:T(8,128)S(1)} custom-call(bf16[2,8,192,384]{3,2,1,0:T(8,128)(2,1)} %shard_map.73.parts_ref, bf16[2,8,192,384]{3,2,1,0:T(8,128)(2,1)} %bitcast.4.x_ref, f32[2,8,384]{2,1,0:T(8,128)S(1)} %shard_map.72.one_ref, f32[2,8,384]{2,1,0:T(8,128)S(1)} %collective-permute-done.8.two_ref), custom_call_target="tpu_custom_call" | custom-call | tf_op jit(solution)/shard_map/pallas_call | solution.py:144
  112.3 14.8 %psum.14 = f32[8,256]{1,0:T(8,128)S(1)} all-reduce(f32[8,256]{1,0:T(8,128)S(1)} %shard_map.75), channel_id=1, replica_groups=mesh['y'=8,'zh'=4,'c'=2,'zl'=2,'x'=4] {'y'}, use_global_device_ids=true, to_apply=%region_0.0 | all-reduce | flops 2048 | bytes 16384 | tf_op jit(solution)/shard_map/psum | solution.py:241
  127.1 11.5 %psum.15 = f32[8,2,128]{2,1,0:T(2,128)S(1)} all-reduce(f32[8,2,128]{2,1,0:T(2,128)S(1)} %reshape.34), channel_id=1, replica_groups=mesh['y'=8,'zh'=4,'c'=2,'zl'=2,'x'=4] {'zh'}, use_global_device_ids=true, to_apply=%region_1.0 | all-reduce | flops 2048 | bytes 16384 | tf_op jit(solution)/shard_map/psum | solution.py:241
  138.6 0.0 all-to-all-done.1.parts_ref
  138.6 0.5 shard_map.74
  139.1 13.7 %all_to_all.15.small_ref = f32[16,8,128]{2,1,0:T(8,128)S(1)} all-to-all(f32[16,8,128]{2,1,0:T(8,128)S(1)} %maximum_maximum_fusion), channel_id=1, replica_groups=mesh['y'=8,'zh'=4,'c'=2,'zl'=2,'x'=4] {'c','zl','x'}, dimensions={0} | all-to-all | bytes 131072 | tf_op jit(solution)/shard_map/all_to_all | solution.py:257
  152.8 1.0 shard_map.76
  153.8 0.1 reshape.35
  153.9 0.7 reshape.36
  (7 shorter events, 0.0 us)
Async XLA Ops:
  0.6 36.2 %copy-start.2 = (bf16[384,384]{1,0:T(8,128)(2,1)S(1)}, bf16[384,384]{1,0:T(8,128)(2,1)}, u32[]{:S(2)}) copy-start(bf16[384,384]{1,0:T(8,128)(2,1)} %tokens_ref) | copy-start | bytes 884740
  23.0 15.7 %collective-permute-start = (bf16[192,1536]{1,0:T(8,128)(2,1)S(1)}, bf16[192,1536]{1,0:T(8,128)(2,1)}, u32[]{:S(2)}, u32[]{:S(2)}) collective-permute-start(bf16[192,1536]{1,0:T(8,128)(2,1)S(1)} %all_gather.3.refs_0_), channel_id=1, source_target_pairs={{64,0},{128,64},{192,128},{256,192},{320,256},{384,320},{448,384},... | collective-permute-start | bytes 1769480 | tf_op jit(solution)/shard_map/ppermute | solution.py:200
  26.2 16.7 %collective-permute-start.1 = (bf16[192,1536]{1,0:T(8,128)(2,1)S(1)}, bf16[192,1536]{1,0:T(8,128)(2,1)}, u32[]{:S(2)}, u32[]{:S(2)}) collective-permute-start(bf16[192,1536]{1,0:T(8,128)(2,1)S(1)} %all_gather.3.refs_0_), channel_id=1, source_target_pairs={{448,0},{0,64},{64,128},{128,192},{192,256},{256,320},{320,384},{3... | collective-permute-start | bytes 1769480 | tf_op jit(solution)/shard_map/ppermute | solution.py:200
  36.9 22.1 %copy-start = (bf16[384,1536]{1,0:T(8,128)(2,1)}, bf16[384,1536]{1,0:T(8,128)(2,1)S(1)}, u32[]{:S(2)}) copy-start(bf16[384,1536]{1,0:T(8,128)(2,1)S(1)} %fusion.34.own_ref) | copy-start | bytes 3538948
  42.9 16.0 %collective-permute-start.2 = (bf16[384,1536]{1,0:T(8,128)(2,1)S(1)}, bf16[384,1536]{1,0:T(8,128)(2,1)S(1)}, u32[]{:S(2)}, u32[]{:S(2)}) collective-permute-start(bf16[384,1536]{1,0:T(8,128)(2,1)S(1)} %fusion.34.own_ref), channel_id=1, source_target_pairs={{0,8},{8,0},{1,9},{9,1},{2,10},{10,2},{3,11},{11,3},{4,12},{12,4},... | collective-permute-start | bytes 3538952 | tf_op jit(solution)/shard_map/ppermute | solution.py:24
  45.6 17.3 %collective-permute-start.3 = (bf16[192,1536]{1,0:T(8,128)(2,1)}, bf16[192,1536]{1,0:T(8,128)(2,1)}, u32[]{:S(2)}, u32[]{:S(2)}) collective-permute-start(bf16[192,1536]{1,0:T(8,128)(2,1)} %collective-permute-done.refs_0_), channel_id=1, source_target_pairs={{64,0},{128,64},{192,128},{256,192},{320,256},{384,320},{448,384},... | collective-permute-start | bytes 1769480 | tf_op jit(solution)/shard_map/ppermute | solution.py:200
  47.5 17.3 %collective-permute-start.5 = (bf16[192,1536]{1,0:T(8,128)(2,1)}, bf16[192,1536]{1,0:T(8,128)(2,1)}, u32[]{:S(2)}, u32[]{:S(2)}) collective-permute-start(bf16[192,1536]{1,0:T(8,128)(2,1)} %collective-permute-done.1.refs_1_), channel_id=1, source_target_pairs={{448,0},{0,64},{64,128},{128,192},{192,256},{256,320},{320,384},{3... | collective-permute-start | bytes 1769480 | tf_op jit(solution)/shard_map/ppermute | solution.py:200
  52.9 36.6 %all-to-all-start = ((bf16[16,192,384]{2,1,0:T(8,128)(2,1)}), bf16[16,192,384]{2,1,0:T(8,128)(2,1)}, u32[]{:S(2)}, u32[]{:S(2)}) async-start(bf16[16,192,384]{2,1,0:T(8,128)(2,1)} %bitcast.2), calls=%async_computation | async-start | bytes 4718592 | tf_op jit(solution)/shard_map/all_to_all | solution.py:217
  58.9 1.1 copy-start.4
  64.9 15.2 %collective-permute-start.4 = (bf16[192,1536]{1,0:T(8,128)(2,1)}, bf16[192,1536]{1,0:T(8,128)(2,1)}, u32[]{:S(2)}, u32[]{:S(2)}) collective-permute-start(bf16[192,1536]{1,0:T(8,128)(2,1)} %collective-permute-done.3.refs_2_), channel_id=1, source_target_pairs={{64,0},{128,64},{192,128},{256,192},{320,256},{384,320},{448,384},... | collective-permute-start | bytes 1769480 | tf_op jit(solution)/shard_map/ppermute | solution.py:200
  66.8 16.8 %collective-permute-start.7 = (bf16[192,1536]{1,0:T(8,128)(2,1)}, bf16[192,1536]{1,0:T(8,128)(2,1)}, u32[]{:S(2)}, u32[]{:S(2)}) collective-permute-start(bf16[192,1536]{1,0:T(8,128)(2,1)} %collective-permute-done.5.refs_3_), channel_id=1, source_target_pairs={{448,0},{0,64},{64,128},{128,192},{192,256},{256,320},{320,384},{3... | collective-permute-start | bytes 1769480 | tf_op jit(solution)/shard_map/ppermute | solution.py:200
  83.6 12.3 %collective-permute-start.6 = (bf16[192,1536]{1,0:T(8,128)(2,1)}, bf16[192,1536]{1,0:T(8,128)(2,1)}, u32[]{:S(2)}, u32[]{:S(2)}) collective-permute-start(bf16[192,1536]{1,0:T(8,128)(2,1)} %collective-permute-done.4.refs_0_), channel_id=1, source_target_pairs={{64,0},{128,64},{192,128},{256,192},{320,256},{384,320},{448,384},... | collective-permute-start | bytes 1769480 | tf_op jit(solution)/shard_map/ppermute | solution.py:200
  89.5 6.3 %copy-start.1 = (bf16[384,1536]{1,0:T(8,128)(2,1)S(1)}, bf16[384,1536]{1,0:T(8,128)(2,1)}, u32[]{:S(2)}) copy-start(bf16[384,1536]{1,0:T(8,128)(2,1)} %copy-done) | copy-start | bytes 3538948
  98.9 8.7 %copy-start.3 = (bf16[384]{0:T(512)(128)(2,1)S(1)}, bf16[384]{0:T(512)(128)(2,1)}, u32[]{:S(2)}) copy-start(bf16[384]{0:T(512)(128)(2,1)} %param.6) | copy-start | bytes 2308
  98.9 39.7 %all-to-all-start.1 = ((bf16[16,192,384]{2,1,0:T(8,128)(2,1)}), bf16[16,192,384]{2,1,0:T(8,128)(2,1)S(1)}, u32[]{:S(2)}, u32[]{:S(2)}) async-start(bf16[16,192,384]{2,1,0:T(8,128)(2,1)} %bitcast.10), calls=%async_computation.1 | async-start | bytes 4718592 | tf_op jit(solution)/shard_map/all_to_all | solution.py:238
  105.6 3.1 %collective-permute-start.8 = (f32[2,8,384]{2,1,0:T(8,128)S(1)}, f32[2,8,384]{2,1,0:T(8,128)S(1)}, u32[]{:S(2)}, u32[]{:S(2)}) collective-permute-start(f32[2,8,384]{2,1,0:T(8,128)S(1)} %shard_map.72.one_ref), channel_id=1, source_target_pairs={{0,8},{8,0},{1,9},{9,1},{2,10},{10,2},{3,11},{11,3},{4,12},{12,4},... | collective-permute-start | bytes 73736 | tf_op jit(solution)/shard_map/ppermute | solution.py:24

commit v12 on v11

--- a/solution.py
+++ b/solution.py
@@ -24,7 +24,7 @@
     return lax.ppermute(array, axis, [(i, i ^ bit) for i in range(n)])
 
 
-def products(groups, d_own, d_other, place, parts):
+def products(groups, d_own, d_other, place, parts, long=False):
     tokens, hidden = d_own.shape
     weights = [w for _, w in groups]
     rows, n = weights[0].shape[0], len(groups)
@@ -62,7 +62,7 @@
         input_output_aliases={} if parts is None else {3 + n: 0},
         compiler_params=WIDE,
         cost_estimate=pl.CostEstimate(
-            flops=1 << 38, bytes_accessed=64 << 20, transcendentals=0
+            flops=1 << 38 if long else rows * hidden * tokens, bytes_accessed=1 << 18, transcendentals=0
         ),
     )(place, d_own, d_other, *weights, *([] if parts is None else [parts]))
 
@@ -215,7 +215,7 @@
     first2, second2 = step(first, 1), step(second, -1)
     d_other = partner(d_own, "c", 2, 1)
     x_all = lax.all_to_all(x_all.reshape(16, share // 2, rows), CHIPS, 0, 0)
-    parts = products([(0, w0)], d_own, d_other, place, None)
+    parts = products([(0, w0)], d_own, d_other, place, None, long=True)
 
     first, second, parts = tie(first2, second2, parts)
     first3, second3 = step(first, 1), step(second, -1)
@@ -233,11 +233,12 @@
         compiler_params=PARAMS,
     )(x_all)
 
+    two = partner(one, "c", 2, 1)
+
     first4, parts, one = together((first4, parts, one))
     parts = products([(4, first4)], d_own, d_other, place, parts)
     received = lax.all_to_all(parts.reshape(16, share // 2, rows), CHIPS, 0, 0)
 
-    two = partner(one, "c", 2, 1)
     shares = lax.psum(lax.psum(gain_share(parts, x_all, one, two), "y"), "zh")
 
     vmem, smem = pl.BlockSpec(memory_space=pltpu.VMEM), pl.BlockSpec(memory_space=pltpu.SMEM)

time: 155 us -> 155 us (level)
  waiting for transfers between devices: 16.4 us -> 13.1 us
  starting transfers between devices: 40.8 us -> 43.5 us
    ppermute x7, waiting for transfers between devices: 15.4 us -> 9.43 us  [step(): lax.ppermute(array, ('y', 'c'), [(a * 2 + c, b * 2 + c) for a, b, c in mo...]
    all_to_all x1, starting transfers between devices: 6.7 us -> 9.44 us  [on_device(): received = lax.all_to_all(parts.reshape(16, share // 2, rows), CHIPS, 0, 0)]
    all_to_all x1, waiting for transfers between devices: 0.01 us -> 2.67 us  [on_device(): x_all = lax.all_to_all(x_all.reshape(16, share // 2, rows), CHIPS, 0, 0)]
  transfers between devices with their start and end apart: 11 -> 11, of which waited for: 6 -> 5; matrix products, arithmetic and copies ran while one was open for 5% -> 5% of each run, Pallas kernels for 13% -> 13%
where the time goes in v12:
time: 155 us; the launch traced here: 154 us
  blocking collectives  62.9 us (41%)
  starting transfers between devices  43.5 us (28%)
  Pallas kernels  24.7 us (16%)
  waiting for transfers between devices  13.1 us (8%)
  other arithmetic  6.89 us (4%)
  local copies, waits for them, and re-layouts  2 us (1%)
    psum x2, blocking collectives, on_device(): shares = lax.psum(lax.psum(gain_share(parts, x_all, one, two), 'y'), 'zh')  25.8 us
    ppermute x7, starting transfers between devices, step(): lax.ppermute(array, ('y', 'c'), [(a * 2 + c, b * 2 + c) for a, b, c in mo...  23.5 us
    all_gather x1, blocking collectives, on_device(): w0 = lax.all_gather(w_in, 'zh', axis=0, tiled=True)  22.4 us
    pallas_call x4, Pallas kernels, products(): pl.pallas_call(kernel, in_specs=[pl.BlockSpec(memory_space=pltpu.SMEM)] +...  15.1 us
    all_to_all x1, blocking collectives, on_device(): small = lax.all_to_all(jnp.concatenate([small, small], axis=0), CHIPS, 0, 0)  14.7 us
    all_to_all x1, starting transfers between devices, on_device(): received = lax.all_to_all(parts.reshape(16, share // 2, rows), CHIPS, 0, 0)  9.44 us
    ppermute x7, waiting for transfers between devices, step(): lax.ppermute(array, ('y', 'c'), [(a * 2 + c, b * 2 + c) for a, b, c in mo...  9.43 us
    convert_element_type x1, other arithmetic, on_device(): d_own = gelu_back(act_cotangent.astype(F32))[0].astype(BF16)  6.81 us
  transfers between devices with their start and end apart: 11, of which 5 were waited for; matrix products, arithmetic and copies ran while one was open for 5% of the time, Pallas kernels for 13%

profile of v12, /device:TPU:1, one launch (start us, length us, event | category | flops | bytes accessed | tf_op | source)
XLA Modules:
  0.0 153.9 jit_solution(12118794255460462874)
XLA Ops:
  0.6 0.0 copy-start.2
  0.6 22.4 %all_gather.3.refs_0_ = bf16[192,1536]{1,0:T(8,128)(2,1)S(1)} all-gather(bf16[48,1536]{1,0:T(8,128)(2,1)} %param.8), channel_id=1, replica_groups=mesh['y'=8,'zh'=4,'c'=2,'zl'=2,'x'=4] {'zh'}, dimensions={0}, use_global_device_ids=true | all-gather | bytes 737280 | tf_op jit(solution)/shard_map/all_gather | solution.py:206
  23.0 3.2 %collective-permute-start = (bf16[192,1536]{1,0:T(8,128)(2,1)S(1)}, bf16[192,1536]{1,0:T(8,128)(2,1)}, u32[]{:S(2)}, u32[]{:S(2)}) collective-permute-start(bf16[192,1536]{1,0:T(8,128)(2,1)S(1)} %all_gather.3.refs_0_), channel_id=1, source_target_pairs={{64,0},{128,64},{192,128},{256,192},{320,256},{384,320},{448,384},... | collective-permute-start | bytes 1769480 | tf_op jit(solution)/shard_map/ppermute | solution.py:200
  26.2 3.8 %collective-permute-start.1 = (bf16[192,1536]{1,0:T(8,128)(2,1)S(1)}, bf16[192,1536]{1,0:T(8,128)(2,1)}, u32[]{:S(2)}, u32[]{:S(2)}) collective-permute-start(bf16[192,1536]{1,0:T(8,128)(2,1)S(1)} %all_gather.3.refs_0_), channel_id=1, source_target_pairs={{448,0},{0,64},{64,128},{128,192},{192,256},{256,320},{320,384},{3... | collective-permute-start | bytes 1769480 | tf_op jit(solution)/shard_map/ppermute | solution.py:200
  30.0 6.8 %fusion.34.own_ref = bf16[384,1536]{1,0:T(8,128)(2,1)S(1)} fusion(bf16[384,1536]{1,0:T(8,128)(2,1)} %param.9, bf16[384,1536]{1,0:T(8,128)(2,1)} %param.7), kind=kLoop, calls=%fused_computation.39 | loop fusion | flops 43646976 | bytes 3538944 | tf_op jit(solution)/shard_map/convert_element_type | solution.py:210
  36.9 0.0 copy-done.2
  36.9 0.0 copy-start
  36.9 1.8 %shard_map.68 = (bf16[384,384]{1,0:T(8,128)(2,1)S(1)}, bf16[2,8,192,384]{3,2,1,0:T(8,128)(2,1)}) custom-call(bf16[384,384]{1,0:T(8,128)(2,1)S(1)} %copy-done.2), custom_call_target="tpu_custom_call" | custom-call | tf_op jit(solution)/shard_map/pallas_call | solution.py:86
  38.7 0.0 collective-permute-done.refs_0_
  38.7 4.2 %collective-permute-done.1.refs_1_ = bf16[192,1536]{1,0:T(8,128)(2,1)} collective-permute-done((bf16[192,1536]{1,0:T(8,128)(2,1)S(1)}, bf16[192,1536]{1,0:T(8,128)(2,1)}, u32[]{:S(2)}, u32[]{:S(2)}) %collective-permute-start.1) | collective-permute-done | bytes 589856 | tf_op jit(solution)/shard_map/ppermute | solution.py:200
  42.9 2.6 %collective-permute-start.2 = (bf16[384,1536]{1,0:T(8,128)(2,1)S(1)}, bf16[384,1536]{1,0:T(8,128)(2,1)S(1)}, u32[]{:S(2)}, u32[]{:S(2)}) collective-permute-start(bf16[384,1536]{1,0:T(8,128)(2,1)S(1)} %fusion.34.own_ref), channel_id=1, source_target_pairs={{0,8},{8,0},{1,9},{9,1},{2,10},{10,2},{3,11},{11,3},{4,12},{12,4},... | collective-permute-start | bytes 3538952 | tf_op jit(solution)/shard_map/ppermute | solution.py:24
  45.5 0.1 pad_add_fusion.place_ref
  45.6 2.0 %collective-permute-start.3 = (bf16[192,1536]{1,0:T(8,128)(2,1)}, bf16[192,1536]{1,0:T(8,128)(2,1)}, u32[]{:S(2)}, u32[]{:S(2)}) collective-permute-start(bf16[192,1536]{1,0:T(8,128)(2,1)} %collective-permute-done.refs_0_), channel_id=1, source_target_pairs={{64,0},{128,64},{192,128},{256,192},{320,256},{384,320},{448,384},... | collective-permute-start | bytes 1769480 | tf_op jit(solution)/shard_map/ppermute | solution.py:200
  47.5 5.4 %collective-permute-start.5 = (bf16[192,1536]{1,0:T(8,128)(2,1)}, bf16[192,1536]{1,0:T(8,128)(2,1)}, u32[]{:S(2)}, u32[]{:S(2)}) collective-permute-start(bf16[192,1536]{1,0:T(8,128)(2,1)} %collective-permute-done.1.refs_1_), channel_id=1, source_target_pairs={{448,0},{0,64},{64,128},{128,192},{192,256},{256,320},{320,384},{3... | collective-permute-start | bytes 1769480 | tf_op jit(solution)/shard_map/ppermute | solution.py:200
  52.9 6.0 %all-to-all-start = ((bf16[16,192,384]{2,1,0:T(8,128)(2,1)}), bf16[16,192,384]{2,1,0:T(8,128)(2,1)}, u32[]{:S(2)}, u32[]{:S(2)}) async-start(bf16[16,192,384]{2,1,0:T(8,128)(2,1)} %bitcast.2), calls=%async_computation | async-start | bytes 4718592 | tf_op jit(solution)/shard_map/all_to_all | solution.py:217
  58.9 0.0 collective-permute-done.2.other_ref
  58.9 0.0 copy-done
  58.9 0.0 copy-start.3
  59.0 1.1 copy-done.3
  60.0 2.8 %shard_map.69.refs_4_ = bf16[2,8,192,384]{3,2,1,0:T(8,128)(2,1)} custom-call(s32[2]{0:T(128)S(1)} %pad_add_fusion.place_ref, bf16[384,1536]{1,0:T(8,128)(2,1)S(1)} %fusion.34.own_ref, bf16[384,1536]{1,0:T(8,128)(2,1)} %copy-done.3, bf16[192,1536]{1,0:T(8,128)(2,1)S(1)} %all_gather.3.refs_0_), custom_call_target="tpu_custom_call" | custom-call | flops 274877906944 | bytes 262144 | tf_op jit(solution)/shard_map/pallas_call | solution.py:51
  62.9 0.0 collective-permute-done.3.refs_2_
  62.9 1.9 %collective-permute-start.4 = (bf16[192,1536]{1,0:T(8,128)(2,1)}, bf16[192,1536]{1,0:T(8,128)(2,1)S(1)}, u32[]{:S(2)}, u32[]{:S(2)}) collective-permute-start(bf16[192,1536]{1,0:T(8,128)(2,1)} %collective-permute-done.3.refs_2_), channel_id=1, source_target_pairs={{64,0},{128,64},{192,128},{256,192},{320,256},{384,320},{448,384},... | collective-permute-start | bytes 1769480 | tf_op jit(solution)/shard_map/ppermute | solution.py:200
  64.8 0.1 collective-permute-done.5.refs_3_
  64.9 5.3 %collective-permute-start.7 = (bf16[192,1536]{1,0:T(8,128)(2,1)}, bf16[192,1536]{1,0:T(8,128)(2,1)S(1)}, u32[]{:S(2)}, u32[]{:S(2)}) collective-permute-start(bf16[192,1536]{1,0:T(8,128)(2,1)} %collective-permute-done.5.refs_3_), channel_id=1, source_target_pairs={{448,0},{0,64},{64,128},{128,192},{192,256},{256,320},{320,384},{3... | collective-permute-start | bytes 1769480 | tf_op jit(solution)/shard_map/ppermute | solution.py:200
  70.2 5.7 %shard_map.70.refs_2_ = bf16[2,8,192,384]{3,2,1,0:T(8,128)(2,1)} custom-call(s32[2]{0:T(128)S(1)} %pad_add_fusion.place_ref, bf16[384,1536]{1,0:T(8,128)(2,1)} %copy-done, bf16[384,1536]{1,0:T(8,128)(2,1)} %copy-done.3, bf16[192,1536]{1,0:T(8,128)(2,1)} %collective-permute-done.refs_0_, ...), custom_call_target="tpu_custom_call", output_to_operand_aliasing={{}: (7, {})} | custom-call | flops 113246208 | bytes 262144 | tf_op jit(solution)/shard_map/pallas_call | solution.py:51
  75.9 0.0 collective-permute-done.4.refs_0_
  75.9 1.9 %collective-permute-start.6 = (bf16[192,1536]{1,0:T(8,128)(2,1)S(1)}, bf16[192,1536]{1,0:T(8,128)(2,1)S(1)}, u32[]{:S(2)}, u32[]{:S(2)}) collective-permute-start(bf16[192,1536]{1,0:T(8,128)(2,1)S(1)} %collective-permute-done.4.refs_0_), channel_id=1, source_target_pairs={{64,0},{128,64},{192,128},{256,192},{320,256},{384,320},{448,384},... | collective-permute-start | bytes 1769480 | tf_op jit(solution)/shard_map/ppermute | solution.py:200
  77.8 5.2 %collective-permute-done.7.refs_1_ = bf16[192,1536]{1,0:T(8,128)(2,1)S(1)} collective-permute-done((bf16[192,1536]{1,0:T(8,128)(2,1)}, bf16[192,1536]{1,0:T(8,128)(2,1)S(1)}, u32[]{:S(2)}, u32[]{:S(2)}) %collective-permute-start.7) | collective-permute-done | bytes 589856 | tf_op jit(solution)/shard_map/ppermute | solution.py:200
  83.0 3.7 %shard_map.71.refs_1_ = bf16[2,8,192,384]{3,2,1,0:T(8,128)(2,1)} custom-call(s32[2]{0:T(128)S(1)} %pad_add_fusion.place_ref, bf16[384,1536]{1,0:T(8,128)(2,1)} %copy-done, bf16[384,1536]{1,0:T(8,128)(2,1)} %copy-done.3, bf16[192,1536]{1,0:T(8,128)(2,1)S(1)} %collective-permute-done.4.refs_0_, ...), custom_call_target="tpu_custom_call", output_to_operand_aliasing={{}: (5, {})} | custom-call | flops 113246208 | bytes 262144 | tf_op jit(solution)/shard_map/pallas_call | solution.py:51
  86.7 0.0 copy-start.1
  86.7 2.7 %all-to-all-done.x_ref = bf16[16,192,384]{2,1,0:T(8,128)(2,1)} async-done(((bf16[16,192,384]{2,1,0:T(8,128)(2,1)}), bf16[16,192,384]{2,1,0:T(8,128)(2,1)}, u32[]{:S(2)}, u32[]{:S(2)}) %all-to-all-start) | async-done | bytes 2359328 | tf_op jit(solution)/shard_map/all_to_all | solution.py:217
  89.4 2.7 %shard_map.72.one_ref = f32[2,8,384]{2,1,0:T(8,128)S(1)} custom-call(bf16[16,192,384]{2,1,0:T(8,128)(2,1)} %all-to-all-done.x_ref), custom_call_target="tpu_custom_call" | custom-call | tf_op jit(solution)/shard_map/pallas_call | solution.py:230
  92.1 0.0 collective-permute-done.6.refs_0_
  92.1 2.9 %shard_map.73.parts_ref = bf16[2,8,192,384]{3,2,1,0:T(8,128)(2,1)} custom-call(s32[2]{0:T(128)S(1)} %pad_add_fusion.place_ref, bf16[384,1536]{1,0:T(8,128)(2,1)S(1)} %copy-done.1, bf16[384,1536]{1,0:T(8,128)(2,1)} %copy-done.3, bf16[192,1536]{1,0:T(8,128)(2,1)S(1)} %collective-permute-done.6.refs_0_, ...), custom_call_target="tpu_custom_call", output_to_operand_aliasing={{}: (4, {})} | custom-call | flops 113246208 | bytes 262144 | tf_op jit(solution)/shard_map/pallas_call | solution.py:51
  95.0 0.0 copy-start.4
  95.0 9.4 %all-to-all-start.1 = ((bf16[16,192,384]{2,1,0:T(8,128)(2,1)}), bf16[16,192,384]{2,1,0:T(8,128)(2,1)S(1)}, u32[]{:S(2)}, u32[]{:S(2)}) async-start(bf16[16,192,384]{2,1,0:T(8,128)(2,1)} %bitcast.10), calls=%async_computation.1 | async-start | bytes 4718592 | tf_op jit(solution)/shard_map/all_to_all | solution.py:240
  104.5 2.0 %collective-permute-start.8 = (f32[2,8,384]{2,1,0:T(8,128)S(1)}, f32[2,8,384]{2,1,0:T(8,128)S(1)}, u32[]{:S(2)}, u32[]{:S(2)}) collective-permute-start(f32[2,8,384]{2,1,0:T(8,128)S(1)} %shard_map.72.one_ref), channel_id=1, source_target_pairs={{0,8},{8,0},{1,9},{9,1},{2,10},{10,2},{3,11},{11,3},{4,12},{12,4},... | collective-permute-start | bytes 73736 | tf_op jit(solution)/shard_map/ppermute | solution.py:24
  106.5 0.1 reshape.38.gain_ref
  106.6 0.9 collective-permute-done.8.two_ref
  107.5 3.6 %shard_map.75 = f32[8,256]{1,0:T(8,128)S(1)} custom-call(bf16[2,8,192,384]{3,2,1,0:T(8,128)(2,1)} %shard_map.73.parts_ref, bf16[2,8,192,384]{3,2,1,0:T(8,128)(2,1)} %bitcast.4.x_ref, f32[2,8,384]{2,1,0:T(8,128)S(1)} %shard_map.72.one_ref, f32[2,8,384]{2,1,0:T(8,128)S(1)} %collective-permute-done.8.two_ref), custom_call_target="tpu_custom_call" | custom-call | tf_op jit(solution)/shard_map/pallas_call | solution.py:144
  111.1 15.5 %psum.14 = f32[8,256]{1,0:T(8,128)S(1)} all-reduce(f32[8,256]{1,0:T(8,128)S(1)} %shard_map.75), channel_id=1, replica_groups=mesh['y'=8,'zh'=4,'c'=2,'zl'=2,'x'=4] {'y'}, use_global_device_ids=true, to_apply=%region_0.0 | all-reduce | flops 2048 | bytes 16384 | tf_op jit(solution)/shard_map/psum | solution.py:242
  126.7 10.3 %psum.15 = f32[8,2,128]{2,1,0:T(2,128)S(1)} all-reduce(f32[8,2,128]{2,1,0:T(2,128)S(1)} %reshape.34), channel_id=1, replica_groups=mesh['y'=8,'zh'=4,'c'=2,'zl'=2,'x'=4] {'zh'}, use_global_device_ids=true, to_apply=%region_1.0 | all-reduce | flops 2048 | bytes 16384 | tf_op jit(solution)/shard_map/psum | solution.py:242
  137.0 0.0 all-to-all-done.1.parts_ref
  137.0 0.5 shard_map.74
  137.5 14.7 %all_to_all.15.small_ref = f32[16,8,128]{2,1,0:T(8,128)S(1)} all-to-all(f32[16,8,128]{2,1,0:T(8,128)S(1)} %maximum_maximum_fusion), channel_id=1, replica_groups=mesh['y'=8,'zh'=4,'c'=2,'zl'=2,'x'=4] {'c','zl','x'}, dimensions={0} | all-to-all | bytes 131072 | tf_op jit(solution)/shard_map/all_to_all | solution.py:258
  152.2 1.0 shard_map.76
  153.2 0.1 reshape.35
  153.3 0.7 reshape.36
  (7 shorter events, 0.0 us)
Async XLA Ops:
  0.6 36.2 %copy-start.2 = (bf16[384,384]{1,0:T(8,128)(2,1)S(1)}, bf16[384,384]{1,0:T(8,128)(2,1)}, u32[]{:S(2)}) copy-start(bf16[384,384]{1,0:T(8,128)(2,1)} %tokens_ref) | copy-start | bytes 884740
  23.0 15.7 %collective-permute-start = (bf16[192,1536]{1,0:T(8,128)(2,1)S(1)}, bf16[192,1536]{1,0:T(8,128)(2,1)}, u32[]{:S(2)}, u32[]{:S(2)}) collective-permute-start(bf16[192,1536]{1,0:T(8,128)(2,1)S(1)} %all_gather.3.refs_0_), channel_id=1, source_target_pairs={{64,0},{128,64},{192,128},{256,192},{320,256},{384,320},{448,384},... | collective-permute-start | bytes 1769480 | tf_op jit(solution)/shard_map/ppermute | solution.py:200
  26.2 16.7 %collective-permute-start.1 = (bf16[192,1536]{1,0:T(8,128)(2,1)S(1)}, bf16[192,1536]{1,0:T(8,128)(2,1)}, u32[]{:S(2)}, u32[]{:S(2)}) collective-permute-start(bf16[192,1536]{1,0:T(8,128)(2,1)S(1)} %all_gather.3.refs_0_), channel_id=1, source_target_pairs={{448,0},{0,64},{64,128},{128,192},{192,256},{256,320},{320,384},{3... | collective-permute-start | bytes 1769480 | tf_op jit(solution)/shard_map/ppermute | solution.py:200
  36.9 22.1 %copy-start = (bf16[384,1536]{1,0:T(8,128)(2,1)}, bf16[384,1536]{1,0:T(8,128)(2,1)S(1)}, u32[]{:S(2)}) copy-start(bf16[384,1536]{1,0:T(8,128)(2,1)S(1)} %fusion.34.own_ref) | copy-start | bytes 3538948
  42.9 16.0 %collective-permute-start.2 = (bf16[384,1536]{1,0:T(8,128)(2,1)S(1)}, bf16[384,1536]{1,0:T(8,128)(2,1)S(1)}, u32[]{:S(2)}, u32[]{:S(2)}) collective-permute-start(bf16[384,1536]{1,0:T(8,128)(2,1)S(1)} %fusion.34.own_ref), channel_id=1, source_target_pairs={{0,8},{8,0},{1,9},{9,1},{2,10},{10,2},{3,11},{11,3},{4,12},{12,4},... | collective-permute-start | bytes 3538952 | tf_op jit(solution)/shard_map/ppermute | solution.py:24
  45.6 17.3 %collective-permute-start.3 = (bf16[192,1536]{1,0:T(8,128)(2,1)}, bf16[192,1536]{1,0:T(8,128)(2,1)}, u32[]{:S(2)}, u32[]{:S(2)}) collective-permute-start(bf16[192,1536]{1,0:T(8,128)(2,1)} %collective-permute-done.refs_0_), channel_id=1, source_target_pairs={{64,0},{128,64},{192,128},{256,192},{320,256},{384,320},{448,384},... | collective-permute-start | bytes 1769480 | tf_op jit(solution)/shard_map/ppermute | solution.py:200
  47.5 17.3 %collective-permute-start.5 = (bf16[192,1536]{1,0:T(8,128)(2,1)}, bf16[192,1536]{1,0:T(8,128)(2,1)}, u32[]{:S(2)}, u32[]{:S(2)}) collective-permute-start(bf16[192,1536]{1,0:T(8,128)(2,1)} %collective-permute-done.1.refs_1_), channel_id=1, source_target_pairs={{448,0},{0,64},{64,128},{128,192},{192,256},{256,320},{320,384},{3... | collective-permute-start | bytes 1769480 | tf_op jit(solution)/shard_map/ppermute | solution.py:200
  52.9 36.5 %all-to-all-start = ((bf16[16,192,384]{2,1,0:T(8,128)(2,1)}), bf16[16,192,384]{2,1,0:T(8,128)(2,1)}, u32[]{:S(2)}, u32[]{:S(2)}) async-start(bf16[16,192,384]{2,1,0:T(8,128)(2,1)} %bitcast.2), calls=%async_computation | async-start | bytes 4718592 | tf_op jit(solution)/shard_map/all_to_all | solution.py:217
  58.9 1.1 copy-start.3
  62.9 13.0 %collective-permute-start.4 = (bf16[192,1536]{1,0:T(8,128)(2,1)}, bf16[192,1536]{1,0:T(8,128)(2,1)S(1)}, u32[]{:S(2)}, u32[]{:S(2)}) collective-permute-start(bf16[192,1536]{1,0:T(8,128)(2,1)} %collective-permute-done.3.refs_2_), channel_id=1, source_target_pairs={{64,0},{128,64},{192,128},{256,192},{320,256},{384,320},{448,384},... | collective-permute-start | bytes 1769480 | tf_op jit(solution)/shard_map/ppermute | solution.py:200
  64.9 18.1 %collective-permute-start.7 = (bf16[192,1536]{1,0:T(8,128)(2,1)}, bf16[192,1536]{1,0:T(8,128)(2,1)S(1)}, u32[]{:S(2)}, u32[]{:S(2)}) collective-permute-start(bf16[192,1536]{1,0:T(8,128)(2,1)} %collective-permute-done.5.refs_3_), channel_id=1, source_target_pairs={{448,0},{0,64},{64,128},{128,192},{192,256},{256,320},{320,384},{3... | collective-permute-start | bytes 1769480 | tf_op jit(solution)/shard_map/ppermute | solution.py:200
  75.9 16.2 %collective-permute-start.6 = (bf16[192,1536]{1,0:T(8,128)(2,1)S(1)}, bf16[192,1536]{1,0:T(8,128)(2,1)S(1)}, u32[]{:S(2)}, u32[]{:S(2)}) collective-permute-start(bf16[192,1536]{1,0:T(8,128)(2,1)S(1)} %collective-permute-done.4.refs_0_), channel_id=1, source_target_pairs={{64,0},{128,64},{192,128},{256,192},{320,256},{384,320},{448,384},... | collective-permute-start | bytes 1769480 | tf_op jit(solution)/shard_map/ppermute | solution.py:200
  86.7 5.4 %copy-start.1 = (bf16[384,1536]{1,0:T(8,128)(2,1)S(1)}, bf16[384,1536]{1,0:T(8,128)(2,1)}, u32[]{:S(2)}) copy-start(bf16[384,1536]{1,0:T(8,128)(2,1)} %copy-done) | copy-start | bytes 3538948
  95.0 11.5 %copy-start.4 = (bf16[384]{0:T(512)(128)(2,1)S(1)}, bf16[384]{0:T(512)(128)(2,1)}, u32[]{:S(2)}) copy-start(bf16[384]{0:T(512)(128)(2,1)} %param.6) | copy-start | bytes 2308
  95.0 42.0 %all-to-all-start.1 = ((bf16[16,192,384]{2,1,0:T(8,128)(2,1)}), bf16[16,192,384]{2,1,0:T(8,128)(2,1)S(1)}, u32[]{:S(2)}, u32[]{:S(2)}) async-start(bf16[16,192,384]{2,1,0:T(8,128)(2,1)} %bitcast.10), calls=%async_computation.1 | async-start | bytes 4718592 | tf_op jit(solution)/shard_map/all_to_all | solution.py:240
  104.5 3.1 %collective-permute-start.8 = (f32[2,8,384]{2,1,0:T(8,128)S(1)}, f32[2,8,384]{2,1,0:T(8,128)S(1)}, u32[]{:S(2)}, u32[]{:S(2)}) collective-permute-start(f32[2,8,384]{2,1,0:T(8,128)S(1)} %shard_map.72.one_ref), channel_id=1, source_target_pairs={{0,8},{8,0},{1,9},{9,1},{2,10},{10,2},{3,11},{11,3},{4,12},{12,4},... | collective-permute-start | bytes 73736 | tf_op jit(solution)/shard_map/ppermute | solution.py:24

commit v13 on v12

--- a/solution.py
+++ b/solution.py
@@ -10,7 +10,8 @@
 DP, MP, CHIPS = ("y", "zh", "c"), ("zl", "x"), ("c", "zl", "x")
 F32, BF16 = jnp.float32, jnp.bfloat16
 SHARD = 48
-HALF = 1536
+SHARE = 384
+EXTRA = 16
 PARAMS = pltpu.CompilerParams(vmem_limit_bytes=20 * 1024 * 1024)
 WIDE = pltpu.CompilerParams(vmem_limit_bytes=52 * 1024 * 1024)
 together = lax.optimization_barrier
@@ -68,12 +69,20 @@
 
 
 def tokens_kernel(tokens_ref, x_ref, send_ref, held, sem):
-    x = tokens_ref[...].astype(F32).T.astype(BF16)
-    x_ref[...] = x
+    x = tokens_ref[...].astype(F32).T
+    x_ref[...] = x.astype(BF16)
+    mean = jnp.sum(x, axis=0, keepdims=True) * (1.0 / SHARE)
+    parts = []
+    for rest in (mean, jnp.sum((x - mean) ** 2, axis=0, keepdims=True)):
+        for _ in range(3):
+            parts.append(rest.astype(BF16).astype(F32))
+            rest = rest - parts[-1]
+    parts = jnp.concatenate(parts + [jnp.zeros((EXTRA - 6, x.shape[1]), F32)], axis=0).astype(BF16)
     copies = []
     for c in range(2):
         for z in range(4):
-            held[c, pl.ds(z * SHARD, SHARD)] = x[(z * 2 + c) * SHARD : (z * 2 + c + 1) * SHARD]
+            held[c, pl.ds(z * SHARD, SHARD)] = x[(z * 2 + c) * SHARD : (z * 2 + c + 1) * SHARD].astype(BF16)
+        held[c, pl.ds(4 * SHARD, EXTRA)] = parts
         for m in range(8):
             copies.append(pltpu.make_async_copy(held.at[c], send_ref.at[c, m], sem.at[c, m]))
             copies[-1].start()
@@ -88,72 +97,69 @@
         out_specs=[pl.BlockSpec(memory_space=pltpu.VMEM), pl.BlockSpec(memory_space=pl.ANY)],
         out_shape=[
             jax.ShapeDtypeStruct((share, rows), BF16),
-            jax.ShapeDtypeStruct((2, 8, share // 2, rows), BF16),
+            jax.ShapeDtypeStruct((2, 8, share // 2 + EXTRA, rows), BF16),
         ],
         scratch_shapes=[
-            pltpu.VMEM((2, share // 2, rows), BF16),
+            pltpu.VMEM((2, share // 2 + EXTRA, rows), BF16),
             pltpu.SemaphoreType.DMA((2, 8)),
         ],
         compiler_params=PARAMS,
     )(tokens)
 
 
-def stats_kernel(x_ref, out_ref):
-    for t in range(2):
-        total = 0.0
-        for m in range(8):
-            total += jnp.sum(x_ref[t * 8 + m].astype(F32), axis=0, keepdims=True)
-        mean = total * (1.0 / HALF)
-        square = 0.0
-        for m in range(8):
-            centred = x_ref[t * 8 + m].astype(F32) - mean
-            square += jnp.sum(centred * centred, axis=0, keepdims=True)
-        out_ref[t] = jnp.concatenate([mean, square] * 4, axis=0)
-
-
-def mean_and_rstd(one, two):
-    mean = (one[0:1] + two[0:1]) * 0.5
-    between = (one[0:1] - mean) ** 2 + (two[0:1] - mean) ** 2
-    variance = (one[1:2] + two[1:2] + HALF * between) * (1.0 / (2 * HALF))
-    return mean, 1.0 / jnp.sqrt(variance + 1e-06)
-
-
-def gain_kernel(parts_ref, x_ref, one_ref, two_ref, out_ref, stat_ref):
+def gain_kernel(parts_ref, x_ref, extra_ref, out_ref, stat_ref):
     @pl.when(pl.program_id(0) == 0)
     def _():
         for t in range(2):
-            mean, rstd = mean_and_rstd(one_ref[t], two_ref[t])
+            means, squares = [], []
+            for m in range(8):
+                rows = extra_ref[t, m].astype(F32)
+                means.append(rows[0:1] + rows[1:2] + rows[2:3])
+                squares.append(rows[3:4] + rows[4:5] + rows[5:6])
+            mean = sum(means) * 0.125
+            between = sum((m - mean) ** 2 for m in means)
+            variance = (sum(squares) + SHARE * between) * (1.0 / (8 * SHARE))
+            rstd = 1.0 / jnp.sqrt(variance + 1e-06)
             stat_ref[t] = jnp.concatenate([mean, rstd] * 4, axis=0)
 
-    per_step = x_ref.shape[1]
+    per_step, features = x_ref.shape[1], parts_ref.shape[2]
     for k in range(per_step):
-        total = jnp.zeros((x_ref.shape[2], 128), F32)
+        total = jnp.zeros((features, 128), F32)
         for t in range(2):
-            xhat = (x_ref[t, k].astype(F32) - stat_ref[t, 0:1]) * stat_ref[t, 1:2]
+            xhat = (x_ref[t, k, :features].astype(F32) - stat_ref[t, 0:1]) * stat_ref[t, 1:2]
             value = parts_ref[t, k].astype(F32) * xhat
             total += value[:, :128] + value[:, 128:256] + value[:, 256:]
-        total = jnp.concatenate([total, jnp.zeros((64, 128), F32)], axis=0)
+        total = jnp.concatenate([total, jnp.zeros((256 - features, 128), F32)], axis=0)
         row = jnp.sum(total.T, axis=0, keepdims=True)
         out_ref[pl.ds(pl.program_id(0) * per_step + k, 1), :] = row
 
 
-def gain_share(parts, x_all, one, two):
+def gain_share(parts, x_all):
     _, _, rows, tokens = parts.shape
-    block = pl.BlockSpec((2, 2, rows, tokens), lambda m: (0, m, 0, 0))
-    stat = pl.BlockSpec((2, 8, tokens), lambda m: (0, 0, 0))
+    x_all = x_all.reshape(2, 8, rows + EXTRA, tokens)
     return pl.pallas_call(
         gain_kernel,
         grid=(4,),
-        in_specs=[block, block, stat, stat],
-        out_specs=pl.BlockSpec((8, 256), lambda m: (0, 0)),
-        scratch_shapes=[pltpu.VMEM((2, 8, tokens), F32)],
-        out_shape=jax.ShapeDtypeStruct((8, 256), F32),
+        in_specs=[
+            pl.BlockSpec((2, 2, rows, tokens), lambda m: (0, m, 0, 0)),
+            pl.BlockSpec((2, 2, rows + EXTRA, tokens), lambda m: (0, m, 0, 0)),
+            pl.BlockSpec((2, 8, EXTRA, tokens), lambda m: (0, 0, rows // EXTRA, 0)),
+        ],
+        out_specs=[
+            pl.BlockSpec((8, 256), lambda m: (0, 0)),
+            pl.BlockSpec((2, 8, tokens), lambda m: (0, 0, 0)),
+        ],
+        out_shape=[
+            jax.ShapeDtypeStruct((8, 256), F32),
+            jax.ShapeDtypeStruct((2, 8, tokens), F32),
+        ],
         compiler_params=WIDE,
-    )(parts, x_all.reshape(parts.shape), one, two)
-
-
-def sum_kernel(core_ref, parts_ref, x_ref, gain_ref, one_ref, two_ref, d_ref, moments_ref):
-    mean, rstd = mean_and_rstd(one_ref[core_ref[0]], two_ref[core_ref[0]])
+    )(parts, x_all, x_all)
+
+
+def sum_kernel(core_ref, parts_ref, x_ref, gain_ref, stat_ref, d_ref, moments_ref):
+    stat = stat_ref[core_ref[0]]
+    mean, rstd = stat[0:1], stat[1:2]
     first, second = 0.0, 0.0
     for z in range(4):
         for c in range(2):
@@ -170,13 +176,13 @@
     moments_ref[...] = jnp.concatenate(rows + [jnp.zeros((2, 128), F32)], axis=0)
 
 
-def final_kernel(here_ref, d_ref, x_ref, one_ref, two_ref, small_ref, out_ref, gain_ref):
+def final_kernel(here_ref, d_ref, x_ref, stat_ref, small_ref, out_ref, gain_ref):
     core = here_ref[0]
-    mean, rstd = mean_and_rstd(one_ref[core], two_ref[core])
+    mean, rstd = stat_ref[core][0:1], stat_ref[core][1:2]
     total = small_ref[core * 8]
     for m in range(1, 8):
         total += small_ref[core * 8 + m]
-    total = total * (1.0 / (2 * HALF))
+    total = total * (1.0 / (8 * SHARE))
     first, second = (jnp.concatenate([total[k + i : k + i + 1] for i in range(3)], axis=1) for k in (0, 3))
     xhat = (x_ref[...].astype(F32) - mean) * rstd
     value = rstd * (d_ref[...] - first - xhat * second)
@@ -214,7 +220,7 @@
     first, second, (d_own, x_all) = tie(first1, second1, (d_own, x_all))
     first2, second2 = step(first, 1), step(second, -1)
     d_other = partner(d_own, "c", 2, 1)
-    x_all = lax.all_to_all(x_all.reshape(16, share // 2, rows), CHIPS, 0, 0)
+    x_all = lax.all_to_all(x_all.reshape(16, -1, rows), CHIPS, 0, 0)
     parts = products([(0, w0)], d_own, d_other, place, None, long=True)
 
     first, second, parts = tie(first2, second2, parts)
@@ -226,31 +232,23 @@
     first4 = step(first, 1)
     parts = products([(3, first3), (5, second)], d_own, d_other, place, parts)
 
-    parts, x_all = together((parts, x_all))
-    one = pl.pallas_call(
-        stats_kernel,
-        out_shape=jax.ShapeDtypeStruct((2, 8, rows), F32),
-        compiler_params=PARAMS,
-    )(x_all)
-
-    two = partner(one, "c", 2, 1)
-
-    first4, parts, one = together((first4, parts, one))
+    first4, parts, x_all = together((first4, parts, x_all))
     parts = products([(4, first4)], d_own, d_other, place, parts)
     received = lax.all_to_all(parts.reshape(16, share // 2, rows), CHIPS, 0, 0)
 
-    shares = lax.psum(lax.psum(gain_share(parts, x_all, one, two), "y"), "zh")
+    shares, stat = gain_share(parts, x_all)
+    shares = lax.psum(lax.psum(shares, "y"), "zh")
 
     vmem, smem = pl.BlockSpec(memory_space=pltpu.VMEM), pl.BlockSpec(memory_space=pltpu.SMEM)
     d_scaled, moments = pl.pallas_call(
         sum_kernel,
-        in_specs=[smem] + [vmem] * 5,
+        in_specs=[smem] + [vmem] * 4,
         out_shape=[
             jax.ShapeDtypeStruct((share, rows), F32),
             jax.ShapeDtypeStruct((8, 128), F32),
         ],
         compiler_params=PARAMS,
-    )(here[1], received, x, gain.astype(F32)[:, None], one, two)
+    )(here[1], received, x, gain.astype(F32)[:, None], stat)
 
     small = jnp.concatenate(
         [jnp.broadcast_to(moments[None, :6], (8, 6, 128)), shares.reshape(8, 2, 128)], axis=1
@@ -258,13 +256,13 @@
     small = lax.all_to_all(jnp.concatenate([small, small], axis=0), CHIPS, 0, 0)
     token_gradient, gain_rows = pl.pallas_call(
         final_kernel,
-        in_specs=[smem] + [vmem] * 5,
+        in_specs=[smem] + [vmem] * 4,
         out_shape=[
             jax.ShapeDtypeStruct((rows, share), BF16),
             jax.ShapeDtypeStruct((8, 256), F32),
         ],
         compiler_params=PARAMS,
-    )(here[1], d_scaled, x, one, two, small)
+    )(here[1], d_scaled, x, stat, small)
     gain_gradient = jnp.swapaxes(gain_rows[:2, : share // 2].reshape(2, 4, SHARD), 0, 1).reshape(share)
     return (token_gradient, gain_gradient)
 

time: 155 us -> 154 us (level)
  waiting for transfers between devices: 13.1 us -> 10.6 us
  blocking collectives: 62.9 us -> 65.1 us
    psum x2, blocking collectives: 25.8 us -> 29 us  [on_device(): shares = lax.psum(lax.psum(shares, 'y'), 'zh')]
    pallas_call x4 -> x3, Pallas kernels: 7.76 us -> 5.22 us  [the longest x1 3.78 us: gain_share(): pl.pallas_call(gain_kernel, grid=(4,), in_specs=[pl.BlockSpec((2, 2, rows...]
    pallas_call x1, Pallas kernels: 1.83 us -> 3.74 us  [transposed(): pl.pallas_call(tokens_kernel, out_specs=[pl.BlockSpec(memory_space=pltpu....]
    ppermute x2 -> x1, starting transfers between devices: 4.56 us -> 3.2 us  [partner(): return lax.ppermute(array, axis, [(i, i ^ bit) for i in range(n)])]
  transfers between devices with their start and end apart: 11 -> 10, of which waited for: 5 -> 5; matrix products, arithmetic and copies ran while one was open for 5% -> 5% of each run, Pallas kernels for 13% -> 13%
where the time goes in v13:
time: 154 us; the launch traced here: 153 us
  blocking collectives  65.1 us (42%)
  starting transfers between devices  42.3 us (27%)
  Pallas kernels  24.1 us (16%)
  waiting for transfers between devices  10.6 us (7%)
  other arithmetic  6.9 us (4%)
  local copies, waits for them, and re-layouts  3.44 us (2%)
    psum x2, blocking collectives, on_device(): shares = lax.psum(lax.psum(shares, 'y'), 'zh')  29 us
    ppermute x7, starting transfers between devices, step(): lax.ppermute(array, ('y', 'c'), [(a * 2 + c, b * 2 + c) for a, b, c in mo...  23.1 us
    all_gather x1, blocking collectives, on_device(): w0 = lax.all_gather(w_in, 'zh', axis=0, tiled=True)  22.4 us
    pallas_call x4, Pallas kernels, products(): pl.pallas_call(kernel, in_specs=[pl.BlockSpec(memory_space=pltpu.SMEM)] +...  15.1 us
    all_to_all x1, blocking collectives, on_device(): small = lax.all_to_all(jnp.concatenate([small, small], axis=0), CHIPS, 0, 0)  13.7 us
    all_to_all x1, starting transfers between devices, on_device(): received = lax.all_to_all(parts.reshape(16, share // 2, rows), CHIPS, 0, 0)  10.1 us
    ppermute x7, waiting for transfers between devices, step(): lax.ppermute(array, ('y', 'c'), [(a * 2 + c, b * 2 + c) for a, b, c in mo...  8.22 us
    convert_element_type x1, other arithmetic, on_device(): d_own = gelu_back(act_cotangent.astype(F32))[0].astype(BF16)  6.81 us
  transfers between devices with their start and end apart: 10, of which 5 were waited for; matrix products, arithmetic and copies ran while one was open for 5% of the time, Pallas kernels for 13%

profile of v13, /device:TPU:1, one launch (start us, length us, event | category | flops | bytes accessed | tf_op | source)
XLA Modules:
  0.0 153.3 jit_solution(17687162782980467380)
XLA Ops:
  0.6 0.0 copy-start.3
  0.6 22.4 %all_gather.3.refs_0_ = bf16[192,1536]{1,0:T(8,128)(2,1)S(1)} all-gather(bf16[48,1536]{1,0:T(8,128)(2,1)} %param.8), channel_id=1, replica_groups=mesh['y'=8,'zh'=4,'c'=2,'zl'=2,'x'=4] {'zh'}, dimensions={0}, use_global_device_ids=true | all-gather | bytes 737280 | tf_op jit(solution)/shard_map/all_gather | solution.py:212
  23.0 3.2 %collective-permute-start = (bf16[192,1536]{1,0:T(8,128)(2,1)S(1)}, bf16[192,1536]{1,0:T(8,128)(2,1)}, u32[]{:S(2)}, u32[]{:S(2)}) collective-permute-start(bf16[192,1536]{1,0:T(8,128)(2,1)S(1)} %all_gather.3.refs_0_), channel_id=1, source_target_pairs={{64,0},{128,64},{192,128},{256,192},{320,256},{384,320},{448,384},... | collective-permute-start | bytes 1769480 | tf_op jit(solution)/shard_map/ppermute | solution.py:206
  26.2 3.8 %collective-permute-start.1 = (bf16[192,1536]{1,0:T(8,128)(2,1)S(1)}, bf16[192,1536]{1,0:T(8,128)(2,1)}, u32[]{:S(2)}, u32[]{:S(2)}) collective-permute-start(bf16[192,1536]{1,0:T(8,128)(2,1)S(1)} %all_gather.3.refs_0_), channel_id=1, source_target_pairs={{448,0},{0,64},{64,128},{128,192},{192,256},{256,320},{320,384},{3... | collective-permute-start | bytes 1769480 | tf_op jit(solution)/shard_map/ppermute | solution.py:206
  30.0 6.8 %fusion.34.own_ref = bf16[384,1536]{1,0:T(8,128)(2,1)S(1)} fusion(bf16[384,1536]{1,0:T(8,128)(2,1)} %param.9, bf16[384,1536]{1,0:T(8,128)(2,1)} %param.7), kind=kLoop, calls=%fused_computation.39 | loop fusion | flops 43646976 | bytes 3538944 | tf_op jit(solution)/shard_map/convert_element_type | solution.py:216
  36.9 0.0 copy-done.3
  36.9 0.0 copy-start
  36.9 3.7 %shard_map.68 = (bf16[384,384]{1,0:T(8,128)(2,1)S(1)}, bf16[2,8,208,384]{3,2,1,0:T(8,128)(2,1)S(1)}) custom-call(bf16[384,384]{1,0:T(8,128)(2,1)S(1)} %copy-done.3), custom_call_target="tpu_custom_call" | custom-call | tf_op jit(solution)/shard_map/pallas_call | solution.py:95
  40.6 0.0 copy-start.2
  40.6 1.5 copy-done.2
  42.1 0.0 collective-permute-done.refs_0_
  42.1 0.8 collective-permute-done.1.refs_1_
  42.9 3.2 %collective-permute-start.2 = (bf16[384,1536]{1,0:T(8,128)(2,1)S(1)}, bf16[384,1536]{1,0:T(8,128)(2,1)S(1)}, u32[]{:S(2)}, u32[]{:S(2)}) collective-permute-start(bf16[384,1536]{1,0:T(8,128)(2,1)S(1)} %fusion.34.own_ref), channel_id=1, source_target_pairs={{0,8},{8,0},{1,9},{9,1},{2,10},{10,2},{3,11},{11,3},{4,12},{12,4},... | collective-permute-start | bytes 3538952 | tf_op jit(solution)/shard_map/ppermute | solution.py:25
  46.1 0.1 pad_add_fusion.place_ref
  46.2 1.9 %collective-permute-start.3 = (bf16[192,1536]{1,0:T(8,128)(2,1)}, bf16[192,1536]{1,0:T(8,128)(2,1)}, u32[]{:S(2)}, u32[]{:S(2)}) collective-permute-start(bf16[192,1536]{1,0:T(8,128)(2,1)} %collective-permute-done.refs_0_), channel_id=1, source_target_pairs={{64,0},{128,64},{192,128},{256,192},{320,256},{384,320},{448,384},... | collective-permute-start | bytes 1769480 | tf_op jit(solution)/shard_map/ppermute | solution.py:206
  48.1 4.9 %collective-permute-start.5 = (bf16[192,1536]{1,0:T(8,128)(2,1)}, bf16[192,1536]{1,0:T(8,128)(2,1)}, u32[]{:S(2)}, u32[]{:S(2)}) collective-permute-start(bf16[192,1536]{1,0:T(8,128)(2,1)} %collective-permute-done.1.refs_1_), channel_id=1, source_target_pairs={{448,0},{0,64},{64,128},{128,192},{192,256},{256,320},{320,384},{3... | collective-permute-start | bytes 1769480 | tf_op jit(solution)/shard_map/ppermute | solution.py:206
  53.0 5.9 %all-to-all-start = ((bf16[16,208,384]{2,1,0:T(8,128)(2,1)}), bf16[16,208,384]{2,1,0:T(8,128)(2,1)}, u32[]{:S(2)}, u32[]{:S(2)}) async-start(bf16[16,208,384]{2,1,0:T(8,128)(2,1)} %bitcast.9), calls=%async_computation | async-start | bytes 5111808 | tf_op jit(solution)/shard_map/all_to_all | solution.py:223
  58.9 0.0 collective-permute-done.2.other_ref
  58.9 0.0 copy-done
  58.9 0.0 copy-start.4
  59.0 1.1 copy-done.4
  60.0 2.9 %shard_map.69.refs_4_ = bf16[2,8,192,384]{3,2,1,0:T(8,128)(2,1)} custom-call(s32[2]{0:T(128)S(1)} %pad_add_fusion.place_ref, bf16[384,1536]{1,0:T(8,128)(2,1)S(1)} %fusion.34.own_ref, bf16[384,1536]{1,0:T(8,128)(2,1)} %copy-done.4, bf16[192,1536]{1,0:T(8,128)(2,1)S(1)} %all_gather.3.refs_0_), custom_call_target="tpu_custom_call" | custom-call | flops 274877906944 | bytes 262144 | tf_op jit(solution)/shard_map/pallas_call | solution.py:52
  62.9 0.0 collective-permute-done.3.refs_2_
  62.9 1.9 %collective-permute-start.4 = (bf16[192,1536]{1,0:T(8,128)(2,1)}, bf16[192,1536]{1,0:T(8,128)(2,1)S(1)}, u32[]{:S(2)}, u32[]{:S(2)}) collective-permute-start(bf16[192,1536]{1,0:T(8,128)(2,1)} %collective-permute-done.3.refs_2_), channel_id=1, source_target_pairs={{64,0},{128,64},{192,128},{256,192},{320,256},{384,320},{448,384},... | collective-permute-start | bytes 1769480 | tf_op jit(solution)/shard_map/ppermute | solution.py:206
  64.8 0.2 collective-permute-done.5.refs_3_
  65.0 5.3 %collective-permute-start.7 = (bf16[192,1536]{1,0:T(8,128)(2,1)}, bf16[192,1536]{1,0:T(8,128)(2,1)S(1)}, u32[]{:S(2)}, u32[]{:S(2)}) collective-permute-start(bf16[192,1536]{1,0:T(8,128)(2,1)} %collective-permute-done.5.refs_3_), channel_id=1, source_target_pairs={{448,0},{0,64},{64,128},{128,192},{192,256},{256,320},{320,384},{3... | collective-permute-start | bytes 1769480 | tf_op jit(solution)/shard_map/ppermute | solution.py:206
  70.3 5.7 %shard_map.70.refs_2_ = bf16[2,8,192,384]{3,2,1,0:T(8,128)(2,1)} custom-call(s32[2]{0:T(128)S(1)} %pad_add_fusion.place_ref, bf16[384,1536]{1,0:T(8,128)(2,1)} %copy-done, bf16[384,1536]{1,0:T(8,128)(2,1)} %copy-done.4, bf16[192,1536]{1,0:T(8,128)(2,1)} %collective-permute-done.refs_0_, ...), custom_call_target="tpu_custom_call", output_to_operand_aliasing={{}: (7, {})} | custom-call | flops 113246208 | bytes 262144 | tf_op jit(solution)/shard_map/pallas_call | solution.py:52
  76.0 0.0 copy-start.1
  76.0 0.0 collective-permute-done.4.refs_0_
  76.0 2.1 %collective-permute-start.6 = (bf16[192,1536]{1,0:T(8,128)(2,1)S(1)}, bf16[192,1536]{1,0:T(8,128)(2,1)S(1)}, u32[]{:S(2)}, u32[]{:S(2)}) collective-permute-start(bf16[192,1536]{1,0:T(8,128)(2,1)S(1)} %collective-permute-done.4.refs_0_), channel_id=1, source_target_pairs={{64,0},{128,64},{192,128},{256,192},{320,256},{384,320},{448,384},... | collective-permute-start | bytes 1769480 | tf_op jit(solution)/shard_map/ppermute | solution.py:206
  78.1 5.0 %collective-permute-done.7.refs_1_ = bf16[192,1536]{1,0:T(8,128)(2,1)S(1)} collective-permute-done((bf16[192,1536]{1,0:T(8,128)(2,1)}, bf16[192,1536]{1,0:T(8,128)(2,1)S(1)}, u32[]{:S(2)}, u32[]{:S(2)}) %collective-permute-start.7) | collective-permute-done | bytes 589856 | tf_op jit(solution)/shard_map/ppermute | solution.py:206
  83.1 3.7 %shard_map.71.refs_1_ = bf16[2,8,192,384]{3,2,1,0:T(8,128)(2,1)} custom-call(s32[2]{0:T(128)S(1)} %pad_add_fusion.place_ref, bf16[384,1536]{1,0:T(8,128)(2,1)} %copy-done, bf16[384,1536]{1,0:T(8,128)(2,1)} %copy-done.4, bf16[192,1536]{1,0:T(8,128)(2,1)S(1)} %collective-permute-done.4.refs_0_, ...), custom_call_target="tpu_custom_call", output_to_operand_aliasing={{}: (5, {})} | custom-call | flops 113246208 | bytes 262144 | tf_op jit(solution)/shard_map/pallas_call | solution.py:52
  86.8 2.3 %collective-permute-done.6.refs_0_ = bf16[192,1536]{1,0:T(8,128)(2,1)S(1)} collective-permute-done((bf16[192,1536]{1,0:T(8,128)(2,1)S(1)}, bf16[192,1536]{1,0:T(8,128)(2,1)S(1)}, u32[]{:S(2)}, u32[]{:S(2)}) %collective-permute-start.6) | collective-permute-done | bytes 589856 | tf_op jit(solution)/shard_map/ppermute | solution.py:206
  89.1 2.4 %all-to-all-done = bf16[16,208,384]{2,1,0:T(8,128)(2,1)} async-done(((bf16[16,208,384]{2,1,0:T(8,128)(2,1)}), bf16[16,208,384]{2,1,0:T(8,128)(2,1)}, u32[]{:S(2)}, u32[]{:S(2)}) %all-to-all-start) | async-done | bytes 2555936 | tf_op jit(solution)/shard_map/all_to_all | solution.py:223
  91.5 2.9 %shard_map.72.parts_ref = bf16[2,8,192,384]{3,2,1,0:T(8,128)(2,1)} custom-call(s32[2]{0:T(128)S(1)} %pad_add_fusion.place_ref, bf16[384,1536]{1,0:T(8,128)(2,1)S(1)} %copy-done.1, bf16[384,1536]{1,0:T(8,128)(2,1)} %copy-done.4, bf16[192,1536]{1,0:T(8,128)(2,1)S(1)} %collective-permute-done.6.refs_0_, ...), custom_call_target="tpu_custom_call", output_to_operand_aliasing={{}: (4, {})} | custom-call | flops 113246208 | bytes 262144 | tf_op jit(solution)/shard_map/pallas_call | solution.py:52
  94.4 0.0 copy-start.5
  94.4 10.1 %all-to-all-start.1 = ((bf16[16,192,384]{2,1,0:T(8,128)(2,1)}), bf16[16,192,384]{2,1,0:T(8,128)(2,1)S(1)}, u32[]{:S(2)}, u32[]{:S(2)}) async-start(bf16[16,192,384]{2,1,0:T(8,128)(2,1)} %bitcast.11), calls=%async_computation.1 | async-start | bytes 4718592 | tf_op jit(solution)/shard_map/all_to_all | solution.py:237
  104.4 0.0 copy-done.5
  104.5 0.1 reshape.38.gain_ref
  104.6 3.8 %shard_map.73 = (f32[8,256]{1,0:T(8,128)S(1)}, f32[2,8,384]{2,1,0:T(8,128)S(1)}) custom-call(bf16[2,8,192,384]{3,2,1,0:T(8,128)(2,1)} %shard_map.72.parts_ref, bf16[2,8,208,384]{3,2,1,0:T(8,128)(2,1)} %bitcast.4.x_ref.extra_ref, bf16[2,8,208,384]{3,2,1,0:T(8,128)(2,1)} %bitcast.4.x_ref.extra_ref), custom_call_target="tpu_custom_call" | custom-call | tf_op jit(solution)/shard_map/pallas_call | solution.py:140
  108.4 15.5 %psum.14 = f32[8,256]{1,0:T(8,128)S(1)} all-reduce(f32[8,256]{1,0:T(8,128)S(1)} %get-tuple-element.49), channel_id=1, replica_groups=mesh['y'=8,'zh'=4,'c'=2,'zl'=2,'x'=4] {'y'}, use_global_device_ids=true, to_apply=%region_0.0 | all-reduce | flops 2048 | bytes 16384 | tf_op jit(solution)/shard_map/psum | solution.py:240
  123.9 13.5 %psum.15 = f32[8,2,128]{2,1,0:T(2,128)S(1)} all-reduce(f32[8,2,128]{2,1,0:T(2,128)S(1)} %reshape.34), channel_id=1, replica_groups=mesh['y'=8,'zh'=4,'c'=2,'zl'=2,'x'=4] {'zh'}, use_global_device_ids=true, to_apply=%region_1.0 | all-reduce | flops 2048 | bytes 16384 | tf_op jit(solution)/shard_map/psum | solution.py:240
  137.4 0.0 all-to-all-done.1.parts_ref
  137.4 0.5 shard_map.74
  138.0 13.7 %all_to_all.15.small_ref = f32[16,8,128]{2,1,0:T(8,128)S(1)} all-to-all(f32[16,8,128]{2,1,0:T(8,128)S(1)} %maximum_maximum_fusion), channel_id=1, replica_groups=mesh['y'=8,'zh'=4,'c'=2,'zl'=2,'x'=4] {'c','zl','x'}, dimensions={0} | all-to-all | bytes 131072 | tf_op jit(solution)/shard_map/all_to_all | solution.py:256
  151.6 0.9 shard_map.75
  152.6 0.1 reshape.35
  152.7 0.7 reshape.36
  (6 shorter events, 0.0 us)
Async XLA Ops:
  0.6 36.2 %copy-start.3 = (bf16[384,384]{1,0:T(8,128)(2,1)S(1)}, bf16[384,384]{1,0:T(8,128)(2,1)}, u32[]{:S(2)}) copy-start(bf16[384,384]{1,0:T(8,128)(2,1)} %tokens_ref) | copy-start | bytes 884740
  23.0 19.1 %collective-permute-start = (bf16[192,1536]{1,0:T(8,128)(2,1)S(1)}, bf16[192,1536]{1,0:T(8,128)(2,1)}, u32[]{:S(2)}, u32[]{:S(2)}) collective-permute-start(bf16[192,1536]{1,0:T(8,128)(2,1)S(1)} %all_gather.3.refs_0_), channel_id=1, source_target_pairs={{64,0},{128,64},{192,128},{256,192},{320,256},{384,320},{448,384},... | collective-permute-start | bytes 1769480 | tf_op jit(solution)/shard_map/ppermute | solution.py:206
  26.2 16.7 %collective-permute-start.1 = (bf16[192,1536]{1,0:T(8,128)(2,1)S(1)}, bf16[192,1536]{1,0:T(8,128)(2,1)}, u32[]{:S(2)}, u32[]{:S(2)}) collective-permute-start(bf16[192,1536]{1,0:T(8,128)(2,1)S(1)} %all_gather.3.refs_0_), channel_id=1, source_target_pairs={{448,0},{0,64},{64,128},{128,192},{192,256},{256,320},{320,384},{3... | collective-permute-start | bytes 1769480 | tf_op jit(solution)/shard_map/ppermute | solution.py:206
  36.9 22.1 %copy-start = (bf16[384,1536]{1,0:T(8,128)(2,1)}, bf16[384,1536]{1,0:T(8,128)(2,1)S(1)}, u32[]{:S(2)}) copy-start(bf16[384,1536]{1,0:T(8,128)(2,1)S(1)} %fusion.34.own_ref) | copy-start | bytes 3538948
  40.6 1.5 copy-start.2
  42.9 16.0 %collective-permute-start.2 = (bf16[384,1536]{1,0:T(8,128)(2,1)S(1)}, bf16[384,1536]{1,0:T(8,128)(2,1)S(1)}, u32[]{:S(2)}, u32[]{:S(2)}) collective-permute-start(bf16[384,1536]{1,0:T(8,128)(2,1)S(1)} %fusion.34.own_ref), channel_id=1, source_target_pairs={{0,8},{8,0},{1,9},{9,1},{2,10},{10,2},{3,11},{11,3},{4,12},{12,4},... | collective-permute-start | bytes 3538952 | tf_op jit(solution)/shard_map/ppermute | solution.py:25
  46.2 16.7 %collective-permute-start.3 = (bf16[192,1536]{1,0:T(8,128)(2,1)}, bf16[192,1536]{1,0:T(8,128)(2,1)}, u32[]{:S(2)}, u32[]{:S(2)}) collective-permute-start(bf16[192,1536]{1,0:T(8,128)(2,1)} %collective-permute-done.refs_0_), channel_id=1, source_target_pairs={{64,0},{128,64},{192,128},{256,192},{320,256},{384,320},{448,384},... | collective-permute-start | bytes 1769480 | tf_op jit(solution)/shard_map/ppermute | solution.py:206
  48.1 16.8 %collective-permute-start.5 = (bf16[192,1536]{1,0:T(8,128)(2,1)}, bf16[192,1536]{1,0:T(8,128)(2,1)}, u32[]{:S(2)}, u32[]{:S(2)}) collective-permute-start(bf16[192,1536]{1,0:T(8,128)(2,1)} %collective-permute-done.1.refs_1_), channel_id=1, source_target_pairs={{448,0},{0,64},{64,128},{128,192},{192,256},{256,320},{320,384},{3... | collective-permute-start | bytes 1769480 | tf_op jit(solution)/shard_map/ppermute | solution.py:206
  53.0 38.5 %all-to-all-start = ((bf16[16,208,384]{2,1,0:T(8,128)(2,1)}), bf16[16,208,384]{2,1,0:T(8,128)(2,1)}, u32[]{:S(2)}, u32[]{:S(2)}) async-start(bf16[16,208,384]{2,1,0:T(8,128)(2,1)} %bitcast.9), calls=%async_computation | async-start | bytes 5111808 | tf_op jit(solution)/shard_map/all_to_all | solution.py:223
  58.9 1.1 copy-start.4
  62.9 13.1 %collective-permute-start.4 = (bf16[192,1536]{1,0:T(8,128)(2,1)}, bf16[192,1536]{1,0:T(8,128)(2,1)S(1)}, u32[]{:S(2)}, u32[]{:S(2)}) collective-permute-start(bf16[192,1536]{1,0:T(8,128)(2,1)} %collective-permute-done.3.refs_2_), channel_id=1, source_target_pairs={{64,0},{128,64},{192,128},{256,192},{320,256},{384,320},{448,384},... | collective-permute-start | bytes 1769480 | tf_op jit(solution)/shard_map/ppermute | solution.py:206
  65.0 18.1 %collective-permute-start.7 = (bf16[192,1536]{1,0:T(8,128)(2,1)}, bf16[192,1536]{1,0:T(8,128)(2,1)S(1)}, u32[]{:S(2)}, u32[]{:S(2)}) collective-permute-start(bf16[192,1536]{1,0:T(8,128)(2,1)} %collective-permute-done.5.refs_3_), channel_id=1, source_target_pairs={{448,0},{0,64},{64,128},{128,192},{192,256},{256,320},{320,384},{3... | collective-permute-start | bytes 1769480 | tf_op jit(solution)/shard_map/ppermute | solution.py:206
  76.0 15.5 %copy-start.1 = (bf16[384,1536]{1,0:T(8,128)(2,1)S(1)}, bf16[384,1536]{1,0:T(8,128)(2,1)}, u32[]{:S(2)}) copy-start(bf16[384,1536]{1,0:T(8,128)(2,1)} %copy-done) | copy-start | bytes 3538948
  76.0 13.1 %collective-permute-start.6 = (bf16[192,1536]{1,0:T(8,128)(2,1)S(1)}, bf16[192,1536]{1,0:T(8,128)(2,1)S(1)}, u32[]{:S(2)}, u32[]{:S(2)}) collective-permute-start(bf16[192,1536]{1,0:T(8,128)(2,1)S(1)} %collective-permute-done.4.refs_0_), channel_id=1, source_target_pairs={{64,0},{128,64},{192,128},{256,192},{320,256},{384,320},{448,384},... | collective-permute-start | bytes 1769480 | tf_op jit(solution)/shard_map/ppermute | solution.py:206
  94.4 10.1 %copy-start.5 = (bf16[384]{0:T(512)(128)(2,1)S(1)}, bf16[384]{0:T(512)(128)(2,1)}, u32[]{:S(2)}) copy-start(bf16[384]{0:T(512)(128)(2,1)} %param.6) | copy-start | bytes 2308
  94.4 43.0 %all-to-all-start.1 = ((bf16[16,192,384]{2,1,0:T(8,128)(2,1)}), bf16[16,192,384]{2,1,0:T(8,128)(2,1)S(1)}, u32[]{:S(2)}, u32[]{:S(2)}) async-start(bf16[16,192,384]{2,1,0:T(8,128)(2,1)} %bitcast.11), calls=%async_computation.1 | async-start | bytes 4718592 | tf_op jit(solution)/shard_map/all_to_all | solution.py:237

commit v14 on v13

--- a/solution.py
+++ b/solution.py
@@ -25,47 +25,59 @@
     return lax.ppermute(array, axis, [(i, i ^ bit) for i in range(n)])
 
 
-def products(groups, d_own, d_other, place, parts, long=False):
-    tokens, hidden = d_own.shape
-    weights = [w for _, w in groups]
-    rows, n = weights[0].shape[0], len(groups)
-
-    def kernel(place_ref, own_ref, other_ref, *refs):
-        w_refs, (out_ref, held, sem) = refs[:n], refs[-3:]
+def products(groups, halves, place, parts, long=False):
+    tokens, hidden = halves[0][1].shape
+    weights, operands = [w for _, w in groups], [d for _, d in halves]
+    rows, n, both = weights[0].shape[0], len(groups), len(halves)
+
+    def kernel(place_ref, *refs):
+        w_refs, d_refs = refs[:n], refs[n : n + both]
+        out_ref, w_held, d_held, held, w_sem, d_sem, sem = refs[-7:]
+        loads = [
+            pltpu.make_async_copy(w, w_held.at[pl.ds(g * rows, rows)], w_sem.at[g])
+            for g, w in enumerate(w_refs)
+        ]
+        d_loads = [pltpu.make_async_copy(d, d_held.at[h], d_sem.at[h]) for h, d in enumerate(d_refs)]
+        for load in loads + d_loads:
+            load.start()
+        for load in loads:
+            load.wait()
         copies = []
-        w = jnp.concatenate([r[...] for r in w_refs], axis=0)
-        for k, d_ref in enumerate((own_ref, other_ref)):
+        for h, (k, _) in enumerate(halves):
+            d_loads[h].wait()
             half = lax.rem(place_ref[1] + k, 2)
             out = lax.dot_general(
-                w, d_ref[...], (((1,), (1,)), ((), ())), preferred_element_type=F32
+                w_held[...], d_held[h], (((1,), (1,)), ((), ())), preferred_element_type=F32
             ).astype(BF16)
             for g, (offset, _) in enumerate(groups):
-                held[k, g] = out[g * rows : (g + 1) * rows]
+                held[h, g] = out[g * rows : (g + 1) * rows]
                 block = lax.rem(place_ref[0] + offset + place_ref[1] * ((8 - 2 * offset) % 8), 8)
                 to = out_ref.at[half, block]
-                copies.append(pltpu.make_async_copy(held.at[k, g], to, sem.at[k, g]))
+                copies.append(pltpu.make_async_copy(held.at[h, g], to, sem.at[h, g]))
                 copies[-1].start()
         for copy in copies:
             copy.wait()
 
-    whole = pl.BlockSpec(memory_space=pltpu.VMEM)
+    anywhere = pl.BlockSpec(memory_space=pl.ANY)
     return pl.pallas_call(
         kernel,
-        in_specs=[pl.BlockSpec(memory_space=pltpu.SMEM)]
-        + [whole] * (2 + n)
-        + [pl.BlockSpec(memory_space=pl.ANY)] * (parts is not None),
-        out_specs=pl.BlockSpec(memory_space=pl.ANY),
+        in_specs=[pl.BlockSpec(memory_space=pltpu.SMEM)] + [anywhere] * (n + both + (parts is not None)),
+        out_specs=anywhere,
         out_shape=jax.ShapeDtypeStruct((2, 8, rows, tokens), BF16),
         scratch_shapes=[
-            pltpu.VMEM((2, n, rows, tokens), BF16),
-            pltpu.SemaphoreType.DMA((2, n)),
-        ],
-        input_output_aliases={} if parts is None else {3 + n: 0},
+            pltpu.VMEM((n * rows, hidden), BF16),
+            pltpu.VMEM((both, tokens, hidden), BF16),
+            pltpu.VMEM((both, n, rows, tokens), BF16),
+            pltpu.SemaphoreType.DMA((n,)),
+            pltpu.SemaphoreType.DMA((both,)),
+            pltpu.SemaphoreType.DMA((both, n)),
+        ],
+        input_output_aliases={} if parts is None else {1 + n + both: 0},
         compiler_params=WIDE,
         cost_estimate=pl.CostEstimate(
             flops=1 << 38 if long else rows * hidden * tokens, bytes_accessed=1 << 18, transcendentals=0
         ),
-    )(place, d_own, d_other, *weights, *([] if parts is None else [parts]))
+    )(place, *weights, *operands, *([] if parts is None else [parts]))
 
 
 def tokens_kernel(tokens_ref, x_ref, send_ref, held, sem):
@@ -103,7 +115,7 @@
             pltpu.VMEM((2, share // 2 + EXTRA, rows), BF16),
             pltpu.SemaphoreType.DMA((2, 8)),
         ],
-        compiler_params=PARAMS,
+        compiler_params=WIDE,
     )(tokens)
 
 
@@ -221,19 +233,21 @@
     first2, second2 = step(first, 1), step(second, -1)
     d_other = partner(d_own, "c", 2, 1)
     x_all = lax.all_to_all(x_all.reshape(16, -1, rows), CHIPS, 0, 0)
-    parts = products([(0, w0)], d_own, d_other, place, None, long=True)
+    parts = products([(0, w0)], [(0, d_own)], place, None, long=True)
 
     first, second, parts = tie(first2, second2, parts)
     first3, second3 = step(first, 1), step(second, -1)
     groups = [(1, first1), (7, second1), (2, first2), (6, second2)]
-    parts = products(groups, d_own, d_other, place, parts)
+    halves = [(0, d_own), (1, d_other)]
+    parts = products([(0, w0)], [(1, d_other)], place, parts)
+    parts = products(groups, halves, place, parts)
 
     first, second, parts = tie(first3, second3, parts)
     first4 = step(first, 1)
-    parts = products([(3, first3), (5, second)], d_own, d_other, place, parts)
+    parts = products([(3, first3), (5, second)], halves, place, parts)
 
     first4, parts, x_all = together((first4, parts, x_all))
-    parts = products([(4, first4)], d_own, d_other, place, parts)
+    parts = products([(4, first4)], halves, place, parts)
     received = lax.all_to_all(parts.reshape(16, share // 2, rows), CHIPS, 0, 0)
 
     shares, stat = gain_share(parts, x_all)

time: 154 us -> 150 us (0.974)
  Pallas kernels: 24.1 us -> 27.8 us
  starting transfers between devices: 42.3 us -> 38.9 us
  local copies, waits for them, and re-layouts: 3.44 us -> 0.89 us
  blocking collectives: 65.1 us -> 62.7 us
    pallas_call x4 -> x5, Pallas kernels: 15.1 us -> 20.7 us  [products(): pl.pallas_call(kernel, in_specs=[pl.BlockSpec(memory_space=pltpu.SMEM)] +...]
    all_to_all x1, starting transfers between devices: 10.1 us -> 7.52 us  [on_device(): received = lax.all_to_all(parts.reshape(16, share // 2, rows), CHIPS, 0, 0)]
    unnamed x12 -> x4, local copies, waits for them, and re-layouts: 2.56 us -> 0.01 us
    all_to_all x1, waiting for transfers between devices: 2.42 us -> 0.18 us  [on_device(): x_all = lax.all_to_all(x_all.reshape(16, -1, rows), CHIPS, 0, 0)]
    ppermute x7, waiting for transfers between devices: 8.22 us -> 10.3 us  [step(): lax.ppermute(array, ('y', 'c'), [(a * 2 + c, b * 2 + c) for a, b, c in mo...]
    all_to_all x1, blocking collectives: 13.7 us -> 11.6 us  [on_device(): small = lax.all_to_all(jnp.concatenate([small, small], axis=0), CHIPS, 0, 0)]
    pallas_call x1, Pallas kernels: 3.74 us -> 1.9 us  [transposed(): pl.pallas_call(tokens_kernel, out_specs=[pl.BlockSpec(memory_space=pltpu....]
  transfers between devices with their start and end apart: 10 -> 10, of which waited for: 5 -> 5; matrix products, arithmetic and copies ran while one was open for 5% -> 5% of each run, Pallas kernels for 13% -> 15%
where the time goes in v14:
time: 150 us; the launch traced here: 149 us
  blocking collectives  62.7 us (42%)
  starting transfers between devices  38.9 us (26%)
  Pallas kernels  27.8 us (19%)
  waiting for transfers between devices  10.5 us (7%)
  other arithmetic  7.7 us (5%)
    psum x2, blocking collectives, on_device(): shares = lax.psum(lax.psum(shares, 'y'), 'zh')  28.7 us
    ppermute x7, starting transfers between devices, step(): lax.ppermute(array, ('y', 'c'), [(a * 2 + c, b * 2 + c) for a, b, c in mo...  22.7 us
    all_gather x1, blocking collectives, on_device(): w0 = lax.all_gather(w_in, 'zh', axis=0, tiled=True)  22.4 us
    pallas_call x5, Pallas kernels, products(): pl.pallas_call(kernel, in_specs=[pl.BlockSpec(memory_space=pltpu.SMEM)] +...  20.7 us
    all_to_all x1, blocking collectives, on_device(): small = lax.all_to_all(jnp.concatenate([small, small], axis=0), CHIPS, 0, 0)  11.6 us
    ppermute x7, waiting for transfers between devices, step(): lax.ppermute(array, ('y', 'c'), [(a * 2 + c, b * 2 + c) for a, b, c in mo...  10.3 us
    convert_element_type x1, other arithmetic, on_device(): d_own = gelu_back(act_cotangent.astype(F32))[0].astype(BF16)  7.61 us
    all_to_all x1, starting transfers between devices, on_device(): received = lax.all_to_all(parts.reshape(16, share // 2, rows), CHIPS, 0, 0)  7.52 us
  transfers between devices with their start and end apart: 10, of which 5 were waited for; matrix products, arithmetic and copies ran while one was open for 5% of the time, Pallas kernels for 15%

profile of v14, /device:TPU:1, one launch (start us, length us, event | category | flops | bytes accessed | tf_op | source)
XLA Modules:
  0.0 149.3 jit_solution(14595987949754324690)
XLA Ops:
  0.6 0.0 copy-start
  0.6 22.4 %all_gather.3.refs_0_ = bf16[192,1536]{1,0:T(8,128)(2,1)S(1)} all-gather(bf16[48,1536]{1,0:T(8,128)(2,1)} %param.8), channel_id=1, replica_groups=mesh['y'=8,'zh'=4,'c'=2,'zl'=2,'x'=4] {'zh'}, dimensions={0}, use_global_device_ids=true | all-gather | bytes 737280 | tf_op jit(solution)/shard_map/all_gather | solution.py:224
  23.0 3.2 %collective-permute-start = (bf16[192,1536]{1,0:T(8,128)(2,1)S(1)}, bf16[192,1536]{1,0:T(8,128)(2,1)}, u32[]{:S(2)}, u32[]{:S(2)}) collective-permute-start(bf16[192,1536]{1,0:T(8,128)(2,1)S(1)} %all_gather.3.refs_0_), channel_id=1, source_target_pairs={{64,0},{128,64},{192,128},{256,192},{320,256},{384,320},{448,384},... | collective-permute-start | bytes 1769480 | tf_op jit(solution)/shard_map/ppermute | solution.py:218
  26.2 3.8 %collective-permute-start.2 = (bf16[192,1536]{1,0:T(8,128)(2,1)S(1)}, bf16[192,1536]{1,0:T(8,128)(2,1)}, u32[]{:S(2)}, u32[]{:S(2)}) collective-permute-start(bf16[192,1536]{1,0:T(8,128)(2,1)S(1)} %all_gather.3.refs_0_), channel_id=1, source_target_pairs={{448,0},{0,64},{64,128},{128,192},{192,256},{256,320},{320,384},{3... | collective-permute-start | bytes 1769480 | tf_op jit(solution)/shard_map/ppermute | solution.py:218
  30.0 7.6 %fusion.34.refs_1_.refs_4_.refs_2_ = bf16[384,1536]{1,0:T(8,128)(2,1)} fusion(bf16[384,1536]{1,0:T(8,128)(2,1)} %param.9, bf16[384,1536]{1,0:T(8,128)(2,1)} %param.7), kind=kLoop, calls=%fused_computation.39 | loop fusion | flops 43646976 | bytes 3538944 | tf_op jit(solution)/shard_map/convert_element_type | solution.py:228
  37.7 0.0 copy-done
  37.7 1.9 %shard_map.68 = (bf16[384,384]{1,0:T(8,128)(2,1)S(1)}, bf16[2,8,208,384]{3,2,1,0:T(8,128)(2,1)}) custom-call(bf16[384,384]{1,0:T(8,128)(2,1)S(1)} %copy-done), custom_call_target="tpu_custom_call" | custom-call | tf_op jit(solution)/shard_map/pallas_call | solution.py:107
  39.6 0.1 pad_add_fusion.place_ref
  39.6 0.0 collective-permute-done.refs_0_
  39.6 3.3 %collective-permute-done.2.refs_1_ = bf16[192,1536]{1,0:T(8,128)(2,1)} collective-permute-done((bf16[192,1536]{1,0:T(8,128)(2,1)S(1)}, bf16[192,1536]{1,0:T(8,128)(2,1)}, u32[]{:S(2)}, u32[]{:S(2)}) %collective-permute-start.2) | collective-permute-done | bytes 589856 | tf_op jit(solution)/shard_map/ppermute | solution.py:218
  42.9 5.4 %collective-permute-start.4 = (bf16[192,1536]{1,0:T(8,128)(2,1)}, bf16[192,1536]{1,0:T(8,128)(2,1)}, u32[]{:S(2)}, u32[]{:S(2)}) collective-permute-start(bf16[192,1536]{1,0:T(8,128)(2,1)} %collective-permute-done.2.refs_1_), channel_id=1, source_target_pairs={{448,0},{0,64},{64,128},{128,192},{192,256},{256,320},{320,384},{3... | collective-permute-start | bytes 1769480 | tf_op jit(solution)/shard_map/ppermute | solution.py:218
  48.3 1.9 %collective-permute-start.1 = (bf16[192,1536]{1,0:T(8,128)(2,1)}, bf16[192,1536]{1,0:T(8,128)(2,1)}, u32[]{:S(2)}, u32[]{:S(2)}) collective-permute-start(bf16[192,1536]{1,0:T(8,128)(2,1)} %collective-permute-done.refs_0_), channel_id=1, source_target_pairs={{64,0},{128,64},{192,128},{256,192},{320,256},{384,320},{448,384},... | collective-permute-start | bytes 1769480 | tf_op jit(solution)/shard_map/ppermute | solution.py:218
  50.3 2.8 %collective-permute-start.5 = (bf16[384,1536]{1,0:T(8,128)(2,1)}, bf16[384,1536]{1,0:T(8,128)(2,1)}, u32[]{:S(2)}, u32[]{:S(2)}) collective-permute-start(bf16[384,1536]{1,0:T(8,128)(2,1)} %fusion.34.refs_1_.refs_4_.refs_2_), channel_id=1, source_target_pairs={{0,8},{8,0},{1,9},{9,1},{2,10},{10,2},{3,11},{11,3},{4,12},{12,4},... | collective-permute-start | bytes 3538952 | tf_op jit(solution)/shard_map/ppermute | solution.py:25
  53.1 5.7 %all-to-all-start = ((bf16[16,208,384]{2,1,0:T(8,128)(2,1)}), bf16[16,208,384]{2,1,0:T(8,128)(2,1)}, u32[]{:S(2)}, u32[]{:S(2)}) async-start(bf16[16,208,384]{2,1,0:T(8,128)(2,1)} %bitcast.11), calls=%async_computation | async-start | bytes 5111808 | tf_op jit(solution)/shard_map/all_to_all | solution.py:235
  58.9 3.2 %shard_map.69.refs_2_ = bf16[2,8,192,384]{3,2,1,0:T(8,128)(2,1)} custom-call(s32[2]{0:T(128)S(1)} %pad_add_fusion.place_ref, bf16[192,1536]{1,0:T(8,128)(2,1)S(1)} %all_gather.3.refs_0_, bf16[384,1536]{1,0:T(8,128)(2,1)} %fusion.34.refs_1_.refs_4_.refs_2_), custom_call_target="tpu_custom_call" | custom-call | flops 274877906944 | bytes 262144 | tf_op jit(solution)/shard_map/pallas_call | solution.py:62
  62.0 1.3 collective-permute-done.1.refs_2_
  63.4 1.9 %collective-permute-start.3 = (bf16[192,1536]{1,0:T(8,128)(2,1)}, bf16[192,1536]{1,0:T(8,128)(2,1)S(1)}, u32[]{:S(2)}, u32[]{:S(2)}) collective-permute-start(bf16[192,1536]{1,0:T(8,128)(2,1)} %collective-permute-done.1.refs_2_), channel_id=1, source_target_pairs={{64,0},{128,64},{192,128},{256,192},{320,256},{384,320},{448,384},... | collective-permute-start | bytes 1769480 | tf_op jit(solution)/shard_map/ppermute | solution.py:218
  65.3 0.0 collective-permute-done.4.refs_3_
  65.3 4.6 %collective-permute-start.7 = (bf16[192,1536]{1,0:T(8,128)(2,1)}, bf16[192,1536]{1,0:T(8,128)(2,1)S(1)}, u32[]{:S(2)}, u32[]{:S(2)}) collective-permute-start(bf16[192,1536]{1,0:T(8,128)(2,1)} %collective-permute-done.4.refs_3_), channel_id=1, source_target_pairs={{448,0},{0,64},{64,128},{128,192},{192,256},{256,320},{320,384},{3... | collective-permute-start | bytes 1769480 | tf_op jit(solution)/shard_map/ppermute | solution.py:218
  69.9 0.0 collective-permute-done.5.refs_1_.refs_5_.refs_3_.refs_2_
  69.9 3.2 %shard_map.70.refs_6_ = bf16[2,8,192,384]{3,2,1,0:T(8,128)(2,1)} custom-call(s32[2]{0:T(128)S(1)} %pad_add_fusion.place_ref, bf16[192,1536]{1,0:T(8,128)(2,1)S(1)} %all_gather.3.refs_0_, bf16[384,1536]{1,0:T(8,128)(2,1)} %collective-permute-done.5.refs_1_.refs_5_.refs_3_.refs_2_, ...), custom_call_target="tpu_custom_call", output_to_operand_aliasing={{}: (3, {})} | custom-call | flops 113246208 | bytes 262144 | tf_op jit(solution)/shard_map/pallas_call | solution.py:62
  73.0 6.1 %shard_map.71.refs_4_ = bf16[2,8,192,384]{3,2,1,0:T(8,128)(2,1)} custom-call(s32[2]{0:T(128)S(1)} %pad_add_fusion.place_ref, bf16[192,1536]{1,0:T(8,128)(2,1)} %collective-permute-done.refs_0_, bf16[192,1536]{1,0:T(8,128)(2,1)} %collective-permute-done.2.refs_1_, bf16[192,1536]{1,0:T(8,128)(2,1)} %collective-permute-done.1.refs_2_, ...), custom_call_target="tpu_custom_call", output_to_operand_aliasing={{}: (7, {})} | custom-call | flops 113246208 | bytes 262144 | tf_op jit(solution)/shard_map/pallas_call | solution.py:62
  79.2 0.0 collective-permute-done.3.refs_0_
  79.2 1.9 %collective-permute-start.6 = (bf16[192,1536]{1,0:T(8,128)(2,1)S(1)}, bf16[192,1536]{1,0:T(8,128)(2,1)S(1)}, u32[]{:S(2)}, u32[]{:S(2)}) collective-permute-start(bf16[192,1536]{1,0:T(8,128)(2,1)S(1)} %collective-permute-done.3.refs_0_), channel_id=1, source_target_pairs={{64,0},{128,64},{192,128},{256,192},{320,256},{384,320},{448,384},... | collective-permute-start | bytes 1769480 | tf_op jit(solution)/shard_map/ppermute | solution.py:218
  81.1 0.3 collective-permute-done.7.refs_1_
  81.4 4.4 %shard_map.72.refs_3_ = bf16[2,8,192,384]{3,2,1,0:T(8,128)(2,1)} custom-call(s32[2]{0:T(128)S(1)} %pad_add_fusion.place_ref, bf16[192,1536]{1,0:T(8,128)(2,1)S(1)} %collective-permute-done.3.refs_0_, bf16[192,1536]{1,0:T(8,128)(2,1)S(1)} %collective-permute-done.7.refs_1_, ...), custom_call_target="tpu_custom_call", output_to_operand_aliasing={{}: (5, {})} | custom-call | flops 113246208 | bytes 262144 | tf_op jit(solution)/shard_map/pallas_call | solution.py:62
  85.8 5.5 %collective-permute-done.6.refs_0_ = bf16[192,1536]{1,0:T(8,128)(2,1)S(1)} collective-permute-done((bf16[192,1536]{1,0:T(8,128)(2,1)S(1)}, bf16[192,1536]{1,0:T(8,128)(2,1)S(1)}, u32[]{:S(2)}, u32[]{:S(2)}) %collective-permute-start.6) | collective-permute-done | bytes 589856 | tf_op jit(solution)/shard_map/ppermute | solution.py:218
  91.2 0.2 all-to-all-done
  91.4 3.8 %shard_map.73.parts_ref = bf16[2,8,192,384]{3,2,1,0:T(8,128)(2,1)} custom-call(s32[2]{0:T(128)S(1)} %pad_add_fusion.place_ref, bf16[192,1536]{1,0:T(8,128)(2,1)S(1)} %collective-permute-done.6.refs_0_, bf16[384,1536]{1,0:T(8,128)(2,1)} %fusion.34.refs_1_.refs_4_.refs_2_, ...), custom_call_target="tpu_custom_call", output_to_operand_aliasing={{}: (4, {})} | custom-call | flops 113246208 | bytes 262144 | tf_op jit(solution)/shard_map/pallas_call | solution.py:62
  95.3 0.0 copy-start.1
  95.3 7.5 %all-to-all-start.1 = ((bf16[16,192,384]{2,1,0:T(8,128)(2,1)}), bf16[16,192,384]{2,1,0:T(8,128)(2,1)S(1)}, u32[]{:S(2)}, u32[]{:S(2)}) async-start(bf16[16,192,384]{2,1,0:T(8,128)(2,1)} %bitcast.10), calls=%async_computation.1 | async-start | bytes 4718592 | tf_op jit(solution)/shard_map/all_to_all | solution.py:251
  102.8 0.0 copy-done.1
  102.8 0.1 reshape.38.gain_ref
  102.9 3.8 %shard_map.74 = (f32[8,256]{1,0:T(8,128)S(1)}, f32[2,8,384]{2,1,0:T(8,128)S(1)}) custom-call(bf16[2,8,192,384]{3,2,1,0:T(8,128)(2,1)} %shard_map.73.parts_ref, bf16[2,8,208,384]{3,2,1,0:T(8,128)(2,1)} %bitcast.4.x_ref.extra_ref, bf16[2,8,208,384]{3,2,1,0:T(8,128)(2,1)} %bitcast.4.x_ref.extra_ref), custom_call_target="tpu_custom_call" | custom-call | tf_op jit(solution)/shard_map/pallas_call | solution.py:152
  106.7 15.5 %psum.14 = f32[8,256]{1,0:T(8,128)S(1)} all-reduce(f32[8,256]{1,0:T(8,128)S(1)} %get-tuple-element.49), channel_id=1, replica_groups=mesh['y'=8,'zh'=4,'c'=2,'zl'=2,'x'=4] {'y'}, use_global_device_ids=true, to_apply=%region_0.0 | all-reduce | flops 2048 | bytes 16384 | tf_op jit(solution)/shard_map/psum | solution.py:254
  122.3 13.2 %psum.15 = f32[8,2,128]{2,1,0:T(2,128)S(1)} all-reduce(f32[8,2,128]{2,1,0:T(2,128)S(1)} %reshape.34), channel_id=1, replica_groups=mesh['y'=8,'zh'=4,'c'=2,'zl'=2,'x'=4] {'zh'}, use_global_device_ids=true, to_apply=%region_1.0 | all-reduce | flops 2048 | bytes 16384 | tf_op jit(solution)/shard_map/psum | solution.py:254
  135.5 0.0 all-to-all-done.1.parts_ref
  135.5 0.5 shard_map.75
  136.0 11.6 %all_to_all.15.small_ref = f32[16,8,128]{2,1,0:T(8,128)S(1)} all-to-all(f32[16,8,128]{2,1,0:T(8,128)S(1)} %maximum_maximum_fusion), channel_id=1, replica_groups=mesh['y'=8,'zh'=4,'c'=2,'zl'=2,'x'=4] {'c','zl','x'}, dimensions={0} | all-to-all | bytes 131072 | tf_op jit(solution)/shard_map/all_to_all | solution.py:270
  147.6 0.9 shard_map.76
  148.6 0.1 reshape.35
  148.7 0.7 reshape.36
  (5 shorter events, 0.0 us)
Async XLA Ops:
  0.6 37.0 %copy-start = (bf16[384,384]{1,0:T(8,128)(2,1)S(1)}, bf16[384,384]{1,0:T(8,128)(2,1)}, u32[]{:S(2)}) copy-start(bf16[384,384]{1,0:T(8,128)(2,1)} %tokens_ref) | copy-start | bytes 884740
  23.0 16.6 %collective-permute-start = (bf16[192,1536]{1,0:T(8,128)(2,1)S(1)}, bf16[192,1536]{1,0:T(8,128)(2,1)}, u32[]{:S(2)}, u32[]{:S(2)}) collective-permute-start(bf16[192,1536]{1,0:T(8,128)(2,1)S(1)} %all_gather.3.refs_0_), channel_id=1, source_target_pairs={{64,0},{128,64},{192,128},{256,192},{320,256},{384,320},{448,384},... | collective-permute-start | bytes 1769480 | tf_op jit(solution)/shard_map/ppermute | solution.py:218
  26.2 16.7 %collective-permute-start.2 = (bf16[192,1536]{1,0:T(8,128)(2,1)S(1)}, bf16[192,1536]{1,0:T(8,128)(2,1)}, u32[]{:S(2)}, u32[]{:S(2)}) collective-permute-start(bf16[192,1536]{1,0:T(8,128)(2,1)S(1)} %all_gather.3.refs_0_), channel_id=1, source_target_pairs={{448,0},{0,64},{64,128},{128,192},{192,256},{256,320},{320,384},{3... | collective-permute-start | bytes 1769480 | tf_op jit(solution)/shard_map/ppermute | solution.py:218
  42.9 22.4 %collective-permute-start.4 = (bf16[192,1536]{1,0:T(8,128)(2,1)}, bf16[192,1536]{1,0:T(8,128)(2,1)}, u32[]{:S(2)}, u32[]{:S(2)}) collective-permute-start(bf16[192,1536]{1,0:T(8,128)(2,1)} %collective-permute-done.2.refs_1_), channel_id=1, source_target_pairs={{448,0},{0,64},{64,128},{128,192},{192,256},{256,320},{320,384},{3... | collective-permute-start | bytes 1769480 | tf_op jit(solution)/shard_map/ppermute | solution.py:218
  48.3 15.0 %collective-permute-start.1 = (bf16[192,1536]{1,0:T(8,128)(2,1)}, bf16[192,1536]{1,0:T(8,128)(2,1)}, u32[]{:S(2)}, u32[]{:S(2)}) collective-permute-start(bf16[192,1536]{1,0:T(8,128)(2,1)} %collective-permute-done.refs_0_), channel_id=1, source_target_pairs={{64,0},{128,64},{192,128},{256,192},{320,256},{384,320},{448,384},... | collective-permute-start | bytes 1769480 | tf_op jit(solution)/shard_map/ppermute | solution.py:218
  50.3 19.6 %collective-permute-start.5 = (bf16[384,1536]{1,0:T(8,128)(2,1)}, bf16[384,1536]{1,0:T(8,128)(2,1)}, u32[]{:S(2)}, u32[]{:S(2)}) collective-permute-start(bf16[384,1536]{1,0:T(8,128)(2,1)} %fusion.34.refs_1_.refs_4_.refs_2_), channel_id=1, source_target_pairs={{0,8},{8,0},{1,9},{9,1},{2,10},{10,2},{3,11},{11,3},{4,12},{12,4},... | collective-permute-start | bytes 3538952 | tf_op jit(solution)/shard_map/ppermute | solution.py:25
  53.1 38.3 %all-to-all-start = ((bf16[16,208,384]{2,1,0:T(8,128)(2,1)}), bf16[16,208,384]{2,1,0:T(8,128)(2,1)}, u32[]{:S(2)}, u32[]{:S(2)}) async-start(bf16[16,208,384]{2,1,0:T(8,128)(2,1)} %bitcast.11), calls=%async_computation | async-start | bytes 5111808 | tf_op jit(solution)/shard_map/all_to_all | solution.py:235
  63.4 15.8 %collective-permute-start.3 = (bf16[192,1536]{1,0:T(8,128)(2,1)}, bf16[192,1536]{1,0:T(8,128)(2,1)S(1)}, u32[]{:S(2)}, u32[]{:S(2)}) collective-permute-start(bf16[192,1536]{1,0:T(8,128)(2,1)} %collective-permute-done.1.refs_2_), channel_id=1, source_target_pairs={{64,0},{128,64},{192,128},{256,192},{320,256},{384,320},{448,384},... | collective-permute-start | bytes 1769480 | tf_op jit(solution)/shard_map/ppermute | solution.py:218
  65.3 16.1 %collective-permute-start.7 = (bf16[192,1536]{1,0:T(8,128)(2,1)}, bf16[192,1536]{1,0:T(8,128)(2,1)S(1)}, u32[]{:S(2)}, u32[]{:S(2)}) collective-permute-start(bf16[192,1536]{1,0:T(8,128)(2,1)} %collective-permute-done.4.refs_3_), channel_id=1, source_target_pairs={{448,0},{0,64},{64,128},{128,192},{192,256},{256,320},{320,384},{3... | collective-permute-start | bytes 1769480 | tf_op jit(solution)/shard_map/ppermute | solution.py:218
  79.2 12.1 %collective-permute-start.6 = (bf16[192,1536]{1,0:T(8,128)(2,1)S(1)}, bf16[192,1536]{1,0:T(8,128)(2,1)S(1)}, u32[]{:S(2)}, u32[]{:S(2)}) collective-permute-start(bf16[192,1536]{1,0:T(8,128)(2,1)S(1)} %collective-permute-done.3.refs_0_), channel_id=1, source_target_pairs={{64,0},{128,64},{192,128},{256,192},{320,256},{384,320},{448,384},... | collective-permute-start | bytes 1769480 | tf_op jit(solution)/shard_map/ppermute | solution.py:218
  95.3 7.5 %copy-start.1 = (bf16[384]{0:T(512)(128)(2,1)S(1)}, bf16[384]{0:T(512)(128)(2,1)}, u32[]{:S(2)}) copy-start(bf16[384]{0:T(512)(128)(2,1)} %param.6) | copy-start | bytes 2308
  95.3 40.2 %all-to-all-start.1 = ((bf16[16,192,384]{2,1,0:T(8,128)(2,1)}), bf16[16,192,384]{2,1,0:T(8,128)(2,1)S(1)}, u32[]{:S(2)}, u32[]{:S(2)}) async-start(bf16[16,192,384]{2,1,0:T(8,128)(2,1)} %bitcast.10), calls=%async_computation.1 | async-start | bytes 4718592 | tf_op jit(solution)/shard_map/all_to_all | solution.py:251

commit v15 on v14

--- a/solution.py
+++ b/solution.py
@@ -27,29 +27,20 @@
 
 def products(groups, halves, place, parts, long=False):
     tokens, hidden = halves[0][1].shape
-    weights, operands = [w for _, w in groups], [d for _, d in halves]
+    weights, operands = [w for _, w in groups], [d for _, d, _ in halves]
     rows, n, both = weights[0].shape[0], len(groups), len(halves)
 
     def kernel(place_ref, *refs):
         w_refs, d_refs = refs[:n], refs[n : n + both]
-        out_ref, w_held, d_held, held, w_sem, d_sem, sem = refs[-7:]
-        loads = [
-            pltpu.make_async_copy(w, w_held.at[pl.ds(g * rows, rows)], w_sem.at[g])
-            for g, w in enumerate(w_refs)
-        ]
-        d_loads = [pltpu.make_async_copy(d, d_held.at[h], d_sem.at[h]) for h, d in enumerate(d_refs)]
-        for load in loads + d_loads:
-            load.start()
-        for load in loads:
-            load.wait()
+        out_ref, held, sem = refs[-3:]
         copies = []
-        for h, (k, _) in enumerate(halves):
-            d_loads[h].wait()
+        w = jnp.concatenate([r[...] for r in w_refs], axis=0)
+        for h, (k, _, count) in enumerate(halves):
             half = lax.rem(place_ref[1] + k, 2)
             out = lax.dot_general(
-                w_held[...], d_held[h], (((1,), (1,)), ((), ())), preferred_element_type=F32
+                w[: count * rows], d_refs[h][...], (((1,), (1,)), ((), ())), preferred_element_type=F32
             ).astype(BF16)
-            for g, (offset, _) in enumerate(groups):
+            for g, (offset, _) in enumerate(groups[:count]):
                 held[h, g] = out[g * rows : (g + 1) * rows]
                 block = lax.rem(place_ref[0] + offset + place_ref[1] * ((8 - 2 * offset) % 8), 8)
                 to = out_ref.at[half, block]
@@ -58,18 +49,14 @@
         for copy in copies:
             copy.wait()
 
-    anywhere = pl.BlockSpec(memory_space=pl.ANY)
+    anywhere, whole = pl.BlockSpec(memory_space=pl.ANY), pl.BlockSpec(memory_space=pltpu.VMEM)
     return pl.pallas_call(
         kernel,
-        in_specs=[pl.BlockSpec(memory_space=pltpu.SMEM)] + [anywhere] * (n + both + (parts is not None)),
+        in_specs=[pl.BlockSpec(memory_space=pltpu.SMEM)] + [whole] * (n + both) + [anywhere] * (parts is not None),
         out_specs=anywhere,
         out_shape=jax.ShapeDtypeStruct((2, 8, rows, tokens), BF16),
         scratch_shapes=[
-            pltpu.VMEM((n * rows, hidden), BF16),
-            pltpu.VMEM((both, tokens, hidden), BF16),
             pltpu.VMEM((both, n, rows, tokens), BF16),
-            pltpu.SemaphoreType.DMA((n,)),
-            pltpu.SemaphoreType.DMA((both,)),
             pltpu.SemaphoreType.DMA((both, n)),
         ],
         input_output_aliases={} if parts is None else {1 + n + both: 0},
@@ -233,21 +220,19 @@
     first2, second2 = step(first, 1), step(second, -1)
     d_other = partner(d_own, "c", 2, 1)
     x_all = lax.all_to_all(x_all.reshape(16, -1, rows), CHIPS, 0, 0)
-    parts = products([(0, w0)], [(0, d_own)], place, None, long=True)
+    parts = products([(0, w0)], [(0, d_own, 1)], place, None, long=True)
 
     first, second, parts = tie(first2, second2, parts)
     first3, second3 = step(first, 1), step(second, -1)
-    groups = [(1, first1), (7, second1), (2, first2), (6, second2)]
-    halves = [(0, d_own), (1, d_other)]
-    parts = products([(0, w0)], [(1, d_other)], place, parts)
-    parts = products(groups, halves, place, parts)
+    groups = [(1, first1), (7, second1), (2, first2), (6, second2), (0, w0)]
+    parts = products(groups, [(0, d_own, 4), (1, d_other, 5)], place, parts)
 
     first, second, parts = tie(first3, second3, parts)
     first4 = step(first, 1)
-    parts = products([(3, first3), (5, second)], halves, place, parts)
+    parts = products([(3, first3), (5, second)], [(0, d_own, 2), (1, d_other, 2)], place, parts)
 
     first4, parts, x_all = together((first4, parts, x_all))
-    parts = products([(4, first4)], halves, place, parts)
+    parts = products([(4, first4)], [(0, d_own, 1), (1, d_other, 1)], place, parts)
     received = lax.all_to_all(parts.reshape(16, share // 2, rows), CHIPS, 0, 0)
 
     shares, stat = gain_share(parts, x_all)

time: 150 us -> 151 us (level)
  Pallas kernels: 27.8 us -> 22.8 us
  waiting for transfers between devices: 10.5 us -> 14.6 us
  starting transfers between devices: 38.9 us -> 40.5 us
    pallas_call x5 -> x4, Pallas kernels: 20.7 us -> 15.7 us  [products(): pl.pallas_call(kernel, in_specs=[pl.BlockSpec(memory_space=pltpu.SMEM)] +...]
    all_to_all x1, waiting for transfers between devices: 0.18 us -> 4.19 us  [on_device(): x_all = lax.all_to_all(x_all.reshape(16, -1, rows), CHIPS, 0, 0)]
  transfers between devices with their start and end apart: 10 -> 10, of which waited for: 5 -> 4; matrix products, arithmetic and copies ran while one was open for 5% -> 5% of each run, Pallas kernels for 15% -> 12%
where the time goes in v15:
time: 151 us
  blocking collectives  63.2 us (42%)
  starting transfers between devices  40.5 us (27%)
  Pallas kernels  22.8 us (15%)
  waiting for transfers between devices  14.6 us (10%)
  other arithmetic  7.68 us (5%)
    psum x2, blocking collectives, on_device(): shares = lax.psum(lax.psum(shares, 'y'), 'zh')  28.7 us
    ppermute x7, starting transfers between devices, step(): lax.ppermute(array, ('y', 'c'), [(a * 2 + c, b * 2 + c) for a, b, c in mo...  23.1 us
    all_gather x1, blocking collectives, on_device(): w0 = lax.all_gather(w_in, 'zh', axis=0, tiled=True)  22.4 us
    pallas_call x4, Pallas kernels, products(): pl.pallas_call(kernel, in_specs=[pl.BlockSpec(memory_space=pltpu.SMEM)] +...  15.7 us
    all_to_all x1, blocking collectives, on_device(): small = lax.all_to_all(jnp.concatenate([small, small], axis=0), CHIPS, 0, 0)  12.1 us
    ppermute x7, waiting for transfers between devices, step(): lax.ppermute(array, ('y', 'c'), [(a * 2 + c, b * 2 + c) for a, b, c in mo...  10.4 us
    all_to_all x1, starting transfers between devices, on_device(): received = lax.all_to_all(parts.reshape(16, share // 2, rows), CHIPS, 0, 0)  8.8 us
    convert_element_type x1, other arithmetic, on_device(): d_own = gelu_back(act_cotangent.astype(F32))[0].astype(BF16)  7.6 us
  transfers between devices with their start and end apart: 10, of which 4 were waited for; matrix products, arithmetic and copies ran while one was open for 5% of the time, Pallas kernels for 12%

profile of v15, /device:TPU:1, one launch (start us, length us, event | category | flops | bytes accessed | tf_op | source)
XLA Modules:
  0.0 150.5 jit_solution(5270579169617076091)
XLA Ops:
  0.6 0.0 copy-start.1
  0.6 22.4 %all_gather.3.refs_0_.refs_4_ = bf16[192,1536]{1,0:T(8,128)(2,1)S(1)} all-gather(bf16[48,1536]{1,0:T(8,128)(2,1)} %param.8), channel_id=1, replica_groups=mesh['y'=8,'zh'=4,'c'=2,'zl'=2,'x'=4] {'zh'}, dimensions={0}, use_global_device_ids=true | all-gather | bytes 737280 | tf_op jit(solution)/shard_map/all_gather | solution.py:211
  23.0 0.0 copy-start
  23.0 3.2 %collective-permute-start = (bf16[192,1536]{1,0:T(8,128)(2,1)S(1)}, bf16[192,1536]{1,0:T(8,128)(2,1)}, u32[]{:S(2)}, u32[]{:S(2)}) collective-permute-start(bf16[192,1536]{1,0:T(8,128)(2,1)S(1)} %all_gather.3.refs_0_.refs_4_), channel_id=1, source_target_pairs={{64,0},{128,64},{192,128},{256,192},{320,256},{384,320},{448,384},... | collective-permute-start | bytes 1769480 | tf_op jit(solution)/shard_map/ppermute | solution.py:205
  26.2 3.8 %collective-permute-start.2 = (bf16[192,1536]{1,0:T(8,128)(2,1)S(1)}, bf16[192,1536]{1,0:T(8,128)(2,1)}, u32[]{:S(2)}, u32[]{:S(2)}) collective-permute-start(bf16[192,1536]{1,0:T(8,128)(2,1)S(1)} %all_gather.3.refs_0_.refs_4_), channel_id=1, source_target_pairs={{448,0},{0,64},{64,128},{128,192},{192,256},{256,320},{320,384},{3... | collective-permute-start | bytes 1769480 | tf_op jit(solution)/shard_map/ppermute | solution.py:205
  30.0 7.6 %fusion.34.refs_1_.refs_5_.refs_2_ = bf16[384,1536]{1,0:T(8,128)(2,1)} fusion(bf16[384,1536]{1,0:T(8,128)(2,1)} %param.9, bf16[384,1536]{1,0:T(8,128)(2,1)} %param.7), kind=kLoop, calls=%fused_computation.39 | loop fusion | flops 43646976 | bytes 3538944 | tf_op jit(solution)/shard_map/convert_element_type | solution.py:215
  37.6 0.0 copy-done.1
  37.6 1.9 %shard_map.68 = (bf16[384,384]{1,0:T(8,128)(2,1)S(1)}, bf16[2,8,208,384]{3,2,1,0:T(8,128)(2,1)}) custom-call(bf16[384,384]{1,0:T(8,128)(2,1)S(1)} %copy-done.1), custom_call_target="tpu_custom_call" | custom-call | tf_op jit(solution)/shard_map/pallas_call | solution.py:94
  39.6 0.1 pad_add_fusion.place_ref
  39.6 0.0 collective-permute-done.refs_0_
  39.6 3.3 %collective-permute-done.2.refs_1_ = bf16[192,1536]{1,0:T(8,128)(2,1)} collective-permute-done((bf16[192,1536]{1,0:T(8,128)(2,1)S(1)}, bf16[192,1536]{1,0:T(8,128)(2,1)}, u32[]{:S(2)}, u32[]{:S(2)}) %collective-permute-start.2) | collective-permute-done | bytes 589856 | tf_op jit(solution)/shard_map/ppermute | solution.py:205
  42.9 2.6 %collective-permute-start.1 = (bf16[192,1536]{1,0:T(8,128)(2,1)}, bf16[192,1536]{1,0:T(8,128)(2,1)}, u32[]{:S(2)}, u32[]{:S(2)}) collective-permute-start(bf16[192,1536]{1,0:T(8,128)(2,1)} %collective-permute-done.refs_0_), channel_id=1, source_target_pairs={{64,0},{128,64},{192,128},{256,192},{320,256},{384,320},{448,384},... | collective-permute-start | bytes 1769480 | tf_op jit(solution)/shard_map/ppermute | solution.py:205
  45.5 4.7 %collective-permute-start.4 = (bf16[192,1536]{1,0:T(8,128)(2,1)}, bf16[192,1536]{1,0:T(8,128)(2,1)}, u32[]{:S(2)}, u32[]{:S(2)}) collective-permute-start(bf16[192,1536]{1,0:T(8,128)(2,1)} %collective-permute-done.2.refs_1_), channel_id=1, source_target_pairs={{448,0},{0,64},{64,128},{128,192},{192,256},{256,320},{320,384},{3... | collective-permute-start | bytes 1769480 | tf_op jit(solution)/shard_map/ppermute | solution.py:205
  50.3 2.8 %collective-permute-start.5 = (bf16[384,1536]{1,0:T(8,128)(2,1)}, bf16[384,1536]{1,0:T(8,128)(2,1)}, u32[]{:S(2)}, u32[]{:S(2)}) collective-permute-start(bf16[384,1536]{1,0:T(8,128)(2,1)} %fusion.34.refs_1_.refs_5_.refs_2_), channel_id=1, source_target_pairs={{0,8},{8,0},{1,9},{9,1},{2,10},{10,2},{3,11},{11,3},{4,12},{12,4},... | collective-permute-start | bytes 3538952 | tf_op jit(solution)/shard_map/ppermute | solution.py:25
  53.1 5.7 %all-to-all-start = ((bf16[16,208,384]{2,1,0:T(8,128)(2,1)}), bf16[16,208,384]{2,1,0:T(8,128)(2,1)}, u32[]{:S(2)}, u32[]{:S(2)}) async-start(bf16[16,208,384]{2,1,0:T(8,128)(2,1)} %bitcast.11), calls=%async_computation | async-start | bytes 5111808 | tf_op jit(solution)/shard_map/all_to_all | solution.py:222
  58.9 0.0 copy-done
  58.9 2.5 %shard_map.69.refs_7_ = bf16[2,8,192,384]{3,2,1,0:T(8,128)(2,1)} custom-call(s32[2]{0:T(128)S(1)} %pad_add_fusion.place_ref, bf16[192,1536]{1,0:T(8,128)(2,1)S(1)} %all_gather.3.refs_0_.refs_4_, bf16[384,1536]{1,0:T(8,128)(2,1)} %fusion.34.refs_1_.refs_5_.refs_2_), custom_call_target="tpu_custom_call" | custom-call | flops 274877906944 | bytes 262144 | tf_op jit(solution)/shard_map/pallas_call | solution.py:53
  61.4 0.0 collective-permute-done.1.refs_2_
  61.4 1.9 %collective-permute-start.3 = (bf16[192,1536]{1,0:T(8,128)(2,1)}, bf16[192,1536]{1,0:T(8,128)(2,1)S(1)}, u32[]{:S(2)}, u32[]{:S(2)}) collective-permute-start(bf16[192,1536]{1,0:T(8,128)(2,1)} %collective-permute-done.1.refs_2_), channel_id=1, source_target_pairs={{64,0},{128,64},{192,128},{256,192},{320,256},{384,320},{448,384},... | collective-permute-start | bytes 1769480 | tf_op jit(solution)/shard_map/ppermute | solution.py:205
  63.3 0.0 collective-permute-done.4.refs_3_
  63.3 4.9 %collective-permute-start.7 = (bf16[192,1536]{1,0:T(8,128)(2,1)}, bf16[192,1536]{1,0:T(8,128)(2,1)S(1)}, u32[]{:S(2)}, u32[]{:S(2)}) collective-permute-start(bf16[192,1536]{1,0:T(8,128)(2,1)} %collective-permute-done.4.refs_3_), channel_id=1, source_target_pairs={{448,0},{0,64},{64,128},{128,192},{192,256},{256,320},{320,384},{3... | collective-permute-start | bytes 1769480 | tf_op jit(solution)/shard_map/ppermute | solution.py:205
  68.2 0.0 collective-permute-done.5.refs_6_.refs_3_.refs_2_
  68.2 6.2 %shard_map.70.refs_4_ = bf16[2,8,192,384]{3,2,1,0:T(8,128)(2,1)} custom-call(s32[2]{0:T(128)S(1)} %pad_add_fusion.place_ref, bf16[192,1536]{1,0:T(8,128)(2,1)} %collective-permute-done.refs_0_, bf16[192,1536]{1,0:T(8,128)(2,1)} %collective-permute-done.2.refs_1_, bf16[192,1536]{1,0:T(8,128)(2,1)} %collective-permute-done.1.refs_2_, ...), custom_call_target="tpu_custom_call", output_to_operand_aliasing={{}: (8, {})} | custom-call | flops 113246208 | bytes 262144 | tf_op jit(solution)/shard_map/pallas_call | solution.py:53
  74.4 0.0 collective-permute-done.3.refs_0_
  74.5 1.9 %collective-permute-start.6 = (bf16[192,1536]{1,0:T(8,128)(2,1)S(1)}, bf16[192,1536]{1,0:T(8,128)(2,1)S(1)}, u32[]{:S(2)}, u32[]{:S(2)}) collective-permute-start(bf16[192,1536]{1,0:T(8,128)(2,1)S(1)} %collective-permute-done.3.refs_0_), channel_id=1, source_target_pairs={{64,0},{128,64},{192,128},{256,192},{320,256},{384,320},{448,384},... | collective-permute-start | bytes 1769480 | tf_op jit(solution)/shard_map/ppermute | solution.py:205
  76.4 5.2 %collective-permute-done.7.refs_1_ = bf16[192,1536]{1,0:T(8,128)(2,1)S(1)} collective-permute-done((bf16[192,1536]{1,0:T(8,128)(2,1)}, bf16[192,1536]{1,0:T(8,128)(2,1)S(1)}, u32[]{:S(2)}, u32[]{:S(2)}) %collective-permute-start.7) | collective-permute-done | bytes 589856 | tf_op jit(solution)/shard_map/ppermute | solution.py:205
  81.6 3.7 %shard_map.71.refs_3_ = bf16[2,8,192,384]{3,2,1,0:T(8,128)(2,1)} custom-call(s32[2]{0:T(128)S(1)} %pad_add_fusion.place_ref, bf16[192,1536]{1,0:T(8,128)(2,1)S(1)} %collective-permute-done.3.refs_0_, bf16[192,1536]{1,0:T(8,128)(2,1)S(1)} %collective-permute-done.7.refs_1_, ...), custom_call_target="tpu_custom_call", output_to_operand_aliasing={{}: (5, {})} | custom-call | flops 113246208 | bytes 262144 | tf_op jit(solution)/shard_map/pallas_call | solution.py:53
  85.3 1.9 %collective-permute-done.6.refs_0_ = bf16[192,1536]{1,0:T(8,128)(2,1)S(1)} collective-permute-done((bf16[192,1536]{1,0:T(8,128)(2,1)S(1)}, bf16[192,1536]{1,0:T(8,128)(2,1)S(1)}, u32[]{:S(2)}, u32[]{:S(2)}) %collective-permute-start.6) | collective-permute-done | bytes 589856 | tf_op jit(solution)/shard_map/ppermute | solution.py:205
  87.2 4.2 %all-to-all-done = bf16[16,208,384]{2,1,0:T(8,128)(2,1)} async-done(((bf16[16,208,384]{2,1,0:T(8,128)(2,1)}), bf16[16,208,384]{2,1,0:T(8,128)(2,1)}, u32[]{:S(2)}, u32[]{:S(2)}) %all-to-all-start) | async-done | bytes 2555936 | tf_op jit(solution)/shard_map/all_to_all | solution.py:222
  91.4 3.2 %shard_map.72.parts_ref = bf16[2,8,192,384]{3,2,1,0:T(8,128)(2,1)} custom-call(s32[2]{0:T(128)S(1)} %pad_add_fusion.place_ref, bf16[192,1536]{1,0:T(8,128)(2,1)S(1)} %collective-permute-done.6.refs_0_, bf16[384,1536]{1,0:T(8,128)(2,1)} %fusion.34.refs_1_.refs_5_.refs_2_, ...), custom_call_target="tpu_custom_call", output_to_operand_aliasing={{}: (4, {})} | custom-call | flops 113246208 | bytes 262144 | tf_op jit(solution)/shard_map/pallas_call | solution.py:53
  94.7 0.0 copy-start.2
  94.7 8.8 %all-to-all-start.1 = ((bf16[16,192,384]{2,1,0:T(8,128)(2,1)}), bf16[16,192,384]{2,1,0:T(8,128)(2,1)S(1)}, u32[]{:S(2)}, u32[]{:S(2)}) async-start(bf16[16,192,384]{2,1,0:T(8,128)(2,1)} %bitcast.10), calls=%async_computation.1 | async-start | bytes 4718592 | tf_op jit(solution)/shard_map/all_to_all | solution.py:236
  103.5 0.0 copy-done.2
  103.5 0.1 reshape.38.gain_ref
  103.6 3.8 %shard_map.73 = (f32[8,256]{1,0:T(8,128)S(1)}, f32[2,8,384]{2,1,0:T(8,128)S(1)}) custom-call(bf16[2,8,192,384]{3,2,1,0:T(8,128)(2,1)} %shard_map.72.parts_ref, bf16[2,8,208,384]{3,2,1,0:T(8,128)(2,1)} %bitcast.4.x_ref.extra_ref, bf16[2,8,208,384]{3,2,1,0:T(8,128)(2,1)} %bitcast.4.x_ref.extra_ref), custom_call_target="tpu_custom_call" | custom-call | tf_op jit(solution)/shard_map/pallas_call | solution.py:139
  107.4 15.5 %psum.14 = f32[8,256]{1,0:T(8,128)S(1)} all-reduce(f32[8,256]{1,0:T(8,128)S(1)} %get-tuple-element.49), channel_id=1, replica_groups=mesh['y'=8,'zh'=4,'c'=2,'zl'=2,'x'=4] {'y'}, use_global_device_ids=true, to_apply=%region_0.0 | all-reduce | flops 2048 | bytes 16384 | tf_op jit(solution)/shard_map/psum | solution.py:239
  122.9 13.2 %psum.15 = f32[8,2,128]{2,1,0:T(2,128)S(1)} all-reduce(f32[8,2,128]{2,1,0:T(2,128)S(1)} %reshape.34), channel_id=1, replica_groups=mesh['y'=8,'zh'=4,'c'=2,'zl'=2,'x'=4] {'zh'}, use_global_device_ids=true, to_apply=%region_1.0 | all-reduce | flops 2048 | bytes 16384 | tf_op jit(solution)/shard_map/psum | solution.py:239
  136.1 0.0 all-to-all-done.1.parts_ref
  136.1 0.5 shard_map.74
  136.7 12.1 %all_to_all.15.small_ref = f32[16,8,128]{2,1,0:T(8,128)S(1)} all-to-all(f32[16,8,128]{2,1,0:T(8,128)S(1)} %maximum_maximum_fusion), channel_id=1, replica_groups=mesh['y'=8,'zh'=4,'c'=2,'zl'=2,'x'=4] {'c','zl','x'}, dimensions={0} | all-to-all | bytes 131072 | tf_op jit(solution)/shard_map/all_to_all | solution.py:255
  148.8 0.9 shard_map.75
  149.8 0.1 reshape.35
  149.9 0.7 reshape.36
  (5 shorter events, 0.0 us)
Async XLA Ops:
  0.6 37.0 %copy-start.1 = (bf16[384,384]{1,0:T(8,128)(2,1)S(1)}, bf16[384,384]{1,0:T(8,128)(2,1)}, u32[]{:S(2)}) copy-start(bf16[384,384]{1,0:T(8,128)(2,1)} %tokens_ref) | copy-start | bytes 884740
  23.0 35.8 %copy-start = (bf16[192,1536]{1,0:T(8,128)(2,1)}, bf16[192,1536]{1,0:T(8,128)(2,1)S(1)}, u32[]{:S(2)}) copy-start(bf16[192,1536]{1,0:T(8,128)(2,1)S(1)} %all_gather.3.refs_0_.refs_4_) | copy-start | bytes 1769476
  23.0 16.6 %collective-permute-start = (bf16[192,1536]{1,0:T(8,128)(2,1)S(1)}, bf16[192,1536]{1,0:T(8,128)(2,1)}, u32[]{:S(2)}, u32[]{:S(2)}) collective-permute-start(bf16[192,1536]{1,0:T(8,128)(2,1)S(1)} %all_gather.3.refs_0_.refs_4_), channel_id=1, source_target_pairs={{64,0},{128,64},{192,128},{256,192},{320,256},{384,320},{448,384},... | collective-permute-start | bytes 1769480 | tf_op jit(solution)/shard_map/ppermute | solution.py:205
  26.2 16.7 %collective-permute-start.2 = (bf16[192,1536]{1,0:T(8,128)(2,1)S(1)}, bf16[192,1536]{1,0:T(8,128)(2,1)}, u32[]{:S(2)}, u32[]{:S(2)}) collective-permute-start(bf16[192,1536]{1,0:T(8,128)(2,1)S(1)} %all_gather.3.refs_0_.refs_4_), channel_id=1, source_target_pairs={{448,0},{0,64},{64,128},{128,192},{192,256},{256,320},{320,384},{3... | collective-permute-start | bytes 1769480 | tf_op jit(solution)/shard_map/ppermute | solution.py:205
  42.9 18.4 %collective-permute-start.1 = (bf16[192,1536]{1,0:T(8,128)(2,1)}, bf16[192,1536]{1,0:T(8,128)(2,1)}, u32[]{:S(2)}, u32[]{:S(2)}) collective-permute-start(bf16[192,1536]{1,0:T(8,128)(2,1)} %collective-permute-done.refs_0_), channel_id=1, source_target_pairs={{64,0},{128,64},{192,128},{256,192},{320,256},{384,320},{448,384},... | collective-permute-start | bytes 1769480 | tf_op jit(solution)/shard_map/ppermute | solution.py:205
  45.5 17.8 %collective-permute-start.4 = (bf16[192,1536]{1,0:T(8,128)(2,1)}, bf16[192,1536]{1,0:T(8,128)(2,1)}, u32[]{:S(2)}, u32[]{:S(2)}) collective-permute-start(bf16[192,1536]{1,0:T(8,128)(2,1)} %collective-permute-done.2.refs_1_), channel_id=1, source_target_pairs={{448,0},{0,64},{64,128},{128,192},{192,256},{256,320},{320,384},{3... | collective-permute-start | bytes 1769480 | tf_op jit(solution)/shard_map/ppermute | solution.py:205
  50.3 17.9 %collective-permute-start.5 = (bf16[384,1536]{1,0:T(8,128)(2,1)}, bf16[384,1536]{1,0:T(8,128)(2,1)}, u32[]{:S(2)}, u32[]{:S(2)}) collective-permute-start(bf16[384,1536]{1,0:T(8,128)(2,1)} %fusion.34.refs_1_.refs_5_.refs_2_), channel_id=1, source_target_pairs={{0,8},{8,0},{1,9},{9,1},{2,10},{10,2},{3,11},{11,3},{4,12},{12,4},... | collective-permute-start | bytes 3538952 | tf_op jit(solution)/shard_map/ppermute | solution.py:25
  53.1 38.3 %all-to-all-start = ((bf16[16,208,384]{2,1,0:T(8,128)(2,1)}), bf16[16,208,384]{2,1,0:T(8,128)(2,1)}, u32[]{:S(2)}, u32[]{:S(2)}) async-start(bf16[16,208,384]{2,1,0:T(8,128)(2,1)} %bitcast.11), calls=%async_computation | async-start | bytes 5111808 | tf_op jit(solution)/shard_map/all_to_all | solution.py:222
  61.4 13.1 %collective-permute-start.3 = (bf16[192,1536]{1,0:T(8,128)(2,1)}, bf16[192,1536]{1,0:T(8,128)(2,1)S(1)}, u32[]{:S(2)}, u32[]{:S(2)}) collective-permute-start(bf16[192,1536]{1,0:T(8,128)(2,1)} %collective-permute-done.1.refs_2_), channel_id=1, source_target_pairs={{64,0},{128,64},{192,128},{256,192},{320,256},{384,320},{448,384},... | collective-permute-start | bytes 1769480 | tf_op jit(solution)/shard_map/ppermute | solution.py:205
  63.3 18.3 %collective-permute-start.7 = (bf16[192,1536]{1,0:T(8,128)(2,1)}, bf16[192,1536]{1,0:T(8,128)(2,1)S(1)}, u32[]{:S(2)}, u32[]{:S(2)}) collective-permute-start(bf16[192,1536]{1,0:T(8,128)(2,1)} %collective-permute-done.4.refs_3_), channel_id=1, source_target_pairs={{448,0},{0,64},{64,128},{128,192},{192,256},{256,320},{320,384},{3... | collective-permute-start | bytes 1769480 | tf_op jit(solution)/shard_map/ppermute | solution.py:205
  74.5 12.8 %collective-permute-start.6 = (bf16[192,1536]{1,0:T(8,128)(2,1)S(1)}, bf16[192,1536]{1,0:T(8,128)(2,1)S(1)}, u32[]{:S(2)}, u32[]{:S(2)}) collective-permute-start(bf16[192,1536]{1,0:T(8,128)(2,1)S(1)} %collective-permute-done.3.refs_0_), channel_id=1, source_target_pairs={{64,0},{128,64},{192,128},{256,192},{320,256},{384,320},{448,384},... | collective-permute-start | bytes 1769480 | tf_op jit(solution)/shard_map/ppermute | solution.py:205
  94.7 8.8 %copy-start.2 = (bf16[384]{0:T(512)(128)(2,1)S(1)}, bf16[384]{0:T(512)(128)(2,1)}, u32[]{:S(2)}) copy-start(bf16[384]{0:T(512)(128)(2,1)} %param.6) | copy-start | bytes 2308
  94.7 41.5 %all-to-all-start.1 = ((bf16[16,192,384]{2,1,0:T(8,128)(2,1)}), bf16[16,192,384]{2,1,0:T(8,128)(2,1)S(1)}, u32[]{:S(2)}, u32[]{:S(2)}) async-start(bf16[16,192,384]{2,1,0:T(8,128)(2,1)} %bitcast.10), calls=%async_computation.1 | async-start | bytes 4718592 | tf_op jit(solution)/shard_map/all_to_all | solution.py:236

commit v16 on v15

--- a/solution.py
+++ b/solution.py
@@ -224,8 +224,9 @@
 
     first, second, parts = tie(first2, second2, parts)
     first3, second3 = step(first, 1), step(second, -1)
-    groups = [(1, first1), (7, second1), (2, first2), (6, second2), (0, w0)]
-    parts = products(groups, [(0, d_own, 4), (1, d_other, 5)], place, parts)
+    groups = [(1, first1), (7, second1), (2, first2), (6, second2)]
+    parts = products([(0, w0)], [(1, d_other, 1)], place, parts)
+    parts = products(groups, [(0, d_own, 4), (1, d_other, 4)], place, parts)
 
     first, second, parts = tie(first3, second3, parts)
     first4 = step(first, 1)

time: 151 us -> 149 us (0.987)
  Pallas kernels: 22.8 us -> 24.8 us
  waiting for transfers between devices: 14.6 us -> 12.9 us
  starting transfers between devices: 40.5 us -> 38.9 us
    all_to_all x1, waiting for transfers between devices: 4.19 us -> 1.08 us  [on_device(): x_all = lax.all_to_all(x_all.reshape(16, -1, rows), CHIPS, 0, 0)]
    pallas_call x4 -> x5, Pallas kernels: 15.7 us -> 17.7 us  [products(): pl.pallas_call(kernel, in_specs=[pl.BlockSpec(memory_space=pltpu.SMEM)] +...]
  transfers between devices with their start and end apart: 10 -> 10, of which waited for: 4 -> 5; matrix products, arithmetic and copies ran while one was open for 5% -> 5% of each run, Pallas kernels for 12% -> 14%
where the time goes in v16:
time: 149 us
  blocking collectives  62.7 us (42%)
  starting transfers between devices  38.9 us (26%)
  Pallas kernels  24.8 us (17%)
  waiting for transfers between devices  12.9 us (9%)
  other arithmetic  7.7 us (5%)
    psum x2, blocking collectives, on_device(): shares = lax.psum(lax.psum(shares, 'y'), 'zh')  28.7 us
    ppermute x7, starting transfers between devices, step(): lax.ppermute(array, ('y', 'c'), [(a * 2 + c, b * 2 + c) for a, b, c in mo...  22.7 us
    all_gather x1, blocking collectives, on_device(): w0 = lax.all_gather(w_in, 'zh', axis=0, tiled=True)  22.4 us
    pallas_call x5, Pallas kernels, products(): pl.pallas_call(kernel, in_specs=[pl.BlockSpec(memory_space=pltpu.SMEM)] +...  17.7 us
    ppermute x7, waiting for transfers between devices, step(): lax.ppermute(array, ('y', 'c'), [(a * 2 + c, b * 2 + c) for a, b, c in mo...  11.8 us
    all_to_all x1, blocking collectives, on_device(): small = lax.all_to_all(jnp.concatenate([small, small], axis=0), CHIPS, 0, 0)  11.6 us
    convert_element_type x1, other arithmetic, on_device(): d_own = gelu_back(act_cotangent.astype(F32))[0].astype(BF16)  7.61 us
    all_to_all x1, starting transfers between devices, on_device(): received = lax.all_to_all(parts.reshape(16, share // 2, rows), CHIPS, 0, 0)  7.52 us
  transfers between devices with their start and end apart: 10, of which 5 were waited for; matrix products, arithmetic and copies ran while one was open for 5% of the time, Pallas kernels for 14%

profile of v16, /device:TPU:1, one launch (start us, length us, event | category | flops | bytes accessed | tf_op | source)
XLA Modules:
  0.0 148.7 jit_solution(9682495160384800896)
XLA Ops:
  0.6 0.0 copy-start
  0.6 22.4 %all_gather.3.refs_0_ = bf16[192,1536]{1,0:T(8,128)(2,1)S(1)} all-gather(bf16[48,1536]{1,0:T(8,128)(2,1)} %param.8), channel_id=1, replica_groups=mesh['y'=8,'zh'=4,'c'=2,'zl'=2,'x'=4] {'zh'}, dimensions={0}, use_global_device_ids=true | all-gather | bytes 737280 | tf_op jit(solution)/shard_map/all_gather | solution.py:211
  23.0 3.2 %collective-permute-start = (bf16[192,1536]{1,0:T(8,128)(2,1)S(1)}, bf16[192,1536]{1,0:T(8,128)(2,1)}, u32[]{:S(2)}, u32[]{:S(2)}) collective-permute-start(bf16[192,1536]{1,0:T(8,128)(2,1)S(1)} %all_gather.3.refs_0_), channel_id=1, source_target_pairs={{64,0},{128,64},{192,128},{256,192},{320,256},{384,320},{448,384},... | collective-permute-start | bytes 1769480 | tf_op jit(solution)/shard_map/ppermute | solution.py:205
  26.2 3.8 %collective-permute-start.2 = (bf16[192,1536]{1,0:T(8,128)(2,1)S(1)}, bf16[192,1536]{1,0:T(8,128)(2,1)}, u32[]{:S(2)}, u32[]{:S(2)}) collective-permute-start(bf16[192,1536]{1,0:T(8,128)(2,1)S(1)} %all_gather.3.refs_0_), channel_id=1, source_target_pairs={{448,0},{0,64},{64,128},{128,192},{192,256},{256,320},{320,384},{3... | collective-permute-start | bytes 1769480 | tf_op jit(solution)/shard_map/ppermute | solution.py:205
  30.0 7.6 %fusion.34.refs_1_.refs_4_.refs_2_ = bf16[384,1536]{1,0:T(8,128)(2,1)} fusion(bf16[384,1536]{1,0:T(8,128)(2,1)} %param.9, bf16[384,1536]{1,0:T(8,128)(2,1)} %param.7), kind=kLoop, calls=%fused_computation.39 | loop fusion | flops 43646976 | bytes 3538944 | tf_op jit(solution)/shard_map/convert_element_type | solution.py:215
  37.7 0.0 copy-done
  37.7 1.9 %shard_map.68 = (bf16[384,384]{1,0:T(8,128)(2,1)S(1)}, bf16[2,8,208,384]{3,2,1,0:T(8,128)(2,1)}) custom-call(bf16[384,384]{1,0:T(8,128)(2,1)S(1)} %copy-done), custom_call_target="tpu_custom_call" | custom-call | tf_op jit(solution)/shard_map/pallas_call | solution.py:94
  39.6 0.1 pad_add_fusion.place_ref
  39.6 0.0 collective-permute-done.refs_0_
  39.6 3.3 %collective-permute-done.2.refs_1_ = bf16[192,1536]{1,0:T(8,128)(2,1)} collective-permute-done((bf16[192,1536]{1,0:T(8,128)(2,1)S(1)}, bf16[192,1536]{1,0:T(8,128)(2,1)}, u32[]{:S(2)}, u32[]{:S(2)}) %collective-permute-start.2) | collective-permute-done | bytes 589856 | tf_op jit(solution)/shard_map/ppermute | solution.py:205
  42.9 5.4 %collective-permute-start.4 = (bf16[192,1536]{1,0:T(8,128)(2,1)}, bf16[192,1536]{1,0:T(8,128)(2,1)}, u32[]{:S(2)}, u32[]{:S(2)}) collective-permute-start(bf16[192,1536]{1,0:T(8,128)(2,1)} %collective-permute-done.2.refs_1_), channel_id=1, source_target_pairs={{448,0},{0,64},{64,128},{128,192},{192,256},{256,320},{320,384},{3... | collective-permute-start | bytes 1769480 | tf_op jit(solution)/shard_map/ppermute | solution.py:205
  48.3 1.9 %collective-permute-start.1 = (bf16[192,1536]{1,0:T(8,128)(2,1)}, bf16[192,1536]{1,0:T(8,128)(2,1)}, u32[]{:S(2)}, u32[]{:S(2)}) collective-permute-start(bf16[192,1536]{1,0:T(8,128)(2,1)} %collective-permute-done.refs_0_), channel_id=1, source_target_pairs={{64,0},{128,64},{192,128},{256,192},{320,256},{384,320},{448,384},... | collective-permute-start | bytes 1769480 | tf_op jit(solution)/shard_map/ppermute | solution.py:205
  50.3 2.8 %collective-permute-start.5 = (bf16[384,1536]{1,0:T(8,128)(2,1)}, bf16[384,1536]{1,0:T(8,128)(2,1)}, u32[]{:S(2)}, u32[]{:S(2)}) collective-permute-start(bf16[384,1536]{1,0:T(8,128)(2,1)} %fusion.34.refs_1_.refs_4_.refs_2_), channel_id=1, source_target_pairs={{0,8},{8,0},{1,9},{9,1},{2,10},{10,2},{3,11},{11,3},{4,12},{12,4},... | collective-permute-start | bytes 3538952 | tf_op jit(solution)/shard_map/ppermute | solution.py:25
  53.1 5.7 %all-to-all-start = ((bf16[16,208,384]{2,1,0:T(8,128)(2,1)}), bf16[16,208,384]{2,1,0:T(8,128)(2,1)}, u32[]{:S(2)}, u32[]{:S(2)}) async-start(bf16[16,208,384]{2,1,0:T(8,128)(2,1)} %bitcast.11), calls=%async_computation | async-start | bytes 5111808 | tf_op jit(solution)/shard_map/all_to_all | solution.py:222
  58.9 2.5 %shard_map.69.refs_2_ = bf16[2,8,192,384]{3,2,1,0:T(8,128)(2,1)} custom-call(s32[2]{0:T(128)S(1)} %pad_add_fusion.place_ref, bf16[192,1536]{1,0:T(8,128)(2,1)S(1)} %all_gather.3.refs_0_, bf16[384,1536]{1,0:T(8,128)(2,1)} %fusion.34.refs_1_.refs_4_.refs_2_), custom_call_target="tpu_custom_call" | custom-call | flops 274877906944 | bytes 262144 | tf_op jit(solution)/shard_map/pallas_call | solution.py:53
  61.4 2.0 %collective-permute-done.1.refs_2_ = bf16[192,1536]{1,0:T(8,128)(2,1)} collective-permute-done((bf16[192,1536]{1,0:T(8,128)(2,1)}, bf16[192,1536]{1,0:T(8,128)(2,1)}, u32[]{:S(2)}, u32[]{:S(2)}) %collective-permute-start.1) | collective-permute-done | bytes 589856 | tf_op jit(solution)/shard_map/ppermute | solution.py:205
  63.4 1.9 %collective-permute-start.3 = (bf16[192,1536]{1,0:T(8,128)(2,1)}, bf16[192,1536]{1,0:T(8,128)(2,1)S(1)}, u32[]{:S(2)}, u32[]{:S(2)}) collective-permute-start(bf16[192,1536]{1,0:T(8,128)(2,1)} %collective-permute-done.1.refs_2_), channel_id=1, source_target_pairs={{64,0},{128,64},{192,128},{256,192},{320,256},{384,320},{448,384},... | collective-permute-start | bytes 1769480 | tf_op jit(solution)/shard_map/ppermute | solution.py:205
  65.3 0.0 collective-permute-done.4.refs_3_
  65.3 4.6 %collective-permute-start.7 = (bf16[192,1536]{1,0:T(8,128)(2,1)}, bf16[192,1536]{1,0:T(8,128)(2,1)S(1)}, u32[]{:S(2)}, u32[]{:S(2)}) collective-permute-start(bf16[192,1536]{1,0:T(8,128)(2,1)} %collective-permute-done.4.refs_3_), channel_id=1, source_target_pairs={{448,0},{0,64},{64,128},{128,192},{192,256},{256,320},{320,384},{3... | collective-permute-start | bytes 1769480 | tf_op jit(solution)/shard_map/ppermute | solution.py:205
  69.9 0.0 collective-permute-done.5.refs_1_.refs_5_.refs_3_.refs_2_
  69.9 2.5 %shard_map.70.refs_6_ = bf16[2,8,192,384]{3,2,1,0:T(8,128)(2,1)} custom-call(s32[2]{0:T(128)S(1)} %pad_add_fusion.place_ref, bf16[192,1536]{1,0:T(8,128)(2,1)S(1)} %all_gather.3.refs_0_, bf16[384,1536]{1,0:T(8,128)(2,1)} %collective-permute-done.5.refs_1_.refs_5_.refs_3_.refs_2_, ...), custom_call_target="tpu_custom_call", output_to_operand_aliasing={{}: (3, {})} | custom-call | flops 113246208 | bytes 262144 | tf_op jit(solution)/shard_map/pallas_call | solution.py:53
  72.4 5.7 %shard_map.71.refs_4_ = bf16[2,8,192,384]{3,2,1,0:T(8,128)(2,1)} custom-call(s32[2]{0:T(128)S(1)} %pad_add_fusion.place_ref, bf16[192,1536]{1,0:T(8,128)(2,1)} %collective-permute-done.refs_0_, bf16[192,1536]{1,0:T(8,128)(2,1)} %collective-permute-done.2.refs_1_, bf16[192,1536]{1,0:T(8,128)(2,1)} %collective-permute-done.1.refs_2_, ...), custom_call_target="tpu_custom_call", output_to_operand_aliasing={{}: (7, {})} | custom-call | flops 113246208 | bytes 262144 | tf_op jit(solution)/shard_map/pallas_call | solution.py:53
  78.1 0.0 collective-permute-done.3.refs_0_
  78.1 1.9 %collective-permute-start.6 = (bf16[192,1536]{1,0:T(8,128)(2,1)S(1)}, bf16[192,1536]{1,0:T(8,128)(2,1)S(1)}, u32[]{:S(2)}, u32[]{:S(2)}) collective-permute-start(bf16[192,1536]{1,0:T(8,128)(2,1)S(1)} %collective-permute-done.3.refs_0_), channel_id=1, source_target_pairs={{64,0},{128,64},{192,128},{256,192},{320,256},{384,320},{448,384},... | collective-permute-start | bytes 1769480 | tf_op jit(solution)/shard_map/ppermute | solution.py:205
  80.0 1.3 collective-permute-done.7.refs_1_
  81.4 3.7 %shard_map.72.refs_3_ = bf16[2,8,192,384]{3,2,1,0:T(8,128)(2,1)} custom-call(s32[2]{0:T(128)S(1)} %pad_add_fusion.place_ref, bf16[192,1536]{1,0:T(8,128)(2,1)S(1)} %collective-permute-done.3.refs_0_, bf16[192,1536]{1,0:T(8,128)(2,1)S(1)} %collective-permute-done.7.refs_1_, ...), custom_call_target="tpu_custom_call", output_to_operand_aliasing={{}: (5, {})} | custom-call | flops 113246208 | bytes 262144 | tf_op jit(solution)/shard_map/pallas_call | solution.py:53
  85.1 5.2 %collective-permute-done.6.refs_0_ = bf16[192,1536]{1,0:T(8,128)(2,1)S(1)} collective-permute-done((bf16[192,1536]{1,0:T(8,128)(2,1)S(1)}, bf16[192,1536]{1,0:T(8,128)(2,1)S(1)}, u32[]{:S(2)}, u32[]{:S(2)}) %collective-permute-start.6) | collective-permute-done | bytes 589856 | tf_op jit(solution)/shard_map/ppermute | solution.py:205
  90.3 1.1 all-to-all-done
  91.4 3.2 %shard_map.73.parts_ref = bf16[2,8,192,384]{3,2,1,0:T(8,128)(2,1)} custom-call(s32[2]{0:T(128)S(1)} %pad_add_fusion.place_ref, bf16[192,1536]{1,0:T(8,128)(2,1)S(1)} %collective-permute-done.6.refs_0_, bf16[384,1536]{1,0:T(8,128)(2,1)} %fusion.34.refs_1_.refs_4_.refs_2_, ...), custom_call_target="tpu_custom_call", output_to_operand_aliasing={{}: (4, {})} | custom-call | flops 113246208 | bytes 262144 | tf_op jit(solution)/shard_map/pallas_call | solution.py:53
  94.7 0.0 copy-start.1
  94.7 7.5 %all-to-all-start.1 = ((bf16[16,192,384]{2,1,0:T(8,128)(2,1)}), bf16[16,192,384]{2,1,0:T(8,128)(2,1)S(1)}, u32[]{:S(2)}, u32[]{:S(2)}) async-start(bf16[16,192,384]{2,1,0:T(8,128)(2,1)} %bitcast.10), calls=%async_computation.1 | async-start | bytes 4718592 | tf_op jit(solution)/shard_map/all_to_all | solution.py:237
  102.2 0.0 copy-done.1
  102.2 0.1 reshape.38.gain_ref
  102.3 3.8 %shard_map.74 = (f32[8,256]{1,0:T(8,128)S(1)}, f32[2,8,384]{2,1,0:T(8,128)S(1)}) custom-call(bf16[2,8,192,384]{3,2,1,0:T(8,128)(2,1)} %shard_map.73.parts_ref, bf16[2,8,208,384]{3,2,1,0:T(8,128)(2,1)} %bitcast.4.x_ref.extra_ref, bf16[2,8,208,384]{3,2,1,0:T(8,128)(2,1)} %bitcast.4.x_ref.extra_ref), custom_call_target="tpu_custom_call" | custom-call | tf_op jit(solution)/shard_map/pallas_call | solution.py:139
  106.1 15.5 %psum.14 = f32[8,256]{1,0:T(8,128)S(1)} all-reduce(f32[8,256]{1,0:T(8,128)S(1)} %get-tuple-element.49), channel_id=1, replica_groups=mesh['y'=8,'zh'=4,'c'=2,'zl'=2,'x'=4] {'y'}, use_global_device_ids=true, to_apply=%region_0.0 | all-reduce | flops 2048 | bytes 16384 | tf_op jit(solution)/shard_map/psum | solution.py:240
  121.7 13.2 %psum.15 = f32[8,2,128]{2,1,0:T(2,128)S(1)} all-reduce(f32[8,2,128]{2,1,0:T(2,128)S(1)} %reshape.34), channel_id=1, replica_groups=mesh['y'=8,'zh'=4,'c'=2,'zl'=2,'x'=4] {'zh'}, use_global_device_ids=true, to_apply=%region_1.0 | all-reduce | flops 2048 | bytes 16384 | tf_op jit(solution)/shard_map/psum | solution.py:240
  134.9 0.0 all-to-all-done.1.parts_ref
  134.9 0.5 shard_map.75
  135.4 11.6 %all_to_all.15.small_ref = f32[16,8,128]{2,1,0:T(8,128)S(1)} all-to-all(f32[16,8,128]{2,1,0:T(8,128)S(1)} %maximum_maximum_fusion), channel_id=1, replica_groups=mesh['y'=8,'zh'=4,'c'=2,'zl'=2,'x'=4] {'c','zl','x'}, dimensions={0} | all-to-all | bytes 131072 | tf_op jit(solution)/shard_map/all_to_all | solution.py:256
  147.0 0.9 shard_map.76
  148.0 0.1 reshape.35
  148.1 0.7 reshape.36
  (5 shorter events, 0.0 us)
Async XLA Ops:
  0.6 37.0 %copy-start = (bf16[384,384]{1,0:T(8,128)(2,1)S(1)}, bf16[384,384]{1,0:T(8,128)(2,1)}, u32[]{:S(2)}) copy-start(bf16[384,384]{1,0:T(8,128)(2,1)} %tokens_ref) | copy-start | bytes 884740
  23.0 16.6 %collective-permute-start = (bf16[192,1536]{1,0:T(8,128)(2,1)S(1)}, bf16[192,1536]{1,0:T(8,128)(2,1)}, u32[]{:S(2)}, u32[]{:S(2)}) collective-permute-start(bf16[192,1536]{1,0:T(8,128)(2,1)S(1)} %all_gather.3.refs_0_), channel_id=1, source_target_pairs={{64,0},{128,64},{192,128},{256,192},{320,256},{384,320},{448,384},... | collective-permute-start | bytes 1769480 | tf_op jit(solution)/shard_map/ppermute | solution.py:205
  26.2 16.7 %collective-permute-start.2 = (bf16[192,1536]{1,0:T(8,128)(2,1)S(1)}, bf16[192,1536]{1,0:T(8,128)(2,1)}, u32[]{:S(2)}, u32[]{:S(2)}) collective-permute-start(bf16[192,1536]{1,0:T(8,128)(2,1)S(1)} %all_gather.3.refs_0_), channel_id=1, source_target_pairs={{448,0},{0,64},{64,128},{128,192},{192,256},{256,320},{320,384},{3... | collective-permute-start | bytes 1769480 | tf_op jit(solution)/shard_map/ppermute | solution.py:205
  42.9 22.4 %collective-permute-start.4 = (bf16[192,1536]{1,0:T(8,128)(2,1)}, bf16[192,1536]{1,0:T(8,128)(2,1)}, u32[]{:S(2)}, u32[]{:S(2)}) collective-permute-start(bf16[192,1536]{1,0:T(8,128)(2,1)} %collective-permute-done.2.refs_1_), channel_id=1, source_target_pairs={{448,0},{0,64},{64,128},{128,192},{192,256},{256,320},{320,384},{3... | collective-permute-start | bytes 1769480 | tf_op jit(solution)/shard_map/ppermute | solution.py:205
  48.3 15.0 %collective-permute-start.1 = (bf16[192,1536]{1,0:T(8,128)(2,1)}, bf16[192,1536]{1,0:T(8,128)(2,1)}, u32[]{:S(2)}, u32[]{:S(2)}) collective-permute-start(bf16[192,1536]{1,0:T(8,128)(2,1)} %collective-permute-done.refs_0_), channel_id=1, source_target_pairs={{64,0},{128,64},{192,128},{256,192},{320,256},{384,320},{448,384},... | collective-permute-start | bytes 1769480 | tf_op jit(solution)/shard_map/ppermute | solution.py:205
  50.3 19.6 %collective-permute-start.5 = (bf16[384,1536]{1,0:T(8,128)(2,1)}, bf16[384,1536]{1,0:T(8,128)(2,1)}, u32[]{:S(2)}, u32[]{:S(2)}) collective-permute-start(bf16[384,1536]{1,0:T(8,128)(2,1)} %fusion.34.refs_1_.refs_4_.refs_2_), channel_id=1, source_target_pairs={{0,8},{8,0},{1,9},{9,1},{2,10},{10,2},{3,11},{11,3},{4,12},{12,4},... | collective-permute-start | bytes 3538952 | tf_op jit(solution)/shard_map/ppermute | solution.py:25
  53.1 38.3 %all-to-all-start = ((bf16[16,208,384]{2,1,0:T(8,128)(2,1)}), bf16[16,208,384]{2,1,0:T(8,128)(2,1)}, u32[]{:S(2)}, u32[]{:S(2)}) async-start(bf16[16,208,384]{2,1,0:T(8,128)(2,1)} %bitcast.11), calls=%async_computation | async-start | bytes 5111808 | tf_op jit(solution)/shard_map/all_to_all | solution.py:222
  63.4 14.7 %collective-permute-start.3 = (bf16[192,1536]{1,0:T(8,128)(2,1)}, bf16[192,1536]{1,0:T(8,128)(2,1)S(1)}, u32[]{:S(2)}, u32[]{:S(2)}) collective-permute-start(bf16[192,1536]{1,0:T(8,128)(2,1)} %collective-permute-done.1.refs_2_), channel_id=1, source_target_pairs={{64,0},{128,64},{192,128},{256,192},{320,256},{384,320},{448,384},... | collective-permute-start | bytes 1769480 | tf_op jit(solution)/shard_map/ppermute | solution.py:205
  65.3 16.1 %collective-permute-start.7 = (bf16[192,1536]{1,0:T(8,128)(2,1)}, bf16[192,1536]{1,0:T(8,128)(2,1)S(1)}, u32[]{:S(2)}, u32[]{:S(2)}) collective-permute-start(bf16[192,1536]{1,0:T(8,128)(2,1)} %collective-permute-done.4.refs_3_), channel_id=1, source_target_pairs={{448,0},{0,64},{64,128},{128,192},{192,256},{256,320},{320,384},{3... | collective-permute-start | bytes 1769480 | tf_op jit(solution)/shard_map/ppermute | solution.py:205
  78.1 12.2 %collective-permute-start.6 = (bf16[192,1536]{1,0:T(8,128)(2,1)S(1)}, bf16[192,1536]{1,0:T(8,128)(2,1)S(1)}, u32[]{:S(2)}, u32[]{:S(2)}) collective-permute-start(bf16[192,1536]{1,0:T(8,128)(2,1)S(1)} %collective-permute-done.3.refs_0_), channel_id=1, source_target_pairs={{64,0},{128,64},{192,128},{256,192},{320,256},{384,320},{448,384},... | collective-permute-start | bytes 1769480 | tf_op jit(solution)/shard_map/ppermute | solution.py:205
  94.7 7.5 %copy-start.1 = (bf16[384]{0:T(512)(128)(2,1)S(1)}, bf16[384]{0:T(512)(128)(2,1)}, u32[]{:S(2)}) copy-start(bf16[384]{0:T(512)(128)(2,1)} %param.6) | copy-start | bytes 2308
  94.7 40.2 %all-to-all-start.1 = ((bf16[16,192,384]{2,1,0:T(8,128)(2,1)}), bf16[16,192,384]{2,1,0:T(8,128)(2,1)S(1)}, u32[]{:S(2)}, u32[]{:S(2)}) async-start(bf16[16,192,384]{2,1,0:T(8,128)(2,1)} %bitcast.10), calls=%async_computation.1 | async-start | bytes 4718592 | tf_op jit(solution)/shard_map/all_to_all | solution.py:237

commit v17 on v16

--- a/solution.py
+++ b/solution.py
@@ -106,9 +106,10 @@
     )(tokens)
 
 
-def gain_kernel(parts_ref, x_ref, extra_ref, out_ref, stat_ref):
+def gain_kernel(y_ref, parts_ref, x_ref, extra_ref, out_ref, stat_ref):
     @pl.when(pl.program_id(0) == 0)
     def _():
+        out_ref[...] = jnp.zeros_like(out_ref)
         for t in range(2):
             means, squares = [], []
             for m in range(8):
@@ -121,39 +122,54 @@
             rstd = 1.0 / jnp.sqrt(variance + 1e-06)
             stat_ref[t] = jnp.concatenate([mean, rstd] * 4, axis=0)
 
-    per_step, features = x_ref.shape[1], parts_ref.shape[2]
-    for k in range(per_step):
-        total = jnp.zeros((features, 128), F32)
-        for t in range(2):
-            xhat = (x_ref[t, k, :features].astype(F32) - stat_ref[t, 0:1]) * stat_ref[t, 1:2]
-            value = parts_ref[t, k].astype(F32) * xhat
-            total += value[:, :128] + value[:, 128:256] + value[:, 256:]
-        total = jnp.concatenate([total, jnp.zeros((256 - features, 128), F32)], axis=0)
-        row = jnp.sum(total.T, axis=0, keepdims=True)
-        out_ref[pl.ds(pl.program_id(0) * per_step + k, 1), :] = row
-
-
-def gain_share(parts, x_all):
+    out_ref[pl.ds(lax.rem(y_ref[0] + 5 + pl.program_id(0), 8), 1), :] = share_row(parts_ref, x_ref, stat_ref)
+
+
+def share_row(parts_ref, x_ref, stat_ref):
+    features = parts_ref.shape[2]
+    total = jnp.zeros((features, 128), F32)
+    for t in range(2):
+        xhat = (x_ref[t, 0, :features].astype(F32) - stat_ref[t, 0:1]) * stat_ref[t, 1:2]
+        value = parts_ref[t, 0].astype(F32) * xhat
+        total += value[:, :128] + value[:, 128:256] + value[:, 256:]
+    total = jnp.concatenate([total, jnp.zeros((256 - features, 128), F32)], axis=0)
+    return jnp.sum(total.T, axis=0, keepdims=True)
+
+
+def last_kernel(y_ref, parts_ref, x_ref, stat_ref, shares_ref, out_ref):
+    out_ref[...] = shares_ref[...]
+    out_ref[pl.ds(lax.rem(y_ref[0] + 4, 8), 1), :] = share_row(parts_ref, x_ref, stat_ref)
+
+
+def gain_shares(parts, x_all, y, early=None):
     _, _, rows, tokens = parts.shape
     x_all = x_all.reshape(2, 8, rows + EXTRA, tokens)
+    first = 5 if early is None else 4
+    blocks = [
+        pl.BlockSpec((2, 1, r, tokens), lambda m, y: (0, lax.rem(y[0] + first + m, 8), 0, 0))
+        for r in (rows, rows + EXTRA)
+    ]
+    shares = pl.BlockSpec((8, 256), lambda m, _: (0, 0))
+    stat = pl.BlockSpec((2, 8, tokens), lambda m, _: (0, 0, 0))
+    shares_shape = jax.ShapeDtypeStruct((8, 256), F32)
+    if early is not None:
+        return pl.pallas_call(
+            last_kernel,
+            grid_spec=pltpu.PrefetchScalarGridSpec(
+                num_scalar_prefetch=1, grid=(1,), in_specs=blocks + [stat, shares], out_specs=shares
+            ),
+            out_shape=shares_shape,
+            compiler_params=WIDE,
+        )(y, parts, x_all, early[1], early[0])
+    extra = pl.BlockSpec((2, 8, EXTRA, tokens), lambda m, _: (0, 0, rows // EXTRA, 0))
     return pl.pallas_call(
         gain_kernel,
-        grid=(4,),
-        in_specs=[
-            pl.BlockSpec((2, 2, rows, tokens), lambda m: (0, m, 0, 0)),
-            pl.BlockSpec((2, 2, rows + EXTRA, tokens), lambda m: (0, m, 0, 0)),
-            pl.BlockSpec((2, 8, EXTRA, tokens), lambda m: (0, 0, rows // EXTRA, 0)),
-        ],
-        out_specs=[
-            pl.BlockSpec((8, 256), lambda m: (0, 0)),
-            pl.BlockSpec((2, 8, tokens), lambda m: (0, 0, 0)),
-        ],
-        out_shape=[
-            jax.ShapeDtypeStruct((8, 256), F32),
-            jax.ShapeDtypeStruct((2, 8, tokens), F32),
-        ],
+        grid_spec=pltpu.PrefetchScalarGridSpec(
+            num_scalar_prefetch=1, grid=(7,), in_specs=blocks + [extra], out_specs=[shares, stat]
+        ),
+        out_shape=[shares_shape, jax.ShapeDtypeStruct((2, 8, tokens), F32)],
         compiler_params=WIDE,
-    )(parts, x_all, x_all)
+    )(y, parts, x_all, x_all)
 
 
 def sum_kernel(core_ref, parts_ref, x_ref, gain_ref, stat_ref, d_ref, moments_ref):
@@ -232,11 +248,14 @@
     first4 = step(first, 1)
     parts = products([(3, first3), (5, second)], [(0, d_own, 2), (1, d_other, 2)], place, parts)
 
-    first4, parts, x_all = together((first4, parts, x_all))
+    parts, x_all = together((parts, x_all))
+    shares, stat = gain_shares(parts, x_all, here[0])
+
+    first4, parts, x_all, shares, stat = together((first4, parts, x_all, shares, stat))
     parts = products([(4, first4)], [(0, d_own, 1), (1, d_other, 1)], place, parts)
     received = lax.all_to_all(parts.reshape(16, share // 2, rows), CHIPS, 0, 0)
 
-    shares, stat = gain_share(parts, x_all)
+    shares = gain_shares(parts, x_all, here[0], (shares, stat))
     shares = lax.psum(lax.psum(shares, "y"), "zh")
 
     vmem, smem = pl.BlockSpec(memory_space=pltpu.VMEM), pl.BlockSpec(memory_space=pltpu.SMEM)

time: 149 us -> 153 us (1.027)
  Pallas kernels: 24.8 us -> 27.5 us
  blocking collectives: 62.7 us -> 65.3 us
  starting transfers between devices: 38.9 us -> 36.7 us
    ppermute x7, waiting for transfers between devices: 11.8 us -> 6.62 us  [step(): lax.ppermute(array, ('y', 'c'), [(a * 2 + c, b * 2 + c) for a, b, c in mo...]
    all_to_all x1, waiting for transfers between devices: 1.08 us -> 6.29 us  [on_device(): x_all = lax.all_to_all(x_all.reshape(16, -1, rows), CHIPS, 0, 0)]
    psum x2, blocking collectives: 28.7 us -> 31.6 us  [on_device(): shares = lax.psum(lax.psum(shares, 'y'), 'zh')]
    pallas_call x1 -> x2, Pallas kernels: 3.78 us -> 6.56 us  [the longest x1 5.3 us: gain_shares(): pl.pallas_call(gain_kernel, grid_spec=pltpu.PrefetchScalarGridSpec(num_sc...]
    all_to_all x1, starting transfers between devices: 7.52 us -> 5.35 us  [on_device(): received = lax.all_to_all(parts.reshape(16, share // 2, rows), CHIPS, 0, 0)]
  transfers between devices with their start and end apart: 10 -> 10, of which waited for: 5 -> 4; matrix products, arithmetic and copies ran while one was open for 5% -> 5% of each run, Pallas kernels for 14% -> 15%
where the time goes in v17:
time: 153 us; the launch traced here: 152 us
  blocking collectives  65.3 us (43%)
  starting transfers between devices  36.7 us (24%)
  Pallas kernels  27.5 us (18%)
  waiting for transfers between devices  12.9 us (8%)
  other arithmetic  7.7 us (5%)
    psum x2, blocking collectives, on_device(): shares = lax.psum(lax.psum(shares, 'y'), 'zh')  31.6 us
    ppermute x7, starting transfers between devices, step(): lax.ppermute(array, ('y', 'c'), [(a * 2 + c, b * 2 + c) for a, b, c in mo...  22.7 us
    all_gather x1, blocking collectives, on_device(): w0 = lax.all_gather(w_in, 'zh', axis=0, tiled=True)  22.4 us
    pallas_call x5, Pallas kernels, products(): pl.pallas_call(kernel, in_specs=[pl.BlockSpec(memory_space=pltpu.SMEM)] +...  17.7 us
    all_to_all x1, blocking collectives, on_device(): small = lax.all_to_all(jnp.concatenate([small, small], axis=0), CHIPS, 0, 0)  11.3 us
    convert_element_type x1, other arithmetic, on_device(): d_own = gelu_back(act_cotangent.astype(F32))[0].astype(BF16)  7.61 us
    ppermute x7, waiting for transfers between devices, step(): lax.ppermute(array, ('y', 'c'), [(a * 2 + c, b * 2 + c) for a, b, c in mo...  6.62 us
    all_to_all x1, waiting for transfers between devices, on_device(): x_all = lax.all_to_all(x_all.reshape(16, -1, rows), CHIPS, 0, 0)  6.29 us
  transfers between devices with their start and end apart: 10, of which 4 were waited for; matrix products, arithmetic and copies ran while one was open for 5% of the time, Pallas kernels for 15%

profile of v17, /device:TPU:1, one launch (start us, length us, event | category | flops | bytes accessed | tf_op | source)
XLA Modules:
  0.0 151.9 jit_solution(7022930482666822626)
XLA Ops:
  0.6 0.0 copy-start
  0.6 22.4 %all_gather.3.refs_0_ = bf16[192,1536]{1,0:T(8,128)(2,1)S(1)} all-gather(bf16[48,1536]{1,0:T(8,128)(2,1)} %param.8), channel_id=1, replica_groups=mesh['y'=8,'zh'=4,'c'=2,'zl'=2,'x'=4] {'zh'}, dimensions={0}, use_global_device_ids=true | all-gather | bytes 737280 | tf_op jit(solution)/shard_map/all_gather | solution.py:227
  23.0 3.2 %collective-permute-start = (bf16[192,1536]{1,0:T(8,128)(2,1)S(1)}, bf16[192,1536]{1,0:T(8,128)(2,1)}, u32[]{:S(2)}, u32[]{:S(2)}) collective-permute-start(bf16[192,1536]{1,0:T(8,128)(2,1)S(1)} %all_gather.3.refs_0_), channel_id=1, source_target_pairs={{64,0},{128,64},{192,128},{256,192},{320,256},{384,320},{448,384},... | collective-permute-start | bytes 1769480 | tf_op jit(solution)/shard_map/ppermute | solution.py:221
  26.2 3.8 %collective-permute-start.2 = (bf16[192,1536]{1,0:T(8,128)(2,1)S(1)}, bf16[192,1536]{1,0:T(8,128)(2,1)}, u32[]{:S(2)}, u32[]{:S(2)}) collective-permute-start(bf16[192,1536]{1,0:T(8,128)(2,1)S(1)} %all_gather.3.refs_0_), channel_id=1, source_target_pairs={{448,0},{0,64},{64,128},{128,192},{192,256},{256,320},{320,384},{3... | collective-permute-start | bytes 1769480 | tf_op jit(solution)/shard_map/ppermute | solution.py:221
  30.0 7.6 %fusion.34.refs_1_.refs_4_.refs_2_ = bf16[384,1536]{1,0:T(8,128)(2,1)} fusion(bf16[384,1536]{1,0:T(8,128)(2,1)} %param.9, bf16[384,1536]{1,0:T(8,128)(2,1)} %param.7), kind=kLoop, calls=%fused_computation.39 | loop fusion | flops 43646976 | bytes 3538944 | tf_op jit(solution)/shard_map/convert_element_type | solution.py:231
  37.7 0.0 copy-done
  37.7 1.9 %shard_map.68 = (bf16[384,384]{1,0:T(8,128)(2,1)S(1)}, bf16[2,8,208,384]{3,2,1,0:T(8,128)(2,1)}) custom-call(bf16[384,384]{1,0:T(8,128)(2,1)S(1)} %copy-done), custom_call_target="tpu_custom_call" | custom-call | tf_op jit(solution)/shard_map/pallas_call | solution.py:94
  39.6 0.1 pad_add_fusion.place_ref
  39.6 0.0 collective-permute-done.refs_0_
  39.6 3.3 %collective-permute-done.2.refs_1_ = bf16[192,1536]{1,0:T(8,128)(2,1)} collective-permute-done((bf16[192,1536]{1,0:T(8,128)(2,1)S(1)}, bf16[192,1536]{1,0:T(8,128)(2,1)}, u32[]{:S(2)}, u32[]{:S(2)}) %collective-permute-start.2) | collective-permute-done | bytes 589856 | tf_op jit(solution)/shard_map/ppermute | solution.py:221
  42.9 5.4 %collective-permute-start.4 = (bf16[192,1536]{1,0:T(8,128)(2,1)}, bf16[192,1536]{1,0:T(8,128)(2,1)}, u32[]{:S(2)}, u32[]{:S(2)}) collective-permute-start(bf16[192,1536]{1,0:T(8,128)(2,1)} %collective-permute-done.2.refs_1_), channel_id=1, source_target_pairs={{448,0},{0,64},{64,128},{128,192},{192,256},{256,320},{320,384},{3... | collective-permute-start | bytes 1769480 | tf_op jit(solution)/shard_map/ppermute | solution.py:221
  48.3 1.9 %collective-permute-start.1 = (bf16[192,1536]{1,0:T(8,128)(2,1)}, bf16[192,1536]{1,0:T(8,128)(2,1)}, u32[]{:S(2)}, u32[]{:S(2)}) collective-permute-start(bf16[192,1536]{1,0:T(8,128)(2,1)} %collective-permute-done.refs_0_), channel_id=1, source_target_pairs={{64,0},{128,64},{192,128},{256,192},{320,256},{384,320},{448,384},... | collective-permute-start | bytes 1769480 | tf_op jit(solution)/shard_map/ppermute | solution.py:221
  50.3 2.8 %collective-permute-start.5 = (bf16[384,1536]{1,0:T(8,128)(2,1)}, bf16[384,1536]{1,0:T(8,128)(2,1)}, u32[]{:S(2)}, u32[]{:S(2)}) collective-permute-start(bf16[384,1536]{1,0:T(8,128)(2,1)} %fusion.34.refs_1_.refs_4_.refs_2_), channel_id=1, source_target_pairs={{0,8},{8,0},{1,9},{9,1},{2,10},{10,2},{3,11},{11,3},{4,12},{12,4},... | collective-permute-start | bytes 3538952 | tf_op jit(solution)/shard_map/ppermute | solution.py:25
  53.1 5.7 %all-to-all-start = ((bf16[16,208,384]{2,1,0:T(8,128)(2,1)}), bf16[16,208,384]{2,1,0:T(8,128)(2,1)}, u32[]{:S(2)}, u32[]{:S(2)}) async-start(bf16[16,208,384]{2,1,0:T(8,128)(2,1)} %bitcast.12), calls=%async_computation | async-start | bytes 5111808 | tf_op jit(solution)/shard_map/all_to_all | solution.py:238
  58.9 2.5 %shard_map.69.refs_2_ = bf16[2,8,192,384]{3,2,1,0:T(8,128)(2,1)} custom-call(s32[2]{0:T(128)S(1)} %pad_add_fusion.place_ref, bf16[192,1536]{1,0:T(8,128)(2,1)S(1)} %all_gather.3.refs_0_, bf16[384,1536]{1,0:T(8,128)(2,1)} %fusion.34.refs_1_.refs_4_.refs_2_), custom_call_target="tpu_custom_call" | custom-call | flops 274877906944 | bytes 262144 | tf_op jit(solution)/shard_map/pallas_call | solution.py:53
  61.4 2.0 %collective-permute-done.1.refs_2_ = bf16[192,1536]{1,0:T(8,128)(2,1)} collective-permute-done((bf16[192,1536]{1,0:T(8,128)(2,1)}, bf16[192,1536]{1,0:T(8,128)(2,1)}, u32[]{:S(2)}, u32[]{:S(2)}) %collective-permute-start.1) | collective-permute-done | bytes 589856 | tf_op jit(solution)/shard_map/ppermute | solution.py:221
  63.4 1.9 %collective-permute-start.3 = (bf16[192,1536]{1,0:T(8,128)(2,1)}, bf16[192,1536]{1,0:T(8,128)(2,1)S(1)}, u32[]{:S(2)}, u32[]{:S(2)}) collective-permute-start(bf16[192,1536]{1,0:T(8,128)(2,1)} %collective-permute-done.1.refs_2_), channel_id=1, source_target_pairs={{64,0},{128,64},{192,128},{256,192},{320,256},{384,320},{448,384},... | collective-permute-start | bytes 1769480 | tf_op jit(solution)/shard_map/ppermute | solution.py:221
  65.3 0.0 collective-permute-done.4.refs_3_
  65.3 4.6 %collective-permute-start.7 = (bf16[192,1536]{1,0:T(8,128)(2,1)}, bf16[192,1536]{1,0:T(8,128)(2,1)S(1)}, u32[]{:S(2)}, u32[]{:S(2)}) collective-permute-start(bf16[192,1536]{1,0:T(8,128)(2,1)} %collective-permute-done.4.refs_3_), channel_id=1, source_target_pairs={{448,0},{0,64},{64,128},{128,192},{192,256},{256,320},{320,384},{3... | collective-permute-start | bytes 1769480 | tf_op jit(solution)/shard_map/ppermute | solution.py:221
  69.9 0.0 collective-permute-done.5.refs_1_.refs_5_.refs_3_.refs_2_
  69.9 2.5 %shard_map.70.refs_6_ = bf16[2,8,192,384]{3,2,1,0:T(8,128)(2,1)} custom-call(s32[2]{0:T(128)S(1)} %pad_add_fusion.place_ref, bf16[192,1536]{1,0:T(8,128)(2,1)S(1)} %all_gather.3.refs_0_, bf16[384,1536]{1,0:T(8,128)(2,1)} %collective-permute-done.5.refs_1_.refs_5_.refs_3_.refs_2_, ...), custom_call_target="tpu_custom_call", output_to_operand_aliasing={{}: (3, {})} | custom-call | flops 113246208 | bytes 262144 | tf_op jit(solution)/shard_map/pallas_call | solution.py:53
  72.4 5.7 %shard_map.71.refs_4_ = bf16[2,8,192,384]{3,2,1,0:T(8,128)(2,1)} custom-call(s32[2]{0:T(128)S(1)} %pad_add_fusion.place_ref, bf16[192,1536]{1,0:T(8,128)(2,1)} %collective-permute-done.refs_0_, bf16[192,1536]{1,0:T(8,128)(2,1)} %collective-permute-done.2.refs_1_, bf16[192,1536]{1,0:T(8,128)(2,1)} %collective-permute-done.1.refs_2_, ...), custom_call_target="tpu_custom_call", output_to_operand_aliasing={{}: (7, {})} | custom-call | flops 113246208 | bytes 262144 | tf_op jit(solution)/shard_map/pallas_call | solution.py:53
  78.1 0.0 collective-permute-done.3.refs_0_
  78.1 1.9 %collective-permute-start.6 = (bf16[192,1536]{1,0:T(8,128)(2,1)S(1)}, bf16[192,1536]{1,0:T(8,128)(2,1)S(1)}, u32[]{:S(2)}, u32[]{:S(2)}) collective-permute-start(bf16[192,1536]{1,0:T(8,128)(2,1)S(1)} %collective-permute-done.3.refs_0_), channel_id=1, source_target_pairs={{64,0},{128,64},{192,128},{256,192},{320,256},{384,320},{448,384},... | collective-permute-start | bytes 1769480 | tf_op jit(solution)/shard_map/ppermute | solution.py:221
  80.0 1.3 collective-permute-done.7.refs_1_
  81.4 3.7 %shard_map.72.parts_ref.refs_3_ = bf16[2,8,192,384]{3,2,1,0:T(8,128)(2,1)} custom-call(s32[2]{0:T(128)S(1)} %pad_add_fusion.place_ref, bf16[192,1536]{1,0:T(8,128)(2,1)S(1)} %collective-permute-done.3.refs_0_, bf16[192,1536]{1,0:T(8,128)(2,1)S(1)} %collective-permute-done.7.refs_1_, ...), custom_call_target="tpu_custom_call", output_to_operand_aliasing={{}: (5, {})} | custom-call | flops 113246208 | bytes 262144 | tf_op jit(solution)/shard_map/pallas_call | solution.py:53
  85.1 6.3 %all-to-all-done = bf16[16,208,384]{2,1,0:T(8,128)(2,1)} async-done(((bf16[16,208,384]{2,1,0:T(8,128)(2,1)}), bf16[16,208,384]{2,1,0:T(8,128)(2,1)}, u32[]{:S(2)}, u32[]{:S(2)}) %all-to-all-start) | async-done | bytes 2555936 | tf_op jit(solution)/shard_map/all_to_all | solution.py:238
  91.4 5.3 %shard_map.73 = (f32[8,256]{1,0:T(8,128)S(1)}, f32[2,8,384]{2,1,0:T(8,128)S(1)}) custom-call(s32[1]{0:T(128)} %bitcast.1.y_ref, bf16[2,8,192,384]{3,2,1,0:T(8,128)(2,1)} %shard_map.72.parts_ref.refs_3_, bf16[2,8,208,384]{3,2,1,0:T(8,128)(2,1)} %bitcast.3.x_ref.extra_ref, bf16[2,8,208,384]{3,2,1,0:T(8,128)(2,1)} %bitcast.3.x_ref.extra_ref), custom_call_target="tpu_custom_call" | custom-call | tf_op jit(solution)/shard_map/pallas_call | solution.py:165
  96.7 0.0 collective-permute-done.6.refs_0_
  96.7 3.2 %shard_map.74.parts_ref = bf16[2,8,192,384]{3,2,1,0:T(8,128)(2,1)} custom-call(s32[2]{0:T(128)S(1)} %pad_add_fusion.place_ref, bf16[192,1536]{1,0:T(8,128)(2,1)S(1)} %collective-permute-done.6.refs_0_, bf16[384,1536]{1,0:T(8,128)(2,1)} %fusion.34.refs_1_.refs_4_.refs_2_, ...), custom_call_target="tpu_custom_call", output_to_operand_aliasing={{}: (4, {})} | custom-call | flops 113246208 | bytes 262144 | tf_op jit(solution)/shard_map/pallas_call | solution.py:53
  100.0 0.0 copy-start.1
  100.0 5.4 %all-to-all-start.1 = ((bf16[16,192,384]{2,1,0:T(8,128)(2,1)}), bf16[16,192,384]{2,1,0:T(8,128)(2,1)S(1)}, u32[]{:S(2)}, u32[]{:S(2)}) async-start(bf16[16,192,384]{2,1,0:T(8,128)(2,1)} %bitcast.11), calls=%async_computation.1 | async-start | bytes 4718592 | tf_op jit(solution)/shard_map/all_to_all | solution.py:256
  105.3 0.0 copy-done.1
  105.3 0.1 reshape.42.gain_ref
  105.5 1.3 shard_map.76
  106.7 14.5 %psum.14 = f32[8,256]{1,0:T(8,128)S(1)} all-reduce(f32[8,256]{1,0:T(8,128)S(1)} %shard_map.76), channel_id=1, replica_groups=mesh['y'=8,'zh'=4,'c'=2,'zl'=2,'x'=4] {'y'}, use_global_device_ids=true, to_apply=%region_0.0 | all-reduce | flops 2048 | bytes 16384 | tf_op jit(solution)/shard_map/psum | solution.py:259
  121.3 17.1 %psum.15 = f32[8,2,128]{2,1,0:T(2,128)S(1)} all-reduce(f32[8,2,128]{2,1,0:T(2,128)S(1)} %reshape.38), channel_id=1, replica_groups=mesh['y'=8,'zh'=4,'c'=2,'zl'=2,'x'=4] {'zh'}, use_global_device_ids=true, to_apply=%region_1.0 | all-reduce | flops 2048 | bytes 16384 | tf_op jit(solution)/shard_map/psum | solution.py:259
  138.4 0.0 all-to-all-done.1.parts_ref
  138.4 0.5 shard_map.75
  138.9 11.3 %all_to_all.15.small_ref = f32[16,8,128]{2,1,0:T(8,128)S(1)} all-to-all(f32[16,8,128]{2,1,0:T(8,128)S(1)} %maximum_maximum_fusion), channel_id=1, replica_groups=mesh['y'=8,'zh'=4,'c'=2,'zl'=2,'x'=4] {'c','zl','x'}, dimensions={0} | all-to-all | bytes 131072 | tf_op jit(solution)/shard_map/all_to_all | solution.py:275
  150.2 0.9 shard_map.77
  151.2 0.1 reshape.39
  151.3 0.7 reshape.40
  (5 shorter events, 0.0 us)
Async XLA Ops:
  0.6 37.0 %copy-start = (bf16[384,384]{1,0:T(8,128)(2,1)S(1)}, bf16[384,384]{1,0:T(8,128)(2,1)}, u32[]{:S(2)}) copy-start(bf16[384,384]{1,0:T(8,128)(2,1)} %tokens_ref) | copy-start | bytes 884740
  23.0 16.6 %collective-permute-start = (bf16[192,1536]{1,0:T(8,128)(2,1)S(1)}, bf16[192,1536]{1,0:T(8,128)(2,1)}, u32[]{:S(2)}, u32[]{:S(2)}) collective-permute-start(bf16[192,1536]{1,0:T(8,128)(2,1)S(1)} %all_gather.3.refs_0_), channel_id=1, source_target_pairs={{64,0},{128,64},{192,128},{256,192},{320,256},{384,320},{448,384},... | collective-permute-start | bytes 1769480 | tf_op jit(solution)/shard_map/ppermute | solution.py:221
  26.2 16.7 %collective-permute-start.2 = (bf16[192,1536]{1,0:T(8,128)(2,1)S(1)}, bf16[192,1536]{1,0:T(8,128)(2,1)}, u32[]{:S(2)}, u32[]{:S(2)}) collective-permute-start(bf16[192,1536]{1,0:T(8,128)(2,1)S(1)} %all_gather.3.refs_0_), channel_id=1, source_target_pairs={{448,0},{0,64},{64,128},{128,192},{192,256},{256,320},{320,384},{3... | collective-permute-start | bytes 1769480 | tf_op jit(solution)/shard_map/ppermute | solution.py:221
  42.9 22.4 %collective-permute-start.4 = (bf16[192,1536]{1,0:T(8,128)(2,1)}, bf16[192,1536]{1,0:T(8,128)(2,1)}, u32[]{:S(2)}, u32[]{:S(2)}) collective-permute-start(bf16[192,1536]{1,0:T(8,128)(2,1)} %collective-permute-done.2.refs_1_), channel_id=1, source_target_pairs={{448,0},{0,64},{64,128},{128,192},{192,256},{256,320},{320,384},{3... | collective-permute-start | bytes 1769480 | tf_op jit(solution)/shard_map/ppermute | solution.py:221
  48.3 15.0 %collective-permute-start.1 = (bf16[192,1536]{1,0:T(8,128)(2,1)}, bf16[192,1536]{1,0:T(8,128)(2,1)}, u32[]{:S(2)}, u32[]{:S(2)}) collective-permute-start(bf16[192,1536]{1,0:T(8,128)(2,1)} %collective-permute-done.refs_0_), channel_id=1, source_target_pairs={{64,0},{128,64},{192,128},{256,192},{320,256},{384,320},{448,384},... | collective-permute-start | bytes 1769480 | tf_op jit(solution)/shard_map/ppermute | solution.py:221
  50.3 19.6 %collective-permute-start.5 = (bf16[384,1536]{1,0:T(8,128)(2,1)}, bf16[384,1536]{1,0:T(8,128)(2,1)}, u32[]{:S(2)}, u32[]{:S(2)}) collective-permute-start(bf16[384,1536]{1,0:T(8,128)(2,1)} %fusion.34.refs_1_.refs_4_.refs_2_), channel_id=1, source_target_pairs={{0,8},{8,0},{1,9},{9,1},{2,10},{10,2},{3,11},{11,3},{4,12},{12,4},... | collective-permute-start | bytes 3538952 | tf_op jit(solution)/shard_map/ppermute | solution.py:25
  53.1 38.3 %all-to-all-start = ((bf16[16,208,384]{2,1,0:T(8,128)(2,1)}), bf16[16,208,384]{2,1,0:T(8,128)(2,1)}, u32[]{:S(2)}, u32[]{:S(2)}) async-start(bf16[16,208,384]{2,1,0:T(8,128)(2,1)} %bitcast.12), calls=%async_computation | async-start | bytes 5111808 | tf_op jit(solution)/shard_map/all_to_all | solution.py:238
  63.4 14.7 %collective-permute-start.3 = (bf16[192,1536]{1,0:T(8,128)(2,1)}, bf16[192,1536]{1,0:T(8,128)(2,1)S(1)}, u32[]{:S(2)}, u32[]{:S(2)}) collective-permute-start(bf16[192,1536]{1,0:T(8,128)(2,1)} %collective-permute-done.1.refs_2_), channel_id=1, source_target_pairs={{64,0},{128,64},{192,128},{256,192},{320,256},{384,320},{448,384},... | collective-permute-start | bytes 1769480 | tf_op jit(solution)/shard_map/ppermute | solution.py:221
  65.3 16.1 %collective-permute-start.7 = (bf16[192,1536]{1,0:T(8,128)(2,1)}, bf16[192,1536]{1,0:T(8,128)(2,1)S(1)}, u32[]{:S(2)}, u32[]{:S(2)}) collective-permute-start(bf16[192,1536]{1,0:T(8,128)(2,1)} %collective-permute-done.4.refs_3_), channel_id=1, source_target_pairs={{448,0},{0,64},{64,128},{128,192},{192,256},{256,320},{320,384},{3... | collective-permute-start | bytes 1769480 | tf_op jit(solution)/shard_map/ppermute | solution.py:221
  78.1 18.6 %collective-permute-start.6 = (bf16[192,1536]{1,0:T(8,128)(2,1)S(1)}, bf16[192,1536]{1,0:T(8,128)(2,1)S(1)}, u32[]{:S(2)}, u32[]{:S(2)}) collective-permute-start(bf16[192,1536]{1,0:T(8,128)(2,1)S(1)} %collective-permute-done.3.refs_0_), channel_id=1, source_target_pairs={{64,0},{128,64},{192,128},{256,192},{320,256},{384,320},{448,384},... | collective-permute-start | bytes 1769480 | tf_op jit(solution)/shard_map/ppermute | solution.py:221
  100.0 5.4 %copy-start.1 = (bf16[384]{0:T(512)(128)(2,1)S(1)}, bf16[384]{0:T(512)(128)(2,1)}, u32[]{:S(2)}) copy-start(bf16[384]{0:T(512)(128)(2,1)} %param.6) | copy-start | bytes 2308
  100.0 38.4 %all-to-all-start.1 = ((bf16[16,192,384]{2,1,0:T(8,128)(2,1)}), bf16[16,192,384]{2,1,0:T(8,128)(2,1)S(1)}, u32[]{:S(2)}, u32[]{:S(2)}) async-start(bf16[16,192,384]{2,1,0:T(8,128)(2,1)} %bitcast.11), calls=%async_computation.1 | async-start | bytes 4718592 | tf_op jit(solution)/shard_map/all_to_all | solution.py:256

commit v18 on v16

--- a/solution.py
+++ b/solution.py
@@ -38,8 +38,8 @@
         for h, (k, _, count) in enumerate(halves):
             half = lax.rem(place_ref[1] + k, 2)
             out = lax.dot_general(
-                w[: count * rows], d_refs[h][...], (((1,), (1,)), ((), ())), preferred_element_type=F32
-            ).astype(BF16)
+                d_refs[h][...], w[: count * rows], (((1,), (1,)), ((), ())), preferred_element_type=F32
+            ).T.astype(BF16)
             for g, (offset, _) in enumerate(groups[:count]):
                 held[h, g] = out[g * rows : (g + 1) * rows]
                 block = lax.rem(place_ref[0] + offset + place_ref[1] * ((8 - 2 * offset) % 8), 8)

time: 149 us -> 149 us (level)
  transfers between devices with their start and end apart: 10 -> 10, of which waited for: 5 -> 5; matrix products, arithmetic and copies ran while one was open for 5% -> 5% of each run, Pallas kernels for 14% -> 13%
where the time goes in v18:
time: 149 us
  blocking collectives  62.7 us (42%)
  starting transfers between devices  38.9 us (26%)
  Pallas kernels  24.5 us (16%)
  waiting for transfers between devices  13.2 us (9%)
  other arithmetic  7.7 us (5%)
    psum x2, blocking collectives, on_device(): shares = lax.psum(lax.psum(shares, 'y'), 'zh')  28.7 us
    ppermute x7, starting transfers between devices, step(): lax.ppermute(array, ('y', 'c'), [(a * 2 + c, b * 2 + c) for a, b, c in mo...  22.7 us
    all_gather x1, blocking collectives, on_device(): w0 = lax.all_gather(w_in, 'zh', axis=0, tiled=True)  22.4 us
    pallas_call x5, Pallas kernels, products(): pl.pallas_call(kernel, in_specs=[pl.BlockSpec(memory_space=pltpu.SMEM)] +...  17.4 us
    ppermute x7, waiting for transfers between devices, step(): lax.ppermute(array, ('y', 'c'), [(a * 2 + c, b * 2 + c) for a, b, c in mo...  11.7 us
    all_to_all x1, blocking collectives, on_device(): small = lax.all_to_all(jnp.concatenate([small, small], axis=0), CHIPS, 0, 0)  11.6 us
    convert_element_type x1, other arithmetic, on_device(): d_own = gelu_back(act_cotangent.astype(F32))[0].astype(BF16)  7.61 us
    all_to_all x1, starting transfers between devices, on_device(): received = lax.all_to_all(parts.reshape(16, share // 2, rows), CHIPS, 0, 0)  7.55 us
  transfers between devices with their start and end apart: 10, of which 5 were waited for; matrix products, arithmetic and copies ran while one was open for 5% of the time, Pallas kernels for 13%

profile of v18, /device:TPU:1, one launch (start us, length us, event | category | flops | bytes accessed | tf_op | source)
XLA Modules:
  0.0 148.7 jit_solution(12491987266452267247)
XLA Ops:
  0.6 0.0 copy-start
  0.6 22.4 %all_gather.3.refs_0_ = bf16[192,1536]{1,0:T(8,128)(2,1)S(1)} all-gather(bf16[48,1536]{1,0:T(8,128)(2,1)} %param.8), channel_id=1, replica_groups=mesh['y'=8,'zh'=4,'c'=2,'zl'=2,'x'=4] {'zh'}, dimensions={0}, use_global_device_ids=true | all-gather | bytes 737280 | tf_op jit(solution)/shard_map/all_gather | solution.py:211
  23.0 3.2 %collective-permute-start = (bf16[192,1536]{1,0:T(8,128)(2,1)S(1)}, bf16[192,1536]{1,0:T(8,128)(2,1)}, u32[]{:S(2)}, u32[]{:S(2)}) collective-permute-start(bf16[192,1536]{1,0:T(8,128)(2,1)S(1)} %all_gather.3.refs_0_), channel_id=1, source_target_pairs={{64,0},{128,64},{192,128},{256,192},{320,256},{384,320},{448,384},... | collective-permute-start | bytes 1769480 | tf_op jit(solution)/shard_map/ppermute | solution.py:205
  26.2 3.8 %collective-permute-start.2 = (bf16[192,1536]{1,0:T(8,128)(2,1)S(1)}, bf16[192,1536]{1,0:T(8,128)(2,1)}, u32[]{:S(2)}, u32[]{:S(2)}) collective-permute-start(bf16[192,1536]{1,0:T(8,128)(2,1)S(1)} %all_gather.3.refs_0_), channel_id=1, source_target_pairs={{448,0},{0,64},{64,128},{128,192},{192,256},{256,320},{320,384},{3... | collective-permute-start | bytes 1769480 | tf_op jit(solution)/shard_map/ppermute | solution.py:205
  30.0 7.6 %fusion.34.refs_1_.refs_4_.refs_2_ = bf16[384,1536]{1,0:T(8,128)(2,1)} fusion(bf16[384,1536]{1,0:T(8,128)(2,1)} %param.9, bf16[384,1536]{1,0:T(8,128)(2,1)} %param.7), kind=kLoop, calls=%fused_computation.39 | loop fusion | flops 43646976 | bytes 3538944 | tf_op jit(solution)/shard_map/convert_element_type | solution.py:215
  37.7 0.0 copy-done
  37.7 1.9 %shard_map.68 = (bf16[384,384]{1,0:T(8,128)(2,1)S(1)}, bf16[2,8,208,384]{3,2,1,0:T(8,128)(2,1)}) custom-call(bf16[384,384]{1,0:T(8,128)(2,1)S(1)} %copy-done), custom_call_target="tpu_custom_call" | custom-call | tf_op jit(solution)/shard_map/pallas_call | solution.py:94
  39.6 0.1 pad_add_fusion.place_ref
  39.6 0.0 collective-permute-done.refs_0_
  39.6 3.3 %collective-permute-done.2.refs_1_ = bf16[192,1536]{1,0:T(8,128)(2,1)} collective-permute-done((bf16[192,1536]{1,0:T(8,128)(2,1)S(1)}, bf16[192,1536]{1,0:T(8,128)(2,1)}, u32[]{:S(2)}, u32[]{:S(2)}) %collective-permute-start.2) | collective-permute-done | bytes 589856 | tf_op jit(solution)/shard_map/ppermute | solution.py:205
  42.9 5.4 %collective-permute-start.4 = (bf16[192,1536]{1,0:T(8,128)(2,1)}, bf16[192,1536]{1,0:T(8,128)(2,1)}, u32[]{:S(2)}, u32[]{:S(2)}) collective-permute-start(bf16[192,1536]{1,0:T(8,128)(2,1)} %collective-permute-done.2.refs_1_), channel_id=1, source_target_pairs={{448,0},{0,64},{64,128},{128,192},{192,256},{256,320},{320,384},{3... | collective-permute-start | bytes 1769480 | tf_op jit(solution)/shard_map/ppermute | solution.py:205
  48.3 1.9 %collective-permute-start.1 = (bf16[192,1536]{1,0:T(8,128)(2,1)}, bf16[192,1536]{1,0:T(8,128)(2,1)}, u32[]{:S(2)}, u32[]{:S(2)}) collective-permute-start(bf16[192,1536]{1,0:T(8,128)(2,1)} %collective-permute-done.refs_0_), channel_id=1, source_target_pairs={{64,0},{128,64},{192,128},{256,192},{320,256},{384,320},{448,384},... | collective-permute-start | bytes 1769480 | tf_op jit(solution)/shard_map/ppermute | solution.py:205
  50.3 2.8 %collective-permute-start.5 = (bf16[384,1536]{1,0:T(8,128)(2,1)}, bf16[384,1536]{1,0:T(8,128)(2,1)}, u32[]{:S(2)}, u32[]{:S(2)}) collective-permute-start(bf16[384,1536]{1,0:T(8,128)(2,1)} %fusion.34.refs_1_.refs_4_.refs_2_), channel_id=1, source_target_pairs={{0,8},{8,0},{1,9},{9,1},{2,10},{10,2},{3,11},{11,3},{4,12},{12,4},... | collective-permute-start | bytes 3538952 | tf_op jit(solution)/shard_map/ppermute | solution.py:25
  53.1 5.7 %all-to-all-start = ((bf16[16,208,384]{2,1,0:T(8,128)(2,1)}), bf16[16,208,384]{2,1,0:T(8,128)(2,1)}, u32[]{:S(2)}, u32[]{:S(2)}) async-start(bf16[16,208,384]{2,1,0:T(8,128)(2,1)} %bitcast.11), calls=%async_computation | async-start | bytes 5111808 | tf_op jit(solution)/shard_map/all_to_all | solution.py:222
  58.9 2.5 %shard_map.69.refs_2_ = bf16[2,8,192,384]{3,2,1,0:T(8,128)(2,1)} custom-call(s32[2]{0:T(128)S(1)} %pad_add_fusion.place_ref, bf16[192,1536]{1,0:T(8,128)(2,1)S(1)} %all_gather.3.refs_0_, bf16[384,1536]{1,0:T(8,128)(2,1)} %fusion.34.refs_1_.refs_4_.refs_2_), custom_call_target="tpu_custom_call" | custom-call | flops 274877906944 | bytes 262144 | tf_op jit(solution)/shard_map/pallas_call | solution.py:53
  61.4 2.0 %collective-permute-done.1.refs_2_ = bf16[192,1536]{1,0:T(8,128)(2,1)} collective-permute-done((bf16[192,1536]{1,0:T(8,128)(2,1)}, bf16[192,1536]{1,0:T(8,128)(2,1)}, u32[]{:S(2)}, u32[]{:S(2)}) %collective-permute-start.1) | collective-permute-done | bytes 589856 | tf_op jit(solution)/shard_map/ppermute | solution.py:205
  63.4 1.9 %collective-permute-start.3 = (bf16[192,1536]{1,0:T(8,128)(2,1)}, bf16[192,1536]{1,0:T(8,128)(2,1)S(1)}, u32[]{:S(2)}, u32[]{:S(2)}) collective-permute-start(bf16[192,1536]{1,0:T(8,128)(2,1)} %collective-permute-done.1.refs_2_), channel_id=1, source_target_pairs={{64,0},{128,64},{192,128},{256,192},{320,256},{384,320},{448,384},... | collective-permute-start | bytes 1769480 | tf_op jit(solution)/shard_map/ppermute | solution.py:205
  65.3 0.0 collective-permute-done.4.refs_3_
  65.3 4.6 %collective-permute-start.7 = (bf16[192,1536]{1,0:T(8,128)(2,1)}, bf16[192,1536]{1,0:T(8,128)(2,1)S(1)}, u32[]{:S(2)}, u32[]{:S(2)}) collective-permute-start(bf16[192,1536]{1,0:T(8,128)(2,1)} %collective-permute-done.4.refs_3_), channel_id=1, source_target_pairs={{448,0},{0,64},{64,128},{128,192},{192,256},{256,320},{320,384},{3... | collective-permute-start | bytes 1769480 | tf_op jit(solution)/shard_map/ppermute | solution.py:205
  69.9 0.0 collective-permute-done.5.refs_1_.refs_5_.refs_3_.refs_2_
  69.9 2.5 %shard_map.70.refs_6_ = bf16[2,8,192,384]{3,2,1,0:T(8,128)(2,1)} custom-call(s32[2]{0:T(128)S(1)} %pad_add_fusion.place_ref, bf16[192,1536]{1,0:T(8,128)(2,1)S(1)} %all_gather.3.refs_0_, bf16[384,1536]{1,0:T(8,128)(2,1)} %collective-permute-done.5.refs_1_.refs_5_.refs_3_.refs_2_, ...), custom_call_target="tpu_custom_call", output_to_operand_aliasing={{}: (3, {})} | custom-call | flops 113246208 | bytes 262144 | tf_op jit(solution)/shard_map/pallas_call | solution.py:53
  72.4 5.3 %shard_map.71.refs_4_ = bf16[2,8,192,384]{3,2,1,0:T(8,128)(2,1)} custom-call(s32[2]{0:T(128)S(1)} %pad_add_fusion.place_ref, bf16[192,1536]{1,0:T(8,128)(2,1)} %collective-permute-done.refs_0_, bf16[192,1536]{1,0:T(8,128)(2,1)} %collective-permute-done.2.refs_1_, bf16[192,1536]{1,0:T(8,128)(2,1)} %collective-permute-done.1.refs_2_, ...), custom_call_target="tpu_custom_call", output_to_operand_aliasing={{}: (7, {})} | custom-call | flops 113246208 | bytes 262144 | tf_op jit(solution)/shard_map/pallas_call | solution.py:53
  77.7 0.0 collective-permute-done.3.refs_0_
  77.7 1.9 %collective-permute-start.6 = (bf16[192,1536]{1,0:T(8,128)(2,1)S(1)}, bf16[192,1536]{1,0:T(8,128)(2,1)S(1)}, u32[]{:S(2)}, u32[]{:S(2)}) collective-permute-start(bf16[192,1536]{1,0:T(8,128)(2,1)S(1)} %collective-permute-done.3.refs_0_), channel_id=1, source_target_pairs={{64,0},{128,64},{192,128},{256,192},{320,256},{384,320},{448,384},... | collective-permute-start | bytes 1769480 | tf_op jit(solution)/shard_map/ppermute | solution.py:205
  79.6 1.7 %collective-permute-done.7.refs_1_ = bf16[192,1536]{1,0:T(8,128)(2,1)S(1)} collective-permute-done((bf16[192,1536]{1,0:T(8,128)(2,1)}, bf16[192,1536]{1,0:T(8,128)(2,1)S(1)}, u32[]{:S(2)}, u32[]{:S(2)}) %collective-permute-start.7) | collective-permute-done | bytes 589856 | tf_op jit(solution)/shard_map/ppermute | solution.py:205
  81.4 3.8 %shard_map.72.refs_3_ = bf16[2,8,192,384]{3,2,1,0:T(8,128)(2,1)} custom-call(s32[2]{0:T(128)S(1)} %pad_add_fusion.place_ref, bf16[192,1536]{1,0:T(8,128)(2,1)S(1)} %collective-permute-done.3.refs_0_, bf16[192,1536]{1,0:T(8,128)(2,1)S(1)} %collective-permute-done.7.refs_1_, ...), custom_call_target="tpu_custom_call", output_to_operand_aliasing={{}: (5, {})} | custom-call | flops 113246208 | bytes 262144 | tf_op jit(solution)/shard_map/pallas_call | solution.py:53
  85.2 4.7 %collective-permute-done.6.refs_0_ = bf16[192,1536]{1,0:T(8,128)(2,1)S(1)} collective-permute-done((bf16[192,1536]{1,0:T(8,128)(2,1)S(1)}, bf16[192,1536]{1,0:T(8,128)(2,1)S(1)}, u32[]{:S(2)}, u32[]{:S(2)}) %collective-permute-start.6) | collective-permute-done | bytes 589856 | tf_op jit(solution)/shard_map/ppermute | solution.py:205
  90.0 1.5 all-to-all-done
  91.4 3.2 %shard_map.73.parts_ref = bf16[2,8,192,384]{3,2,1,0:T(8,128)(2,1)} custom-call(s32[2]{0:T(128)S(1)} %pad_add_fusion.place_ref, bf16[192,1536]{1,0:T(8,128)(2,1)S(1)} %collective-permute-done.6.refs_0_, bf16[384,1536]{1,0:T(8,128)(2,1)} %fusion.34.refs_1_.refs_4_.refs_2_, ...), custom_call_target="tpu_custom_call", output_to_operand_aliasing={{}: (4, {})} | custom-call | flops 113246208 | bytes 262144 | tf_op jit(solution)/shard_map/pallas_call | solution.py:53
  94.7 0.0 copy-start.1
  94.7 7.5 %all-to-all-start.1 = ((bf16[16,192,384]{2,1,0:T(8,128)(2,1)}), bf16[16,192,384]{2,1,0:T(8,128)(2,1)S(1)}, u32[]{:S(2)}, u32[]{:S(2)}) async-start(bf16[16,192,384]{2,1,0:T(8,128)(2,1)} %bitcast.10), calls=%async_computation.1 | async-start | bytes 4718592 | tf_op jit(solution)/shard_map/all_to_all | solution.py:237
  102.2 0.0 copy-done.1
  102.2 0.1 reshape.38.gain_ref
  102.3 3.8 %shard_map.74 = (f32[8,256]{1,0:T(8,128)S(1)}, f32[2,8,384]{2,1,0:T(8,128)S(1)}) custom-call(bf16[2,8,192,384]{3,2,1,0:T(8,128)(2,1)} %shard_map.73.parts_ref, bf16[2,8,208,384]{3,2,1,0:T(8,128)(2,1)} %bitcast.4.x_ref.extra_ref, bf16[2,8,208,384]{3,2,1,0:T(8,128)(2,1)} %bitcast.4.x_ref.extra_ref), custom_call_target="tpu_custom_call" | custom-call | tf_op jit(solution)/shard_map/pallas_call | solution.py:139
  106.1 15.5 %psum.14 = f32[8,256]{1,0:T(8,128)S(1)} all-reduce(f32[8,256]{1,0:T(8,128)S(1)} %get-tuple-element.49), channel_id=1, replica_groups=mesh['y'=8,'zh'=4,'c'=2,'zl'=2,'x'=4] {'y'}, use_global_device_ids=true, to_apply=%region_0.0 | all-reduce | flops 2048 | bytes 16384 | tf_op jit(solution)/shard_map/psum | solution.py:240
  121.7 13.2 %psum.15 = f32[8,2,128]{2,1,0:T(2,128)S(1)} all-reduce(f32[8,2,128]{2,1,0:T(2,128)S(1)} %reshape.34), channel_id=1, replica_groups=mesh['y'=8,'zh'=4,'c'=2,'zl'=2,'x'=4] {'zh'}, use_global_device_ids=true, to_apply=%region_1.0 | all-reduce | flops 2048 | bytes 16384 | tf_op jit(solution)/shard_map/psum | solution.py:240
  134.9 0.0 all-to-all-done.1.parts_ref
  134.9 0.5 shard_map.75
  135.4 11.6 %all_to_all.15.small_ref = f32[16,8,128]{2,1,0:T(8,128)S(1)} all-to-all(f32[16,8,128]{2,1,0:T(8,128)S(1)} %maximum_maximum_fusion), channel_id=1, replica_groups=mesh['y'=8,'zh'=4,'c'=2,'zl'=2,'x'=4] {'c','zl','x'}, dimensions={0} | all-to-all | bytes 131072 | tf_op jit(solution)/shard_map/all_to_all | solution.py:256
  147.0 0.9 shard_map.76
  148.0 0.1 reshape.35
  148.1 0.7 reshape.36
  (5 shorter events, 0.0 us)
Async XLA Ops:
  0.6 37.0 %copy-start = (bf16[384,384]{1,0:T(8,128)(2,1)S(1)}, bf16[384,384]{1,0:T(8,128)(2,1)}, u32[]{:S(2)}) copy-start(bf16[384,384]{1,0:T(8,128)(2,1)} %tokens_ref) | copy-start | bytes 884740
  23.0 16.6 %collective-permute-start = (bf16[192,1536]{1,0:T(8,128)(2,1)S(1)}, bf16[192,1536]{1,0:T(8,128)(2,1)}, u32[]{:S(2)}, u32[]{:S(2)}) collective-permute-start(bf16[192,1536]{1,0:T(8,128)(2,1)S(1)} %all_gather.3.refs_0_), channel_id=1, source_target_pairs={{64,0},{128,64},{192,128},{256,192},{320,256},{384,320},{448,384},... | collective-permute-start | bytes 1769480 | tf_op jit(solution)/shard_map/ppermute | solution.py:205
  26.2 16.7 %collective-permute-start.2 = (bf16[192,1536]{1,0:T(8,128)(2,1)S(1)}, bf16[192,1536]{1,0:T(8,128)(2,1)}, u32[]{:S(2)}, u32[]{:S(2)}) collective-permute-start(bf16[192,1536]{1,0:T(8,128)(2,1)S(1)} %all_gather.3.refs_0_), channel_id=1, source_target_pairs={{448,0},{0,64},{64,128},{128,192},{192,256},{256,320},{320,384},{3... | collective-permute-start | bytes 1769480 | tf_op jit(solution)/shard_map/ppermute | solution.py:205
  42.9 22.4 %collective-permute-start.4 = (bf16[192,1536]{1,0:T(8,128)(2,1)}, bf16[192,1536]{1,0:T(8,128)(2,1)}, u32[]{:S(2)}, u32[]{:S(2)}) collective-permute-start(bf16[192,1536]{1,0:T(8,128)(2,1)} %collective-permute-done.2.refs_1_), channel_id=1, source_target_pairs={{448,0},{0,64},{64,128},{128,192},{192,256},{256,320},{320,384},{3... | collective-permute-start | bytes 1769480 | tf_op jit(solution)/shard_map/ppermute | solution.py:205
  48.3 15.0 %collective-permute-start.1 = (bf16[192,1536]{1,0:T(8,128)(2,1)}, bf16[192,1536]{1,0:T(8,128)(2,1)}, u32[]{:S(2)}, u32[]{:S(2)}) collective-permute-start(bf16[192,1536]{1,0:T(8,128)(2,1)} %collective-permute-done.refs_0_), channel_id=1, source_target_pairs={{64,0},{128,64},{192,128},{256,192},{320,256},{384,320},{448,384},... | collective-permute-start | bytes 1769480 | tf_op jit(solution)/shard_map/ppermute | solution.py:205
  50.3 19.6 %collective-permute-start.5 = (bf16[384,1536]{1,0:T(8,128)(2,1)}, bf16[384,1536]{1,0:T(8,128)(2,1)}, u32[]{:S(2)}, u32[]{:S(2)}) collective-permute-start(bf16[384,1536]{1,0:T(8,128)(2,1)} %fusion.34.refs_1_.refs_4_.refs_2_), channel_id=1, source_target_pairs={{0,8},{8,0},{1,9},{9,1},{2,10},{10,2},{3,11},{11,3},{4,12},{12,4},... | collective-permute-start | bytes 3538952 | tf_op jit(solution)/shard_map/ppermute | solution.py:25
  53.1 38.3 %all-to-all-start = ((bf16[16,208,384]{2,1,0:T(8,128)(2,1)}), bf16[16,208,384]{2,1,0:T(8,128)(2,1)}, u32[]{:S(2)}, u32[]{:S(2)}) async-start(bf16[16,208,384]{2,1,0:T(8,128)(2,1)} %bitcast.11), calls=%async_computation | async-start | bytes 5111808 | tf_op jit(solution)/shard_map/all_to_all | solution.py:222
  63.4 14.3 %collective-permute-start.3 = (bf16[192,1536]{1,0:T(8,128)(2,1)}, bf16[192,1536]{1,0:T(8,128)(2,1)S(1)}, u32[]{:S(2)}, u32[]{:S(2)}) collective-permute-start(bf16[192,1536]{1,0:T(8,128)(2,1)} %collective-permute-done.1.refs_2_), channel_id=1, source_target_pairs={{64,0},{128,64},{192,128},{256,192},{320,256},{384,320},{448,384},... | collective-permute-start | bytes 1769480 | tf_op jit(solution)/shard_map/ppermute | solution.py:205
  65.3 16.1 %collective-permute-start.7 = (bf16[192,1536]{1,0:T(8,128)(2,1)}, bf16[192,1536]{1,0:T(8,128)(2,1)S(1)}, u32[]{:S(2)}, u32[]{:S(2)}) collective-permute-start(bf16[192,1536]{1,0:T(8,128)(2,1)} %collective-permute-done.4.refs_3_), channel_id=1, source_target_pairs={{448,0},{0,64},{64,128},{128,192},{192,256},{256,320},{320,384},{3... | collective-permute-start | bytes 1769480 | tf_op jit(solution)/shard_map/ppermute | solution.py:205
  77.7 12.2 %collective-permute-start.6 = (bf16[192,1536]{1,0:T(8,128)(2,1)S(1)}, bf16[192,1536]{1,0:T(8,128)(2,1)S(1)}, u32[]{:S(2)}, u32[]{:S(2)}) collective-permute-start(bf16[192,1536]{1,0:T(8,128)(2,1)S(1)} %collective-permute-done.3.refs_0_), channel_id=1, source_target_pairs={{64,0},{128,64},{192,128},{256,192},{320,256},{384,320},{448,384},... | collective-permute-start | bytes 1769480 | tf_op jit(solution)/shard_map/ppermute | solution.py:205
  94.7 7.6 %copy-start.1 = (bf16[384]{0:T(512)(128)(2,1)S(1)}, bf16[384]{0:T(512)(128)(2,1)}, u32[]{:S(2)}) copy-start(bf16[384]{0:T(512)(128)(2,1)} %param.6) | copy-start | bytes 2308
  94.7 40.2 %all-to-all-start.1 = ((bf16[16,192,384]{2,1,0:T(8,128)(2,1)}), bf16[16,192,384]{2,1,0:T(8,128)(2,1)S(1)}, u32[]{:S(2)}, u32[]{:S(2)}) async-start(bf16[16,192,384]{2,1,0:T(8,128)(2,1)} %bitcast.10), calls=%async_computation.1 | async-start | bytes 4718592 | tf_op jit(solution)/shard_map/all_to_all | solution.py:237
